TPU v7x, 128 devices: a whole 4x4x4 slice. The times are simulated.
128 devices in a mesh: bin: 8 (over x, z_hi), tile: 16 (over z_lo, y, core).
Axes of the slice: x: 4, y: 4, z: 4 (z_hi: 2, z_lo: 2; z = z_hi * 2 + z_lo), core: 2. Of those that a mesh axis runs over, the one named last changes fastest.
Arguments:
- embeddings: bfloat16 [8192, 512], P('bin'), may hold values from -6 to 6
- w_left: bfloat16 [512, 128], replicated, may hold values from -0.25 to 0.25
- w_right: bfloat16 [512, 128], replicated, may hold values from -0.25 to 0.25
- pair_bias: float32 [5, 128], replicated, may hold values from -3 to 3
- w_pair: bfloat16 [128, 128], replicated, may hold values from -0.5 to 0.5
- b_pair: float32 [128], replicated, may hold values from -3 to 3
- w_out: float32 [128], replicated, may hold values from -0.5 to 0.5
- tile_list: int32 [8, 16, 6, 3], P('bin', 'tile'), may hold values from -1 to 63, as said below
- target: bfloat16 [8, 16, 6, 128, 128], P('bin', 'tile'), may hold values from -6 to 6
Outputs:
- predicted: bfloat16 [8, 16, 6, 128, 128], P('bin', 'tile')
- grad_emb: bfloat16 [8192, 512], P('bin')
- grad_wleft: float32 [512, 128], replicated
- grad_wright: float32 [512, 128], replicated
- grad_bias: float32 [5, 128], replicated
- grad_wpair: float32 [128, 128], replicated
- grad_bpair: float32 [128], replicated
- grad_wout: float32 [128], replicated
Inputs may be any that keep to these rules, and one draw needn't show every extreme that they name: `tile_list`: each device's listed tiles come first, then empty slots with -1 in all three fields. A listed tile of a device in bin block b has its row block among b*8 .. (b+1)*8 - 1, offset 0..4, column block = row block + offset, below 64; no tile is listed twice. In every draw one device of each bin block lists 6 tiles.
All inputs are finite; a program needn't handle non-finite values.
Results may differ from a plain program's by a relative error of at most 0.011.
Values may be sent and summed in bfloat16 or wider, within the bound.
No kernel may reach another device: no remote copies, remote signals or barrier semaphores. Data moves between devices by JAX's collectives and lax.ppermute only.
A program may use at most 64 MiB of HBM per device.

v0:
```python
import jax
import jax.numpy as jnp
from jax import lax
from jax.sharding import PartitionSpec as P


def from_behind(block, axis, distance):
    devices = range(lax.axis_size(axis))
    route = [(i - distance, i) for i in devices if i - distance in devices]
    return lax.ppermute(block, axis, route)


def tile_pass(row_panel, col_panel, bias_row, target_tile, w_pair, b_pair, w_out):
    tile_width = row_panel.shape[0]
    feature_count = row_panel.shape[1]
    pre_one = (
        row_panel.astype(jnp.float32)[:, None, :]
        + col_panel.astype(jnp.float32)[None, :, :]
        + bias_row
    )
    first_act = (
        jnp.maximum(pre_one, 0.0)
        .astype(jnp.bfloat16)
        .reshape(tile_width * tile_width, feature_count)
    )
    pre_two = jnp.dot(first_act, w_pair, preferred_element_type=jnp.float32) + b_pair
    second_act = jnp.maximum(pre_two, 0.0)
    contact = jnp.sum(second_act * w_out, axis=1)
    residual_slope = (contact - target_tile.reshape(-1).astype(jnp.float32)) / tile_width
    back_two = (residual_slope[:, None] * w_out * (pre_two > 0)).astype(jnp.bfloat16)
    grad_out = jnp.sum(residual_slope[:, None] * second_act, axis=0)
    grad_bpair = jnp.sum(back_two.astype(jnp.float32), axis=0)
    grad_wpair = jnp.dot(first_act.T, back_two, preferred_element_type=jnp.float32)
    back_one = jnp.dot(back_two, w_pair.T, preferred_element_type=jnp.float32).reshape(
        tile_width, tile_width, feature_count
    )
    back_one = jnp.where(pre_one > 0, back_one, 0.0)
    return (
        contact.reshape(tile_width, tile_width).astype(jnp.bfloat16),
        jnp.sum(back_one, axis=1),
        jnp.sum(back_one, axis=0),
        jnp.sum(back_one, axis=(0, 1)),
        grad_wpair,
        grad_bpair,
        grad_out,
    )


def process(
    row_source,
    row_base,
    col_source,
    col_base,
    slot_list,
    slot_target,
    slot_total,
    pair_bias,
    w_pair,
    b_pair,
    w_out,
):
    slot_count = slot_list.shape[0]
    tile_width = slot_target.shape[1]
    diag_count = pair_bias.shape[0]
    initial = (
        jnp.zeros((slot_count, tile_width, tile_width), jnp.bfloat16),
        jnp.zeros(row_source.shape, jnp.float32),
        jnp.zeros(col_source.shape, jnp.float32),
        jnp.zeros(pair_bias.shape, jnp.float32),
        jnp.zeros(w_pair.shape, jnp.float32),
        jnp.zeros(b_pair.shape, jnp.float32),
        jnp.zeros(w_out.shape, jnp.float32),
    )

    def visit_slot(index_slot, running):
        predicted, row_grad, col_grad, bias_grad, wpair_grad, bpair_grad, out_grad = running
        slot_entry = slot_list[index_slot]
        start_row = (slot_entry[0] - row_base) * tile_width
        start_col = (slot_entry[1] - col_base) * tile_width
        offset_now = slot_entry[2]
        panel_row = lax.dynamic_slice_in_dim(row_source, start_row, tile_width, 0)
        panel_col = lax.dynamic_slice_in_dim(col_source, start_col, tile_width, 0)
        bias_row = lax.dynamic_index_in_dim(pair_bias, offset_now, 0, keepdims=False)
        pass_out = tile_pass(
            panel_row, panel_col, bias_row, slot_target[index_slot], w_pair, b_pair, w_out
        )
        predicted = lax.dynamic_update_index_in_dim(predicted, pass_out[0], index_slot, 0)
        row_grad = lax.dynamic_update_slice_in_dim(
            row_grad,
            lax.dynamic_slice_in_dim(row_grad, start_row, tile_width, 0) + pass_out[1],
            start_row,
            0,
        )
        col_grad = lax.dynamic_update_slice_in_dim(
            col_grad,
            lax.dynamic_slice_in_dim(col_grad, start_col, tile_width, 0) + pass_out[2],
            start_col,
            0,
        )
        hits = (jnp.arange(diag_count, dtype=jnp.int32) == offset_now).astype(jnp.float32)
        bias_grad = bias_grad + hits[:, None] * pass_out[3]
        return (
            predicted,
            row_grad,
            col_grad,
            bias_grad,
            wpair_grad + pass_out[4],
            bpair_grad + pass_out[5],
            out_grad + pass_out[6],
        )

    return lax.fori_loop(0, slot_total, visit_slot, initial)


def per_device(embeddings, w_left, w_right, pair_bias, w_pair, b_pair, w_out, tile_list, target):
    bin_index = lax.axis_index("bin")
    tile_index = lax.axis_index("tile")
    tile_count = lax.axis_size("tile")
    shard_rows = embeddings.shape[0]
    tile_width = target.shape[-1]
    block_count = shard_rows // tile_width
    share_rows = shard_rows // tile_count
    row_base = bin_index * block_count
    share_emb = lax.dynamic_slice_in_dim(embeddings, tile_index * share_rows, share_rows, 0)
    left_share = jnp.dot(share_emb, w_left, preferred_element_type=jnp.float32).astype(jnp.bfloat16)
    right_share = jnp.dot(share_emb, w_right, preferred_element_type=jnp.float32).astype(
        jnp.bfloat16
    )
    row_source, own_right = (
        lax.all_gather(left_share, "tile", axis=0, tiled=True),
        lax.all_gather(right_share, "tile", axis=0, tiled=True),
    )
    next_right = from_behind(own_right, "bin", -1)
    col_source = jnp.concatenate([own_right, next_right], axis=0)
    own_list = tile_list[0, 0]
    own_total = jnp.sum((own_list[:, 2] >= 0).astype(jnp.int32))
    result = process(
        row_source,
        row_base,
        col_source,
        row_base,
        own_list,
        target[0, 0],
        own_total,
        pair_bias,
        w_pair,
        b_pair,
        w_out,
    )
    predicted = result[0]
    row_grad, col_grad = (result[1], result[2])
    own_cols = col_grad[:shard_rows] + from_behind(col_grad[shard_rows:], "bin", 1)
    row_share, col_share = (
        lax.psum_scatter(row_grad, "tile", scatter_dimension=0, tiled=True),
        lax.psum_scatter(own_cols, "tile", scatter_dimension=0, tiled=True),
    )
    row_low = row_share.astype(jnp.bfloat16)
    col_low = col_share.astype(jnp.bfloat16)
    grad_rows = (
        jnp.dot(row_low, w_left.T, preferred_element_type=jnp.float32)
        + jnp.dot(col_low, w_right.T, preferred_element_type=jnp.float32)
    ).astype(jnp.bfloat16)
    grad_emb = lax.all_gather(grad_rows, "tile", axis=0, tiled=True)
    weight_sums = lax.psum(
        (
            jnp.dot(share_emb.T, row_low, preferred_element_type=jnp.float32),
            jnp.dot(share_emb.T, col_low, preferred_element_type=jnp.float32),
            result[3],
            result[4],
            result[5],
            result[6],
        ),
        ("bin", "tile"),
    )
    return (
        predicted[None, None],
        grad_emb,
        weight_sums[0],
        weight_sums[1],
        weight_sums[2],
        weight_sums[3],
        weight_sums[4],
        weight_sums[5],
    )


def solution(mesh):
    return jax.shard_map(
        per_device,
        mesh=mesh,
        in_specs=(
            P("bin", None),
            P(),
            P(),
            P(),
            P(),
            P(),
            P(),
            P("bin", "tile", None, None),
            P("bin", "tile", None, None, None),
        ),
        out_specs=(
            P("bin", "tile", None, None, None),
            P("bin", None),
            P(),
            P(),
            P(),
            P(),
            P(),
            P(),
        ),
        check_vma=False,
    )
```

profile of v0, /device:TPU:1, one launch (start us, length us, event | category | flops | bytes accessed | tf_op | source)
XLA Modules:
  0.0 576.3 jit_solution(4982525365195079666)
XLA Ops:
  7.2 1.2 copy-done
  9.5 22.3 %all_gather.10 = bf16[1024,128]{1,0:T(8,128)(2,1)S(1)} all-gather(bf16[64,128]{1,0:T(8,128)(2,1)S(1)} %convolution_convert_fusion), channel_id=1, replica_groups=mesh['bin'=8,'tile'=16] {'tile'}, dimensions={0}, use_global_device_ids=true | all-gather | bytes 278528 | tf_op jit(solution)/shard_map/all_gather | solution.py:131
  31.8 1.3 collective-permute-start
  35.5 18.9 %all_gather.9 = bf16[1024,128]{1,0:T(8,128)(2,1)} all-gather(bf16[64,128]{1,0:T(8,128)(2,1)S(1)} %convolution_convert_fusion.1), channel_id=1, replica_groups=mesh['bin'=8,'tile'=16] {'tile'}, dimensions={0}, use_global_device_ids=true | all-gather | bytes 278528 | tf_op jit(solution)/shard_map/all_gather | solution.py:130
  55.3 66.5 %while.22 = (s32[]{:T(128)}, bf16[6,128,128]{2,1,0:T(8,128)(2,1)}, f32[1024,128]{1,0:T(8,128)S(1)}, f32[2048,128]{1,0:T(8,128)S(1)}, f32[5,128]{1,0:T(8,128)S(1)...) while((s32[]{:T(128)}, bf16[6,128,128]{2,1,0:T(8,128)(2,1)}, ...), condition=%wide.region_8.9_spmd, body=%wide.region_1.8_spmd.sunk | while | flops 1669432448 | bytes 119163552 | solution.py:112
  58.7 4.5 broadcast_add_fusion.2
  65.8 3.9 maximum_convert_fusion.2
  69.8 2.5 multiply_reduce_fusion.3
  73.6 7.1 %convert_reduce_fusion.2 = (f32[128]{0:T(128)S(1)}, bf16[16384,128]{1,0:T(8,128)(2,1)S(1)}, f32[128]{0:T(128)S(1)}) fusion(f32[128]{0:T(128)S(1)} %copy-done.5, f32[16384]{0:T(1024)S(1)} %fusion.51, f32[16384,128]{1,0:T(8,128)S(1)} %get-tuple-element.298), kind=kLoop, calls=%fused_computation.3.clone.1 | loop fusion | flops 18874112 | bytes 12649984 | tf_op jit(solution)/shard_map/while/body/reduce_sum | solution.py:32
  80.8 2.4 select_reduce_fusion.2
  83.2 3.0 fusion.52
  86.9 1.3 convolution_add_fusion.4
  91.6 4.5 broadcast_add_fusion.2
  98.7 3.9 maximum_convert_fusion.2
  102.7 2.5 multiply_reduce_fusion.3
  106.5 7.1 %convert_reduce_fusion.2 = (f32[128]{0:T(128)S(1)}, bf16[16384,128]{1,0:T(8,128)(2,1)S(1)}, f32[128]{0:T(128)S(1)}) fusion(f32[128]{0:T(128)S(1)} %copy-done.5, f32[16384]{0:T(1024)S(1)} %fusion.51, f32[16384,128]{1,0:T(8,128)S(1)} %get-tuple-element.298), kind=kLoop, calls=%fused_computation.3.clone.1 | loop fusion | flops 18874112 | bytes 12649984 | tf_op jit(solution)/shard_map/while/body/reduce_sum | solution.py:32
  113.7 2.4 select_reduce_fusion.2
  116.1 3.0 fusion.52
  119.8 1.3 convolution_add_fusion.4
  122.7 1.3 collective-permute-start.1
  124.1 7.0 %collective-permute-done.1 = f32[1024,128]{1,0:T(8,128)S(1)} collective-permute-done((f32[1024,128]{1,0:T(8,128)S(1)}, f32[1024,128]{1,0:T(8,128)S(1)}, u32[]{:S(2)}, u32[]{:S(2)}) %collective-permute-start.1) | collective-permute-done | bytes 524320 | tf_op jit(solution)/shard_map/ppermute | solution.py:10
  132.0 179.9 %reduce-scatter.3.cloned.1.call-done = f32[64,128]{1,0:T(8,128)} async-done(((f32[1024,128]{1,0:T(8,128)}), f32[64,128]{1,0:T(8,128)}) %reduce-scatter.3.cloned.1.call-update) | async-done | bytes 32784 | tf_op jit(solution)/shard_map/reduce_scatter | solution.py:154
  312.8 60.8 %reduce-scatter.5.cloned.1.call-done = f32[64,128]{1,0:T(8,128)} async-done(((f32[1024,128]{1,0:T(8,128)}), f32[64,128]{1,0:T(8,128)}) %reduce-scatter.5.cloned.1.call-update) | async-done | bytes 32784 | tf_op jit(solution)/shard_map/reduce_scatter | solution.py:155
  373.6 1.7 fusion.5
  375.4 1.7 fusion.8
  377.1 1.7 fusion.6
  378.8 68.4 %all-reduce = (f32[5,128]{1,0:T(8,128)}, f32[128]{0:T(128)}, f32[128]{0:T(128)}) all-reduce(f32[5,128]{1,0:T(8,128)S(1)} %get-tuple-element.110, f32[128]{0:T(128)S(1)} %get-tuple-element.112, f32[128]{0:T(128)S(1)} %get-tuple-element.113), channel_id=1, replica_groups=mesh['bin'=8,'tile'=16] {'bin','tile'}, use_global_device_ids=true, to_apply=%region_13.14 | all-reduce | flops 896 | bytes 7168 | tf_op jit(solution)/shard_map/psum | solution.py:164
  447.2 115.5 %all-reduce.4.cloned.1.call-done = (f32[512,128]{1,0:T(8,128)}, f32[512,128]{1,0:T(8,128)}, f32[128,128]{1,0:T(8,128)}) async-done(((f32[512,128]{1,0:T(8,128)}, f32[512,128]{1,0:T(8,128)}, f32[128,128]{1,0:T(8,128)}), (f32[512,128]{1,0:T(8,128)}, f32[512,128]{1,0:T(8,128)}, f32[128,128]{1,0:T(8,128)})) %all-reduce.4.cloned.1.call-update) | async-done | bytes 589840 | tf_op jit(solution)/shard_map/psum | solution.py:164
  562.7 2.3 copy.51
  565.0 1.7 copy.52
  566.6 1.7 copy.53
  568.3 1.5 copy.54
  (78 shorter events, 15.7 us)
Async XLA Ops:
  7.2 1.2 copy-start
  7.2 304.7 %reduce-scatter.3.cloned.1.call-start = ((), (), s32[]{:S(2)}) async-start(), calls=%async_computation.2 | async-start | bytes 557056 | tf_op jit(solution)/shard_map/reduce_scatter | solution.py:154
  31.8 22.6 %collective-permute-start = (bf16[1024,128]{1,0:T(8,128)(2,1)S(1)}, bf16[1024,128]{1,0:T(8,128)(2,1)S(1)}, u32[]{:S(2)}, u32[]{:S(2)}) collective-permute-start(bf16[1024,128]{1,0:T(8,128)(2,1)S(1)} %all_gather.10), channel_id=1, source_target_pairs={{16,0},{32,16},{48,32},{64,48},{80,64},{96,80},{112,96},{17,1},{33... | collective-permute-start | bytes 786440 | tf_op jit(solution)/shard_map/ppermute | solution.py:10
  55.3 256.6 %copy-start.4 = (bf16[512,128]{1,0:T(8,128)(2,1)S(1)}, bf16[512,128]{1,0:T(8,128)(2,1)}, u32[]{:S(2)}) copy-start(bf16[512,128]{1,0:T(8,128)(2,1)} %param.12) | copy-start | bytes 393220
  63.2 6.6 %copy-start.2 = (bf16[128,128]{1,0:T(8,128)(2,1)S(1)}, bf16[128,128]{1,0:T(8,128)(2,1)}, u32[]{:S(2)}) copy-start(bf16[128,128]{1,0:T(8,128)(2,1)} %get-tuple-element.372) | copy-start | bytes 98308 | tf_op jit(solution)/shard_map/while
  63.2 6.6 %copy-start.5 = (f32[128]{0:T(128)S(1)}, f32[128]{0:T(128)}, u32[]{:S(2)}) copy-start(f32[128]{0:T(128)} %get-tuple-element.374) | copy-start | bytes 1540 | tf_op jit(solution)/shard_map/while
  63.2 6.6 %copy-start.6 = (f32[128]{0:T(128)S(1)}, f32[128]{0:T(128)}, u32[]{:S(2)}) copy-start(f32[128]{0:T(128)} %get-tuple-element.373) | copy-start | bytes 1540 | tf_op jit(solution)/shard_map/while
  69.7 11.0 %slice-start = ((s8[8388608]{0:T(1024)(128)(4,1)}), s8[4194304]{0:T(1024)(128)(4,1)S(1)}, s32[]{:S(2)}) async-start(s8[8388608]{0:T(1024)(128)(4,1)} %bitcast.64), calls=%async_computation.6 | async-start | bytes 8388608 | tf_op jit(solution)/shard_map/while
  69.8 11.0 %slice-start.1 = ((s8[8388608]{0:T(1024)(128)(4,1)}), s8[4194304]{0:T(1024)(128)(4,1)S(1)}, s32[]{:S(2)}) async-start(s8[8388608]{0:T(1024)(128)(4,1)} %bitcast.64), calls=%async_computation.7 | async-start | bytes 8388608 | tf_op jit(solution)/shard_map/while
  96.1 6.6 %copy-start.2 = (bf16[128,128]{1,0:T(8,128)(2,1)S(1)}, bf16[128,128]{1,0:T(8,128)(2,1)}, u32[]{:S(2)}) copy-start(bf16[128,128]{1,0:T(8,128)(2,1)} %get-tuple-element.372) | copy-start | bytes 98308 | tf_op jit(solution)/shard_map/while
  96.1 6.6 %copy-start.5 = (f32[128]{0:T(128)S(1)}, f32[128]{0:T(128)}, u32[]{:S(2)}) copy-start(f32[128]{0:T(128)} %get-tuple-element.374) | copy-start | bytes 1540 | tf_op jit(solution)/shard_map/while
  96.1 6.6 %copy-start.6 = (f32[128]{0:T(128)S(1)}, f32[128]{0:T(128)}, u32[]{:S(2)}) copy-start(f32[128]{0:T(128)} %get-tuple-element.373) | copy-start | bytes 1540 | tf_op jit(solution)/shard_map/while
  102.6 11.0 %slice-start = ((s8[8388608]{0:T(1024)(128)(4,1)}), s8[4194304]{0:T(1024)(128)(4,1)S(1)}, s32[]{:S(2)}) async-start(s8[8388608]{0:T(1024)(128)(4,1)} %bitcast.64), calls=%async_computation.6 | async-start | bytes 8388608 | tf_op jit(solution)/shard_map/while
  102.7 11.0 %slice-start.1 = ((s8[8388608]{0:T(1024)(128)(4,1)}), s8[4194304]{0:T(1024)(128)(4,1)S(1)}, s32[]{:S(2)}) async-start(s8[8388608]{0:T(1024)(128)(4,1)} %bitcast.64), calls=%async_computation.7 | async-start | bytes 8388608 | tf_op jit(solution)/shard_map/while
  121.8 0.8 copy-start.1
  121.8 256.9 %copy-start.3 = (f32[128,128]{1,0:T(8,128)}, f32[128,128]{1,0:T(8,128)S(1)}, u32[]{:S(2)}) copy-start(f32[128,128]{1,0:T(8,128)S(1)} %get-tuple-element.111) | copy-start | bytes 196612
  122.6 250.9 %reduce-scatter.5.cloned.1.call-start = ((), (), s32[]{:S(2)}) async-start(), calls=%async_computation.3 | async-start | bytes 557056 | tf_op jit(solution)/shard_map/reduce_scatter | solution.py:155
  122.7 8.4 %collective-permute-start.1 = (f32[1024,128]{1,0:T(8,128)S(1)}, f32[1024,128]{1,0:T(8,128)S(1)}, u32[]{:S(2)}, u32[]{:S(2)}) collective-permute-start(f32[1024,128]{1,0:T(8,128)S(1)} %slice.23), channel_id=1, source_target_pairs={{0,16},{16,32},{32,48},{48,64},{64,80},{80,96},{96,112},{1,17},{17... | collective-permute-start | bytes 1572872 | tf_op jit(solution)/shard_map/ppermute | solution.py:10
  132.0 315.2 %all-gather.2.cloned.1.call-start = ((), (), s32[]{:S(2)}) async-start(), calls=%async_computation.4 | async-start | bytes 1114112 | tf_op jit(solution)/shard_map/all_gather | solution.py:163
  375.3 187.4 %all-reduce.4.cloned.1.call-start = ((), (), s32[]{:S(2)}) async-start(), calls=%async_computation.5 | async-start | bytes 1179648 | tf_op jit(solution)/shard_map/psum | solution.py:164
Sparse Core Ops, SparseCore 0:
  122.8 189.1 reduce-scatter.2
  314.4 59.1 reduce-scatter.4
  375.9 35.1 all-gather.1
  416.6 146.0 all-reduce.3
where the time goes:
time: 579 us; the launch traced here: 576 us
  waiting for transfers between devices  363 us (63%)
  blocking collectives  110 us (19%)
  other arithmetic  44.3 us (8%)
  matrix products  20.4 us (4%)
  between operations  13.9 us (2%)
  local copies, waits for them, and re-layouts  13.2 us (2%)
  loops' own time  8.8 us (2%)
    reduce_scatter x1, waiting for transfers between devices, per_device(): lax.psum_scatter(row_grad, 'tile', scatter_dimension=0, tiled=True)  180 us
    psum x1, waiting for transfers between devices, per_device(): lax.psum((jnp.dot(share_emb.T, row_low, preferred_element_type=jnp.float3...  116 us
    psum x1, blocking collectives, per_device(): lax.psum((jnp.dot(share_emb.T, row_low, preferred_element_type=jnp.float3...  68.4 us
    reduce_scatter x1, waiting for transfers between devices, per_device(): lax.psum_scatter(own_cols, 'tile', scatter_dimension=0, tiled=True)  60.8 us
    all_gather x1, blocking collectives, per_device(): lax.all_gather(right_share, 'tile', axis=0, tiled=True)  22.3 us
    all_gather x1, blocking collectives, per_device(): lax.all_gather(left_share, 'tile', axis=0, tiled=True)  18.9 us
    reduce_sum x2, other arithmetic, tile_pass(): grad_bpair = jnp.sum(back_two.astype(jnp.float32), axis=0)  14.2 us
  transfers between devices with their start and end apart: 6, of which 4 were waited for; matrix products, arithmetic and copies ran while one was open for 1% of the time, Pallas kernels for 0%

commit v1 on v0

v1 whole, which is shorter than its diff:
```python
import jax
import jax.numpy as jnp
from jax import lax
from jax.experimental import pallas as pl
from jax.experimental.pallas import tpu as pltpu
from jax.sharding import PartitionSpec as P

F32 = jnp.float32
BF16 = jnp.bfloat16
GROUP = 16
SHARE = 4
VMEM = pl.BlockSpec(memory_space=pltpu.VMEM)
SMEM = pl.BlockSpec(memory_space=pltpu.SMEM)
LIMIT = pltpu.CompilerParams(vmem_limit_bytes=32 * 1024 * 1024)


def place():
    tile = lax.axis_index("tile")
    return lax.rem(tile, 2), lax.div(tile, 8)


def project_kernel(
    emb_hbm, left_hbm, right_hbm, left_ref, right_ref, full_ref, emb_ref, left_w_ref, right_w_ref, sems
):
    copies = [
        pltpu.make_async_copy(source, target, sems.at[k])
        for k, (source, target) in enumerate(
            ((left_hbm, left_w_ref), (right_hbm, right_w_ref), (emb_hbm, emb_ref))
        )
    ]
    for copy in copies:
        copy.start()
    for copy in copies:
        copy.wait()
    core, z_lo = place()
    width = left_w_ref.shape[1]
    half = width // 2
    step = width // SHARE
    blocks = emb_ref.shape[0] // width
    weights = jnp.concatenate([left_w_ref[...], right_w_ref[...]], axis=1)
    for block in range(0, blocks, 2):
        both = jnp.dot(
            emb_ref[block * width : (block + 2) * width, :],
            weights,
            preferred_element_type=F32,
        ).astype(BF16).astype(F32)
        for k in range(2):
            left = both[k * width : (k + 1) * width, :width]
            at = (block + k) * half
            left_ref[at : at + half, :width] = left[:half]
            left_ref[at : at + half, width:] = left[half:]
        full_ref[block * width : (block + 2) * width, :] = both[:, width:]
    quarter = (core * 2 + z_lo) * step
    for block in range(blocks):
        at = pl.multiple_of(block * width + quarter, step)
        right_ref[block * step : (block + 1) * step, :] = full_ref[pl.ds(at, step), :]


def split_kernel(list_mine, list_other, mine_ref, other_ref, keep_ref, send_ref, list_ref, flip_ref):
    core, z_lo = place()
    for ref, owner in ((list_mine, core), (list_other, 1 - core)):
        for slot in range(ref.shape[0]):
            for k in range(3):
                list_ref[owner * ref.shape[0] + slot, k] = ref[slot, k]
    slots, width, _ = mine_ref.shape
    step = width // SHARE
    keep_at = pl.multiple_of((core * 2 + z_lo) * step, step)
    send_at = pl.multiple_of((core * 2 + 1 - z_lo) * step, step)
    for ref, owner in ((mine_ref, core), (other_ref, 1 - core)):
        for slot in range(slots):
            flip_ref[slot] = (ref[slot].astype(F32) * (1.0 / width)).T
            keep_ref[owner * slots + slot] = flip_ref[slot, pl.ds(keep_at, step), :].astype(BF16)
            send_ref[owner * slots + slot] = flip_ref[slot, pl.ds(send_at, step), :].astype(BF16)


def join_kernel(keep_ref, back_ref, other_ref, pred_ref, flip_ref):
    core, z_lo = place()
    slots, width, _ = pred_ref.shape
    step = width // SHARE
    spots = [
        pl.multiple_of((side * 2 + deep) * step, step)
        for side in (core, 1 - core)
        for deep in (z_lo, 1 - z_lo)
    ]
    for slot in range(slots):
        flip_ref[slot, pl.ds(spots[0], step), :] = keep_ref[core * slots + slot].astype(F32)
        flip_ref[slot, pl.ds(spots[1], step), :] = back_ref[core * slots + slot].astype(F32)
        flip_ref[slot, pl.ds(spots[2], step), :] = other_ref[slot, :step].astype(F32)
        flip_ref[slot, pl.ds(spots[3], step), :] = other_ref[slot, step:].astype(F32)
        pred_ref[slot] = flip_ref[slot].T.astype(BF16)


def pair_kernel(
    list_a, list_b,
    left_ref, right_ref, emb_ref, next_ref, right_w_ref, bias_ref, target_a, target_b,
    w_ref, b_ref, out_ref,
    pred_a, pred_b, sum_ref, col_ref, edge_ref,
    table, right_all, target_all, pred_all, row_all, col_all, outer_all, bias_all,
    w_two, out_two, back_two, b_two, first_0, first_1, slope_0, slope_1,
):
    core, z_lo = place()
    chip_slots, step, width = target_a.shape
    pairs = width // 2
    blocks = left_ref.shape[0] // pairs
    chunks = pairs // GROUP

    count = jnp.int32(0)
    for source, ref in enumerate((list_a, list_b)):
        for slot in range(chip_slots):
            offset = ref[slot, 2]
            table[3 * count] = lax.rem(ref[slot, 0], blocks)
            table[3 * count + 1] = offset
            table[3 * count + 2] = source * chip_slots + slot
            count = count + jnp.where(offset >= 0, 1, 0)

    w = w_ref[...].astype(F32)
    w_out = out_ref[...]
    back = (w * w_out).T.astype(BF16)
    spread = jnp.broadcast_to(w_out * (1.0 / width), (width, width)).T.astype(BF16)
    for ref, block in ((w_two, w_ref[...]), (out_two, spread), (back_two, back)):
        ref[...] = jnp.zeros_like(ref)
        ref[:width, :width] = block
        ref[width:, width:] = block
    b_two[:, :width] = b_ref[...]
    b_two[:, width:] = b_ref[...]
    own = right_ref.shape[0]
    right_all[:own, :] = right_ref[...]
    right_next = jnp.dot(next_ref[...], right_w_ref[...], preferred_element_type=F32)
    right_all[own:, :] = right_next.astype(BF16).astype(F32)
    target_all[:chip_slots] = target_a[...].astype(F32)
    target_all[chip_slots:] = target_b[...].astype(F32)
    for ref in (pred_all, row_all, col_all, outer_all, bias_all, first_1, slope_1):
        ref[...] = jnp.zeros_like(ref)
    lane = lax.broadcasted_iota(jnp.int32, (step, width), 1)
    spot = lax.rem(lane, pairs)
    ones = jnp.ones((8, GROUP * step), BF16)

    def forward(turn, first_ref, slope_ref):
        job = lax.div(turn, chunks)
        chunk = lax.rem(turn, chunks)
        block, offset, slot = table[3 * job], table[3 * job + 1], table[3 * job + 2]
        at = block * pairs + chunk * GROUP
        shift = chunk * GROUP
        right = right_all[pl.ds(pl.multiple_of((block + offset) * step, step), step), :]
        right = right + bias_ref[pl.ds(offset, 1), :]
        right = jnp.concatenate([right, right], axis=1)
        target = pltpu.roll(target_all[slot], lax.rem(width - shift, width), 1)
        pre = jnp.concatenate(
            [left_ref[pl.ds(at + p, 1), :] + right for p in range(GROUP)], axis=0
        )
        first = jnp.maximum(pre, 0.0).astype(BF16)
        first_ref[...] = first
        act = jnp.dot(first, w_two[...], preferred_element_type=F32) + b_two[...]
        second = jnp.maximum(act, 0.0).astype(BF16)
        contact = jnp.dot(second, out_two[...], preferred_element_type=F32)
        found = jnp.zeros((step, width), F32)
        wanted = []
        for p in range(GROUP):
            pair = []
            for s in range(2):
                k = p + s * pairs
                here = contact[p * step : (p + 1) * step, s * width : (s + 1) * width]
                found = jnp.where(lane == k, here, found)
                pair.append(jnp.broadcast_to(target[:, k : k + 1], (step, width)))
            wanted.append(jnp.concatenate(pair, axis=1))
        slope = (contact - jnp.concatenate(wanted, axis=0)).astype(BF16)
        slope_ref[...] = jnp.where(second > 0, slope, jnp.zeros_like(slope))
        mine = (spot >= shift) & (spot < shift + GROUP)
        pred_all[slot] = jnp.where(mine, pltpu.roll(found, shift, 1), pred_all[slot])

    def backward(turn, first_ref, slope_ref):
        job = lax.div(turn, chunks)
        chunk = lax.rem(turn, chunks)
        block, offset = table[3 * job], table[3 * job + 1]
        at = pl.multiple_of(block * pairs + chunk * GROUP, GROUP)
        first = first_ref[...]
        slope = slope_ref[...]
        back = jnp.dot(slope, back_two[...], preferred_element_type=F32)
        back = jnp.where(first.astype(F32) > 0.0, back, 0.0)
        rows = []
        cols = jnp.zeros((step, 2 * width), F32)
        for p in range(GROUP):
            here = back[p * step : (p + 1) * step]
            rows.append(jnp.sum(here, axis=0, keepdims=True))
            cols = cols + here
        row_all[pl.ds(at, GROUP), :] += jnp.concatenate(rows, axis=0)
        cols = cols[:, :width] + cols[:, width:]
        col_at = pl.multiple_of((block + offset) * step, step)
        col_all[pl.ds(col_at, step), :] += cols
        bias_all[pl.ds(offset, 1), :] += jnp.sum(cols, axis=0, keepdims=True)
        outer = jnp.zeros((width + 8, width), F32)
        for s in range(2):
            lhs = jnp.concatenate([first[:, s * width : (s + 1) * width].T, ones], axis=0)
            outer = outer + jnp.dot(
                lhs, slope[:, s * width : (s + 1) * width], preferred_element_type=F32
            )
        outer_all[...] += outer

    def body(pass_at, _):
        turn = 2 * pass_at
        backward(jnp.maximum(turn - 1, 0), first_1, slope_1)
        forward(turn, first_0, slope_0)
        backward(turn, first_0, slope_0)
        forward(turn + 1, first_1, slope_1)
        return 0

    turns = count * chunks
    lax.fori_loop(0, lax.div(turns, 2), body, 0)

    @pl.when(count > 0)
    def _():
        backward(turns - 1, first_1, slope_1)

    pred = (pred_all[...] * float(width)).astype(BF16)
    pred_a[...] = pred[:chip_slots]
    pred_b[...] = pred[chip_slots:]
    outer = outer_all[:width]
    sum_d = outer_all[width : width + 1]
    bias = bias_all[...]
    line = lax.broadcasted_iota(jnp.int32, bias.shape, 0)
    sum_out = jnp.sum(w * outer, axis=0, keepdims=True) + b_ref[...] * sum_d
    vectors = jnp.where(line == 5, sum_d * w_out, bias)
    vectors = jnp.where(line == 6, sum_out, vectors)
    outer = outer * w_out
    high = vectors.astype(BF16).astype(F32)
    rest = (high, vectors - high)
    col = col_all[...].astype(BF16)
    quarter = (core * 2 + z_lo) * step
    rows = []
    embs = []
    for block in range(blocks):
        here = row_all[block * pairs : (block + 1) * pairs, :].astype(BF16)
        rows += [here[:, :width], here[:, width:]]
        embs.append(emb_ref[pl.ds(pl.multiple_of(block * width + quarter, step), step), :])
    embs.append(next_ref[...])
    contract = (((0,), (0,)), ((), ()))
    grads = (
        lax.dot_general(
            jnp.concatenate(rows, axis=0), emb_ref[...], contract, preferred_element_type=F32
        ).astype(BF16),
        lax.dot_general(
            col, jnp.concatenate(embs, axis=0), contract, preferred_element_type=F32
        ).astype(BF16),
    )
    chips = sum_ref.shape[1]
    for side in range(2):
        for chip in range(chips):
            share = side * chips + chip
            sum_ref[side, chip, :pairs, :] = rows[share]
            grad = grads[side][:, chip // 2 * width : (chip // 2 + 1) * width]
            sum_ref[side, chip, pairs:width, :] = grad[chip % 2 * pairs : (chip % 2 + 1) * pairs]
            more = rest[share] if share < 2 else jnp.zeros_like(high)
            sum_ref[side, chip, width:, :] = jnp.concatenate(
                [outer[8 * share : 8 * share + 8], more], axis=0
            ).astype(BF16)
    col_ref[...] = col_all[:own]
    edge_ref[...] = col[own:]


def last_kernel(
    mine_ref, other_ref, left_w_ref, right_w_ref,
    emb_ref, left_ref, right_ref, bias_ref, w_ref, b_ref, out_ref,
    both_ref, flat_ref,
):
    core, _ = place()
    width = left_w_ref.shape[1]
    pairs = width // 2
    step = width // SHARE
    chips = mine_ref.shape[0]
    lows = []
    for side, grad_ref in enumerate((left_ref, right_ref)):
        for chip in range(chips):
            share = side * chips + chip
            block = jnp.where(core == side, mine_ref[chip], other_ref[chip])
            both_ref[share * pairs : (share + 1) * pairs, :width] = block[:pairs]
            z_lo, y = chip // SHARE, chip % SHARE
            for k in range(2):
                to = (2 * y + k) * width + (side * 2 + z_lo) * step
                at = width + 16 + k * step
                both_ref[to : to + step, width:] = block[at : at + step]
            flat_ref[chip * pairs : (chip + 1) * pairs, :] = block[pairs:width].astype(F32)
            small = block[width : width + 16].astype(F32)
            w_ref[8 * share : 8 * share + 8, :] = small[:8]
            lows.append(small[8:])
        for k in range(chips // 2):
            grad_ref[k * width : (k + 1) * width, :] = flat_ref[k * width : (k + 1) * width, :].T
    vectors = lows[0] + lows[1]
    bias_ref[...] = vectors[:5]
    b_ref[...] = vectors[5:6]
    out_ref[...] = vectors[6:7]
    weights = jnp.concatenate([left_w_ref[...], right_w_ref[...]], axis=1)
    part = 2 * width
    for k in range(both_ref.shape[0] // part):
        emb_ref[k * part : (k + 1) * part, :] = lax.dot_general(
            both_ref[k * part : (k + 1) * part, :],
            weights,
            (((1,), (1,)), ((), ())),
            preferred_element_type=F32,
        ).astype(BF16)


def shape(*dims, dtype=F32):
    return jax.ShapeDtypeStruct(dims, dtype)


def call(kernel, outs, scratch, *args, lists=0, space=VMEM, list_out=0):
    return pl.pallas_call(
        kernel,
        out_shape=outs,
        in_specs=[SMEM] * lists + [space] * (len(args) - lists),
        out_specs=(VMEM,) * (len(outs) - list_out) + (SMEM,) * list_out,
        scratch_shapes=scratch,
        compiler_params=LIMIT,
    )(*args)


def shifted(block, axis, distance):
    devices = range(lax.axis_size(axis))
    route = [(i - distance, i) for i in devices if i - distance in devices]
    return lax.ppermute(block, axis, route)


def swapped(block, axis, bits):
    return lax.ppermute(block, axis, [(i, i ^ bits) for i in range(lax.axis_size(axis))])


def chosen(block, index, size):
    return lax.dynamic_slice_in_dim(block, index * size, size, 0)


def across(block, axis, groups=None):
    return lax.all_to_all(block, axis, 0, 0, axis_index_groups=groups, tiled=True)


def summed(blocks):
    return jnp.sum(blocks.astype(F32), axis=0).astype(BF16)


def per_device(embeddings, w_left, w_right, pair_bias, w_pair, b_pair, w_out, tile_list, target):
    core, z_lo = place()
    slots, width = target.shape[2:4]
    rows, features = embeddings.shape
    blocks = rows // width
    pairs = width // 2
    part = rows // SHARE
    step = width // SHARE
    edge = part // 2
    chip = 2 * slots
    chips = lax.axis_size("tile") // 2
    target = target[0, 0]
    lists = tile_list[0, 0]

    target_other = swapped(target, "tile", 1)
    list_other = swapped(lists, "tile", 1)
    emb_edge = lax.dynamic_slice_in_dim(
        embeddings.reshape(blocks, SHARE, step, features)[: blocks // 2], core * 2 + z_lo, 1, 1
    ).reshape(edge, features)
    emb_next = shifted(emb_edge, "bin", -1)
    left, right = call(
        project_kernel,
        (shape(rows // 2, 2 * width), shape(part, width)),
        [
            pltpu.VMEM((rows, width), F32),
            pltpu.VMEM((rows, features), BF16),
            pltpu.VMEM((features, width), BF16),
            pltpu.VMEM((features, width), BF16),
            pltpu.SemaphoreType.DMA((3,)),
        ],
        embeddings, w_left, w_right, space=pl.BlockSpec(memory_space=pl.ANY),
    )
    quarter = shape(chip, step, width, dtype=BF16)
    target_keep, target_send, list_chip = call(
        split_kernel, (quarter, quarter, shape(chip, 3, dtype=jnp.int32)),
        [pltpu.VMEM((slots, width, width), F32)],
        lists, list_other, target, target_other, lists=2, list_out=1,
    )
    target_deep = swapped(target_send, "tile", 8)
    list_deep = swapped(list_chip, "tile", 8)

    chunk = (GROUP * step, 2 * width)
    pred_keep, pred_send, sums, col, col_edge = call(
        pair_kernel,
        (
            quarter,
            quarter,
            shape(2, chips, width + 16, width, dtype=BF16),
            shape(part, width),
            shape(edge, width, dtype=BF16),
        ),
        [
            pltpu.SMEM((3 * 2 * chip + 8,), jnp.int32),
            pltpu.VMEM((part + edge, width), F32),
            pltpu.VMEM((2 * chip, step, width), F32),
            pltpu.VMEM((2 * chip, step, width), F32),
            pltpu.VMEM((rows // 2, 2 * width), F32),
            pltpu.VMEM((part + edge, width), F32),
            pltpu.VMEM((width + 8, width), F32),
            pltpu.VMEM((8, width), F32),
            pltpu.VMEM((2 * width, 2 * width), BF16),
            pltpu.VMEM((2 * width, 2 * width), BF16),
            pltpu.VMEM((2 * width, 2 * width), BF16),
            pltpu.VMEM((1, 2 * width), F32),
            pltpu.VMEM(chunk, BF16),
            pltpu.VMEM(chunk, BF16),
            pltpu.VMEM(chunk, BF16),
            pltpu.VMEM(chunk, BF16),
        ],
        list_chip, list_deep, left, right, embeddings, emb_next, w_right, pair_bias,
        target_keep, target_deep, w_pair, b_pair[None], w_out[None], lists=2,
    )
    sums_other = swapped(lax.dynamic_index_in_dim(sums, 1 - core, 0, keepdims=False), "tile", 1)
    col_before = shifted(col_edge, "bin", 1)
    sums = lax.dynamic_index_in_dim(sums, core, 0, keepdims=False)
    sums = (sums.astype(F32) + sums_other.astype(F32)).astype(BF16)
    col = jnp.concatenate([col[:edge] + col_before.astype(F32), col[edge:]], axis=0).astype(BF16)
    col = col.reshape(1, chips // 2, 2 * step, width)
    here = (jnp.arange(2) == z_lo).reshape(2, 1, 1, 1)
    col = jnp.where(here, col, jnp.zeros_like(col)).reshape(chips, 2 * step, width)
    groups = [list(range(k, 2 * chips, 2)) for k in range(2)]
    share = summed(across(jnp.concatenate([sums, col], axis=1), "tile", groups))
    weight = share[pairs : width + 16]
    weight = jnp.broadcast_to(weight[None], (lax.axis_size("bin"), *weight.shape))
    weight = summed(across(weight, "bin"))
    share = jnp.concatenate([share[:pairs], weight, share[width + 16 :]], axis=0)
    mine = across(jnp.broadcast_to(share[None], (chips, *share.shape)), "tile", groups)
    other = swapped(mine, "tile", 1)

    pred_back = swapped(pred_send, "tile", 8)
    pred_other = swapped(
        jnp.concatenate(
            [chosen(pred_keep, 1 - core, slots), chosen(pred_back, 1 - core, slots)], axis=1
        ),
        "tile",
        1,
    )
    (predicted,) = call(
        join_kernel, (shape(slots, width, width, dtype=BF16),),
        [pltpu.VMEM((slots, width, width), F32)],
        pred_keep, pred_back, pred_other,
    )
    grads = call(
        last_kernel,
        (
            shape(rows, features, dtype=BF16),
            shape(features, width),
            shape(features, width),
            shape(5, width),
            shape(width, width),
            shape(1, width),
            shape(1, width),
        ),
        [pltpu.VMEM((rows, 2 * width), BF16), pltpu.VMEM((features, width), F32)],
        mine, other, w_left, w_right,
    )
    return (predicted[None, None], *grads[:5], grads[5][0], grads[6][0])


def solution(mesh):
    return jax.shard_map(
        per_device,
        mesh=mesh,
        in_specs=(
            P("bin", None),
            P(),
            P(),
            P(),
            P(),
            P(),
            P(),
            P("bin", "tile", None, None),
            P("bin", "tile", None, None, None),
        ),
        out_specs=(
            P("bin", "tile", None, None, None),
            P("bin", None),
            P(),
            P(),
            P(),
            P(),
            P(),
            P(),
        ),
        check_vma=False,
    )
```

time: 579 us -> 101 us (0.17)
  waiting for transfers between devices: 363 us -> 20.2 us
  blocking collectives: 110 us -> 11 us
  other arithmetic: 44.3 us -> 0.32 us
  starting transfers between devices: 2.77 us -> 38.2 us
  Pallas kernels: 0 us -> 24 us
  matrix products: 20.4 us -> 0 us
  between operations: 13.9 us -> 0.84 us
  loops' own time: 8.8 us -> 0 us
  local copies, waits for them, and re-layouts: 13.2 us -> 5.4 us
    reduce_scatter x2 -> x0, waiting for transfers between devices: 241 us -> none  [the longest x1 180 us: per_device(): lax.psum_scatter(row_grad, 'tile', scatter_dimension=0, tiled=True)]
    psum x1 -> x0, waiting for transfers between devices: 116 us -> none  [per_device(): lax.psum((jnp.dot(share_emb.T, row_low, preferred_element_type=jnp.float3...]
    psum x1 -> x0, blocking collectives: 68.4 us -> none  [per_device(): lax.psum((jnp.dot(share_emb.T, row_low, preferred_element_type=jnp.float3...]
    all_gather x2 -> x0, blocking collectives: 41.3 us -> none  [the longest x1 22.3 us: per_device(): lax.all_gather(right_share, 'tile', axis=0, tiled=True)]
    pallas_call x0 -> x5, Pallas kernels: none -> 24 us  [call(): pl.pallas_call(kernel, out_shape=outs, in_specs=[SMEM] * lists + [space]...]
    reduce_sum x5 -> x2, other arithmetic: 20.8 us -> 0.09 us  [summed(): return jnp.sum(blocks.astype(F32), axis=0).astype(BF16)]
    dot_general x12 -> x0, matrix products: 20.4 us -> none  [the longest x2 4.92 us: tile_pass(): jnp.dot(first_act, w_pair, preferred_element_type=jnp.float32) + b_pair]
    ppermute x2 -> x10, starting transfers between devices: 2.6 us -> 21.2 us  [the longest x2 10.9 us: shifted(): return lax.ppermute(block, axis, route)]
  transfers between devices with their start and end apart: 6 -> 12, of which waited for: 4 -> 7; matrix products, arithmetic and copies ran while one was open for 1% -> 0% of each run, Pallas kernels for 0% -> 3%
where the time goes in v1:
time: 101 us; the launch traced here: 100 us
  starting transfers between devices  38.2 us (38%)
  Pallas kernels  24 us (24%)
  waiting for transfers between devices  20.2 us (20%)
  blocking collectives  11 us (11%)
  local copies, waits for them, and re-layouts  5.4 us (5%)
    pallas_call x5, Pallas kernels, call(): pl.pallas_call(kernel, out_shape=outs, in_specs=[SMEM] * lists + [space]...  24 us
    all_to_all x2, starting transfers between devices, across(): lax.all_to_all(block, axis, 0, 0, axis_index_groups=groups, tiled=True)  17 us
    all_to_all x2, waiting for transfers between devices, across(): lax.all_to_all(block, axis, 0, 0, axis_index_groups=groups, tiled=True)  12.5 us
    all_to_all x1, blocking collectives, across(): lax.all_to_all(block, axis, 0, 0, axis_index_groups=groups, tiled=True)  11 us
    ppermute x2, starting transfers between devices, shifted(): return lax.ppermute(block, axis, route)  10.9 us
    ppermute x8, starting transfers between devices, swapped(): lax.ppermute(block, axis, [(i, i ^ bits) for i in range(lax.axis_size(axi...  10.3 us
    ppermute x8, waiting for transfers between devices, swapped(): lax.ppermute(block, axis, [(i, i ^ bits) for i in range(lax.axis_size(axi...  7.18 us
    unnamed x20, local copies, waits for them, and re-layouts  2.52 us
  transfers between devices with their start and end apart: 12, of which 7 were waited for; matrix products, arithmetic and copies ran while one was open for 0% of the time, Pallas kernels for 3%

profile of v1, /device:TPU:1, one launch (start us, length us, event | category | flops | bytes accessed | tf_op | source)
XLA Modules:
  0.0 100.0 jit_solution(12679423216155986381)
XLA Ops:
  0.6 1.5 %collective-permute-start.1 = (bf16[6,128,128]{2,1,0:T(8,128)(2,1)}, bf16[6,128,128]{2,1,0:T(8,128)(2,1)S(1)}, u32[]{:S(2)}, u32[]{:S(2)}) collective-permute-start(bf16[6,128,128]{2,1,0:T(8,128)(2,1)} %bitcast.20), channel_id=1, source_target_pairs={{0,1},{1,0},{2,3},{3,2},{4,5},{5,4},{6,7},{7,6},{8,9},{9,8},{10,11... | collective-permute-start | bytes 589832 | tf_op jit(solution)/shard_map/ppermute | solution.py:324
  2.1 1.1 %slice-done = bf16[512,512]{1,0:T(8,128)(2,1)S(1)} async-done(((bf16[1024,512]{1,0:T(8,128)(2,1)}), bf16[512,512]{1,0:T(8,128)(2,1)S(1)}, s32[]{:S(2)}) %slice-start) | async-done | bytes 524312 | tf_op jit(solution)/shard_map/slice | solution.py:356
  3.2 1.3 %collective-permute-start.3 = (bf16[128,512]{1,0:T(8,128)(2,1)S(1)}, bf16[128,512]{1,0:T(8,128)(2,1)S(1)}, u32[]{:S(2)}, u32[]{:S(2)}) collective-permute-start(bf16[128,512]{1,0:T(8,128)(2,1)S(1)} %bitcast.28), channel_id=1, source_target_pairs={{16,0},{32,16},{48,32},{64,48},{80,64},{96,80},{112,96},{17,1},{33... | collective-permute-start | bytes 393224 | tf_op jit(solution)/shard_map/ppermute | solution.py:320
  4.5 0.1 copy.23
  4.6 1.1 %collective-permute-done.list_other = s32[6,3]{1,0:T(8,128)S(1)} collective-permute-done((s32[6,3]{1,0:T(8,128)S(1)}, s32[6,3]{1,0:T(8,128)S(1)}, u32[]{:S(2)}, u32[]{:S(2)}) %collective-permute-start) | collective-permute-done | bytes 104 | tf_op jit(solution)/shard_map/ppermute | solution.py:324
  5.8 0.9 copy-done.4
  6.7 1.6 %shard_map.152 = (bf16[12,32,128]{2,1,0:T(8,128)(2,1)S(1)}, bf16[12,32,128]{2,1,0:T(8,128)(2,1)S(1)}, s32[12,3]{1,0:T(8,128)S(1)}) custom-call(s32[6,3]{1,0:T(8,128)S(1)} %bitcast.23, s32[6,3]{1,0:T(8,128)S(1)} %collective-permute-done.list_other, bf16[6,128,128]{2,1,0:T(8,128)(2,1)S(1)} %bitcast.21, bf16[6,128,128]{2,1,0:T(8,128)(2,1)S(1)} %collective-permute-done.1.other_ref), custom_call_target="tpu_custom_call" | custom-call | tf_op jit(solution)/shard_map/pallas_call | solution.py:307
  8.3 1.8 %collective-permute-start.4 = (bf16[12,32,128]{2,1,0:T(8,128)(2,1)S(1)}, bf16[12,32,128]{2,1,0:T(8,128)(2,1)S(1)}, u32[]{:S(2)}, u32[]{:S(2)}) collective-permute-start(bf16[12,32,128]{2,1,0:T(8,128)(2,1)S(1)} %get-tuple-element.29), channel_id=1, source_target_pairs={{0,8},{1,9},{2,10},{3,11},{4,12},{5,13},{6,14},{7,15},{8,0},{9,1},... | collective-permute-start | bytes 294920 | tf_op jit(solution)/shard_map/ppermute | solution.py:324
  10.2 0.1 broadcast_in_dim.56
  10.3 0.9 copy-done.2
  11.2 0.9 shard_map.153
  12.1 0.5 collective-permute-done.3.next_ref
  12.6 3.6 %collective-permute-done.2.list_b = s32[12,3]{1,0:T(8,128)S(1)} collective-permute-done((s32[12,3]{1,0:T(8,128)S(1)}, s32[12,3]{1,0:T(8,128)S(1)}, u32[]{:S(2)}, u32[]{:S(2)}) %collective-permute-start.2) | collective-permute-done | bytes 176 | tf_op jit(solution)/shard_map/ppermute | solution.py:324
  16.2 0.7 copy-done.6
  16.9 19.1 %shard_map.154 = (bf16[12,32,128]{2,1,0:T(8,128)(2,1)S(1)}, bf16[12,32,128]{2,1,0:T(8,128)(2,1)S(1)}, bf16[2,8,144,128]{3,2,1,0:T(8,128)(2,1)S(1)}, f32[256,128]{1,0:T(8,128)S(1)}, bf16[128,128]{1,0:T(8,128)(2,1)S(1)}) custom-call(s32[12,3]{1,0:T(8,128)S(1)} %get-tuple-element.25.list_a, s32[12,3]{1,0:T(8,128)S(1)} %collective-permute-done.2.list_b, ...), custom_call_target="tpu_custom_call" | custom-call | tf_op jit(solution)/shard_map/pallas_call | solution.py:307
  36.0 9.6 %collective-permute-start.8 = (bf16[128,128]{1,0:T(8,128)(2,1)S(1)}, bf16[128,128]{1,0:T(8,128)(2,1)S(1)}, u32[]{:S(2)}, u32[]{:S(2)}) collective-permute-start(bf16[128,128]{1,0:T(8,128)(2,1)S(1)} %get-tuple-element.34), channel_id=1, source_target_pairs={{0,16},{16,32},{32,48},{48,64},{64,80},{80,96},{96,112},{1,17},{17... | collective-permute-start | bytes 98312 | tf_op jit(solution)/shard_map/ppermute | solution.py:320
  45.7 1.6 %collective-permute-start.7 = (bf16[8,144,128]{2,1,0:T(8,128)(2,1)S(1)}, bf16[8,144,128]{2,1,0:T(8,128)(2,1)S(1)}, u32[]{:S(2)}, u32[]{:S(2)}) collective-permute-start(bf16[8,144,128]{2,1,0:T(8,128)(2,1)S(1)} %dynamic-slice_bitcast_fusion), channel_id=1, source_target_pairs={{0,1},{1,0},{2,3},{3,2},{4,5},{5,4},{6,7},{7,6},{8,9},{9,8},{10,11... | collective-permute-start | bytes 884744 | tf_op jit(solution)/shard_map/ppermute | solution.py:324
  47.5 1.1 %collective-permute-done.7 = bf16[8,144,128]{2,1,0:T(8,128)(2,1)S(1)} collective-permute-done((bf16[8,144,128]{2,1,0:T(8,128)(2,1)S(1)}, bf16[8,144,128]{2,1,0:T(8,128)(2,1)S(1)}, u32[]{:S(2)}, u32[]{:S(2)}) %collective-permute-start.7) | collective-permute-done | bytes 294944 | tf_op jit(solution)/shard_map/ppermute | solution.py:324
  48.5 0.1 fusion
  48.7 11.0 %all_to_all.15 = bf16[8,208,128]{2,1,0:T(8,128)(2,1)S(1)} all-to-all(bf16[8,208,128]{2,1,0:T(8,128)(2,1)S(1)} %pad_maximum_fusion), channel_id=1, replica_groups={{0,2,4,6,8,10,12,14},{1,3,5,7,9,11,13,15},{16,18,20,22,24,26,28,30},{17..., dimensions={0} | all-to-all | bytes 851968 | tf_op jit(solution)/shard_map/all_to_all | solution.py:332
  59.8 0.7 broadcast_in_dim.61
  60.5 13.5 %all-to-all-start.1 = ((bf16[8,80,128]{2,1,0:T(8,128)(2,1)}), bf16[8,80,128]{2,1,0:T(8,128)(2,1)S(1)}, u32[]{:S(2)}, u32[]{:S(2)}) async-start(bf16[8,80,128]{2,1,0:T(8,128)(2,1)} %broadcast_in_dim.61), calls=%async_computation.1 | async-start | bytes 327680 | tf_op jit(solution)/shard_map/all_to_all | solution.py:332
  74.0 6.9 %all-to-all-done.1 = bf16[8,80,128]{2,1,0:T(8,128)(2,1)S(1)} async-done(((bf16[8,80,128]{2,1,0:T(8,128)(2,1)}), bf16[8,80,128]{2,1,0:T(8,128)(2,1)S(1)}, u32[]{:S(2)}, u32[]{:S(2)}) %all-to-all-start.1) | async-done | bytes 163872 | tf_op jit(solution)/shard_map/all_to_all | solution.py:332
  81.0 0.8 broadcast_in_dim.62
  81.8 3.5 %all-to-all-start.2 = ((bf16[8,208,128]{2,1,0:T(8,128)(2,1)}), bf16[8,208,128]{2,1,0:T(8,128)(2,1)S(1)}, u32[]{:S(2)}, u32[]{:S(2)}) async-start(bf16[8,208,128]{2,1,0:T(8,128)(2,1)} %broadcast_in_dim.62), calls=%async_computation.2 | async-start | bytes 851968 | tf_op jit(solution)/shard_map/all_to_all | solution.py:332
  85.2 1.4 %collective-permute-start.5 = (bf16[12,32,128]{2,1,0:T(8,128)(2,1)S(1)}, bf16[12,32,128]{2,1,0:T(8,128)(2,1)S(1)}, u32[]{:S(2)}, u32[]{:S(2)}) collective-permute-start(bf16[12,32,128]{2,1,0:T(8,128)(2,1)S(1)} %get-tuple-element.31), channel_id=1, source_target_pairs={{0,8},{1,9},{2,10},{3,11},{4,12},{5,13},{6,14},{7,15},{8,0},{9,1},... | collective-permute-start | bytes 294920 | tf_op jit(solution)/shard_map/ppermute | solution.py:324
  86.6 5.6 %all-to-all-done.2.mine_ref = bf16[8,208,128]{2,1,0:T(8,128)(2,1)S(1)} async-done(((bf16[8,208,128]{2,1,0:T(8,128)(2,1)}), bf16[8,208,128]{2,1,0:T(8,128)(2,1)S(1)}, u32[]{:S(2)}, u32[]{:S(2)}) %all-to-all-start.2) | async-done | bytes 426016 | tf_op jit(solution)/shard_map/all_to_all | solution.py:332
  92.2 3.8 %collective-permute-start.9 = (bf16[8,208,128]{2,1,0:T(8,128)(2,1)S(1)}, bf16[8,208,128]{2,1,0:T(8,128)(2,1)S(1)}, u32[]{:S(2)}, u32[]{:S(2)}) collective-permute-start(bf16[8,208,128]{2,1,0:T(8,128)(2,1)S(1)} %all-to-all-done.2.mine_ref), channel_id=1, source_target_pairs={{0,1},{1,0},{2,3},{3,2},{4,5},{5,4},{6,7},{7,6},{8,9},{9,8},{10,11... | collective-permute-start | bytes 1277960 | tf_op jit(solution)/shard_map/ppermute | solution.py:324
  96.1 0.1 collective-permute-start.6
  96.2 1.4 %collective-permute-done.6.other_ref = bf16[6,64,128]{2,1,0:T(8,128)(2,1)S(1)} collective-permute-done((bf16[6,64,128]{2,1,0:T(8,128)(2,1)S(1)}, bf16[6,64,128]{2,1,0:T(8,128)(2,1)S(1)}, u32[]{:S(2)}, u32[]{:S(2)}) %collective-permute-start.6) | collective-permute-done | bytes 98336 | tf_op jit(solution)/shard_map/ppermute | solution.py:324
  97.6 0.8 shard_map.155
  98.4 1.6 %shard_map.156 = (bf16[1024,512]{1,0:T(8,128)(2,1)}, f32[512,128]{1,0:T(8,128)}, f32[512,128]{1,0:T(8,128)}, f32[5,128]{1,0:T(8,128)}, f32[128,128]{1,0:T(8,128)}, /*index=5*/f32[1,128]{1,0:T(1,128)}, f32[1,128]{1,0:T(1,128)}) custom-call(bf16[8,208,128]{2,1,0:T(8,128)(2,1)S(1)} %all-to-all-done.2.mine_ref, ...), custom_call_target="tpu_custom_call" | custom-call | tf_op jit(solution)/shard_map/pallas_call | solution.py:307
  (42 shorter events, 0.5 us)
Async XLA Ops:
  0.6 5.1 %collective-permute-start.1 = (bf16[6,128,128]{2,1,0:T(8,128)(2,1)}, bf16[6,128,128]{2,1,0:T(8,128)(2,1)S(1)}, u32[]{:S(2)}, u32[]{:S(2)}) collective-permute-start(bf16[6,128,128]{2,1,0:T(8,128)(2,1)} %bitcast.20), channel_id=1, source_target_pairs={{0,1},{1,0},{2,3},{3,2},{4,5},{5,4},{6,7},{7,6},{8,9},{9,8},{10,11... | collective-permute-start | bytes 589832 | tf_op jit(solution)/shard_map/ppermute | solution.py:324
  2.1 2.4 %copy-start.9 = (s32[1,1,6,3]{2,1,3,0:T(1,128)S(1)}, s32[1,1,6,3]{2,1,3,0:T(1,128)}, u32[]{:S(2)}) copy-start(s32[1,1,6,3]{2,1,3,0:T(1,128)} %param.16) | copy-start | bytes 220
  2.1 1.1 %slice-start = ((bf16[1024,512]{1,0:T(8,128)(2,1)}), bf16[512,512]{1,0:T(8,128)(2,1)S(1)}, s32[]{:S(2)}) async-start(bf16[1024,512]{1,0:T(8,128)(2,1)} %emb_ref.1), calls=%async_computation.3 | async-start | bytes 1048576 | tf_op jit(solution)/shard_map/slice | solution.py:356
  2.1 8.2 %copy-start = (bf16[1024,512]{1,0:T(8,128)(2,1)S(1)}, bf16[1024,512]{1,0:T(8,128)(2,1)}, u32[]{:S(2)}) copy-start(bf16[1024,512]{1,0:T(8,128)(2,1)} %emb_ref.1) | copy-start | bytes 3145732
  3.2 9.4 %collective-permute-start.3 = (bf16[128,512]{1,0:T(8,128)(2,1)S(1)}, bf16[128,512]{1,0:T(8,128)(2,1)S(1)}, u32[]{:S(2)}, u32[]{:S(2)}) collective-permute-start(bf16[128,512]{1,0:T(8,128)(2,1)S(1)} %bitcast.28), channel_id=1, source_target_pairs={{16,0},{32,16},{48,32},{64,48},{80,64},{96,80},{112,96},{17,1},{33... | collective-permute-start | bytes 393224 | tf_op jit(solution)/shard_map/ppermute | solution.py:320
  4.6 1.2 %collective-permute-start = (s32[6,3]{1,0:T(8,128)S(1)}, s32[6,3]{1,0:T(8,128)S(1)}, u32[]{:S(2)}, u32[]{:S(2)}) collective-permute-start(s32[6,3]{1,0:T(8,128)S(1)} %bitcast.22), channel_id=1, source_target_pairs={{0,1},{1,0},{2,3},{3,2},{4,5},{5,4},{6,7},{7,6},{8,9},{9,8},{10,11... | collective-permute-start | bytes 224 | tf_op jit(solution)/shard_map/ppermute | solution.py:324
  4.6 5.7 %copy-start.1 = (bf16[512,128]{1,0:T(8,128)(2,1)S(1)}, bf16[512,128]{1,0:T(8,128)(2,1)}, u32[]{:S(2)}) copy-start(bf16[512,128]{1,0:T(8,128)(2,1)} %right_w_ref.3) | copy-start | bytes 393220
  5.8 0.9 copy-start.4
  8.3 7.9 %collective-permute-start.4 = (bf16[12,32,128]{2,1,0:T(8,128)(2,1)S(1)}, bf16[12,32,128]{2,1,0:T(8,128)(2,1)S(1)}, u32[]{:S(2)}, u32[]{:S(2)}) collective-permute-start(bf16[12,32,128]{2,1,0:T(8,128)(2,1)S(1)} %get-tuple-element.29), channel_id=1, source_target_pairs={{0,8},{1,9},{2,10},{3,11},{4,12},{5,13},{6,14},{7,15},{8,0},{9,1},... | collective-permute-start | bytes 294920 | tf_op jit(solution)/shard_map/ppermute | solution.py:324
  10.3 5.9 %collective-permute-start.2 = (s32[12,3]{1,0:T(8,128)S(1)}, s32[12,3]{1,0:T(8,128)S(1)}, u32[]{:S(2)}, u32[]{:S(2)}) collective-permute-start(s32[12,3]{1,0:T(8,128)S(1)} %get-tuple-element.25.list_a), channel_id=1, source_target_pairs={{0,8},{1,9},{2,10},{3,11},{4,12},{5,13},{6,14},{7,15},{8,0},{9,1},... | collective-permute-start | bytes 440 | tf_op jit(solution)/shard_map/ppermute | solution.py:324
  10.3 0.9 copy-start.2
  11.2 5.0 %copy-start.5 = (bf16[128,128]{1,0:T(8,128)(2,1)S(1)}, bf16[128,128]{1,0:T(8,128)(2,1)}, u32[]{:S(2)}) copy-start(bf16[128,128]{1,0:T(8,128)(2,1)} %w_ref.1) | copy-start | bytes 98308
  16.2 0.7 copy-start.6
  16.2 0.7 copy-start.7
  16.2 0.7 copy-start.8
  36.0 11.3 %collective-permute-start.8 = (bf16[128,128]{1,0:T(8,128)(2,1)S(1)}, bf16[128,128]{1,0:T(8,128)(2,1)S(1)}, u32[]{:S(2)}, u32[]{:S(2)}) collective-permute-start(bf16[128,128]{1,0:T(8,128)(2,1)S(1)} %get-tuple-element.34), channel_id=1, source_target_pairs={{0,16},{16,32},{32,48},{48,64},{64,80},{80,96},{96,112},{1,17},{17... | collective-permute-start | bytes 98312 | tf_op jit(solution)/shard_map/ppermute | solution.py:320
  45.7 2.8 %collective-permute-start.7 = (bf16[8,144,128]{2,1,0:T(8,128)(2,1)S(1)}, bf16[8,144,128]{2,1,0:T(8,128)(2,1)S(1)}, u32[]{:S(2)}, u32[]{:S(2)}) collective-permute-start(bf16[8,144,128]{2,1,0:T(8,128)(2,1)S(1)} %dynamic-slice_bitcast_fusion), channel_id=1, source_target_pairs={{0,1},{1,0},{2,3},{3,2},{4,5},{5,4},{6,7},{7,6},{8,9},{9,8},{10,11... | collective-permute-start | bytes 884744 | tf_op jit(solution)/shard_map/ppermute | solution.py:324
  60.5 20.4 %all-to-all-start.1 = ((bf16[8,80,128]{2,1,0:T(8,128)(2,1)}), bf16[8,80,128]{2,1,0:T(8,128)(2,1)S(1)}, u32[]{:S(2)}, u32[]{:S(2)}) async-start(bf16[8,80,128]{2,1,0:T(8,128)(2,1)} %broadcast_in_dim.61), calls=%async_computation.1 | async-start | bytes 327680 | tf_op jit(solution)/shard_map/all_to_all | solution.py:332
  81.8 10.5 %all-to-all-start.2 = ((bf16[8,208,128]{2,1,0:T(8,128)(2,1)}), bf16[8,208,128]{2,1,0:T(8,128)(2,1)S(1)}, u32[]{:S(2)}, u32[]{:S(2)}) async-start(bf16[8,208,128]{2,1,0:T(8,128)(2,1)} %broadcast_in_dim.62), calls=%async_computation.2 | async-start | bytes 851968 | tf_op jit(solution)/shard_map/all_to_all | solution.py:332
  85.2 10.8 %collective-permute-start.5 = (bf16[12,32,128]{2,1,0:T(8,128)(2,1)S(1)}, bf16[12,32,128]{2,1,0:T(8,128)(2,1)S(1)}, u32[]{:S(2)}, u32[]{:S(2)}) collective-permute-start(bf16[12,32,128]{2,1,0:T(8,128)(2,1)S(1)} %get-tuple-element.31), channel_id=1, source_target_pairs={{0,8},{1,9},{2,10},{3,11},{4,12},{5,13},{6,14},{7,15},{8,0},{9,1},... | collective-permute-start | bytes 294920 | tf_op jit(solution)/shard_map/ppermute | solution.py:324
  92.2 6.2 %collective-permute-start.9 = (bf16[8,208,128]{2,1,0:T(8,128)(2,1)S(1)}, bf16[8,208,128]{2,1,0:T(8,128)(2,1)S(1)}, u32[]{:S(2)}, u32[]{:S(2)}) collective-permute-start(bf16[8,208,128]{2,1,0:T(8,128)(2,1)S(1)} %all-to-all-done.2.mine_ref), channel_id=1, source_target_pairs={{0,1},{1,0},{2,3},{3,2},{4,5},{5,4},{6,7},{7,6},{8,9},{9,8},{10,11... | collective-permute-start | bytes 1277960 | tf_op jit(solution)/shard_map/ppermute | solution.py:324
  96.1 2.4 %copy-start.3 = (bf16[512,128]{1,0:T(8,128)(2,1)S(1)}, bf16[512,128]{1,0:T(8,128)(2,1)}, u32[]{:S(2)}) copy-start(bf16[512,128]{1,0:T(8,128)(2,1)} %left_w_ref.1) | copy-start | bytes 393220
  96.1 1.5 %collective-permute-start.6 = (bf16[6,64,128]{2,1,0:T(8,128)(2,1)S(1)}, bf16[6,64,128]{2,1,0:T(8,128)(2,1)S(1)}, u32[]{:S(2)}, u32[]{:S(2)}) collective-permute-start(bf16[6,64,128]{2,1,0:T(8,128)(2,1)S(1)} %pad_maximum_fusion.1), channel_id=1, source_target_pairs={{0,1},{1,0},{2,3},{3,2},{4,5},{5,4},{6,7},{7,6},{8,9},{9,8},{10,11... | collective-permute-start | bytes 294920 | tf_op jit(solution)/shard_map/ppermute | solution.py:324

commit v2 on v1

v2 whole, which is shorter than its diff:
```python
import jax
import jax.numpy as jnp
from jax import lax
from jax.experimental import pallas as pl
from jax.experimental.pallas import tpu as pltpu
from jax.sharding import PartitionSpec as P

F32 = jnp.float32
BF16 = jnp.bfloat16
BATCH = 2
NEVER = -1e38
VMEM = pl.BlockSpec(memory_space=pltpu.VMEM)
SMEM = pl.BlockSpec(memory_space=pltpu.SMEM)
HBM = pl.BlockSpec(memory_space=pl.ANY)
LIMIT = pltpu.CompilerParams(vmem_limit_bytes=32 * 1024 * 1024)


def place():
    return lax.axis_index("tile")


def project_kernel(
    emb_hbm, left_hbm, right_hbm, left_ref, right_ref, full_ref, emb_ref, left_w_ref, right_w_ref, sems
):
    copies = [
        pltpu.make_async_copy(source, target, sems.at[k])
        for k, (source, target) in enumerate(
            ((left_hbm, left_w_ref), (right_hbm, right_w_ref), (emb_hbm, emb_ref))
        )
    ]
    for copy in copies:
        copy.start()
    for copy in copies:
        copy.wait()
    tile = place()
    width = left_w_ref.shape[1]
    half = width // 2
    blocks = emb_ref.shape[0] // width
    step = right_ref.shape[0] // blocks
    weights = jnp.concatenate([left_w_ref[...], right_w_ref[...]], axis=1)
    for block in range(0, blocks, 2):
        both = jnp.dot(
            emb_ref[block * width : (block + 2) * width, :],
            weights,
            preferred_element_type=F32,
        ).astype(BF16).astype(F32)
        for k in range(2):
            left = both[k * width : (k + 1) * width, :width]
            at = (block + k) * half
            left_ref[at : at + half, :width] = left[:half]
            left_ref[at : at + half, width:] = left[half:]
        full_ref[block * width : (block + 2) * width, :] = both[:, width:]
    for block in range(blocks):
        at = pl.multiple_of(block * width + tile * step, step)
        right_ref[block * step : (block + 1) * step, :] = full_ref[pl.ds(at, step), :]


def split_kernel(list_ref, target_hbm, send_ref, target_ref, flip_ref, sem):
    copy = pltpu.make_async_copy(target_hbm, target_ref, sem)
    copy.start()
    slots, width, _ = target_ref.shape
    shares = send_ref.shape[0]
    step = width // shares
    line = lax.broadcasted_iota(jnp.int32, (step, width), 0)
    lane = lax.broadcasted_iota(jnp.int32, (step, width), 1)
    listed = jnp.zeros((step, width), jnp.int32)
    for slot in range(slots):
        for k in range(3):
            listed = jnp.where((line == 0) & (lane == 3 * slot + k), list_ref[k, 0, slot], listed)
    listed = listed.astype(F32)
    copy.wait()
    for slot in range(slots):
        flip_ref[slot] = (target_ref[slot].astype(F32) * (1.0 / width)).T
    spare = send_ref.shape[1] - (slots + 1) * step
    for share in range(shares):
        pieces = [flip_ref[slot, share * step : (share + 1) * step, :] for slot in range(slots)]
        pieces += [listed, jnp.zeros((spare, width), F32)]
        send_ref[share] = jnp.concatenate(pieces, axis=0).astype(BF16)


def join_kernel(back_ref, pred_ref, flip_ref):
    slots, width, _ = pred_ref.shape
    shares = back_ref.shape[0]
    step = width // shares
    at = back_ref.shape[1] - slots * step
    for share in range(shares):
        block = back_ref[share, at:, :].astype(F32)
        for slot in range(slots):
            flip_ref[slot, share * step : (share + 1) * step, :] = block[
                slot * step : (slot + 1) * step
            ]
    for slot in range(slots):
        pred_ref[slot] = flip_ref[slot].T.astype(BF16)


def pair_kernel(
    left_ref, right_ref, emb_ref, cols_ref, next_ref, right_w_ref, bias_ref, target_ref,
    w_ref, b_ref, out_ref,
    sum_ref, col_ref, edge_ref,
    table, lists, list_sem, list_all, right_all, target_all, pred_all, row_all, col_all,
    outer_all, bias_all, w_two, out_two, back_two, b_two, first_0, first_1, slope_0, slope_1,
):
    width = w_ref.shape[0]
    pairs = width // 2
    blocks = left_ref.shape[0] // pairs
    shares = target_ref.shape[0]
    step = width // shares
    slots = target_ref.shape[1] // step - 2
    groups = target_all.shape[0] - 1
    spread_bits = (width // step).bit_length() - 1

    for share in range(shares):
        rows = target_ref[share].astype(F32)
        list_all[share : share + 1] = rows[slots * step : slots * step + 1].astype(jnp.int32)
    copy = pltpu.make_async_copy(list_all, lists, list_sem)
    copy.start()

    w = w_ref[...].astype(F32)
    w_out = out_ref[...]
    back = (w * w_out).T.astype(BF16)
    spread = jnp.broadcast_to(w_out * (1.0 / width), (width, width)).T.astype(BF16)
    for ref, block in ((w_two, w_ref[...]), (out_two, spread), (back_two, back)):
        ref[...] = jnp.zeros_like(ref)
        ref[:width, :width] = block
        ref[width:, width:] = block
    b_two[:, :width] = b_ref[...]
    b_two[:, width:] = b_ref[...]
    own = right_ref.shape[0]
    right_all[:own, :] = right_ref[...]
    right_next = jnp.dot(next_ref[...], right_w_ref[...], preferred_element_type=F32)
    right_all[own:, :] = right_next.astype(BF16).astype(F32)
    rows = [target_ref[share].astype(F32)[: slots * step] for share in range(shares)]
    rows = jnp.concatenate(rows, axis=0)
    for group in range(groups):
        target_all[group] = rows[group * width : (group + 1) * width].T
    target_all[groups] = jnp.zeros((width, width), F32)
    for ref in (pred_all, row_all, col_all, outer_all, bias_all, first_1, slope_1):
        ref[...] = jnp.zeros_like(ref)
    lane = lax.broadcasted_iota(jnp.int32, (width, width), 1)
    ones = jnp.ones((16, BATCH * step * pairs), BF16)

    copy.wait()
    count = jnp.int32(0)
    for share in range(shares):
        for slot in range(slots):
            offset = lists[share, 3 * slot + 2]
            table[0, count] = lists[share, 3 * slot] & (blocks - 1)
            table[1, count] = offset
            table[2, count] = share * slots + slot
            count = count + jnp.where(offset >= 0, 1, 0)
    for spare in range(2 * BATCH):
        table[0, count + spare] = 0
        table[1, count + spare] = 0
        table[2, count + spare] = shares * slots

    def forward(turn, first_ref, slope_ref):
        pre = []
        wanted = []
        shifts = []
        floors = []
        for k in range(BATCH):
            job = turn * BATCH + k
            block, offset, slot = table[0, job], table[1, job], table[2, job]
            shift = (slot & (width // step - 1)) * step
            shifts.append((slot >> spread_bits, shift))
            at = pl.multiple_of(block * pairs, pairs)
            col_at = pl.multiple_of((block + offset) * step, step)
            right = right_all[pl.ds(col_at, step), :] + bias_ref[pl.ds(offset, 1), :]
            right = jnp.concatenate([right, right], axis=1)
            left = left_ref[pl.ds(at, pairs), :]
            pre += [left + right[j : j + 1, :] for j in range(step)]
            target = pltpu.roll(
                target_all[slot >> spread_bits], (width - shift) & (width - 1), 1
            )
            for j in range(step):
                want = jnp.broadcast_to(target[:, j : j + 1], (width, width))
                wanted.append(jnp.concatenate([want[:pairs], want[pairs:]], axis=1))
            floor = jnp.where(job < count, b_two[...], jnp.full((1, 2 * width), NEVER, F32))
            floors.append(jnp.broadcast_to(floor, (step * pairs, 2 * width)))
        first = jnp.maximum(jnp.concatenate(pre, axis=0), 0.0).astype(BF16)
        first_ref[...] = first
        act = jnp.dot(first, w_two[...], preferred_element_type=F32)
        act = act + jnp.concatenate(floors, axis=0)
        second = jnp.maximum(act, 0.0).astype(BF16)
        contact = jnp.dot(second, out_two[...], preferred_element_type=F32)
        slope = (contact - jnp.concatenate(wanted, axis=0)).astype(BF16)
        slope_ref[...] = jnp.where(second > 0, slope, jnp.zeros_like(slope))
        for k, (group, shift) in enumerate(shifts):
            found = jnp.zeros((width, width), F32)
            for j in range(step):
                here = contact[(k * step + j) * pairs : (k * step + j + 1) * pairs]
                here = jnp.concatenate([here[:, :width], here[:, width:]], axis=0)
                found = jnp.where(lane == j, here, found)
            mine = (lane >= shift) & (lane < shift + step)
            pred_all[group] = jnp.where(mine, pltpu.roll(found, shift, 1), pred_all[group])

    def backward(turn, first_ref, slope_ref):
        first = first_ref[...]
        slope = slope_ref[...]
        back = jnp.dot(slope, back_two[...], preferred_element_type=F32)
        back = jnp.where(first.astype(F32) > 0.0, back, 0.0)
        for k in range(BATCH):
            job = turn * BATCH + k
            block, offset = table[0, job], table[1, job]
            at = pl.multiple_of(block * pairs, pairs)
            rows = jnp.zeros((pairs, 2 * width), F32)
            cols = []
            for j in range(step):
                here = back[(k * step + j) * pairs : (k * step + j + 1) * pairs]
                rows = rows + here
                col = jnp.sum(here, axis=0, keepdims=True)
                cols.append(col[:, :width] + col[:, width:])
            row_all[pl.ds(at, pairs), :] += rows
            cols = jnp.concatenate(cols, axis=0)
            col_at = pl.multiple_of((block + offset) * step, step)
            col_all[pl.ds(col_at, step), :] += cols
            bias_all[pl.ds(offset, 1), :] += jnp.sum(cols, axis=0, keepdims=True)
        lhs = jnp.concatenate([first.T, ones], axis=0)
        outer_all[...] += jnp.dot(lhs, slope, preferred_element_type=F32)

    def body(pass_at, _):
        turn = 2 * pass_at
        backward(jnp.maximum(turn - 1, 0), first_1, slope_1)
        forward(turn, first_0, slope_0)
        backward(turn, first_0, slope_0)
        forward(turn + 1, first_1, slope_1)
        return 0

    passes = lax.div(count + 2 * BATCH - 1, 2 * BATCH)
    lax.fori_loop(0, passes, body, 0)
    backward(jnp.maximum(2 * passes - 1, 0), first_1, slope_1)

    flat = [(pred_all[group] * float(width)).T for group in range(groups)]
    flat = jnp.concatenate(flat, axis=0).astype(BF16)
    for share in range(shares):
        sum_ref[share, width + 16 :, :] = flat[share * slots * step : (share + 1) * slots * step]
    outer = outer_all[:width, :width] + outer_all[width : 2 * width, width:]
    sum_d = outer_all[2 * width : 2 * width + 1, :width] + outer_all[2 * width : 2 * width + 1, width:]
    bias = bias_all[...]
    line = lax.broadcasted_iota(jnp.int32, bias.shape, 0)
    sum_out = jnp.sum(w * outer, axis=0, keepdims=True) + b_ref[...] * sum_d
    vectors = jnp.where(line == 5, sum_d * w_out, bias)
    vectors = jnp.where(line == 6, sum_out, vectors)
    outer = outer * w_out
    high = vectors.astype(BF16).astype(F32)
    rest = (high, vectors - high)
    col = col_all[...].astype(BF16)
    rows = []
    for block in range(blocks):
        here = row_all[block * pairs : (block + 1) * pairs, :].astype(BF16)
        rows += [here[:, :width], here[:, width:]]
    embs = [cols_ref[...], next_ref[...]]
    contract = (((0,), (0,)), ((), ()))
    grads = (
        lax.dot_general(
            jnp.concatenate(rows, axis=0), emb_ref[...], contract, preferred_element_type=F32
        ).astype(BF16),
        lax.dot_general(
            col, jnp.concatenate(embs, axis=0), contract, preferred_element_type=F32
        ).astype(BF16),
    )
    half = shares // 2
    for share in range(shares):
        side, at = share // half, share % half
        sum_ref[share, :pairs, :] = rows[share]
        grad = grads[side][:, at // 2 * width : (at // 2 + 1) * width]
        sum_ref[share, pairs:width, :] = grad[at % 2 * pairs : (at % 2 + 1) * pairs]
        more = rest[share] if share < 2 else jnp.zeros_like(high)
        sum_ref[share, width : width + 16, :] = jnp.concatenate(
            [outer[8 * share : 8 * share + 8], more], axis=0
        ).astype(BF16)
    col_ref[...] = col_all[:own]
    edge_ref[...] = col[own:]


def last_kernel(
    mine_ref, other_ref, left_w_ref, right_w_ref,
    emb_ref, left_ref, right_ref, bias_ref, w_ref, b_ref, out_ref,
    both_ref, flat_ref, col_ref,
):
    core = lax.rem(place(), 2)
    width = left_w_ref.shape[1]
    pairs = width // 2
    chips = mine_ref.shape[0]
    step = width // (2 * chips)
    lows = []
    for share in range(2 * chips):
        block = jnp.where(core == share % 2, mine_ref[share // 2], other_ref[share // 2])
        both_ref[share * pairs : (share + 1) * pairs, :width] = block[:pairs]
        block = block.astype(F32)
        for k in range(col_ref.shape[0] // width):
            to = k * width + share * step
            at = width + 16 + k * step
            col_ref[to : to + step, :] = block[at : at + step]
        flat_ref[share * pairs : (share + 1) * pairs, :] = block[pairs:width]
        small = block[width : width + 16]
        w_ref[8 * share : 8 * share + 8, :] = small[:8]
        lows.append(small[8:])
    for side, grad_ref in enumerate((left_ref, right_ref)):
        for k in range(chips // 2):
            at = (side * chips // 2 + k) * width
            grad_ref[k * width : (k + 1) * width, :] = flat_ref[at : at + width, :].T
    both_ref[:, width:] = col_ref[...].astype(BF16)
    vectors = lows[0] + lows[1]
    bias_ref[...] = vectors[:5]
    b_ref[...] = vectors[5:6]
    out_ref[...] = vectors[6:7]
    weights = jnp.concatenate([left_w_ref[...], right_w_ref[...]], axis=1)
    part = 2 * width
    for k in range(both_ref.shape[0] // part):
        emb_ref[k * part : (k + 1) * part, :] = lax.dot_general(
            both_ref[k * part : (k + 1) * part, :],
            weights,
            (((1,), (1,)), ((), ())),
            preferred_element_type=F32,
        ).astype(BF16)


def shape(*dims, dtype=F32):
    return jax.ShapeDtypeStruct(dims, dtype)


def call(kernel, outs, scratch, *args, lists=0, space=VMEM):
    return pl.pallas_call(
        kernel,
        out_shape=outs,
        in_specs=[SMEM] * lists + [space] * (len(args) - lists),
        out_specs=(VMEM,) * len(outs),
        scratch_shapes=scratch,
        compiler_params=LIMIT,
    )(*args)


def shifted(block, axis, distance):
    devices = range(lax.axis_size(axis))
    route = [(i - distance, i) for i in devices if i - distance in devices]
    return lax.ppermute(block, axis, route)


def swapped(block, axis, bits):
    return lax.ppermute(block, axis, [(i, i ^ bits) for i in range(lax.axis_size(axis))])


def across(block, axis, groups=None):
    return lax.all_to_all(block, axis, 0, 0, axis_index_groups=groups, tiled=True)


def per_device(embeddings, w_left, w_right, pair_bias, w_pair, b_pair, w_out, tile_list, target):
    tile = place()
    core = lax.rem(tile, 2)
    slots, width = target.shape[2:4]
    rows, features = embeddings.shape
    blocks = rows // width
    pairs = width // 2
    shares = lax.axis_size("tile")
    chips = shares // 2
    step = width // shares
    part = rows // shares
    edge = part // 2
    target = target[0, 0]
    lists = jnp.transpose(tile_list, (0, 3, 1, 2)).reshape(3, 1, slots)

    emb_cols = lax.dynamic_slice_in_dim(
        embeddings.reshape(blocks, shares, step, features), tile, 1, 1
    ).reshape(part, features)
    emb_next = shifted(emb_cols[:edge], "bin", -1)
    (target_send,) = call(
        split_kernel, (shape(shares, (slots + 2) * step, width, dtype=BF16),),
        [
            pltpu.VMEM((slots, width, width), BF16),
            pltpu.VMEM((slots, width, width), F32),
            pltpu.SemaphoreType.DMA,
        ],
        lists, target, lists=1, space=HBM,
    )
    left, right = call(
        project_kernel,
        (shape(rows // 2, 2 * width), shape(part, width)),
        [
            pltpu.VMEM((rows, width), F32),
            pltpu.VMEM((rows, features), BF16),
            pltpu.VMEM((features, width), BF16),
            pltpu.VMEM((features, width), BF16),
            pltpu.SemaphoreType.DMA((3,)),
        ],
        embeddings, w_left, w_right, space=HBM,
    )
    target_send, emb_next = lax.optimization_barrier((target_send, emb_next))
    target_all = across(target_send, "tile")

    chunk = (BATCH * step * pairs, 2 * width)
    grouped = (slots * shares * step // width + 1, width, width)
    sums, col, col_edge = call(
        pair_kernel,
        (
            shape(shares, width + 16 + slots * step, width, dtype=BF16),
            shape(part, width),
            shape(edge, width, dtype=BF16),
        ),
        [
            pltpu.SMEM((3, slots * shares + 2 * BATCH), jnp.int32),
            pltpu.SMEM((shares, width), jnp.int32),
            pltpu.SemaphoreType.DMA,
            pltpu.VMEM((shares, width), jnp.int32),
            pltpu.VMEM((part + edge, width), F32),
            pltpu.VMEM(grouped, F32),
            pltpu.VMEM(grouped, F32),
            pltpu.VMEM((rows // 2, 2 * width), F32),
            pltpu.VMEM((part + edge, width), F32),
            pltpu.VMEM((2 * width + 16, 2 * width), F32),
            pltpu.VMEM((8, width), F32),
            pltpu.VMEM((2 * width, 2 * width), BF16),
            pltpu.VMEM((2 * width, 2 * width), BF16),
            pltpu.VMEM((2 * width, 2 * width), BF16),
            pltpu.VMEM((1, 2 * width), F32),
            pltpu.VMEM(chunk, BF16),
            pltpu.VMEM(chunk, BF16),
            pltpu.VMEM(chunk, BF16),
            pltpu.VMEM(chunk, BF16),
        ],
        left, right, embeddings, emb_cols, emb_next, w_right, pair_bias,
        target_all, w_pair, b_pair[None], w_out[None],
    )
    sums = across(sums, "tile")
    share = jnp.sum(sums[:, : width + 16].astype(F32), axis=0).astype(BF16)
    weight = share[pairs:]
    bins = lax.axis_size("bin")
    here = lax.axis_index("bin")
    before = jnp.zeros((edge, width), F32)
    mask = 1
    while mask < bins:
        met = swapped(jnp.concatenate([weight, col_edge], axis=0), "bin", mask).astype(F32)
        weight = (weight.astype(F32) + met[: weight.shape[0]]).astype(BF16)
        before = jnp.where((here ^ mask) + 1 == here, met[weight.shape[0] :], before)
        mask = 2 * mask + 1
    col = jnp.concatenate([col[:edge] + before, col[edge:]], axis=0).astype(BF16)
    share = jnp.concatenate([share[:pairs], weight, col], axis=0)
    groups = [list(range(k, shares, 2)) for k in range(2)]
    mine = across(jnp.broadcast_to(share[None], (chips, *share.shape)), "tile", groups)
    other = swapped(mine, "tile", 1)
    (predicted,) = call(
        join_kernel, (shape(slots, width, width, dtype=BF16),),
        [pltpu.VMEM((slots, width, width), F32)],
        sums,
    )
    grads = call(
        last_kernel,
        (
            shape(rows, features, dtype=BF16),
            shape(features, width),
            shape(features, width),
            shape(5, width),
            shape(width, width),
            shape(1, width),
            shape(1, width),
        ),
        [
            pltpu.VMEM((rows, 2 * width), BF16),
            pltpu.VMEM((2 * features, width), F32),
            pltpu.VMEM((rows, width), F32),
        ],
        mine, other, w_left, w_right,
    )
    return (predicted[None, None], *grads[:5], grads[5][0], grads[6][0])


def solution(mesh):
    return jax.shard_map(
        per_device,
        mesh=mesh,
        in_specs=(
            P("bin", None),
            P(),
            P(),
            P(),
            P(),
            P(),
            P(),
            P("bin", "tile", None, None),
            P("bin", "tile", None, None, None),
        ),
        out_specs=(
            P("bin", "tile", None, None, None),
            P("bin", None),
            P(),
            P(),
            P(),
            P(),
            P(),
            P(),
        ),
        check_vma=False,
    )
```

time: 101 us -> 95.1 us (0.942)
  starting transfers between devices: 38.2 us -> 22.9 us
  blocking collectives: 11 us -> 25.5 us
  waiting for transfers between devices: 20.2 us -> 16.7 us
    all_to_all x1 -> x2, blocking collectives: 11 us -> 25.5 us  [across(): lax.all_to_all(block, axis, 0, 0, axis_index_groups=groups, tiled=True)]
    all_to_all x2 -> x1, starting transfers between devices: 17 us -> 7.02 us  [across(): lax.all_to_all(block, axis, 0, 0, axis_index_groups=groups, tiled=True)]
    ppermute x2 -> x1, starting transfers between devices: 10.9 us -> 1.29 us  [shifted(): return lax.ppermute(block, axis, route)]
    all_to_all x2 -> x1, waiting for transfers between devices: 12.5 us -> 5.39 us  [across(): lax.all_to_all(block, axis, 0, 0, axis_index_groups=groups, tiled=True)]
    ppermute x8 -> x4, starting transfers between devices: 10.3 us -> 14.6 us  [swapped(): lax.ppermute(block, axis, [(i, i ^ bits) for i in range(lax.axis_size(axi...]
    ppermute x2 -> x1, waiting for transfers between devices: 0.55 us -> 3.01 us  [shifted(): return lax.ppermute(block, axis, route)]
    unnamed x20 -> x23, local copies, waits for them, and re-layouts: 2.52 us -> 4.15 us
    ppermute x8 -> x4, waiting for transfers between devices: 7.18 us -> 8.31 us  [swapped(): lax.ppermute(block, axis, [(i, i ^ bits) for i in range(lax.axis_size(axi...]
  transfers between devices with their start and end apart: 12 -> 6, of which waited for: 7 -> 6; matrix products, arithmetic and copies ran while one was open for 0% -> 0% of each run, Pallas kernels for 3% -> 4%
where the time goes in v2:
time: 95.1 us; the launch traced here: 94.6 us
  blocking collectives  25.5 us (27%)
  Pallas kernels  23.6 us (25%)
  starting transfers between devices  22.9 us (24%)
  waiting for transfers between devices  16.7 us (18%)
  local copies, waits for them, and re-layouts  4.91 us (5%)
    all_to_all x2, blocking collectives, across(): lax.all_to_all(block, axis, 0, 0, axis_index_groups=groups, tiled=True)  25.5 us
    pallas_call x5, Pallas kernels, call(): pl.pallas_call(kernel, out_shape=outs, in_specs=[SMEM] * lists + [space]...  23.6 us
    ppermute x4, starting transfers between devices, swapped(): lax.ppermute(block, axis, [(i, i ^ bits) for i in range(lax.axis_size(axi...  14.6 us
    ppermute x4, waiting for transfers between devices, swapped(): lax.ppermute(block, axis, [(i, i ^ bits) for i in range(lax.axis_size(axi...  8.31 us
    all_to_all x1, starting transfers between devices, across(): lax.all_to_all(block, axis, 0, 0, axis_index_groups=groups, tiled=True)  7.02 us
    all_to_all x1, waiting for transfers between devices, across(): lax.all_to_all(block, axis, 0, 0, axis_index_groups=groups, tiled=True)  5.39 us
    unnamed x23, local copies, waits for them, and re-layouts  4.15 us
    ppermute x1, waiting for transfers between devices, shifted(): return lax.ppermute(block, axis, route)  3.01 us
  transfers between devices with their start and end apart: 6, of which 6 were waited for; matrix products, arithmetic and copies ran while one was open for 0% of the time, Pallas kernels for 4%

profile of v2, /device:TPU:1, one launch (start us, length us, event | category | flops | bytes accessed | tf_op | source)
XLA Modules:
  0.0 94.6 jit_solution(94440995562348766)
XLA Ops:
  0.6 0.9 dynamic-slice_bitcast_fusion.1
  1.6 1.3 %collective-permute-start = (bf16[32,512]{1,0:T(8,128)(2,1)S(1)}, bf16[32,512]{1,0:T(8,128)(2,1)S(1)}, u32[]{:S(2)}, u32[]{:S(2)}) collective-permute-start(bf16[32,512]{1,0:T(8,128)(2,1)S(1)} %slice_bitcast_fusion), channel_id=1, source_target_pairs={{16,0},{32,16},{48,32},{64,48},{80,64},{96,80},{112,96},{17,1},{33... | collective-permute-start | bytes 98312 | tf_op jit(solution)/shard_map/ppermute | solution.py:337
  2.9 0.0 copy-start.4
  2.9 0.9 copy-done.4
  3.8 0.7 copy-done.7
  4.5 1.7 %shard_map.153 = bf16[16,64,128]{2,1,0:T(8,128)(2,1)} custom-call(s32[3,1,6]{2,1,0:T(1,128)S(1)} %bitcast.19, bf16[6,128,128]{2,1,0:T(8,128)(2,1)S(1)} %bitcast.18), custom_call_target="tpu_custom_call" | custom-call | tf_op jit(solution)/shard_map/pallas_call | solution.py:324
  6.2 0.0 copy-start.1
  6.2 3.0 %collective-permute-done.next_ref = bf16[32,512]{1,0:T(8,128)(2,1)S(1)} collective-permute-done((bf16[32,512]{1,0:T(8,128)(2,1)S(1)}, bf16[32,512]{1,0:T(8,128)(2,1)S(1)}, u32[]{:S(2)}, u32[]{:S(2)}) %collective-permute-start) | collective-permute-done | bytes 32800 | tf_op jit(solution)/shard_map/ppermute | solution.py:337
  9.2 7.0 %all-to-all-start = ((bf16[16,64,128]{2,1,0:T(8,128)(2,1)}), bf16[16,64,128]{2,1,0:T(8,128)(2,1)S(1)}, u32[]{:S(2)}, u32[]{:S(2)}) async-start(bf16[16,64,128]{2,1,0:T(8,128)(2,1)} %shard_map.153), calls=%async_computation | async-start | bytes 524288 | tf_op jit(solution)/shard_map/all_to_all | solution.py:345
  16.3 0.0 copy-start.2
  16.3 0.9 copy-done.2
  17.2 0.9 shard_map.152
  18.0 5.4 %all-to-all-done.target_ref = bf16[16,64,128]{2,1,0:T(8,128)(2,1)S(1)} async-done(((bf16[16,64,128]{2,1,0:T(8,128)(2,1)}), bf16[16,64,128]{2,1,0:T(8,128)(2,1)S(1)}, u32[]{:S(2)}, u32[]{:S(2)}) %all-to-all-start) | async-done | bytes 262176 | tf_op jit(solution)/shard_map/all_to_all | solution.py:345
  23.4 0.7 copy-done.6
  24.1 18.7 %shard_map.154 = (bf16[16,192,128]{2,1,0:T(8,128)(2,1)S(1)}, f32[64,128]{1,0:T(8,128)S(1)}, bf16[32,128]{1,0:T(8,128)(2,1)S(1)}) custom-call(f32[512,256]{1,0:T(8,128)S(1)} %get-tuple-element.22.left_ref, f32[64,128]{1,0:T(8,128)S(1)} %get-tuple-element.23.right_ref, bf16[1024,512]{1,0:T(8,128)(2,1)S(1)} %copy-done, ...), custom_call_target="tpu_custom_call" | custom-call | tf_op jit(solution)/shard_map/pallas_call | solution.py:324
  42.8 16.1 %all_to_all.15.back_ref = bf16[16,192,128]{2,1,0:T(8,128)(2,1)S(1)} all-to-all(bf16[16,192,128]{2,1,0:T(8,128)(2,1)S(1)} %get-tuple-element.26), channel_id=1, replica_groups=mesh['bin'=8,'tile'=16] {'tile'}, dimensions={0} | all-to-all | bytes 1572864 | tf_op jit(solution)/shard_map/all_to_all | solution.py:345
  58.9 0.1 slice_reduce_fusion
  59.0 0.0 copy-start.10
  59.0 2.6 %collective-permute-start.1 = (bf16[112,128]{1,0:T(8,128)(2,1)S(1)}, bf16[112,128]{1,0:T(8,128)(2,1)S(1)}, u32[]{:S(2)}, u32[]{:S(2)}) collective-permute-start(bf16[112,128]{1,0:T(8,128)(2,1)S(1)} %pad_maximum_fusion.3), channel_id=1, source_target_pairs={{0,16},{16,0},{32,48},{48,32},{64,80},{80,64},{96,112},{112,96},{1... | collective-permute-start | bytes 86024 | tf_op jit(solution)/shard_map/ppermute | solution.py:341
  61.7 1.7 %collective-permute-done.1 = bf16[112,128]{1,0:T(8,128)(2,1)S(1)} collective-permute-done((bf16[112,128]{1,0:T(8,128)(2,1)S(1)}, bf16[112,128]{1,0:T(8,128)(2,1)S(1)}, u32[]{:S(2)}, u32[]{:S(2)}) %collective-permute-start.1) | collective-permute-done | bytes 28704 | tf_op jit(solution)/shard_map/ppermute | solution.py:341
  63.4 5.2 %collective-permute-start.2 = (bf16[112,128]{1,0:T(8,128)(2,1)S(1)}, bf16[112,128]{1,0:T(8,128)(2,1)S(1)}, u32[]{:S(2)}, u32[]{:S(2)}) collective-permute-start(bf16[112,128]{1,0:T(8,128)(2,1)S(1)} %pad_maximum_fusion.2), channel_id=1, source_target_pairs={{0,48},{16,32},{32,16},{48,0},{64,112},{80,96},{96,80},{112,64},{1... | collective-permute-start | bytes 86024 | tf_op jit(solution)/shard_map/ppermute | solution.py:341
  68.6 1.3 %collective-permute-done.2 = bf16[112,128]{1,0:T(8,128)(2,1)S(1)} collective-permute-done((bf16[112,128]{1,0:T(8,128)(2,1)S(1)}, bf16[112,128]{1,0:T(8,128)(2,1)S(1)}, u32[]{:S(2)}, u32[]{:S(2)}) %collective-permute-start.2) | collective-permute-done | bytes 28704 | tf_op jit(solution)/shard_map/ppermute | solution.py:341
  69.9 1.6 %collective-permute-start.3 = (bf16[112,128]{1,0:T(8,128)(2,1)S(1)}, bf16[112,128]{1,0:T(8,128)(2,1)S(1)}, u32[]{:S(2)}, u32[]{:S(2)}) collective-permute-start(bf16[112,128]{1,0:T(8,128)(2,1)S(1)} %pad_maximum_fusion.1), channel_id=1, source_target_pairs={{0,112},{16,96},{32,80},{48,64},{64,48},{80,32},{96,16},{112,0},{1... | collective-permute-start | bytes 86024 | tf_op jit(solution)/shard_map/ppermute | solution.py:341
  71.5 4.8 %collective-permute-done.3 = bf16[112,128]{1,0:T(8,128)(2,1)S(1)} collective-permute-done((bf16[112,128]{1,0:T(8,128)(2,1)S(1)}, bf16[112,128]{1,0:T(8,128)(2,1)S(1)}, u32[]{:S(2)}, u32[]{:S(2)}) %collective-permute-start.3) | collective-permute-done | bytes 28704 | tf_op jit(solution)/shard_map/ppermute | solution.py:341
  76.3 0.0 slice-start
  76.3 0.7 slice-done
  77.0 0.1 broadcast_in_dim.22
  77.1 9.4 %all_to_all.16.mine_ref = bf16[8,208,128]{2,1,0:T(8,128)(2,1)S(1)} all-to-all(bf16[8,208,128]{2,1,0:T(8,128)(2,1)S(1)} %broadcast_in_dim.22), channel_id=1, replica_groups={{0,2,4,6,8,10,12,14},{1,3,5,7,9,11,13,15},{16,18,20,22,24,26,28,30},{17..., dimensions={0} | all-to-all | bytes 851968 | tf_op jit(solution)/shard_map/all_to_all | solution.py:345
  86.5 5.1 %collective-permute-start.4 = (bf16[8,208,128]{2,1,0:T(8,128)(2,1)S(1)}, bf16[8,208,128]{2,1,0:T(8,128)(2,1)S(1)}, u32[]{:S(2)}, u32[]{:S(2)}) collective-permute-start(bf16[8,208,128]{2,1,0:T(8,128)(2,1)S(1)} %all_to_all.16.mine_ref), channel_id=1, source_target_pairs={{0,1},{1,0},{2,3},{3,2},{4,5},{5,4},{6,7},{7,6},{8,9},{9,8},{10,11... | collective-permute-start | bytes 1277960 | tf_op jit(solution)/shard_map/ppermute | solution.py:341
  91.6 0.8 shard_map.155
  92.4 0.6 collective-permute-done.4.other_ref
  93.0 1.6 %shard_map.156 = (bf16[1024,512]{1,0:T(8,128)(2,1)}, f32[512,128]{1,0:T(8,128)}, f32[512,128]{1,0:T(8,128)}, f32[5,128]{1,0:T(8,128)}, f32[128,128]{1,0:T(8,128)}, /*index=5*/f32[1,128]{1,0:T(1,128)}, f32[1,128]{1,0:T(1,128)}) custom-call(bf16[8,208,128]{2,1,0:T(8,128)(2,1)S(1)} %all_to_all.16.mine_ref, ...), custom_call_target="tpu_custom_call" | custom-call | tf_op jit(solution)/shard_map/pallas_call | solution.py:324
  (28 shorter events, 0.1 us)
Async XLA Ops:
  0.6 15.6 %copy-start = (bf16[1024,512]{1,0:T(8,128)(2,1)S(1)}, bf16[1024,512]{1,0:T(8,128)(2,1)}, u32[]{:S(2)}) copy-start(bf16[1024,512]{1,0:T(8,128)(2,1)} %emb_ref.1) | copy-start | bytes 3145732
  1.6 7.6 %collective-permute-start = (bf16[32,512]{1,0:T(8,128)(2,1)S(1)}, bf16[32,512]{1,0:T(8,128)(2,1)S(1)}, u32[]{:S(2)}, u32[]{:S(2)}) collective-permute-start(bf16[32,512]{1,0:T(8,128)(2,1)S(1)} %slice_bitcast_fusion), channel_id=1, source_target_pairs={{16,0},{32,16},{48,32},{64,48},{80,64},{96,80},{112,96},{17,1},{33... | collective-permute-start | bytes 98312 | tf_op jit(solution)/shard_map/ppermute | solution.py:337
  2.9 0.9 copy-start.4
  3.8 0.7 copy-start.7
  6.2 10.1 %copy-start.1 = (bf16[512,128]{1,0:T(8,128)(2,1)S(1)}, bf16[512,128]{1,0:T(8,128)(2,1)}, u32[]{:S(2)}) copy-start(bf16[512,128]{1,0:T(8,128)(2,1)} %right_w_ref.3) | copy-start | bytes 393220
  9.2 14.2 %all-to-all-start = ((bf16[16,64,128]{2,1,0:T(8,128)(2,1)}), bf16[16,64,128]{2,1,0:T(8,128)(2,1)S(1)}, u32[]{:S(2)}, u32[]{:S(2)}) async-start(bf16[16,64,128]{2,1,0:T(8,128)(2,1)} %shard_map.153), calls=%async_computation | async-start | bytes 524288 | tf_op jit(solution)/shard_map/all_to_all | solution.py:345
  16.3 0.9 copy-start.2
  17.2 6.3 %copy-start.5 = (bf16[128,128]{1,0:T(8,128)(2,1)S(1)}, bf16[128,128]{1,0:T(8,128)(2,1)}, u32[]{:S(2)}) copy-start(bf16[128,128]{1,0:T(8,128)(2,1)} %w_ref.1) | copy-start | bytes 98308
  23.4 0.7 copy-start.6
  23.4 0.7 copy-start.8
  23.4 0.7 copy-start.9
  59.0 12.5 %copy-start.10 = (bf16[144,128]{1,0:T(8,128)(2,1)}, bf16[144,128]{1,0:T(8,128)(2,1)S(1)}, u32[]{:S(2)}) copy-start(bf16[144,128]{1,0:T(8,128)(2,1)S(1)} %slice_reduce_fusion) | copy-start | bytes 110596
  59.0 4.3 %collective-permute-start.1 = (bf16[112,128]{1,0:T(8,128)(2,1)S(1)}, bf16[112,128]{1,0:T(8,128)(2,1)S(1)}, u32[]{:S(2)}, u32[]{:S(2)}) collective-permute-start(bf16[112,128]{1,0:T(8,128)(2,1)S(1)} %pad_maximum_fusion.3), channel_id=1, source_target_pairs={{0,16},{16,0},{32,48},{48,32},{64,80},{80,64},{96,112},{112,96},{1... | collective-permute-start | bytes 86024 | tf_op jit(solution)/shard_map/ppermute | solution.py:341
  63.4 6.5 %collective-permute-start.2 = (bf16[112,128]{1,0:T(8,128)(2,1)S(1)}, bf16[112,128]{1,0:T(8,128)(2,1)S(1)}, u32[]{:S(2)}, u32[]{:S(2)}) collective-permute-start(bf16[112,128]{1,0:T(8,128)(2,1)S(1)} %pad_maximum_fusion.2), channel_id=1, source_target_pairs={{0,48},{16,32},{32,16},{48,0},{64,112},{80,96},{96,80},{112,64},{1... | collective-permute-start | bytes 86024 | tf_op jit(solution)/shard_map/ppermute | solution.py:341
  69.9 6.4 %collective-permute-start.3 = (bf16[112,128]{1,0:T(8,128)(2,1)S(1)}, bf16[112,128]{1,0:T(8,128)(2,1)S(1)}, u32[]{:S(2)}, u32[]{:S(2)}) collective-permute-start(bf16[112,128]{1,0:T(8,128)(2,1)S(1)} %pad_maximum_fusion.1), channel_id=1, source_target_pairs={{0,112},{16,96},{32,80},{48,64},{64,48},{80,32},{96,16},{112,0},{1... | collective-permute-start | bytes 86024 | tf_op jit(solution)/shard_map/ppermute | solution.py:341
  76.3 0.7 slice-start
  86.5 6.5 %copy-start.3 = (bf16[512,128]{1,0:T(8,128)(2,1)S(1)}, bf16[512,128]{1,0:T(8,128)(2,1)}, u32[]{:S(2)}) copy-start(bf16[512,128]{1,0:T(8,128)(2,1)} %left_w_ref.1) | copy-start | bytes 393220
  86.5 6.5 %collective-permute-start.4 = (bf16[8,208,128]{2,1,0:T(8,128)(2,1)S(1)}, bf16[8,208,128]{2,1,0:T(8,128)(2,1)S(1)}, u32[]{:S(2)}, u32[]{:S(2)}) collective-permute-start(bf16[8,208,128]{2,1,0:T(8,128)(2,1)S(1)} %all_to_all.16.mine_ref), channel_id=1, source_target_pairs={{0,1},{1,0},{2,3},{3,2},{4,5},{5,4},{6,7},{7,6},{8,9},{9,8},{10,11... | collective-permute-start | bytes 1277960 | tf_op jit(solution)/shard_map/ppermute | solution.py:341

commit v3 on v2

--- a/solution.py
+++ b/solution.py
@@ -9,34 +9,55 @@
 BF16 = jnp.bfloat16
 BATCH = 2
 NEVER = -1e38
+BIN_MASKS = (2, 6, 4)
 VMEM = pl.BlockSpec(memory_space=pltpu.VMEM)
-SMEM = pl.BlockSpec(memory_space=pltpu.SMEM)
 HBM = pl.BlockSpec(memory_space=pl.ANY)
-LIMIT = pltpu.CompilerParams(vmem_limit_bytes=32 * 1024 * 1024)
 
 
 def place():
     return lax.axis_index("tile")
 
 
-def project_kernel(
-    emb_hbm, left_hbm, right_hbm, left_ref, right_ref, full_ref, emb_ref, left_w_ref, right_w_ref, sems
+def prepare_kernel(
+    list_hbm, target_hbm, emb_hbm, left_hbm, right_hbm,
+    send_ref, left_ref, right_ref, cols_ref, edge_ref,
+    list_ref, target_ref, emb_ref, left_w_ref, right_w_ref, flip_ref, listed_ref, full_ref, sems,
 ):
     copies = [
         pltpu.make_async_copy(source, target, sems.at[k])
         for k, (source, target) in enumerate(
-            ((left_hbm, left_w_ref), (right_hbm, right_w_ref), (emb_hbm, emb_ref))
+            (
+                (target_hbm, target_ref),
+                (list_hbm, list_ref),
+                (left_hbm, left_w_ref),
+                (right_hbm, right_w_ref),
+                (emb_hbm, emb_ref),
+            )
         )
     ]
     for copy in copies:
         copy.start()
-    for copy in copies:
+    slots, width, _ = target_ref.shape
+    shares = send_ref.shape[0]
+    step = width // shares
+    half = width // 2
+    blocks = emb_ref.shape[0] // width
+    listed_ref[...] = jnp.zeros_like(listed_ref)
+    copies[0].wait()
+    for slot in range(slots):
+        flip_ref[slot] = (target_ref[slot].astype(F32) * (1.0 / width)).T
+    copies[1].wait()
+    for k in range(3):
+        listed_ref[k : k + 1, :slots] = list_ref[k].astype(F32)
+    listed = listed_ref[...]
+    spare = send_ref.shape[1] - (slots + 1) * step
+    for share in range(shares):
+        pieces = [flip_ref[slot, share * step : (share + 1) * step, :] for slot in range(slots)]
+        pieces += [listed, jnp.zeros((spare, width), F32)]
+        send_ref[share] = jnp.concatenate(pieces, axis=0).astype(BF16)
+    for copy in copies[2:]:
         copy.wait()
     tile = place()
-    width = left_w_ref.shape[1]
-    half = width // 2
-    blocks = emb_ref.shape[0] // width
-    step = right_ref.shape[0] // blocks
     weights = jnp.concatenate([left_w_ref[...], right_w_ref[...]], axis=1)
     for block in range(0, blocks, 2):
         both = jnp.dot(
@@ -50,32 +71,16 @@
             left_ref[at : at + half, :width] = left[:half]
             left_ref[at : at + half, width:] = left[half:]
         full_ref[block * width : (block + 2) * width, :] = both[:, width:]
+    rows = []
     for block in range(blocks):
         at = pl.multiple_of(block * width + tile * step, step)
         right_ref[block * step : (block + 1) * step, :] = full_ref[pl.ds(at, step), :]
-
-
-def split_kernel(list_ref, target_hbm, send_ref, target_ref, flip_ref, sem):
-    copy = pltpu.make_async_copy(target_hbm, target_ref, sem)
-    copy.start()
-    slots, width, _ = target_ref.shape
-    shares = send_ref.shape[0]
-    step = width // shares
-    line = lax.broadcasted_iota(jnp.int32, (step, width), 0)
-    lane = lax.broadcasted_iota(jnp.int32, (step, width), 1)
-    listed = jnp.zeros((step, width), jnp.int32)
-    for slot in range(slots):
-        for k in range(3):
-            listed = jnp.where((line == 0) & (lane == 3 * slot + k), list_ref[k, 0, slot], listed)
-    listed = listed.astype(F32)
-    copy.wait()
-    for slot in range(slots):
-        flip_ref[slot] = (target_ref[slot].astype(F32) * (1.0 / width)).T
-    spare = send_ref.shape[1] - (slots + 1) * step
-    for share in range(shares):
-        pieces = [flip_ref[slot, share * step : (share + 1) * step, :] for slot in range(slots)]
-        pieces += [listed, jnp.zeros((spare, width), F32)]
-        send_ref[share] = jnp.concatenate(pieces, axis=0).astype(BF16)
+        at = pl.multiple_of(block * width + (tile >> 1) * (2 * step), 2 * step)
+        near = emb_ref[pl.ds(at, 2 * step), :].astype(F32)
+        rows.append(jnp.where((tile & 1) == 0, near[:step], near[step:]))
+    rows = jnp.concatenate(rows, axis=0).astype(BF16)
+    cols_ref[...] = rows
+    edge_ref[...] = rows[: edge_ref.shape[0]]
 
 
 def join_kernel(back_ref, pred_ref, flip_ref):
@@ -111,7 +116,9 @@
 
     for share in range(shares):
         rows = target_ref[share].astype(F32)
-        list_all[share : share + 1] = rows[slots * step : slots * step + 1].astype(jnp.int32)
+        for k in range(3):
+            at = slots * step + k
+            list_all[k, share : share + 1] = rows[at : at + 1].astype(jnp.int32)
     copy = pltpu.make_async_copy(list_all, lists, list_sem)
     copy.start()
 
@@ -143,8 +150,8 @@
     count = jnp.int32(0)
     for share in range(shares):
         for slot in range(slots):
-            offset = lists[share, 3 * slot + 2]
-            table[0, count] = lists[share, 3 * slot] & (blocks - 1)
+            offset = lists[2, share, slot]
+            table[0, count] = lists[0, share, slot] & (blocks - 1)
             table[1, count] = offset
             table[2, count] = share * slots + slot
             count = count + jnp.where(offset >= 0, 1, 0)
@@ -320,14 +327,14 @@
     return jax.ShapeDtypeStruct(dims, dtype)
 
 
-def call(kernel, outs, scratch, *args, lists=0, space=VMEM):
+def call(kernel, outs, scratch, *args, space=VMEM, limit=32):
     return pl.pallas_call(
         kernel,
         out_shape=outs,
-        in_specs=[SMEM] * lists + [space] * (len(args) - lists),
+        in_specs=[space] * len(args),
         out_specs=(VMEM,) * len(outs),
         scratch_shapes=scratch,
-        compiler_params=LIMIT,
+        compiler_params=pltpu.CompilerParams(vmem_limit_bytes=limit * 1024 * 1024),
     )(*args)
 
 
@@ -360,33 +367,30 @@
     target = target[0, 0]
     lists = jnp.transpose(tile_list, (0, 3, 1, 2)).reshape(3, 1, slots)
 
-    emb_cols = lax.dynamic_slice_in_dim(
-        embeddings.reshape(blocks, shares, step, features), tile, 1, 1
-    ).reshape(part, features)
-    emb_next = shifted(emb_cols[:edge], "bin", -1)
-    (target_send,) = call(
-        split_kernel, (shape(shares, (slots + 2) * step, width, dtype=BF16),),
+    target_send, left, right, emb_cols, emb_edge = call(
+        prepare_kernel,
+        (
+            shape(shares, (slots + 2) * step, width, dtype=BF16),
+            shape(rows // 2, 2 * width),
+            shape(part, width),
+            shape(part, features, dtype=BF16),
+            shape(edge, features, dtype=BF16),
+        ),
         [
+            pltpu.VMEM(lists.shape, jnp.int32),
             pltpu.VMEM((slots, width, width), BF16),
-            pltpu.VMEM((slots, width, width), F32),
-            pltpu.SemaphoreType.DMA,
-        ],
-        lists, target, lists=1, space=HBM,
-    )
-    left, right = call(
-        project_kernel,
-        (shape(rows // 2, 2 * width), shape(part, width)),
-        [
-            pltpu.VMEM((rows, width), F32),
             pltpu.VMEM((rows, features), BF16),
             pltpu.VMEM((features, width), BF16),
             pltpu.VMEM((features, width), BF16),
-            pltpu.SemaphoreType.DMA((3,)),
+            pltpu.VMEM((slots, width, width), F32),
+            pltpu.VMEM((step, width), F32),
+            pltpu.VMEM((rows, width), F32),
+            pltpu.SemaphoreType.DMA((5,)),
         ],
-        embeddings, w_left, w_right, space=HBM,
+        lists, target, embeddings, w_left, w_right, space=HBM, limit=56,
     )
-    target_send, emb_next = lax.optimization_barrier((target_send, emb_next))
     target_all = across(target_send, "tile")
+    emb_next = shifted(emb_edge, "bin", -1)
 
     chunk = (BATCH * step * pairs, 2 * width)
     grouped = (slots * shares * step // width + 1, width, width)
@@ -399,9 +403,9 @@
         ),
         [
             pltpu.SMEM((3, slots * shares + 2 * BATCH), jnp.int32),
-            pltpu.SMEM((shares, width), jnp.int32),
+            pltpu.SMEM((3, shares, width), jnp.int32),
             pltpu.SemaphoreType.DMA,
-            pltpu.VMEM((shares, width), jnp.int32),
+            pltpu.VMEM((3, shares, width), jnp.int32),
             pltpu.VMEM((part + edge, width), F32),
             pltpu.VMEM(grouped, F32),
             pltpu.VMEM(grouped, F32),
@@ -424,15 +428,18 @@
     sums = across(sums, "tile")
     share = jnp.sum(sums[:, : width + 16].astype(F32), axis=0).astype(BF16)
     weight = share[pairs:]
-    bins = lax.axis_size("bin")
     here = lax.axis_index("bin")
-    before = jnp.zeros((edge, width), F32)
-    mask = 1
-    while mask < bins:
-        met = swapped(jnp.concatenate([weight, col_edge], axis=0), "bin", mask).astype(F32)
-        weight = (weight.astype(F32) + met[: weight.shape[0]]).astype(BF16)
-        before = jnp.where((here ^ mask) + 1 == here, met[weight.shape[0] :], before)
-        mask = 2 * mask + 1
+    count = weight.shape[0]
+    met = swapped(jnp.concatenate([weight, col_edge], axis=0), "bin", 1)
+    weight = (weight.astype(F32) + met[:count].astype(F32)).astype(BF16)
+    passed = met[count:]
+    before = jnp.where(here % 2 == 1, passed.astype(F32), jnp.zeros((edge, width), F32))
+    message = jnp.concatenate([weight, passed], axis=0)
+    mets = [swapped(message, "bin", mask).astype(F32) for mask in BIN_MASKS]
+    near, wrapped, far = [met[:count] for met in mets]
+    weight = ((weight.astype(F32) + near) + (far + wrapped)).astype(BF16)
+    for mask, met in zip(BIN_MASKS[:2], mets):
+        before = jnp.where((here % 2 == 0) & ((here ^ mask) + 2 == here), met[count:], before)
     col = jnp.concatenate([col[:edge] + before, col[edge:]], axis=0).astype(BF16)
     share = jnp.concatenate([share[:pairs], weight, col], axis=0)
     groups = [list(range(k, shares, 2)) for k in range(2)]

time: 95.1 us -> 87.9 us (0.924)
  waiting for transfers between devices: 16.7 us -> 9.59 us
  blocking collectives: 25.5 us -> 28.5 us
  local copies, waits for them, and re-layouts: 4.91 us -> 2.49 us
  starting transfers between devices: 22.9 us -> 21.2 us
    all_to_all x1, waiting for transfers between devices: 5.39 us -> 0.09 us  [across(): lax.all_to_all(block, axis, 0, 0, axis_index_groups=groups, tiled=True)]
    ppermute x4 -> x5, waiting for transfers between devices: 8.31 us -> 3.72 us  [swapped(): lax.ppermute(block, axis, [(i, i ^ bits) for i in range(lax.axis_size(axi...]
    all_to_all x2, blocking collectives: 25.5 us -> 28.5 us  [across(): lax.all_to_all(block, axis, 0, 0, axis_index_groups=groups, tiled=True)]
    ppermute x1, waiting for transfers between devices: 3.01 us -> 5.78 us  [shifted(): return lax.ppermute(block, axis, route)]
    unnamed x23 -> x24, local copies, waits for them, and re-layouts: 4.15 us -> 1.73 us
    ppermute x4 -> x5, starting transfers between devices: 14.6 us -> 12.4 us  [swapped(): lax.ppermute(block, axis, [(i, i ^ bits) for i in range(lax.axis_size(axi...]
    pallas_call x5 -> x4, Pallas kernels: 23.6 us -> 24.4 us  [call(): pl.pallas_call(kernel, out_shape=outs, in_specs=[space] * len(args), out_...]
  transfers between devices with their start and end apart: 6 -> 7, of which waited for: 6 -> 6; matrix products, arithmetic and copies ran while one was open for 0% -> 0% of each run, Pallas kernels for 4% -> 1%
where the time goes in v3:
time: 87.9 us; the launch traced here: 87.2 us
  blocking collectives  28.5 us (32%)
  Pallas kernels  24.4 us (28%)
  starting transfers between devices  21.2 us (24%)
  waiting for transfers between devices  9.59 us (11%)
  local copies, waits for them, and re-layouts  2.49 us (3%)
    all_to_all x2, blocking collectives, across(): lax.all_to_all(block, axis, 0, 0, axis_index_groups=groups, tiled=True)  28.5 us
    pallas_call x4, Pallas kernels, call(): pl.pallas_call(kernel, out_shape=outs, in_specs=[space] * len(args), out_...  24.4 us
    ppermute x5, starting transfers between devices, swapped(): lax.ppermute(block, axis, [(i, i ^ bits) for i in range(lax.axis_size(axi...  12.4 us
    all_to_all x1, starting transfers between devices, across(): lax.all_to_all(block, axis, 0, 0, axis_index_groups=groups, tiled=True)  7.48 us
    ppermute x1, waiting for transfers between devices, shifted(): return lax.ppermute(block, axis, route)  5.78 us
    ppermute x5, waiting for transfers between devices, swapped(): lax.ppermute(block, axis, [(i, i ^ bits) for i in range(lax.axis_size(axi...  3.72 us
  transfers between devices with their start and end apart: 7, of which 6 were waited for; matrix products, arithmetic and copies ran while one was open for 0% of the time, Pallas kernels for 1%

profile of v3, /device:TPU:1, one launch (start us, length us, event | category | flops | bytes accessed | tf_op | source)
XLA Modules:
  0.0 87.2 jit_solution(14159276187686400382)
XLA Ops:
  0.6 2.8 %shard_map.152 = (bf16[16,64,128]{2,1,0:T(8,128)(2,1)}, f32[512,256]{1,0:T(8,128)}, f32[64,128]{1,0:T(8,128)}, bf16[64,512]{1,0:T(8,128)(2,1)}, bf16[32,512]{1,0:T(8,128)(2,1)}) custom-call(s32[3,1,6]{2,1,0:T(1,128)} %bitcast.13, bf16[6,128,128]{2,1,0:T(8,128)(2,1)} %bitcast.11, bf16[1024,512]{1,0:T(8,128)(2,1)} %emb_ref.1, bf16[512,128]{1,0:T(8,128)(2,1)} %left_w_ref.1, ...), custom_call_target="tpu_custom_call" | custom-call | tf_op jit(solution)/shard_map/pallas_call | solution.py:331
  3.5 0.0 copy-start.11
  3.5 0.0 copy-start.1
  3.5 0.0 copy-start.4
  3.5 0.0 copy-start.5
  3.5 0.0 copy-start.6
  3.5 7.5 %all-to-all-start = ((bf16[16,64,128]{2,1,0:T(8,128)(2,1)}), bf16[16,64,128]{2,1,0:T(8,128)(2,1)S(1)}, u32[]{:S(2)}, u32[]{:S(2)}) async-start(bf16[16,64,128]{2,1,0:T(8,128)(2,1)} %get-tuple-element.27), calls=%async_computation | async-start | bytes 524288 | tf_op jit(solution)/shard_map/all_to_all | solution.py:352
  11.0 1.3 %collective-permute-start = (bf16[32,512]{1,0:T(8,128)(2,1)S(1)}, bf16[32,512]{1,0:T(8,128)(2,1)S(1)}, u32[]{:S(2)}, u32[]{:S(2)}) collective-permute-start(bf16[32,512]{1,0:T(8,128)(2,1)S(1)} %copy-done.11), channel_id=1, source_target_pairs={{16,0},{32,16},{48,32},{64,48},{80,64},{96,80},{112,96},{17,1},{33... | collective-permute-start | bytes 98312 | tf_op jit(solution)/shard_map/ppermute | solution.py:344
  12.3 5.8 %collective-permute-done.next_ref = bf16[32,512]{1,0:T(8,128)(2,1)S(1)} collective-permute-done((bf16[32,512]{1,0:T(8,128)(2,1)S(1)}, bf16[32,512]{1,0:T(8,128)(2,1)S(1)}, u32[]{:S(2)}, u32[]{:S(2)}) %collective-permute-start) | collective-permute-done | bytes 32800 | tf_op jit(solution)/shard_map/ppermute | solution.py:344
  18.1 0.1 all-to-all-done.target_ref
  18.3 0.6 copy-done.7
  18.9 1.0 %copy-done.3 = f32[512,256]{1,0:T(8,128)S(1)} copy-done((f32[512,256]{1,0:T(8,128)S(1)}, f32[512,256]{1,0:T(8,128)}, u32[]{:S(2)}) %copy-start.3) | copy-done | bytes 524312
  19.9 19.2 %shard_map.153 = (bf16[16,192,128]{2,1,0:T(8,128)(2,1)S(1)}, f32[64,128]{1,0:T(8,128)S(1)}, bf16[32,128]{1,0:T(8,128)(2,1)S(1)}) custom-call(f32[512,256]{1,0:T(8,128)S(1)} %copy-done.3, f32[64,128]{1,0:T(8,128)S(1)} %copy-done.6, bf16[1024,512]{1,0:T(8,128)(2,1)S(1)} %copy-done, bf16[64,512]{1,0:T(8,128)(2,1)S(1)} %copy-done.4, ...), custom_call_target="tpu_custom_call" | custom-call | tf_op jit(solution)/shard_map/pallas_call | solution.py:331
  39.2 18.8 %all_to_all.15.back_ref = bf16[16,192,128]{2,1,0:T(8,128)(2,1)S(1)} all-to-all(bf16[16,192,128]{2,1,0:T(8,128)(2,1)S(1)} %get-tuple-element.28), channel_id=1, replica_groups=mesh['bin'=8,'tile'=16] {'tile'}, dimensions={0} | all-to-all | bytes 1572864 | tf_op jit(solution)/shard_map/all_to_all | solution.py:352
  58.0 0.1 slice_reduce_fusion
  58.1 0.0 copy-start.10
  58.1 3.9 %collective-permute-start.1 = (bf16[112,128]{1,0:T(8,128)(2,1)S(1)}, bf16[112,128]{1,0:T(8,128)(2,1)S(1)}, u32[]{:S(2)}, u32[]{:S(2)}) collective-permute-start(bf16[112,128]{1,0:T(8,128)(2,1)S(1)} %pad_maximum_fusion.1), channel_id=1, source_target_pairs={{0,16},{16,0},{32,48},{48,32},{64,80},{80,64},{96,112},{112,96},{1... | collective-permute-start | bytes 86024 | tf_op jit(solution)/shard_map/ppermute | solution.py:348
  62.0 1.3 %collective-permute-done.1 = bf16[112,128]{1,0:T(8,128)(2,1)S(1)} collective-permute-done((bf16[112,128]{1,0:T(8,128)(2,1)S(1)}, bf16[112,128]{1,0:T(8,128)(2,1)S(1)}, u32[]{:S(2)}, u32[]{:S(2)}) %collective-permute-start.1) | collective-permute-done | bytes 28704 | tf_op jit(solution)/shard_map/ppermute | solution.py:348
  63.3 0.1 collective-permute-start.4
  63.4 1.5 %collective-permute-start.2 = (bf16[112,128]{1,0:T(8,128)(2,1)S(1)}, bf16[112,128]{1,0:T(8,128)(2,1)S(1)}, u32[]{:S(2)}, u32[]{:S(2)}) collective-permute-start(bf16[112,128]{1,0:T(8,128)(2,1)S(1)} %pad_maximum_fusion.2), channel_id=1, source_target_pairs={{0,32},{16,48},{32,0},{48,16},{64,96},{80,112},{96,64},{112,80},{1... | collective-permute-start | bytes 86024 | tf_op jit(solution)/shard_map/ppermute | solution.py:348
  64.9 2.3 %collective-permute-start.3 = (bf16[112,128]{1,0:T(8,128)(2,1)S(1)}, bf16[112,128]{1,0:T(8,128)(2,1)S(1)}, u32[]{:S(2)}, u32[]{:S(2)}) collective-permute-start(bf16[112,128]{1,0:T(8,128)(2,1)S(1)} %pad_maximum_fusion.2), channel_id=1, source_target_pairs={{0,64},{16,80},{32,96},{48,112},{64,0},{80,16},{96,32},{112,48},{1... | collective-permute-start | bytes 86024 | tf_op jit(solution)/shard_map/ppermute | solution.py:348
  67.3 0.1 collective-permute-done.4
  67.3 0.0 collective-permute-done.2
  67.3 1.8 %collective-permute-done.3 = bf16[112,128]{1,0:T(8,128)(2,1)S(1)} collective-permute-done((bf16[112,128]{1,0:T(8,128)(2,1)S(1)}, bf16[112,128]{1,0:T(8,128)(2,1)S(1)}, u32[]{:S(2)}, u32[]{:S(2)}) %collective-permute-start.3) | collective-permute-done | bytes 28704 | tf_op jit(solution)/shard_map/ppermute | solution.py:348
  69.2 0.0 slice-start
  69.2 0.7 slice-done
  69.9 0.1 broadcast_in_dim.22
  70.0 9.7 %all_to_all.16.mine_ref = bf16[8,208,128]{2,1,0:T(8,128)(2,1)S(1)} all-to-all(bf16[8,208,128]{2,1,0:T(8,128)(2,1)S(1)} %broadcast_in_dim.22), channel_id=1, replica_groups={{0,2,4,6,8,10,12,14},{1,3,5,7,9,11,13,15},{16,18,20,22,24,26,28,30},{17..., dimensions={0} | all-to-all | bytes 851968 | tf_op jit(solution)/shard_map/all_to_all | solution.py:352
  79.6 4.6 %collective-permute-start.5 = (bf16[8,208,128]{2,1,0:T(8,128)(2,1)S(1)}, bf16[8,208,128]{2,1,0:T(8,128)(2,1)S(1)}, u32[]{:S(2)}, u32[]{:S(2)}) collective-permute-start(bf16[8,208,128]{2,1,0:T(8,128)(2,1)S(1)} %all_to_all.16.mine_ref), channel_id=1, source_target_pairs={{0,1},{1,0},{2,3},{3,2},{4,5},{5,4},{6,7},{7,6},{8,9},{9,8},{10,11... | collective-permute-start | bytes 1277960 | tf_op jit(solution)/shard_map/ppermute | solution.py:348
  84.2 0.8 shard_map.154
  85.0 0.6 collective-permute-done.5.other_ref
  85.6 1.6 %shard_map.155 = (bf16[1024,512]{1,0:T(8,128)(2,1)}, f32[512,128]{1,0:T(8,128)}, f32[512,128]{1,0:T(8,128)}, f32[5,128]{1,0:T(8,128)}, f32[128,128]{1,0:T(8,128)}, /*index=5*/f32[1,128]{1,0:T(1,128)}, f32[1,128]{1,0:T(1,128)}) custom-call(bf16[8,208,128]{2,1,0:T(8,128)(2,1)S(1)} %all_to_all.16.mine_ref, ...), custom_call_target="tpu_custom_call" | custom-call | tf_op jit(solution)/shard_map/pallas_call | solution.py:331
  (27 shorter events, 0.1 us)
Async XLA Ops:
  0.6 17.6 %copy-start = (bf16[1024,512]{1,0:T(8,128)(2,1)S(1)}, bf16[1024,512]{1,0:T(8,128)(2,1)}, u32[]{:S(2)}) copy-start(bf16[1024,512]{1,0:T(8,128)(2,1)} %emb_ref.1) | copy-start | bytes 3145732
  3.5 7.5 %copy-start.11 = (bf16[32,512]{1,0:T(8,128)(2,1)S(1)}, bf16[32,512]{1,0:T(8,128)(2,1)}, u32[]{:S(2)}) copy-start(bf16[32,512]{1,0:T(8,128)(2,1)} %get-tuple-element.26) | copy-start | bytes 98308
  3.5 14.7 %copy-start.1 = (bf16[512,128]{1,0:T(8,128)(2,1)S(1)}, bf16[512,128]{1,0:T(8,128)(2,1)}, u32[]{:S(2)}) copy-start(bf16[512,128]{1,0:T(8,128)(2,1)} %right_w_ref.3) | copy-start | bytes 393220
  3.5 14.7 %copy-start.4 = (bf16[64,512]{1,0:T(8,128)(2,1)S(1)}, bf16[64,512]{1,0:T(8,128)(2,1)}, u32[]{:S(2)}) copy-start(bf16[64,512]{1,0:T(8,128)(2,1)} %get-tuple-element.25.cols_ref) | copy-start | bytes 196612
  3.5 14.7 %copy-start.5 = (bf16[128,128]{1,0:T(8,128)(2,1)S(1)}, bf16[128,128]{1,0:T(8,128)(2,1)}, u32[]{:S(2)}) copy-start(bf16[128,128]{1,0:T(8,128)(2,1)} %w_ref.1) | copy-start | bytes 98308
  3.5 14.7 %copy-start.6 = (f32[64,128]{1,0:T(8,128)S(1)}, f32[64,128]{1,0:T(8,128)}, u32[]{:S(2)}) copy-start(f32[64,128]{1,0:T(8,128)} %get-tuple-element.24.right_ref) | copy-start | bytes 98308
  3.5 14.7 %all-to-all-start = ((bf16[16,64,128]{2,1,0:T(8,128)(2,1)}), bf16[16,64,128]{2,1,0:T(8,128)(2,1)S(1)}, u32[]{:S(2)}, u32[]{:S(2)}) async-start(bf16[16,64,128]{2,1,0:T(8,128)(2,1)} %get-tuple-element.27), calls=%async_computation | async-start | bytes 524288 | tf_op jit(solution)/shard_map/all_to_all | solution.py:352
  11.0 7.1 %collective-permute-start = (bf16[32,512]{1,0:T(8,128)(2,1)S(1)}, bf16[32,512]{1,0:T(8,128)(2,1)S(1)}, u32[]{:S(2)}, u32[]{:S(2)}) collective-permute-start(bf16[32,512]{1,0:T(8,128)(2,1)S(1)} %copy-done.11), channel_id=1, source_target_pairs={{16,0},{32,16},{48,32},{64,48},{80,64},{96,80},{112,96},{17,1},{33... | collective-permute-start | bytes 98312 | tf_op jit(solution)/shard_map/ppermute | solution.py:344
  18.2 0.7 copy-start.7
  18.2 0.7 copy-start.8
  18.2 0.7 copy-start.9
  18.9 1.0 %copy-start.3 = (f32[512,256]{1,0:T(8,128)S(1)}, f32[512,256]{1,0:T(8,128)}, u32[]{:S(2)}) copy-start(f32[512,256]{1,0:T(8,128)} %get-tuple-element.23.left_ref) | copy-start | bytes 1572868
  58.1 9.2 %copy-start.10 = (bf16[144,128]{1,0:T(8,128)(2,1)}, bf16[144,128]{1,0:T(8,128)(2,1)S(1)}, u32[]{:S(2)}) copy-start(bf16[144,128]{1,0:T(8,128)(2,1)S(1)} %slice_reduce_fusion) | copy-start | bytes 110596
  58.1 5.2 %collective-permute-start.1 = (bf16[112,128]{1,0:T(8,128)(2,1)S(1)}, bf16[112,128]{1,0:T(8,128)(2,1)S(1)}, u32[]{:S(2)}, u32[]{:S(2)}) collective-permute-start(bf16[112,128]{1,0:T(8,128)(2,1)S(1)} %pad_maximum_fusion.1), channel_id=1, source_target_pairs={{0,16},{16,0},{32,48},{48,32},{64,80},{80,64},{96,112},{112,96},{1... | collective-permute-start | bytes 86024 | tf_op jit(solution)/shard_map/ppermute | solution.py:348
  63.3 4.0 %collective-permute-start.4 = (bf16[112,128]{1,0:T(8,128)(2,1)S(1)}, bf16[112,128]{1,0:T(8,128)(2,1)S(1)}, u32[]{:S(2)}, u32[]{:S(2)}) collective-permute-start(bf16[112,128]{1,0:T(8,128)(2,1)S(1)} %pad_maximum_fusion.2), channel_id=1, source_target_pairs={{0,96},{16,112},{32,64},{48,80},{64,32},{80,48},{96,0},{112,16},{1... | collective-permute-start | bytes 86024 | tf_op jit(solution)/shard_map/ppermute | solution.py:348
  63.4 3.9 %collective-permute-start.2 = (bf16[112,128]{1,0:T(8,128)(2,1)S(1)}, bf16[112,128]{1,0:T(8,128)(2,1)S(1)}, u32[]{:S(2)}, u32[]{:S(2)}) collective-permute-start(bf16[112,128]{1,0:T(8,128)(2,1)S(1)} %pad_maximum_fusion.2), channel_id=1, source_target_pairs={{0,32},{16,48},{32,0},{48,16},{64,96},{80,112},{96,64},{112,80},{1... | collective-permute-start | bytes 86024 | tf_op jit(solution)/shard_map/ppermute | solution.py:348
  64.9 4.2 %collective-permute-start.3 = (bf16[112,128]{1,0:T(8,128)(2,1)S(1)}, bf16[112,128]{1,0:T(8,128)(2,1)S(1)}, u32[]{:S(2)}, u32[]{:S(2)}) collective-permute-start(bf16[112,128]{1,0:T(8,128)(2,1)S(1)} %pad_maximum_fusion.2), channel_id=1, source_target_pairs={{0,64},{16,80},{32,96},{48,112},{64,0},{80,16},{96,32},{112,48},{1... | collective-permute-start | bytes 86024 | tf_op jit(solution)/shard_map/ppermute | solution.py:348
  69.2 0.7 slice-start
  79.6 6.0 %copy-start.2 = (bf16[512,128]{1,0:T(8,128)(2,1)S(1)}, bf16[512,128]{1,0:T(8,128)(2,1)}, u32[]{:S(2)}) copy-start(bf16[512,128]{1,0:T(8,128)(2,1)} %left_w_ref.1) | copy-start | bytes 393220
  79.6 6.0 %collective-permute-start.5 = (bf16[8,208,128]{2,1,0:T(8,128)(2,1)S(1)}, bf16[8,208,128]{2,1,0:T(8,128)(2,1)S(1)}, u32[]{:S(2)}, u32[]{:S(2)}) collective-permute-start(bf16[8,208,128]{2,1,0:T(8,128)(2,1)S(1)} %all_to_all.16.mine_ref), channel_id=1, source_target_pairs={{0,1},{1,0},{2,3},{3,2},{4,5},{5,4},{6,7},{7,6},{8,9},{9,8},{10,11... | collective-permute-start | bytes 1277960 | tf_op jit(solution)/shard_map/ppermute | solution.py:348

commit v4 on v3

--- a/solution.py
+++ b/solution.py
@@ -18,46 +18,26 @@
     return lax.axis_index("tile")
 
 
-def prepare_kernel(
-    list_hbm, target_hbm, emb_hbm, left_hbm, right_hbm,
-    send_ref, left_ref, right_ref, cols_ref, edge_ref,
-    list_ref, target_ref, emb_ref, left_w_ref, right_w_ref, flip_ref, listed_ref, full_ref, sems,
+def project_kernel(
+    emb_hbm, left_hbm, right_hbm,
+    left_ref, right_ref, cols_ref, edge_ref,
+    emb_ref, left_w_ref, right_w_ref, full_ref, sems,
 ):
     copies = [
         pltpu.make_async_copy(source, target, sems.at[k])
         for k, (source, target) in enumerate(
-            (
-                (target_hbm, target_ref),
-                (list_hbm, list_ref),
-                (left_hbm, left_w_ref),
-                (right_hbm, right_w_ref),
-                (emb_hbm, emb_ref),
-            )
+            ((left_hbm, left_w_ref), (right_hbm, right_w_ref), (emb_hbm, emb_ref))
         )
     ]
     for copy in copies:
         copy.start()
-    slots, width, _ = target_ref.shape
-    shares = send_ref.shape[0]
-    step = width // shares
+    for copy in copies:
+        copy.wait()
+    tile = place()
+    width = left_w_ref.shape[1]
     half = width // 2
     blocks = emb_ref.shape[0] // width
-    listed_ref[...] = jnp.zeros_like(listed_ref)
-    copies[0].wait()
-    for slot in range(slots):
-        flip_ref[slot] = (target_ref[slot].astype(F32) * (1.0 / width)).T
-    copies[1].wait()
-    for k in range(3):
-        listed_ref[k : k + 1, :slots] = list_ref[k].astype(F32)
-    listed = listed_ref[...]
-    spare = send_ref.shape[1] - (slots + 1) * step
-    for share in range(shares):
-        pieces = [flip_ref[slot, share * step : (share + 1) * step, :] for slot in range(slots)]
-        pieces += [listed, jnp.zeros((spare, width), F32)]
-        send_ref[share] = jnp.concatenate(pieces, axis=0).astype(BF16)
-    for copy in copies[2:]:
-        copy.wait()
-    tile = place()
+    step = right_ref.shape[0] // blocks
     weights = jnp.concatenate([left_w_ref[...], right_w_ref[...]], axis=1)
     for block in range(0, blocks, 2):
         both = jnp.dot(
@@ -83,17 +63,48 @@
     edge_ref[...] = rows[: edge_ref.shape[0]]
 
 
-def join_kernel(back_ref, pred_ref, flip_ref):
+def split_kernel(
+    list_mine, list_other, target_mine, target_other, send_ref, flip_ref, listed_ref
+):
+    core = place() & 1
+    slots, width, _ = target_mine.shape
+    chips = send_ref.shape[0]
+    step = width // (2 * chips)
+    listed_ref[...] = jnp.zeros_like(listed_ref)
+    for side in range(2):
+        mine = core == side
+        for k in range(3):
+            listed_ref[3 * side + k : 3 * side + k + 1, :slots] = jnp.where(
+                mine, list_mine[k], list_other[k]
+            ).astype(F32)
+        for slot in range(slots):
+            block = jnp.where(mine, target_mine[slot], target_other[slot]).astype(F32)
+            flip_ref[side * slots + slot] = (block * (1.0 / width)).T
+    listed = listed_ref[...].astype(BF16)
+    for chip in range(chips):
+        for side in range(2):
+            at = (2 * chip + core) * step
+            at = pl.multiple_of(at, step)
+            pieces = [
+                flip_ref[side * slots + slot, pl.ds(at, step), :] for slot in range(slots)
+            ]
+            send_ref[chip, side * slots * step : (side + 1) * slots * step, :] = jnp.concatenate(
+                pieces, axis=0
+            ).astype(BF16)
+        send_ref[chip, 2 * slots * step :, :] = listed
+
+
+def join_kernel(mine_ref, other_ref, pred_ref, flip_ref):
+    core = place() & 1
     slots, width, _ = pred_ref.shape
-    shares = back_ref.shape[0]
-    step = width // shares
-    at = back_ref.shape[1] - slots * step
-    for share in range(shares):
-        block = back_ref[share, at:, :].astype(F32)
-        for slot in range(slots):
-            flip_ref[slot, share * step : (share + 1) * step, :] = block[
-                slot * step : (slot + 1) * step
-            ]
+    chips = mine_ref.shape[0]
+    step = width // (2 * chips)
+    for chip in range(chips):
+        for ref, side in ((mine_ref, core), (other_ref, 1 - core)):
+            block = ref[chip].astype(F32)
+            to = pl.multiple_of((2 * chip + side) * step, step)
+            for slot in range(slots):
+                flip_ref[slot, pl.ds(to, step), :] = block[slot * step : (slot + 1) * step]
     for slot in range(slots):
         pred_ref[slot] = flip_ref[slot].T.astype(BF16)
 
@@ -101,24 +112,27 @@
 def pair_kernel(
     left_ref, right_ref, emb_ref, cols_ref, next_ref, right_w_ref, bias_ref, target_ref,
     w_ref, b_ref, out_ref,
-    sum_ref, col_ref, edge_ref,
+    keep_ref, send_ref, pred_ref, col_ref, edge_ref,
     table, lists, list_sem, list_all, right_all, target_all, pred_all, row_all, col_all,
     outer_all, bias_all, w_two, out_two, back_two, b_two, first_0, first_1, slope_0, slope_1,
 ):
     width = w_ref.shape[0]
     pairs = width // 2
     blocks = left_ref.shape[0] // pairs
-    shares = target_ref.shape[0]
+    chips = target_ref.shape[0]
+    shares = 2 * chips
     step = width // shares
-    slots = target_ref.shape[1] // step - 2
+    slots = target_ref.shape[1] // (2 * step) - 1
+    core = place() & 1
     groups = target_all.shape[0] - 1
     spread_bits = (width // step).bit_length() - 1
 
-    for share in range(shares):
-        rows = target_ref[share].astype(F32)
-        for k in range(3):
-            at = slots * step + k
-            list_all[k, share : share + 1] = rows[at : at + 1].astype(jnp.int32)
+    for chip in range(chips):
+        rows = target_ref[chip, 2 * slots * step :, :].astype(F32).astype(jnp.int32)
+        for side in range(2):
+            for k in range(3):
+                at = 3 * side + k
+                list_all[k, 2 * chip + side : 2 * chip + side + 1] = rows[at : at + 1]
     copy = pltpu.make_async_copy(list_all, lists, list_sem)
     copy.start()
 
@@ -136,7 +150,7 @@
     right_all[:own, :] = right_ref[...]
     right_next = jnp.dot(next_ref[...], right_w_ref[...], preferred_element_type=F32)
     right_all[own:, :] = right_next.astype(BF16).astype(F32)
-    rows = [target_ref[share].astype(F32)[: slots * step] for share in range(shares)]
+    rows = [target_ref[chip, : 2 * slots * step, :].astype(F32) for chip in range(chips)]
     rows = jnp.concatenate(rows, axis=0)
     for group in range(groups):
         target_all[group] = rows[group * width : (group + 1) * width].T
@@ -239,8 +253,8 @@
 
     flat = [(pred_all[group] * float(width)).T for group in range(groups)]
     flat = jnp.concatenate(flat, axis=0).astype(BF16)
-    for share in range(shares):
-        sum_ref[share, width + 16 :, :] = flat[share * slots * step : (share + 1) * slots * step]
+    for chip in range(chips):
+        pred_ref[chip] = flat[chip * 2 * slots * step : (chip + 1) * 2 * slots * step]
     outer = outer_all[:width, :width] + outer_all[width : 2 * width, width:]
     sum_d = outer_all[2 * width : 2 * width + 1, :width] + outer_all[2 * width : 2 * width + 1, width:]
     bias = bias_all[...]
@@ -266,16 +280,19 @@
             col, jnp.concatenate(embs, axis=0), contract, preferred_element_type=F32
         ).astype(BF16),
     )
-    half = shares // 2
-    for share in range(shares):
-        side, at = share // half, share % half
-        sum_ref[share, :pairs, :] = rows[share]
+    def message(share):
+        side, at = share // chips, share % chips
         grad = grads[side][:, at // 2 * width : (at // 2 + 1) * width]
-        sum_ref[share, pairs:width, :] = grad[at % 2 * pairs : (at % 2 + 1) * pairs]
         more = rest[share] if share < 2 else jnp.zeros_like(high)
-        sum_ref[share, width : width + 16, :] = jnp.concatenate(
-            [outer[8 * share : 8 * share + 8], more], axis=0
-        ).astype(BF16)
+        small = jnp.concatenate([outer[8 * share : 8 * share + 8], more], axis=0)
+        return jnp.concatenate(
+            [rows[share], grad[at % 2 * pairs : (at % 2 + 1) * pairs], small.astype(BF16)], axis=0
+        )
+
+    for chip in range(chips):
+        even, odd = message(2 * chip), message(2 * chip + 1)
+        keep_ref[chip] = jnp.where(core == 0, even, odd)
+        send_ref[chip] = jnp.where(core == 0, odd, even)
     col_ref[...] = col_all[:own]
     edge_ref[...] = col[own:]
 
@@ -367,37 +384,45 @@
     target = target[0, 0]
     lists = jnp.transpose(tile_list, (0, 3, 1, 2)).reshape(3, 1, slots)
 
-    target_send, left, right, emb_cols, emb_edge = call(
-        prepare_kernel,
+    target_other = swapped(target, "tile", 1)
+    lists_other = swapped(lists, "tile", 1)
+    left, right, emb_cols, emb_edge = call(
+        project_kernel,
         (
-            shape(shares, (slots + 2) * step, width, dtype=BF16),
             shape(rows // 2, 2 * width),
             shape(part, width),
             shape(part, features, dtype=BF16),
             shape(edge, features, dtype=BF16),
         ),
         [
-            pltpu.VMEM(lists.shape, jnp.int32),
-            pltpu.VMEM((slots, width, width), BF16),
             pltpu.VMEM((rows, features), BF16),
             pltpu.VMEM((features, width), BF16),
             pltpu.VMEM((features, width), BF16),
-            pltpu.VMEM((slots, width, width), F32),
-            pltpu.VMEM((step, width), F32),
             pltpu.VMEM((rows, width), F32),
-            pltpu.SemaphoreType.DMA((5,)),
+            pltpu.SemaphoreType.DMA((3,)),
         ],
-        lists, target, embeddings, w_left, w_right, space=HBM, limit=56,
-    )
-    target_all = across(target_send, "tile")
+        embeddings, w_left, w_right, space=HBM,
+    )
     emb_next = shifted(emb_edge, "bin", -1)
+    target_other, emb_cols = lax.optimization_barrier((target_other, emb_cols))
+    (target_send,) = call(
+        split_kernel,
+        (shape(chips, 2 * (slots + 1) * step, width, dtype=BF16),),
+        [pltpu.VMEM((2 * slots, width, width), F32), pltpu.VMEM((2 * step, width), F32)],
+        lists, lists_other, target, target_other,
+    )
+    groups = [list(range(k, shares, 2)) for k in range(2)]
+    target_all = across(target_send, "tile", groups)
 
     chunk = (BATCH * step * pairs, 2 * width)
     grouped = (slots * shares * step // width + 1, width, width)
-    sums, col, col_edge = call(
+    half = shape(chips, width + 16, width, dtype=BF16)
+    sums, sums_send, pred, col, col_edge = call(
         pair_kernel,
         (
-            shape(shares, width + 16 + slots * step, width, dtype=BF16),
+            half,
+            half,
+            shape(chips, 2 * slots * step, width, dtype=BF16),
             shape(part, width),
             shape(edge, width, dtype=BF16),
         ),
@@ -425,7 +450,13 @@
         left, right, embeddings, emb_cols, emb_next, w_right, pair_bias,
         target_all, w_pair, b_pair[None], w_out[None],
     )
-    sums = across(sums, "tile")
+    sums = (sums.astype(F32) + swapped(sums_send, "tile", 1).astype(F32)).astype(BF16)
+    sums = across(jnp.concatenate([sums, pred], axis=1), "tile", groups)
+    pred = sums[:, width + 16 :].reshape(chips, 2, slots * step, width)
+    pred_mine, pred_send = [
+        lax.dynamic_index_in_dim(pred, side, 1, keepdims=False) for side in (core, 1 - core)
+    ]
+    pred_other = swapped(pred_send, "tile", 1)
     share = jnp.sum(sums[:, : width + 16].astype(F32), axis=0).astype(BF16)
     weight = share[pairs:]
     here = lax.axis_index("bin")
@@ -442,13 +473,13 @@
         before = jnp.where((here % 2 == 0) & ((here ^ mask) + 2 == here), met[count:], before)
     col = jnp.concatenate([col[:edge] + before, col[edge:]], axis=0).astype(BF16)
     share = jnp.concatenate([share[:pairs], weight, col], axis=0)
-    groups = [list(range(k, shares, 2)) for k in range(2)]
+    share, pred_other = lax.optimization_barrier((share, pred_other))
     mine = across(jnp.broadcast_to(share[None], (chips, *share.shape)), "tile", groups)
     other = swapped(mine, "tile", 1)
     (predicted,) = call(
         join_kernel, (shape(slots, width, width, dtype=BF16),),
         [pltpu.VMEM((slots, width, width), F32)],
-        sums,
+        pred_mine, pred_other,
     )
     grads = call(
         last_kernel,

time: 87.9 us -> 86.9 us (0.989)
  starting transfers between devices: 21.2 us -> 26.5 us
  blocking collectives: 28.5 us -> 23.4 us
  Pallas kernels: 24.4 us -> 21.6 us
  local copies, waits for them, and re-layouts: 2.49 us -> 4.51 us
    ppermute x5 -> x9, starting transfers between devices: 12.4 us -> 19.4 us  [swapped(): lax.ppermute(block, axis, [(i, i ^ bits) for i in range(lax.axis_size(axi...]
    all_to_all x2, blocking collectives: 28.5 us -> 23.4 us  [across(): lax.all_to_all(block, axis, 0, 0, axis_index_groups=groups, tiled=True)]
    pallas_call x4 -> x5, Pallas kernels: 24.4 us -> 21.6 us  [call(): pl.pallas_call(kernel, out_shape=outs, in_specs=[space] * len(args), out_...]
    unnamed x24 -> x26, local copies, waits for them, and re-layouts: 1.73 us -> 3.73 us
    all_to_all x1, starting transfers between devices: 7.48 us -> 5.76 us  [across(): lax.all_to_all(block, axis, 0, 0, axis_index_groups=groups, tiled=True)]
    ppermute x5 -> x9, waiting for transfers between devices: 3.72 us -> 3.56 us  [swapped(): lax.ppermute(block, axis, [(i, i ^ bits) for i in range(lax.axis_size(axi...]
  transfers between devices with their start and end apart: 7 -> 11, of which waited for: 6 -> 6; matrix products, arithmetic and copies ran while one was open for 0% -> 0% of each run, Pallas kernels for 1% -> 2%
where the time goes in v4:
time: 86.9 us; the launch traced here: 86.4 us
  starting transfers between devices  26.5 us (30%)
  blocking collectives  23.4 us (27%)
  Pallas kernels  21.6 us (25%)
  waiting for transfers between devices  9.35 us (11%)
  local copies, waits for them, and re-layouts  4.51 us (5%)
    all_to_all x2, blocking collectives, across(): lax.all_to_all(block, axis, 0, 0, axis_index_groups=groups, tiled=True)  23.4 us
    pallas_call x5, Pallas kernels, call(): pl.pallas_call(kernel, out_shape=outs, in_specs=[space] * len(args), out_...  21.6 us
    ppermute x9, starting transfers between devices, swapped(): lax.ppermute(block, axis, [(i, i ^ bits) for i in range(lax.axis_size(axi...  19.4 us
    all_to_all x1, starting transfers between devices, across(): lax.all_to_all(block, axis, 0, 0, axis_index_groups=groups, tiled=True)  5.76 us
    ppermute x1, waiting for transfers between devices, shifted(): return lax.ppermute(block, axis, route)  5.62 us
    unnamed x26, local copies, waits for them, and re-layouts  3.73 us
    ppermute x9, waiting for transfers between devices, swapped(): lax.ppermute(block, axis, [(i, i ^ bits) for i in range(lax.axis_size(axi...  3.56 us
  transfers between devices with their start and end apart: 11, of which 6 were waited for; matrix products, arithmetic and copies ran while one was open for 0% of the time, Pallas kernels for 2%

profile of v4, /device:TPU:1, one launch (start us, length us, event | category | flops | bytes accessed | tf_op | source)
XLA Modules:
  0.0 86.4 jit_solution(10577175506860635595)
XLA Ops:
  0.6 1.5 %collective-permute-start = (bf16[6,128,128]{2,1,0:T(8,128)(2,1)}, bf16[6,128,128]{2,1,0:T(8,128)(2,1)S(1)}, u32[]{:S(2)}, u32[]{:S(2)}) collective-permute-start(bf16[6,128,128]{2,1,0:T(8,128)(2,1)} %bitcast.18), channel_id=1, source_target_pairs={{0,1},{1,0},{2,3},{3,2},{4,5},{5,4},{6,7},{7,6},{8,9},{9,8},{10,11... | collective-permute-start | bytes 589832 | tf_op jit(solution)/shard_map/ppermute | solution.py:365
  2.1 0.6 collective-permute-start.2
  2.7 1.2 %copy-done = bf16[1024,512]{1,0:T(8,128)(2,1)S(1)} copy-done((bf16[1024,512]{1,0:T(8,128)(2,1)S(1)}, bf16[1024,512]{1,0:T(8,128)(2,1)}, u32[]{:S(2)}) %copy-start) | copy-done | bytes 1048600
  4.0 0.9 %copy-done.2 = bf16[512,128]{1,0:T(8,128)(2,1)S(1)} copy-done((bf16[512,128]{1,0:T(8,128)(2,1)S(1)}, bf16[512,128]{1,0:T(8,128)(2,1)}, u32[]{:S(2)}) %copy-start.2) | copy-done | bytes 131096
  4.9 0.9 %copy-done.4 = bf16[512,128]{1,0:T(8,128)(2,1)S(1)} copy-done((bf16[512,128]{1,0:T(8,128)(2,1)S(1)}, bf16[512,128]{1,0:T(8,128)(2,1)}, u32[]{:S(2)}) %copy-start.4) | copy-done | bytes 131096
  5.8 0.9 %shard_map.152 = (f32[512,256]{1,0:T(8,128)S(1)}, f32[64,128]{1,0:T(8,128)S(1)}, bf16[64,512]{1,0:T(8,128)(2,1)S(1)}, bf16[32,512]{1,0:T(8,128)(2,1)S(1)}) custom-call(bf16[1024,512]{1,0:T(8,128)(2,1)S(1)} %copy-done, bf16[512,128]{1,0:T(8,128)(2,1)S(1)} %copy-done.4, bf16[512,128]{1,0:T(8,128)(2,1)S(1)} %copy-done.2), custom_call_target="tpu_custom_call" | custom-call | tf_op jit(solution)/shard_map/pallas_call | solution.py:348
  6.7 0.0 copy-done.6
  6.7 1.1 %shard_map.153 = bf16[8,112,128]{2,1,0:T(8,128)(2,1)} custom-call(s32[3,1,6]{2,1,0:T(1,128)S(1)} %bitcast.21, s32[3,1,6]{2,1,0:T(1,128)S(1)} %collective-permute-done.2.list_other, bf16[6,128,128]{2,1,0:T(8,128)(2,1)S(1)} %bitcast.19, bf16[6,128,128]{2,1,0:T(8,128)(2,1)S(1)} %collective-permute-done.target_other), custom_call_target="tpu_custom_call" | custom-call | tf_op jit(solution)/shard_map/pallas_call | solution.py:348
  7.8 5.8 %all-to-all-start = ((bf16[8,112,128]{2,1,0:T(8,128)(2,1)}), bf16[8,112,128]{2,1,0:T(8,128)(2,1)S(1)}, u32[]{:S(2)}, u32[]{:S(2)}) async-start(bf16[8,112,128]{2,1,0:T(8,128)(2,1)} %shard_map.153), calls=%async_computation | async-start | bytes 458752 | tf_op jit(solution)/shard_map/all_to_all | solution.py:369
  13.5 1.3 %collective-permute-start.1 = (bf16[32,512]{1,0:T(8,128)(2,1)S(1)}, bf16[32,512]{1,0:T(8,128)(2,1)S(1)}, u32[]{:S(2)}, u32[]{:S(2)}) collective-permute-start(bf16[32,512]{1,0:T(8,128)(2,1)S(1)} %get-tuple-element.32), channel_id=1, source_target_pairs={{16,0},{32,16},{48,32},{64,48},{80,64},{96,80},{112,96},{17,1},{33... | collective-permute-start | bytes 98312 | tf_op jit(solution)/shard_map/ppermute | solution.py:361
  14.8 5.6 %collective-permute-done.1.next_ref = bf16[32,512]{1,0:T(8,128)(2,1)S(1)} collective-permute-done((bf16[32,512]{1,0:T(8,128)(2,1)S(1)}, bf16[32,512]{1,0:T(8,128)(2,1)S(1)}, u32[]{:S(2)}, u32[]{:S(2)}) %collective-permute-start.1) | collective-permute-done | bytes 32800 | tf_op jit(solution)/shard_map/ppermute | solution.py:361
  20.5 0.2 all-to-all-done.target_ref
  20.7 0.6 copy-done.10
  21.3 17.2 %shard_map.154 = (bf16[8,144,128]{2,1,0:T(8,128)(2,1)S(1)}, bf16[8,144,128]{2,1,0:T(8,128)(2,1)S(1)}, bf16[8,96,128]{2,1,0:T(8,128)(2,1)S(1)}, f32[64,128]{1,0:T(8,128)S(1)}, bf16[32,128]{1,0:T(8,128)(2,1)S(1)}) custom-call(f32[512,256]{1,0:T(8,128)S(1)} %get-tuple-element.28.left_ref, f32[64,128]{1,0:T(8,128)S(1)} %get-tuple-element.29.right_ref, ...), custom_call_target="tpu_custom_call" | custom-call | tf_op jit(solution)/shard_map/pallas_call | solution.py:348
  38.5 0.9 %collective-permute-start.3 = (bf16[8,144,128]{2,1,0:T(8,128)(2,1)S(1)}, bf16[8,144,128]{2,1,0:T(8,128)(2,1)S(1)}, u32[]{:S(2)}, u32[]{:S(2)}) collective-permute-start(bf16[8,144,128]{2,1,0:T(8,128)(2,1)S(1)} %get-tuple-element.35), channel_id=1, source_target_pairs={{0,1},{1,0},{2,3},{3,2},{4,5},{5,4},{6,7},{7,6},{8,9},{9,8},{10,11... | collective-permute-start | bytes 884744 | tf_op jit(solution)/shard_map/ppermute | solution.py:365
  39.4 1.2 %collective-permute-done.3 = bf16[8,144,128]{2,1,0:T(8,128)(2,1)S(1)} collective-permute-done((bf16[8,144,128]{2,1,0:T(8,128)(2,1)S(1)}, bf16[8,144,128]{2,1,0:T(8,128)(2,1)S(1)}, u32[]{:S(2)}, u32[]{:S(2)}) %collective-permute-start.3) | collective-permute-done | bytes 294944 | tf_op jit(solution)/shard_map/ppermute | solution.py:365
  40.6 0.1 add_convert_fusion
  40.8 14.0 %all_to_all.15 = bf16[8,240,128]{2,1,0:T(8,128)(2,1)S(1)} all-to-all(bf16[8,240,128]{2,1,0:T(8,128)(2,1)S(1)} %pad_maximum_fusion), channel_id=1, replica_groups={{0,2,4,6,8,10,12,14},{1,3,5,7,9,11,13,15},{16,18,20,22,24,26,28,30},{17..., dimensions={0} | all-to-all | bytes 983040 | tf_op jit(solution)/shard_map/all_to_all | solution.py:369
  54.8 2.6 %collective-permute-start.4 = (bf16[112,128]{1,0:T(8,128)(2,1)S(1)}, bf16[112,128]{1,0:T(8,128)(2,1)S(1)}, u32[]{:S(2)}, u32[]{:S(2)}) collective-permute-start(bf16[112,128]{1,0:T(8,128)(2,1)S(1)} %pad_maximum_fusion.2), channel_id=1, source_target_pairs={{0,16},{16,0},{32,48},{48,32},{64,80},{80,64},{96,112},{112,96},{1... | collective-permute-start | bytes 86024 | tf_op jit(solution)/shard_map/ppermute | solution.py:365
  57.5 1.6 %collective-permute-done.4 = bf16[112,128]{1,0:T(8,128)(2,1)S(1)} collective-permute-done((bf16[112,128]{1,0:T(8,128)(2,1)S(1)}, bf16[112,128]{1,0:T(8,128)(2,1)S(1)}, u32[]{:S(2)}, u32[]{:S(2)}) %collective-permute-start.4) | collective-permute-done | bytes 28704 | tf_op jit(solution)/shard_map/ppermute | solution.py:365
  59.1 4.2 %collective-permute-start.7 = (bf16[112,128]{1,0:T(8,128)(2,1)S(1)}, bf16[112,128]{1,0:T(8,128)(2,1)S(1)}, u32[]{:S(2)}, u32[]{:S(2)}) collective-permute-start(bf16[112,128]{1,0:T(8,128)(2,1)S(1)} %pad_maximum_fusion.3), channel_id=1, source_target_pairs={{0,96},{16,112},{32,64},{48,80},{64,32},{80,48},{96,0},{112,16},{1... | collective-permute-start | bytes 86024 | tf_op jit(solution)/shard_map/ppermute | solution.py:365
  63.4 0.4 collective-permute-start.6
  63.7 0.3 collective-permute-start.5
  64.0 3.5 %collective-permute-start.8 = (bf16[8,48,128]{2,1,0:T(8,128)(2,1)S(1)}, bf16[8,48,128]{2,1,0:T(8,128)(2,1)S(1)}, u32[]{:S(2)}, u32[]{:S(2)}) collective-permute-start(bf16[8,48,128]{2,1,0:T(8,128)(2,1)S(1)} %get-tuple-element.48), channel_id=1, source_target_pairs={{0,1},{1,0},{2,3},{3,2},{4,5},{5,4},{6,7},{7,6},{8,9},{9,8},{10,11... | collective-permute-start | bytes 294920 | tf_op jit(solution)/shard_map/ppermute | solution.py:365
  67.7 0.7 slice-done
  68.4 0.1 collective-permute-done.8.other_ref
  68.5 0.1 broadcast_in_dim.22
  68.6 9.4 %all_to_all.16.mine_ref = bf16[8,208,128]{2,1,0:T(8,128)(2,1)S(1)} all-to-all(bf16[8,208,128]{2,1,0:T(8,128)(2,1)S(1)} %broadcast_in_dim.22), channel_id=1, replica_groups={{0,2,4,6,8,10,12,14},{1,3,5,7,9,11,13,15},{16,18,20,22,24,26,28,30},{17..., dimensions={0} | all-to-all | bytes 851968 | tf_op jit(solution)/shard_map/all_to_all | solution.py:369
  78.0 5.4 %collective-permute-start.9 = (bf16[8,208,128]{2,1,0:T(8,128)(2,1)S(1)}, bf16[8,208,128]{2,1,0:T(8,128)(2,1)S(1)}, u32[]{:S(2)}, u32[]{:S(2)}) collective-permute-start(bf16[8,208,128]{2,1,0:T(8,128)(2,1)S(1)} %all_to_all.16.mine_ref), channel_id=1, source_target_pairs={{0,1},{1,0},{2,3},{3,2},{4,5},{5,4},{6,7},{7,6},{8,9},{9,8},{10,11... | collective-permute-start | bytes 1277960 | tf_op jit(solution)/shard_map/ppermute | solution.py:365
  83.4 0.8 shard_map.155
  84.2 0.5 collective-permute-done.9.other_ref
  84.8 1.6 %shard_map.156 = (bf16[1024,512]{1,0:T(8,128)(2,1)}, f32[512,128]{1,0:T(8,128)}, f32[512,128]{1,0:T(8,128)}, f32[5,128]{1,0:T(8,128)}, f32[128,128]{1,0:T(8,128)}, /*index=5*/f32[1,128]{1,0:T(1,128)}, f32[1,128]{1,0:T(1,128)}) custom-call(bf16[8,208,128]{2,1,0:T(8,128)(2,1)S(1)} %all_to_all.16.mine_ref, ...), custom_call_target="tpu_custom_call" | custom-call | tf_op jit(solution)/shard_map/pallas_call | solution.py:348
  (42 shorter events, 0.3 us)
Async XLA Ops:
  0.6 1.5 %copy-start.9 = (s32[1,1,6,3]{2,1,3,0:T(1,128)S(1)}, s32[1,1,6,3]{2,1,3,0:T(1,128)}, u32[]{:S(2)}) copy-start(s32[1,1,6,3]{2,1,3,0:T(1,128)} %param.16) | copy-start | bytes 220
  0.6 6.0 %collective-permute-start = (bf16[6,128,128]{2,1,0:T(8,128)(2,1)}, bf16[6,128,128]{2,1,0:T(8,128)(2,1)S(1)}, u32[]{:S(2)}, u32[]{:S(2)}) collective-permute-start(bf16[6,128,128]{2,1,0:T(8,128)(2,1)} %bitcast.18), channel_id=1, source_target_pairs={{0,1},{1,0},{2,3},{3,2},{4,5},{5,4},{6,7},{7,6},{8,9},{9,8},{10,11... | collective-permute-start | bytes 589832 | tf_op jit(solution)/shard_map/ppermute | solution.py:365
  2.1 4.5 %collective-permute-start.2 = (s32[3,1,6]{2,1,0:T(1,128)S(1)}, s32[3,1,6]{2,1,0:T(1,128)S(1)}, u32[]{:S(2)}, u32[]{:S(2)}) collective-permute-start(s32[3,1,6]{2,1,0:T(1,128)S(1)} %bitcast.20), channel_id=1, source_target_pairs={{0,1},{1,0},{2,3},{3,2},{4,5},{5,4},{6,7},{7,6},{8,9},{9,8},{10,11... | collective-permute-start | bytes 224 | tf_op jit(solution)/shard_map/ppermute | solution.py:365
  2.7 1.2 %copy-start = (bf16[1024,512]{1,0:T(8,128)(2,1)S(1)}, bf16[1024,512]{1,0:T(8,128)(2,1)}, u32[]{:S(2)}) copy-start(bf16[1024,512]{1,0:T(8,128)(2,1)} %emb_ref.1) | copy-start | bytes 3145732
  4.0 0.9 %copy-start.2 = (bf16[512,128]{1,0:T(8,128)(2,1)S(1)}, bf16[512,128]{1,0:T(8,128)(2,1)}, u32[]{:S(2)}) copy-start(bf16[512,128]{1,0:T(8,128)(2,1)} %right_w_ref.3) | copy-start | bytes 393220
  4.9 0.9 %copy-start.4 = (bf16[512,128]{1,0:T(8,128)(2,1)S(1)}, bf16[512,128]{1,0:T(8,128)(2,1)}, u32[]{:S(2)}) copy-start(bf16[512,128]{1,0:T(8,128)(2,1)} %left_w_ref.1) | copy-start | bytes 393220
  5.8 0.9 %copy-start.6 = (bf16[1,1,6,128,128]{4,3,2,1,0:T(8,128)(2,1)S(1)}, bf16[1,1,6,128,128]{4,3,2,1,0:T(8,128)(2,1)}, u32[]{:S(2)}) copy-start(bf16[1,1,6,128,128]{4,3,2,1,0:T(8,128)(2,1)} %param.17) | copy-start | bytes 589828
  5.8 14.9 %copy-start.1 = (bf16[1024,512]{1,0:T(8,128)(2,1)S(1)}, bf16[1024,512]{1,0:T(8,128)(2,1)}, u32[]{:S(2)}) copy-start(bf16[1024,512]{1,0:T(8,128)(2,1)} %emb_ref.1) | copy-start | bytes 3145732
  7.8 12.9 %copy-start.3 = (bf16[512,128]{1,0:T(8,128)(2,1)S(1)}, bf16[512,128]{1,0:T(8,128)(2,1)}, u32[]{:S(2)}) copy-start(bf16[512,128]{1,0:T(8,128)(2,1)} %right_w_ref.3) | copy-start | bytes 393220
  7.8 12.9 %copy-start.7 = (bf16[128,128]{1,0:T(8,128)(2,1)S(1)}, bf16[128,128]{1,0:T(8,128)(2,1)}, u32[]{:S(2)}) copy-start(bf16[128,128]{1,0:T(8,128)(2,1)} %w_ref.1) | copy-start | bytes 98308
  7.8 12.8 %all-to-all-start = ((bf16[8,112,128]{2,1,0:T(8,128)(2,1)}), bf16[8,112,128]{2,1,0:T(8,128)(2,1)S(1)}, u32[]{:S(2)}, u32[]{:S(2)}) async-start(bf16[8,112,128]{2,1,0:T(8,128)(2,1)} %shard_map.153), calls=%async_computation | async-start | bytes 458752 | tf_op jit(solution)/shard_map/all_to_all | solution.py:369
  13.5 7.1 %copy-start.8 = (f32[5,128]{1,0:T(8,128)S(1)}, f32[5,128]{1,0:T(8,128)}, u32[]{:S(2)}) copy-start(f32[5,128]{1,0:T(8,128)} %bias_ref.1) | copy-start | bytes 7684
  13.5 6.9 %collective-permute-start.1 = (bf16[32,512]{1,0:T(8,128)(2,1)S(1)}, bf16[32,512]{1,0:T(8,128)(2,1)S(1)}, u32[]{:S(2)}, u32[]{:S(2)}) collective-permute-start(bf16[32,512]{1,0:T(8,128)(2,1)S(1)} %get-tuple-element.32), channel_id=1, source_target_pairs={{16,0},{32,16},{48,32},{64,48},{80,64},{96,80},{112,96},{17,1},{33... | collective-permute-start | bytes 98312 | tf_op jit(solution)/shard_map/ppermute | solution.py:361
  20.6 0.7 copy-start.10
  20.6 0.7 copy-start.11
  38.5 2.1 %collective-permute-start.3 = (bf16[8,144,128]{2,1,0:T(8,128)(2,1)S(1)}, bf16[8,144,128]{2,1,0:T(8,128)(2,1)S(1)}, u32[]{:S(2)}, u32[]{:S(2)}) collective-permute-start(bf16[8,144,128]{2,1,0:T(8,128)(2,1)S(1)} %get-tuple-element.35), channel_id=1, source_target_pairs={{0,1},{1,0},{2,3},{3,2},{4,5},{5,4},{6,7},{7,6},{8,9},{9,8},{10,11... | collective-permute-start | bytes 884744 | tf_op jit(solution)/shard_map/ppermute | solution.py:365
  54.8 9.3 %copy-start.12 = (bf16[144,128]{1,0:T(8,128)(2,1)}, bf16[144,128]{1,0:T(8,128)(2,1)S(1)}, u32[]{:S(2)}) copy-start(bf16[144,128]{1,0:T(8,128)(2,1)S(1)} %slice_reduce_fusion) | copy-start | bytes 110596
  54.8 4.3 %collective-permute-start.4 = (bf16[112,128]{1,0:T(8,128)(2,1)S(1)}, bf16[112,128]{1,0:T(8,128)(2,1)S(1)}, u32[]{:S(2)}, u32[]{:S(2)}) collective-permute-start(bf16[112,128]{1,0:T(8,128)(2,1)S(1)} %pad_maximum_fusion.2), channel_id=1, source_target_pairs={{0,16},{16,0},{32,48},{48,32},{64,80},{80,64},{96,112},{112,96},{1... | collective-permute-start | bytes 86024 | tf_op jit(solution)/shard_map/ppermute | solution.py:365
  59.1 8.4 %collective-permute-start.7 = (bf16[112,128]{1,0:T(8,128)(2,1)S(1)}, bf16[112,128]{1,0:T(8,128)(2,1)S(1)}, u32[]{:S(2)}, u32[]{:S(2)}) collective-permute-start(bf16[112,128]{1,0:T(8,128)(2,1)S(1)} %pad_maximum_fusion.3), channel_id=1, source_target_pairs={{0,96},{16,112},{32,64},{48,80},{64,32},{80,48},{96,0},{112,16},{1... | collective-permute-start | bytes 86024 | tf_op jit(solution)/shard_map/ppermute | solution.py:365
  63.4 4.3 %collective-permute-start.6 = (bf16[112,128]{1,0:T(8,128)(2,1)S(1)}, bf16[112,128]{1,0:T(8,128)(2,1)S(1)}, u32[]{:S(2)}, u32[]{:S(2)}) collective-permute-start(bf16[112,128]{1,0:T(8,128)(2,1)S(1)} %pad_maximum_fusion.3), channel_id=1, source_target_pairs={{0,64},{16,80},{32,96},{48,112},{64,0},{80,16},{96,32},{112,48},{1... | collective-permute-start | bytes 86024 | tf_op jit(solution)/shard_map/ppermute | solution.py:365
  63.7 3.9 %collective-permute-start.5 = (bf16[112,128]{1,0:T(8,128)(2,1)S(1)}, bf16[112,128]{1,0:T(8,128)(2,1)S(1)}, u32[]{:S(2)}, u32[]{:S(2)}) collective-permute-start(bf16[112,128]{1,0:T(8,128)(2,1)S(1)} %pad_maximum_fusion.3), channel_id=1, source_target_pairs={{0,32},{16,48},{32,0},{48,16},{64,96},{80,112},{96,64},{112,80},{1... | collective-permute-start | bytes 86024 | tf_op jit(solution)/shard_map/ppermute | solution.py:365
  64.0 4.5 %collective-permute-start.8 = (bf16[8,48,128]{2,1,0:T(8,128)(2,1)S(1)}, bf16[8,48,128]{2,1,0:T(8,128)(2,1)S(1)}, u32[]{:S(2)}, u32[]{:S(2)}) collective-permute-start(bf16[8,48,128]{2,1,0:T(8,128)(2,1)S(1)} %get-tuple-element.48), channel_id=1, source_target_pairs={{0,1},{1,0},{2,3},{3,2},{4,5},{5,4},{6,7},{7,6},{8,9},{9,8},{10,11... | collective-permute-start | bytes 294920 | tf_op jit(solution)/shard_map/ppermute | solution.py:365
  67.6 0.7 slice-start
  78.0 6.8 %collective-permute-start.9 = (bf16[8,208,128]{2,1,0:T(8,128)(2,1)S(1)}, bf16[8,208,128]{2,1,0:T(8,128)(2,1)S(1)}, u32[]{:S(2)}, u32[]{:S(2)}) collective-permute-start(bf16[8,208,128]{2,1,0:T(8,128)(2,1)S(1)} %all_to_all.16.mine_ref), channel_id=1, source_target_pairs={{0,1},{1,0},{2,3},{3,2},{4,5},{5,4},{6,7},{7,6},{8,9},{9,8},{10,11... | collective-permute-start | bytes 1277960 | tf_op jit(solution)/shard_map/ppermute | solution.py:365
  83.4 1.4 %copy-start.5 = (bf16[512,128]{1,0:T(8,128)(2,1)S(1)}, bf16[512,128]{1,0:T(8,128)(2,1)}, u32[]{:S(2)}) copy-start(bf16[512,128]{1,0:T(8,128)(2,1)} %left_w_ref.1) | copy-start | bytes 393220

commit v5 on v4

--- a/solution.py
+++ b/solution.py
@@ -139,13 +139,14 @@
     w = w_ref[...].astype(F32)
     w_out = out_ref[...]
     back = (w * w_out).T.astype(BF16)
-    spread = jnp.broadcast_to(w_out * (1.0 / width), (width, width)).T.astype(BF16)
-    for ref, block in ((w_two, w_ref[...]), (out_two, spread), (back_two, back)):
+    for ref, block in ((w_two, w_ref[...]), (back_two, back)):
         ref[...] = jnp.zeros_like(ref)
         ref[:width, :width] = block
         ref[width:, width:] = block
     b_two[:, :width] = b_ref[...]
     b_two[:, width:] = b_ref[...]
+    out_two[:, :width] = w_out * (1.0 / width)
+    out_two[:, width:] = w_out * (1.0 / width)
     own = right_ref.shape[0]
     right_all[:own, :] = right_ref[...]
     right_next = jnp.dot(next_ref[...], right_w_ref[...], preferred_element_type=F32)
@@ -202,10 +203,19 @@
         first_ref[...] = first
         act = jnp.dot(first, w_two[...], preferred_element_type=F32)
         act = act + jnp.concatenate(floors, axis=0)
-        second = jnp.maximum(act, 0.0).astype(BF16)
-        contact = jnp.dot(second, out_two[...], preferred_element_type=F32)
-        slope = (contact - jnp.concatenate(wanted, axis=0)).astype(BF16)
-        slope_ref[...] = jnp.where(second > 0, slope, jnp.zeros_like(slope))
+        parts = jnp.maximum(act, 0.0) * out_two[...]
+        contact = jnp.concatenate(
+            [
+                jnp.broadcast_to(
+                    jnp.sum(parts[:, s * width : (s + 1) * width], axis=1, keepdims=True),
+                    (parts.shape[0], width),
+                )
+                for s in range(2)
+            ],
+            axis=1,
+        )
+        slope = contact - jnp.concatenate(wanted, axis=0)
+        slope_ref[...] = jnp.where(act > 0.0, slope, 0.0).astype(BF16)
         for k, (group, shift) in enumerate(shifts):
             found = jnp.zeros((width, width), F32)
             for j in range(step):
@@ -401,7 +411,7 @@
             pltpu.VMEM((rows, width), F32),
             pltpu.SemaphoreType.DMA((3,)),
         ],
-        embeddings, w_left, w_right, space=HBM,
+        embeddings, w_left, w_right, space=HBM, limit=56,
     )
     emb_next = shifted(emb_edge, "bin", -1)
     target_other, emb_cols = lax.optimization_barrier((target_other, emb_cols))
@@ -412,6 +422,9 @@
         lists, lists_other, target, target_other,
     )
     groups = [list(range(k, shares, 2)) for k in range(2)]
+    target_send, emb_next, left, right, emb_cols = lax.optimization_barrier(
+        (target_send, emb_next, left, right, emb_cols)
+    )
     target_all = across(target_send, "tile", groups)
 
     chunk = (BATCH * step * pairs, 2 * width)
@@ -439,7 +452,7 @@
             pltpu.VMEM((2 * width + 16, 2 * width), F32),
             pltpu.VMEM((8, width), F32),
             pltpu.VMEM((2 * width, 2 * width), BF16),
-            pltpu.VMEM((2 * width, 2 * width), BF16),
+            pltpu.VMEM((1, 2 * width), F32),
             pltpu.VMEM((2 * width, 2 * width), BF16),
             pltpu.VMEM((1, 2 * width), F32),
             pltpu.VMEM(chunk, BF16),

time: 86.9 us -> 95 us (1.093)
  blocking collectives: 23.4 us -> 31.6 us
  Pallas kernels: 21.6 us -> 28.9 us
  starting transfers between devices: 26.5 us -> 22.6 us
  local copies, waits for them, and re-layouts: 4.51 us -> 1.45 us
    all_to_all x2 -> x3, blocking collectives: 23.4 us -> 31.6 us  [across(): lax.all_to_all(block, axis, 0, 0, axis_index_groups=groups, tiled=True)]
    pallas_call x5, Pallas kernels: 21.6 us -> 28.9 us  [call(): pl.pallas_call(kernel, out_shape=outs, in_specs=[space] * len(args), out_...]
    all_to_all x1 -> x0, starting transfers between devices: 5.76 us -> none  [across(): lax.all_to_all(block, axis, 0, 0, axis_index_groups=groups, tiled=True)]
    unnamed x26, local copies, waits for them, and re-layouts: 3.73 us -> 0.66 us
    ppermute x9, starting transfers between devices: 19.4 us -> 21.3 us  [swapped(): lax.ppermute(block, axis, [(i, i ^ bits) for i in range(lax.axis_size(axi...]
    ppermute x1, waiting for transfers between devices: 5.62 us -> 4.54 us  [shifted(): return lax.ppermute(block, axis, route)]
  transfers between devices with their start and end apart: 11 -> 10, of which waited for: 6 -> 6; matrix products, arithmetic and copies ran while one was open for 0% -> 0% of each run, Pallas kernels for 2% -> 4%
where the time goes in v5:
time: 95 us; the launch traced here: 94.6 us
  blocking collectives  31.6 us (33%)
  Pallas kernels  28.9 us (30%)
  starting transfers between devices  22.6 us (24%)
  waiting for transfers between devices  8.93 us (9%)
  local copies, waits for them, and re-layouts  1.45 us (2%)
    all_to_all x3, blocking collectives, across(): lax.all_to_all(block, axis, 0, 0, axis_index_groups=groups, tiled=True)  31.6 us
    pallas_call x5, Pallas kernels, call(): pl.pallas_call(kernel, out_shape=outs, in_specs=[space] * len(args), out_...  28.9 us
    ppermute x9, starting transfers between devices, swapped(): lax.ppermute(block, axis, [(i, i ^ bits) for i in range(lax.axis_size(axi...  21.3 us
    ppermute x1, waiting for transfers between devices, shifted(): return lax.ppermute(block, axis, route)  4.54 us
    ppermute x9, waiting for transfers between devices, swapped(): lax.ppermute(block, axis, [(i, i ^ bits) for i in range(lax.axis_size(axi...  4.39 us
  transfers between devices with their start and end apart: 10, of which 6 were waited for; matrix products, arithmetic and copies ran while one was open for 0% of the time, Pallas kernels for 4%

profile of v5, /device:TPU:1, one launch (start us, length us, event | category | flops | bytes accessed | tf_op | source)
XLA Modules:
  0.0 94.6 jit_solution(4661562976360962979)
XLA Ops:
  0.7 1.5 %collective-permute-start.1 = (bf16[6,128,128]{2,1,0:T(8,128)(2,1)}, bf16[6,128,128]{2,1,0:T(8,128)(2,1)S(1)}, u32[]{:S(2)}, u32[]{:S(2)}) collective-permute-start(bf16[6,128,128]{2,1,0:T(8,128)(2,1)} %bitcast.18), channel_id=1, source_target_pairs={{0,1},{1,0},{2,3},{3,2},{4,5},{5,4},{6,7},{7,6},{8,9},{9,8},{10,11... | collective-permute-start | bytes 589832 | tf_op jit(solution)/shard_map/ppermute | solution.py:375
  2.2 2.6 %shard_map.152 = (f32[512,256]{1,0:T(8,128)}, f32[64,128]{1,0:T(8,128)}, bf16[64,512]{1,0:T(8,128)(2,1)}, bf16[32,512]{1,0:T(8,128)(2,1)}) custom-call(bf16[1024,512]{1,0:T(8,128)(2,1)} %emb_ref.1, bf16[512,128]{1,0:T(8,128)(2,1)} %left_w_ref.1, bf16[512,128]{1,0:T(8,128)(2,1)} %right_w_ref.3), custom_call_target="tpu_custom_call" | custom-call | tf_op jit(solution)/shard_map/pallas_call | solution.py:358
  4.8 0.0 copy-start.9
  4.8 1.3 %collective-permute-start.2 = (bf16[32,512]{1,0:T(8,128)(2,1)}, bf16[32,512]{1,0:T(8,128)(2,1)S(1)}, u32[]{:S(2)}, u32[]{:S(2)}) collective-permute-start(bf16[32,512]{1,0:T(8,128)(2,1)} %get-tuple-element.35), channel_id=1, source_target_pairs={{16,0},{32,16},{48,32},{64,48},{80,64},{96,80},{112,96},{17,1},{33... | collective-permute-start | bytes 98312 | tf_op jit(solution)/shard_map/ppermute | solution.py:371
  6.1 0.2 collective-permute-start
  6.3 1.1 %collective-permute-done.list_other = s32[3,1,6]{2,1,0:T(1,128)S(1)} collective-permute-done((s32[3,1,6]{2,1,0:T(1,128)S(1)}, s32[3,1,6]{2,1,0:T(1,128)S(1)}, u32[]{:S(2)}, u32[]{:S(2)}) %collective-permute-start) | collective-permute-done | bytes 104 | tf_op jit(solution)/shard_map/ppermute | solution.py:375
  7.4 0.4 shard_map.153
  7.7 4.5 %collective-permute-done.2.next_ref = bf16[32,512]{1,0:T(8,128)(2,1)S(1)} collective-permute-done((bf16[32,512]{1,0:T(8,128)(2,1)}, bf16[32,512]{1,0:T(8,128)(2,1)S(1)}, u32[]{:S(2)}, u32[]{:S(2)}) %collective-permute-start.2) | collective-permute-done | bytes 32800 | tf_op jit(solution)/shard_map/ppermute | solution.py:371
  12.3 0.0 copy-start.8
  12.3 10.6 %all_to_all.15.target_ref = bf16[8,112,128]{2,1,0:T(8,128)(2,1)S(1)} all-to-all(bf16[8,112,128]{2,1,0:T(8,128)(2,1)S(1)} %shard_map.153), channel_id=1, replica_groups={{0,2,4,6,8,10,12,14},{1,3,5,7,9,11,13,15},{16,18,20,22,24,26,28,30},{17..., dimensions={0} | all-to-all | bytes 458752 | tf_op jit(solution)/shard_map/all_to_all | solution.py:379
  23.0 0.6 copy-done.10
  23.6 0.0 copy-done.11
  23.6 23.4 %shard_map.154 = (bf16[8,144,128]{2,1,0:T(8,128)(2,1)S(1)}, bf16[8,144,128]{2,1,0:T(8,128)(2,1)S(1)}, bf16[8,96,128]{2,1,0:T(8,128)(2,1)S(1)}, f32[64,128]{1,0:T(8,128)S(1)}, bf16[32,128]{1,0:T(8,128)(2,1)S(1)}) custom-call(f32[512,256]{1,0:T(8,128)S(1)} %copy-done.3, f32[64,128]{1,0:T(8,128)S(1)} %copy-done.7, bf16[1024,512]{1,0:T(8,128)(2,1)S(1)} %copy-done, ...), custom_call_target="tpu_custom_call" | custom-call | tf_op jit(solution)/shard_map/pallas_call | solution.py:358
  47.0 2.6 %collective-permute-start.3 = (bf16[8,144,128]{2,1,0:T(8,128)(2,1)S(1)}, bf16[8,144,128]{2,1,0:T(8,128)(2,1)S(1)}, u32[]{:S(2)}, u32[]{:S(2)}) collective-permute-start(bf16[8,144,128]{2,1,0:T(8,128)(2,1)S(1)} %get-tuple-element.45), channel_id=1, source_target_pairs={{0,1},{1,0},{2,3},{3,2},{4,5},{5,4},{6,7},{7,6},{8,9},{9,8},{10,11... | collective-permute-start | bytes 884744 | tf_op jit(solution)/shard_map/ppermute | solution.py:375
  49.6 1.2 %collective-permute-done.3 = bf16[8,144,128]{2,1,0:T(8,128)(2,1)S(1)} collective-permute-done((bf16[8,144,128]{2,1,0:T(8,128)(2,1)S(1)}, bf16[8,144,128]{2,1,0:T(8,128)(2,1)S(1)}, u32[]{:S(2)}, u32[]{:S(2)}) %collective-permute-start.3) | collective-permute-done | bytes 294944 | tf_op jit(solution)/shard_map/ppermute | solution.py:375
  50.8 0.1 add_convert_fusion
  50.9 11.6 %all_to_all.16 = bf16[8,240,128]{2,1,0:T(8,128)(2,1)S(1)} all-to-all(bf16[8,240,128]{2,1,0:T(8,128)(2,1)S(1)} %pad_maximum_fusion), channel_id=1, replica_groups={{0,2,4,6,8,10,12,14},{1,3,5,7,9,11,13,15},{16,18,20,22,24,26,28,30},{17..., dimensions={0} | all-to-all | bytes 983040 | tf_op jit(solution)/shard_map/all_to_all | solution.py:379
  62.6 0.0 copy-start.12
  62.6 4.6 %collective-permute-start.4 = (bf16[112,128]{1,0:T(8,128)(2,1)S(1)}, bf16[112,128]{1,0:T(8,128)(2,1)S(1)}, u32[]{:S(2)}, u32[]{:S(2)}) collective-permute-start(bf16[112,128]{1,0:T(8,128)(2,1)S(1)} %pad_maximum_fusion.2), channel_id=1, source_target_pairs={{0,16},{16,0},{32,48},{48,32},{64,80},{80,64},{96,112},{112,96},{1... | collective-permute-start | bytes 86024 | tf_op jit(solution)/shard_map/ppermute | solution.py:375
  67.2 1.2 %collective-permute-done.4 = bf16[112,128]{1,0:T(8,128)(2,1)S(1)} collective-permute-done((bf16[112,128]{1,0:T(8,128)(2,1)S(1)}, bf16[112,128]{1,0:T(8,128)(2,1)S(1)}, u32[]{:S(2)}, u32[]{:S(2)}) %collective-permute-start.4) | collective-permute-done | bytes 28704 | tf_op jit(solution)/shard_map/ppermute | solution.py:375
  68.5 3.3 %collective-permute-start.7 = (bf16[112,128]{1,0:T(8,128)(2,1)S(1)}, bf16[112,128]{1,0:T(8,128)(2,1)S(1)}, u32[]{:S(2)}, u32[]{:S(2)}) collective-permute-start(bf16[112,128]{1,0:T(8,128)(2,1)S(1)} %pad_maximum_fusion.3), channel_id=1, source_target_pairs={{0,96},{16,112},{32,64},{48,80},{64,32},{80,48},{96,0},{112,16},{1... | collective-permute-start | bytes 86024 | tf_op jit(solution)/shard_map/ppermute | solution.py:375
  71.9 0.4 collective-permute-start.6
  72.2 0.3 collective-permute-start.5
  72.6 3.3 %collective-permute-start.8 = (bf16[8,48,128]{2,1,0:T(8,128)(2,1)S(1)}, bf16[8,48,128]{2,1,0:T(8,128)(2,1)S(1)}, u32[]{:S(2)}, u32[]{:S(2)}) collective-permute-start(bf16[8,48,128]{2,1,0:T(8,128)(2,1)S(1)} %get-tuple-element.58), channel_id=1, source_target_pairs={{0,1},{1,0},{2,3},{3,2},{4,5},{5,4},{6,7},{7,6},{8,9},{9,8},{10,11... | collective-permute-start | bytes 294920 | tf_op jit(solution)/shard_map/ppermute | solution.py:375
  75.9 0.3 collective-permute-done.6
  76.2 0.7 slice-done
  76.9 0.1 broadcast_in_dim.22
  77.0 9.4 %all_to_all.17.mine_ref = bf16[8,208,128]{2,1,0:T(8,128)(2,1)S(1)} all-to-all(bf16[8,208,128]{2,1,0:T(8,128)(2,1)S(1)} %broadcast_in_dim.22), channel_id=1, replica_groups={{0,2,4,6,8,10,12,14},{1,3,5,7,9,11,13,15},{16,18,20,22,24,26,28,30},{17..., dimensions={0} | all-to-all | bytes 851968 | tf_op jit(solution)/shard_map/all_to_all | solution.py:379
  86.4 5.2 %collective-permute-start.9 = (bf16[8,208,128]{2,1,0:T(8,128)(2,1)S(1)}, bf16[8,208,128]{2,1,0:T(8,128)(2,1)S(1)}, u32[]{:S(2)}, u32[]{:S(2)}) collective-permute-start(bf16[8,208,128]{2,1,0:T(8,128)(2,1)S(1)} %all_to_all.17.mine_ref), channel_id=1, source_target_pairs={{0,1},{1,0},{2,3},{3,2},{4,5},{5,4},{6,7},{7,6},{8,9},{9,8},{10,11... | collective-permute-start | bytes 1277960 | tf_op jit(solution)/shard_map/ppermute | solution.py:375
  91.7 0.8 shard_map.155
  92.5 0.5 collective-permute-done.9.other_ref
  93.1 1.6 %shard_map.156 = (bf16[1024,512]{1,0:T(8,128)(2,1)}, f32[512,128]{1,0:T(8,128)}, f32[512,128]{1,0:T(8,128)}, f32[5,128]{1,0:T(8,128)}, f32[128,128]{1,0:T(8,128)}, /*index=5*/f32[1,128]{1,0:T(1,128)}, f32[1,128]{1,0:T(1,128)}) custom-call(bf16[8,208,128]{2,1,0:T(8,128)(2,1)S(1)} %all_to_all.17.mine_ref, ...), custom_call_target="tpu_custom_call" | custom-call | tf_op jit(solution)/shard_map/pallas_call | solution.py:358
  (41 shorter events, 0.2 us)
Async XLA Ops:
  0.6 6.7 %copy-start.4 = (bf16[1,1,6,128,128]{4,3,2,1,0:T(8,128)(2,1)S(1)}, bf16[1,1,6,128,128]{4,3,2,1,0:T(8,128)(2,1)}, u32[]{:S(2)}) copy-start(bf16[1,1,6,128,128]{4,3,2,1,0:T(8,128)(2,1)} %param.17) | copy-start | bytes 589828
  0.6 22.3 %copy-start = (bf16[1024,512]{1,0:T(8,128)(2,1)S(1)}, bf16[1024,512]{1,0:T(8,128)(2,1)}, u32[]{:S(2)}) copy-start(bf16[1024,512]{1,0:T(8,128)(2,1)} %emb_ref.1) | copy-start | bytes 3145732
  0.7 5.7 %collective-permute-start.1 = (bf16[6,128,128]{2,1,0:T(8,128)(2,1)}, bf16[6,128,128]{2,1,0:T(8,128)(2,1)S(1)}, u32[]{:S(2)}, u32[]{:S(2)}) collective-permute-start(bf16[6,128,128]{2,1,0:T(8,128)(2,1)} %bitcast.18), channel_id=1, source_target_pairs={{0,1},{1,0},{2,3},{3,2},{4,5},{5,4},{6,7},{7,6},{8,9},{9,8},{10,11... | collective-permute-start | bytes 589832 | tf_op jit(solution)/shard_map/ppermute | solution.py:375
  4.8 1.3 %copy-start.9 = (s32[1,1,6,3]{2,1,3,0:T(1,128)S(1)}, s32[1,1,6,3]{2,1,3,0:T(1,128)}, u32[]{:S(2)}) copy-start(s32[1,1,6,3]{2,1,3,0:T(1,128)} %param.16) | copy-start | bytes 220
  4.8 7.5 %collective-permute-start.2 = (bf16[32,512]{1,0:T(8,128)(2,1)}, bf16[32,512]{1,0:T(8,128)(2,1)S(1)}, u32[]{:S(2)}, u32[]{:S(2)}) collective-permute-start(bf16[32,512]{1,0:T(8,128)(2,1)} %get-tuple-element.35), channel_id=1, source_target_pairs={{16,0},{32,16},{48,32},{64,48},{80,64},{96,80},{112,96},{17,1},{33... | collective-permute-start | bytes 98312 | tf_op jit(solution)/shard_map/ppermute | solution.py:371
  6.1 1.2 %collective-permute-start = (s32[3,1,6]{2,1,0:T(1,128)S(1)}, s32[3,1,6]{2,1,0:T(1,128)S(1)}, u32[]{:S(2)}, u32[]{:S(2)}) collective-permute-start(s32[3,1,6]{2,1,0:T(1,128)S(1)} %bitcast.20), channel_id=1, source_target_pairs={{0,1},{1,0},{2,3},{3,2},{4,5},{5,4},{6,7},{7,6},{8,9},{9,8},{10,11... | collective-permute-start | bytes 224 | tf_op jit(solution)/shard_map/ppermute | solution.py:375
  6.3 16.6 %copy-start.3 = (f32[512,256]{1,0:T(8,128)S(1)}, f32[512,256]{1,0:T(8,128)}, u32[]{:S(2)}) copy-start(f32[512,256]{1,0:T(8,128)} %get-tuple-element.39.left_ref) | copy-start | bytes 1572868
  12.3 10.6 %copy-start.1 = (bf16[512,128]{1,0:T(8,128)(2,1)S(1)}, bf16[512,128]{1,0:T(8,128)(2,1)}, u32[]{:S(2)}) copy-start(bf16[512,128]{1,0:T(8,128)(2,1)} %right_w_ref.3) | copy-start | bytes 393220
  12.3 10.6 %copy-start.5 = (bf16[64,512]{1,0:T(8,128)(2,1)S(1)}, bf16[64,512]{1,0:T(8,128)(2,1)}, u32[]{:S(2)}) copy-start(bf16[64,512]{1,0:T(8,128)(2,1)} %get-tuple-element.41.cols_ref) | copy-start | bytes 196612
  12.3 10.7 %copy-start.6 = (bf16[128,128]{1,0:T(8,128)(2,1)S(1)}, bf16[128,128]{1,0:T(8,128)(2,1)}, u32[]{:S(2)}) copy-start(bf16[128,128]{1,0:T(8,128)(2,1)} %w_ref.1) | copy-start | bytes 98308
  12.3 10.7 %copy-start.7 = (f32[64,128]{1,0:T(8,128)S(1)}, f32[64,128]{1,0:T(8,128)}, u32[]{:S(2)}) copy-start(f32[64,128]{1,0:T(8,128)} %get-tuple-element.40.right_ref) | copy-start | bytes 98308
  12.3 10.7 %copy-start.8 = (f32[5,128]{1,0:T(8,128)S(1)}, f32[5,128]{1,0:T(8,128)}, u32[]{:S(2)}) copy-start(f32[5,128]{1,0:T(8,128)} %bias_ref.1) | copy-start | bytes 7684
  22.9 0.7 copy-start.10
  22.9 0.7 copy-start.11
  47.0 3.8 %collective-permute-start.3 = (bf16[8,144,128]{2,1,0:T(8,128)(2,1)S(1)}, bf16[8,144,128]{2,1,0:T(8,128)(2,1)S(1)}, u32[]{:S(2)}, u32[]{:S(2)}) collective-permute-start(bf16[8,144,128]{2,1,0:T(8,128)(2,1)S(1)} %get-tuple-element.45), channel_id=1, source_target_pairs={{0,1},{1,0},{2,3},{3,2},{4,5},{5,4},{6,7},{7,6},{8,9},{9,8},{10,11... | collective-permute-start | bytes 884744 | tf_op jit(solution)/shard_map/ppermute | solution.py:375
  62.6 10.0 %copy-start.12 = (bf16[144,128]{1,0:T(8,128)(2,1)}, bf16[144,128]{1,0:T(8,128)(2,1)S(1)}, u32[]{:S(2)}) copy-start(bf16[144,128]{1,0:T(8,128)(2,1)S(1)} %slice_reduce_fusion) | copy-start | bytes 110596
  62.6 5.9 %collective-permute-start.4 = (bf16[112,128]{1,0:T(8,128)(2,1)S(1)}, bf16[112,128]{1,0:T(8,128)(2,1)S(1)}, u32[]{:S(2)}, u32[]{:S(2)}) collective-permute-start(bf16[112,128]{1,0:T(8,128)(2,1)S(1)} %pad_maximum_fusion.2), channel_id=1, source_target_pairs={{0,16},{16,0},{32,48},{48,32},{64,80},{80,64},{96,112},{112,96},{1... | collective-permute-start | bytes 86024 | tf_op jit(solution)/shard_map/ppermute | solution.py:375
  68.5 7.3 %collective-permute-start.7 = (bf16[112,128]{1,0:T(8,128)(2,1)S(1)}, bf16[112,128]{1,0:T(8,128)(2,1)S(1)}, u32[]{:S(2)}, u32[]{:S(2)}) collective-permute-start(bf16[112,128]{1,0:T(8,128)(2,1)S(1)} %pad_maximum_fusion.3), channel_id=1, source_target_pairs={{0,96},{16,112},{32,64},{48,80},{64,32},{80,48},{96,0},{112,16},{1... | collective-permute-start | bytes 86024 | tf_op jit(solution)/shard_map/ppermute | solution.py:375
  71.9 4.3 %collective-permute-start.6 = (bf16[112,128]{1,0:T(8,128)(2,1)S(1)}, bf16[112,128]{1,0:T(8,128)(2,1)S(1)}, u32[]{:S(2)}, u32[]{:S(2)}) collective-permute-start(bf16[112,128]{1,0:T(8,128)(2,1)S(1)} %pad_maximum_fusion.3), channel_id=1, source_target_pairs={{0,64},{16,80},{32,96},{48,112},{64,0},{80,16},{96,32},{112,48},{1... | collective-permute-start | bytes 86024 | tf_op jit(solution)/shard_map/ppermute | solution.py:375
  72.2 3.6 %collective-permute-start.5 = (bf16[112,128]{1,0:T(8,128)(2,1)S(1)}, bf16[112,128]{1,0:T(8,128)(2,1)S(1)}, u32[]{:S(2)}, u32[]{:S(2)}) collective-permute-start(bf16[112,128]{1,0:T(8,128)(2,1)S(1)} %pad_maximum_fusion.3), channel_id=1, source_target_pairs={{0,32},{16,48},{32,0},{48,16},{64,96},{80,112},{96,64},{112,80},{1... | collective-permute-start | bytes 86024 | tf_op jit(solution)/shard_map/ppermute | solution.py:375
  72.6 4.4 %collective-permute-start.8 = (bf16[8,48,128]{2,1,0:T(8,128)(2,1)S(1)}, bf16[8,48,128]{2,1,0:T(8,128)(2,1)S(1)}, u32[]{:S(2)}, u32[]{:S(2)}) collective-permute-start(bf16[8,48,128]{2,1,0:T(8,128)(2,1)S(1)} %get-tuple-element.58), channel_id=1, source_target_pairs={{0,1},{1,0},{2,3},{3,2},{4,5},{5,4},{6,7},{7,6},{8,9},{9,8},{10,11... | collective-permute-start | bytes 294920 | tf_op jit(solution)/shard_map/ppermute | solution.py:375
  76.2 0.7 slice-start
  86.4 6.6 %collective-permute-start.9 = (bf16[8,208,128]{2,1,0:T(8,128)(2,1)S(1)}, bf16[8,208,128]{2,1,0:T(8,128)(2,1)S(1)}, u32[]{:S(2)}, u32[]{:S(2)}) collective-permute-start(bf16[8,208,128]{2,1,0:T(8,128)(2,1)S(1)} %all_to_all.17.mine_ref), channel_id=1, source_target_pairs={{0,1},{1,0},{2,3},{3,2},{4,5},{5,4},{6,7},{7,6},{8,9},{9,8},{10,11... | collective-permute-start | bytes 1277960 | tf_op jit(solution)/shard_map/ppermute | solution.py:375
  91.7 1.4 %copy-start.2 = (bf16[512,128]{1,0:T(8,128)(2,1)S(1)}, bf16[512,128]{1,0:T(8,128)(2,1)}, u32[]{:S(2)}) copy-start(bf16[512,128]{1,0:T(8,128)(2,1)} %left_w_ref.1) | copy-start | bytes 393220

commit v6 on v4

--- a/solution.py
+++ b/solution.py
@@ -9,7 +9,6 @@
 BF16 = jnp.bfloat16
 BATCH = 2
 NEVER = -1e38
-BIN_MASKS = (2, 6, 4)
 VMEM = pl.BlockSpec(memory_space=pltpu.VMEM)
 HBM = pl.BlockSpec(memory_space=pl.ANY)
 
@@ -20,7 +19,7 @@
 
 def project_kernel(
     emb_hbm, left_hbm, right_hbm,
-    left_ref, right_ref, cols_ref, edge_ref,
+    left_ref, right_ref,
     emb_ref, left_w_ref, right_w_ref, full_ref, sems,
 ):
     copies = [
@@ -51,16 +50,9 @@
             left_ref[at : at + half, :width] = left[:half]
             left_ref[at : at + half, width:] = left[half:]
         full_ref[block * width : (block + 2) * width, :] = both[:, width:]
-    rows = []
     for block in range(blocks):
         at = pl.multiple_of(block * width + tile * step, step)
         right_ref[block * step : (block + 1) * step, :] = full_ref[pl.ds(at, step), :]
-        at = pl.multiple_of(block * width + (tile >> 1) * (2 * step), 2 * step)
-        near = emb_ref[pl.ds(at, 2 * step), :].astype(F32)
-        rows.append(jnp.where((tile & 1) == 0, near[:step], near[step:]))
-    rows = jnp.concatenate(rows, axis=0).astype(BF16)
-    cols_ref[...] = rows
-    edge_ref[...] = rows[: edge_ref.shape[0]]
 
 
 def split_kernel(
@@ -192,9 +184,9 @@
             pre += [left + right[j : j + 1, :] for j in range(step)]
             target = pltpu.roll(
                 target_all[slot >> spread_bits], (width - shift) & (width - 1), 1
-            )
+            ).astype(BF16)
             for j in range(step):
-                want = jnp.broadcast_to(target[:, j : j + 1], (width, width))
+                want = jnp.broadcast_to(target[:, j : j + 1], (width, width)).astype(F32)
                 wanted.append(jnp.concatenate([want[:pairs], want[pairs:]], axis=1))
             floor = jnp.where(job < count, b_two[...], jnp.full((1, 2 * width), NEVER, F32))
             floors.append(jnp.broadcast_to(floor, (step * pairs, 2 * width)))
@@ -295,6 +287,50 @@
         send_ref[chip] = jnp.where(core == 0, odd, even)
     col_ref[...] = col_all[:own]
     edge_ref[...] = col[own:]
+
+
+def share_kernel(sum_ref, edge_ref, row_ref, message_ref, mine_ref, send_ref):
+    core = place() & 1
+    chips, _, width = sum_ref.shape
+    pairs = width // 2
+    head = width + 16
+    slot_rows = mine_ref.shape[1]
+    total = jnp.zeros((head, width), F32)
+    for chip in range(chips):
+        total = total + sum_ref[chip, :head, :].astype(F32)
+        first = sum_ref[chip, head : head + slot_rows, :]
+        second = sum_ref[chip, head + slot_rows :, :]
+        mine_ref[chip] = jnp.where(core == 0, first, second)
+        send_ref[chip] = jnp.where(core == 0, second, first)
+    total = total.astype(BF16)
+    row_ref[...] = total[:pairs]
+    for bin_at in range(message_ref.shape[0]):
+        message_ref[bin_at, : head - pairs, :] = total[pairs:]
+        message_ref[bin_at, head - pairs :, :] = edge_ref[...]
+
+
+def total_kernel(met_ref, row_ref, col_ref, message_ref):
+    here = lax.axis_index("bin")
+    bins = met_ref.shape[0]
+    width = row_ref.shape[1]
+    pairs = row_ref.shape[0]
+    edge = col_ref.shape[0] // 2
+    count = met_ref.shape[1] - edge
+    total = jnp.zeros((count, width), F32)
+    before = jnp.zeros((edge, width), F32)
+    for bin_at in range(bins):
+        total = total + met_ref[bin_at, :count, :].astype(F32)
+        near = met_ref[bin_at, count:, :].astype(F32)
+        before = jnp.where(here == bin_at + 1, near, before)
+    total = total.astype(BF16)
+    col = col_ref[...]
+    top = (col[:edge] + before).astype(BF16)
+    low = col[edge:].astype(BF16)
+    for chip in range(message_ref.shape[0]):
+        message_ref[chip, :pairs, :] = row_ref[...]
+        message_ref[chip, pairs : pairs + count, :] = total
+        message_ref[chip, pairs + count : pairs + count + edge, :] = top
+        message_ref[chip, pairs + count + edge :, :] = low
 
 
 def last_kernel(
@@ -384,16 +420,15 @@
     target = target[0, 0]
     lists = jnp.transpose(tile_list, (0, 3, 1, 2)).reshape(3, 1, slots)
 
+    emb_cols = lax.dynamic_slice_in_dim(
+        embeddings.reshape(blocks, shares, step, features), tile, 1, 1
+    ).reshape(part, features)
+    emb_next = shifted(emb_cols[:edge], "bin", -1)
     target_other = swapped(target, "tile", 1)
     lists_other = swapped(lists, "tile", 1)
-    left, right, emb_cols, emb_edge = call(
+    left, right = call(
         project_kernel,
-        (
-            shape(rows // 2, 2 * width),
-            shape(part, width),
-            shape(part, features, dtype=BF16),
-            shape(edge, features, dtype=BF16),
-        ),
+        (shape(rows // 2, 2 * width), shape(part, width)),
         [
             pltpu.VMEM((rows, features), BF16),
             pltpu.VMEM((features, width), BF16),
@@ -401,10 +436,9 @@
             pltpu.VMEM((rows, width), F32),
             pltpu.SemaphoreType.DMA((3,)),
         ],
-        embeddings, w_left, w_right, space=HBM,
-    )
-    emb_next = shifted(emb_edge, "bin", -1)
-    target_other, emb_cols = lax.optimization_barrier((target_other, emb_cols))
+        embeddings, w_left, w_right, space=HBM, limit=56,
+    )
+    target_other, emb_next, left = lax.optimization_barrier((target_other, emb_next, left))
     (target_send,) = call(
         split_kernel,
         (shape(chips, 2 * (slots + 1) * step, width, dtype=BF16),),
@@ -452,29 +486,26 @@
     )
     sums = (sums.astype(F32) + swapped(sums_send, "tile", 1).astype(F32)).astype(BF16)
     sums = across(jnp.concatenate([sums, pred], axis=1), "tile", groups)
-    pred = sums[:, width + 16 :].reshape(chips, 2, slots * step, width)
-    pred_mine, pred_send = [
-        lax.dynamic_index_in_dim(pred, side, 1, keepdims=False) for side in (core, 1 - core)
-    ]
+    bins = lax.axis_size("bin")
+    row, weight, pred_mine, pred_send = call(
+        share_kernel,
+        (
+            shape(pairs, width, dtype=BF16),
+            shape(bins, pairs + 16 + edge, width, dtype=BF16),
+            shape(chips, slots * step, width, dtype=BF16),
+            shape(chips, slots * step, width, dtype=BF16),
+        ),
+        [], sums, col_edge,
+    )
+    weight = across(weight, "bin")
+    (mine,) = call(
+        total_kernel,
+        (shape(chips, width + 16 + part, width, dtype=BF16),),
+        [], weight, row, col,
+    )
+    mine = across(mine, "tile", groups)
+    mine, pred_send = lax.optimization_barrier((mine, pred_send))
     pred_other = swapped(pred_send, "tile", 1)
-    share = jnp.sum(sums[:, : width + 16].astype(F32), axis=0).astype(BF16)
-    weight = share[pairs:]
-    here = lax.axis_index("bin")
-    count = weight.shape[0]
-    met = swapped(jnp.concatenate([weight, col_edge], axis=0), "bin", 1)
-    weight = (weight.astype(F32) + met[:count].astype(F32)).astype(BF16)
-    passed = met[count:]
-    before = jnp.where(here % 2 == 1, passed.astype(F32), jnp.zeros((edge, width), F32))
-    message = jnp.concatenate([weight, passed], axis=0)
-    mets = [swapped(message, "bin", mask).astype(F32) for mask in BIN_MASKS]
-    near, wrapped, far = [met[:count] for met in mets]
-    weight = ((weight.astype(F32) + near) + (far + wrapped)).astype(BF16)
-    for mask, met in zip(BIN_MASKS[:2], mets):
-        before = jnp.where((here % 2 == 0) & ((here ^ mask) + 2 == here), met[count:], before)
-    col = jnp.concatenate([col[:edge] + before, col[edge:]], axis=0).astype(BF16)
-    share = jnp.concatenate([share[:pairs], weight, col], axis=0)
-    share, pred_other = lax.optimization_barrier((share, pred_other))
-    mine = across(jnp.broadcast_to(share[None], (chips, *share.shape)), "tile", groups)
     other = swapped(mine, "tile", 1)
     (predicted,) = call(
         join_kernel, (shape(slots, width, width, dtype=BF16),),

time: 86.9 us -> 88.5 us (1.018)
  blocking collectives: 23.4 us -> 50.3 us
  starting transfers between devices: 26.5 us -> 8.87 us
  waiting for transfers between devices: 9.35 us -> 5.92 us
  local copies, waits for them, and re-layouts: 4.51 us -> 1.59 us
    all_to_all x2 -> x4, blocking collectives: 23.4 us -> 50.3 us  [across(): lax.all_to_all(block, axis, 0, 0, axis_index_groups=groups, tiled=True)]
    ppermute x9 -> x5, starting transfers between devices: 19.4 us -> 7.58 us  [swapped(): lax.ppermute(block, axis, [(i, i ^ bits) for i in range(lax.axis_size(axi...]
    all_to_all x1 -> x0, starting transfers between devices: 5.76 us -> none  [across(): lax.all_to_all(block, axis, 0, 0, axis_index_groups=groups, tiled=True)]
    unnamed x26 -> x22, local copies, waits for them, and re-layouts: 3.73 us -> 0.74 us
    ppermute x1, waiting for transfers between devices: 5.62 us -> 3.17 us  [shifted(): return lax.ppermute(block, axis, route)]
    ppermute x9 -> x5, waiting for transfers between devices: 3.56 us -> 2.75 us  [swapped(): lax.ppermute(block, axis, [(i, i ^ bits) for i in range(lax.axis_size(axi...]
    pallas_call x5 -> x7, Pallas kernels: 21.6 us -> 21.3 us  [call(): pl.pallas_call(kernel, out_shape=outs, in_specs=[space] * len(args), out_...]
  transfers between devices with their start and end apart: 11 -> 6, of which waited for: 6 -> 3; matrix products, arithmetic and copies ran while one was open for 0% -> 1% of each run, Pallas kernels for 2% -> 4%
where the time goes in v6:
time: 88.5 us; the launch traced here: 88.8 us
  blocking collectives  50.3 us (57%)
  Pallas kernels  21.3 us (24%)
  starting transfers between devices  8.87 us (10%)
  waiting for transfers between devices  5.92 us (7%)
  local copies, waits for them, and re-layouts  1.59 us (2%)
    all_to_all x4, blocking collectives, across(): lax.all_to_all(block, axis, 0, 0, axis_index_groups=groups, tiled=True)  50.3 us
    pallas_call x7, Pallas kernels, call(): pl.pallas_call(kernel, out_shape=outs, in_specs=[space] * len(args), out_...  21.3 us
    ppermute x5, starting transfers between devices, swapped(): lax.ppermute(block, axis, [(i, i ^ bits) for i in range(lax.axis_size(axi...  7.58 us
    ppermute x1, waiting for transfers between devices, shifted(): return lax.ppermute(block, axis, route)  3.17 us
    ppermute x5, waiting for transfers between devices, swapped(): lax.ppermute(block, axis, [(i, i ^ bits) for i in range(lax.axis_size(axi...  2.75 us
  transfers between devices with their start and end apart: 6, of which 3 were waited for; matrix products, arithmetic and copies ran while one was open for 1% of the time, Pallas kernels for 4%

profile of v6, /device:TPU:1, one launch (start us, length us, event | category | flops | bytes accessed | tf_op | source)
XLA Modules:
  0.0 88.8 jit_solution(15554960127735112422)
XLA Ops:
  0.6 1.5 %collective-permute-start = (bf16[6,128,128]{2,1,0:T(8,128)(2,1)}, bf16[6,128,128]{2,1,0:T(8,128)(2,1)S(1)}, u32[]{:S(2)}, u32[]{:S(2)}) collective-permute-start(bf16[6,128,128]{2,1,0:T(8,128)(2,1)} %bitcast.18), channel_id=1, source_target_pairs={{0,1},{1,0},{2,3},{3,2},{4,5},{5,4},{6,7},{7,6},{8,9},{9,8},{10,11... | collective-permute-start | bytes 589832 | tf_op jit(solution)/shard_map/ppermute | solution.py:401
  2.1 0.8 dynamic-slice_bitcast_fusion
  3.0 0.0 copy-start.8
  3.0 1.3 %collective-permute-start.1 = (bf16[32,512]{1,0:T(8,128)(2,1)S(1)}, bf16[32,512]{1,0:T(8,128)(2,1)S(1)}, u32[]{:S(2)}, u32[]{:S(2)}) collective-permute-start(bf16[32,512]{1,0:T(8,128)(2,1)S(1)} %slice_bitcast_fusion), channel_id=1, source_target_pairs={{16,0},{32,16},{48,32},{64,48},{80,64},{96,80},{112,96},{17,1},{33... | collective-permute-start | bytes 98312 | tf_op jit(solution)/shard_map/ppermute | solution.py:397
  4.3 0.0 copy-done.8
  4.3 0.0 copy-start.4
  4.3 0.0 copy-start
  4.3 0.1 collective-permute-start.2
  4.4 2.7 %shard_map.152 = (f32[512,256]{1,0:T(8,128)}, f32[64,128]{1,0:T(8,128)}) custom-call(bf16[1024,512]{1,0:T(8,128)(2,1)} %emb_ref.1, bf16[512,128]{1,0:T(8,128)(2,1)} %left_w_ref.1, bf16[512,128]{1,0:T(8,128)(2,1)} %right_w_ref.3), custom_call_target="tpu_custom_call" | custom-call | tf_op jit(solution)/shard_map/pallas_call | solution.py:384
  7.2 3.2 %collective-permute-done.1.next_ref = bf16[32,512]{1,0:T(8,128)(2,1)S(1)} collective-permute-done((bf16[32,512]{1,0:T(8,128)(2,1)S(1)}, bf16[32,512]{1,0:T(8,128)(2,1)S(1)}, u32[]{:S(2)}, u32[]{:S(2)}) %collective-permute-start.1) | collective-permute-done | bytes 32800 | tf_op jit(solution)/shard_map/ppermute | solution.py:397
  10.3 0.0 collective-permute-done.target_other
  10.3 0.0 collective-permute-done.2.list_other
  10.4 0.4 shard_map.153
  10.7 0.0 copy-start.5
  10.8 0.0 copy-start.6
  10.8 10.6 %all_to_all.20.target_ref = bf16[8,112,128]{2,1,0:T(8,128)(2,1)S(1)} all-to-all(bf16[8,112,128]{2,1,0:T(8,128)(2,1)S(1)} %shard_map.153), channel_id=1, replica_groups={{0,2,4,6,8,10,12,14},{1,3,5,7,9,11,13,15},{16,18,20,22,24,26,28,30},{17..., dimensions={0} | all-to-all | bytes 458752 | tf_op jit(solution)/shard_map/all_to_all | solution.py:405
  21.4 0.6 copy-done.7
  22.1 15.6 %shard_map.154 = (bf16[8,144,128]{2,1,0:T(8,128)(2,1)S(1)}, bf16[8,144,128]{2,1,0:T(8,128)(2,1)S(1)}, bf16[8,96,128]{2,1,0:T(8,128)(2,1)S(1)}, f32[64,128]{1,0:T(8,128)S(1)}, bf16[32,128]{1,0:T(8,128)(2,1)S(1)}) custom-call(f32[512,256]{1,0:T(8,128)S(1)} %copy-done.3, f32[64,128]{1,0:T(8,128)S(1)} %copy-done.6, bf16[1024,512]{1,0:T(8,128)(2,1)S(1)} %copy-done, ...), custom_call_target="tpu_custom_call" | custom-call | tf_op jit(solution)/shard_map/pallas_call | solution.py:384
  37.7 2.4 %collective-permute-start.3 = (bf16[8,144,128]{2,1,0:T(8,128)(2,1)S(1)}, bf16[8,144,128]{2,1,0:T(8,128)(2,1)S(1)}, u32[]{:S(2)}, u32[]{:S(2)}) collective-permute-start(bf16[8,144,128]{2,1,0:T(8,128)(2,1)S(1)} %get-tuple-element.37), channel_id=1, source_target_pairs={{0,1},{1,0},{2,3},{3,2},{4,5},{5,4},{6,7},{7,6},{8,9},{9,8},{10,11... | collective-permute-start | bytes 884744 | tf_op jit(solution)/shard_map/ppermute | solution.py:401
  40.1 1.2 %collective-permute-done.3 = bf16[8,144,128]{2,1,0:T(8,128)(2,1)S(1)} collective-permute-done((bf16[8,144,128]{2,1,0:T(8,128)(2,1)S(1)}, bf16[8,144,128]{2,1,0:T(8,128)(2,1)S(1)}, u32[]{:S(2)}, u32[]{:S(2)}) %collective-permute-start.3) | collective-permute-done | bytes 294944 | tf_op jit(solution)/shard_map/ppermute | solution.py:401
  41.3 0.1 add_convert_fusion
  41.4 11.6 %all_to_all.21.sum_ref = bf16[8,240,128]{2,1,0:T(8,128)(2,1)S(1)} all-to-all(bf16[8,240,128]{2,1,0:T(8,128)(2,1)S(1)} %pad_maximum_fusion), channel_id=1, replica_groups={{0,2,4,6,8,10,12,14},{1,3,5,7,9,11,13,15},{16,18,20,22,24,26,28,30},{17..., dimensions={0} | all-to-all | bytes 983040 | tf_op jit(solution)/shard_map/all_to_all | solution.py:405
  53.0 0.1 shard_map.155
  53.1 18.5 %all_to_all.22.met_ref = bf16[8,112,128]{2,1,0:T(8,128)(2,1)S(1)} all-to-all(bf16[8,112,128]{2,1,0:T(8,128)(2,1)S(1)} %get-tuple-element.41), channel_id=1, replica_groups=mesh['bin'=8,'tile'=16] {'bin'}, dimensions={0} | all-to-all | bytes 458752 | tf_op jit(solution)/shard_map/all_to_all | solution.py:405
  71.7 9.5 %all_to_all.23.mine_ref = bf16[8,208,128]{2,1,0:T(8,128)(2,1)S(1)} all-to-all(bf16[8,208,128]{2,1,0:T(8,128)(2,1)S(1)} %shard_map.156), channel_id=1, replica_groups={{0,2,4,6,8,10,12,14},{1,3,5,7,9,11,13,15},{16,18,20,22,24,26,28,30},{17..., dimensions={0} | all-to-all | bytes 851968 | tf_op jit(solution)/shard_map/all_to_all | solution.py:405
  81.2 3.6 %collective-permute-start.5 = (bf16[8,208,128]{2,1,0:T(8,128)(2,1)S(1)}, bf16[8,208,128]{2,1,0:T(8,128)(2,1)S(1)}, u32[]{:S(2)}, u32[]{:S(2)}) collective-permute-start(bf16[8,208,128]{2,1,0:T(8,128)(2,1)S(1)} %all_to_all.23.mine_ref), channel_id=1, source_target_pairs={{0,1},{1,0},{2,3},{3,2},{4,5},{5,4},{6,7},{7,6},{8,9},{9,8},{10,11... | collective-permute-start | bytes 1277960 | tf_op jit(solution)/shard_map/ppermute | solution.py:401
  84.8 0.0 collective-permute-start.4
  84.8 1.5 %collective-permute-done.4.other_ref = bf16[8,48,128]{2,1,0:T(8,128)(2,1)S(1)} collective-permute-done((bf16[8,48,128]{2,1,0:T(8,128)(2,1)S(1)}, bf16[8,48,128]{2,1,0:T(8,128)(2,1)S(1)}, u32[]{:S(2)}, u32[]{:S(2)}) %collective-permute-start.4) | collective-permute-done | bytes 98336 | tf_op jit(solution)/shard_map/ppermute | solution.py:401
  86.4 0.8 shard_map.157
  87.2 0.0 collective-permute-done.5.other_ref
  87.2 0.1 copy-done.2
  87.3 1.6 %shard_map.158 = (bf16[1024,512]{1,0:T(8,128)(2,1)}, f32[512,128]{1,0:T(8,128)}, f32[512,128]{1,0:T(8,128)}, f32[5,128]{1,0:T(8,128)}, f32[128,128]{1,0:T(8,128)}, /*index=5*/f32[1,128]{1,0:T(1,128)}, f32[1,128]{1,0:T(1,128)}) custom-call(bf16[8,208,128]{2,1,0:T(8,128)(2,1)S(1)} %all_to_all.23.mine_ref, ...), custom_call_target="tpu_custom_call" | custom-call | tf_op jit(solution)/shard_map/pallas_call | solution.py:384
  (17 shorter events, 0.1 us)
Async XLA Ops:
  0.6 9.7 %collective-permute-start = (bf16[6,128,128]{2,1,0:T(8,128)(2,1)}, bf16[6,128,128]{2,1,0:T(8,128)(2,1)S(1)}, u32[]{:S(2)}, u32[]{:S(2)}) collective-permute-start(bf16[6,128,128]{2,1,0:T(8,128)(2,1)} %bitcast.18), channel_id=1, source_target_pairs={{0,1},{1,0},{2,3},{3,2},{4,5},{5,4},{6,7},{7,6},{8,9},{9,8},{10,11... | collective-permute-start | bytes 589832 | tf_op jit(solution)/shard_map/ppermute | solution.py:401
  3.0 1.3 %copy-start.8 = (s32[1,1,6,3]{2,1,3,0:T(1,128)S(1)}, s32[1,1,6,3]{2,1,3,0:T(1,128)}, u32[]{:S(2)}) copy-start(s32[1,1,6,3]{2,1,3,0:T(1,128)} %param.16) | copy-start | bytes 220
  3.0 7.3 %collective-permute-start.1 = (bf16[32,512]{1,0:T(8,128)(2,1)S(1)}, bf16[32,512]{1,0:T(8,128)(2,1)S(1)}, u32[]{:S(2)}, u32[]{:S(2)}) collective-permute-start(bf16[32,512]{1,0:T(8,128)(2,1)S(1)} %slice_bitcast_fusion), channel_id=1, source_target_pairs={{16,0},{32,16},{48,32},{64,48},{80,64},{96,80},{112,96},{17,1},{33... | collective-permute-start | bytes 98312 | tf_op jit(solution)/shard_map/ppermute | solution.py:397
  4.3 6.0 %copy-start.4 = (bf16[1,1,6,128,128]{4,3,2,1,0:T(8,128)(2,1)S(1)}, bf16[1,1,6,128,128]{4,3,2,1,0:T(8,128)(2,1)}, u32[]{:S(2)}) copy-start(bf16[1,1,6,128,128]{4,3,2,1,0:T(8,128)(2,1)} %param.17) | copy-start | bytes 589828
  4.3 17.1 %copy-start = (bf16[1024,512]{1,0:T(8,128)(2,1)S(1)}, bf16[1024,512]{1,0:T(8,128)(2,1)}, u32[]{:S(2)}) copy-start(bf16[1024,512]{1,0:T(8,128)(2,1)} %emb_ref.1) | copy-start | bytes 3145732
  4.3 6.0 %collective-permute-start.2 = (s32[3,1,6]{2,1,0:T(1,128)S(1)}, s32[3,1,6]{2,1,0:T(1,128)S(1)}, u32[]{:S(2)}, u32[]{:S(2)}) collective-permute-start(s32[3,1,6]{2,1,0:T(1,128)S(1)} %bitcast.20), channel_id=1, source_target_pairs={{0,1},{1,0},{2,3},{3,2},{4,5},{5,4},{6,7},{7,6},{8,9},{9,8},{10,11... | collective-permute-start | bytes 224 | tf_op jit(solution)/shard_map/ppermute | solution.py:401
  10.3 11.1 %copy-start.3 = (f32[512,256]{1,0:T(8,128)S(1)}, f32[512,256]{1,0:T(8,128)}, u32[]{:S(2)}) copy-start(f32[512,256]{1,0:T(8,128)} %get-tuple-element.32.left_ref) | copy-start | bytes 1572868
  10.7 10.7 %copy-start.1 = (bf16[512,128]{1,0:T(8,128)(2,1)S(1)}, bf16[512,128]{1,0:T(8,128)(2,1)}, u32[]{:S(2)}) copy-start(bf16[512,128]{1,0:T(8,128)(2,1)} %right_w_ref.3) | copy-start | bytes 393220
  10.7 10.7 %copy-start.5 = (bf16[128,128]{1,0:T(8,128)(2,1)S(1)}, bf16[128,128]{1,0:T(8,128)(2,1)}, u32[]{:S(2)}) copy-start(bf16[128,128]{1,0:T(8,128)(2,1)} %w_ref.1) | copy-start | bytes 98308
  10.8 10.7 %copy-start.6 = (f32[64,128]{1,0:T(8,128)S(1)}, f32[64,128]{1,0:T(8,128)}, u32[]{:S(2)}) copy-start(f32[64,128]{1,0:T(8,128)} %get-tuple-element.33.right_ref) | copy-start | bytes 98308
  21.4 0.7 copy-start.7
  21.4 0.7 copy-start.9
  21.4 0.7 copy-start.10
  37.7 3.6 %collective-permute-start.3 = (bf16[8,144,128]{2,1,0:T(8,128)(2,1)S(1)}, bf16[8,144,128]{2,1,0:T(8,128)(2,1)S(1)}, u32[]{:S(2)}, u32[]{:S(2)}) collective-permute-start(bf16[8,144,128]{2,1,0:T(8,128)(2,1)S(1)} %get-tuple-element.37), channel_id=1, source_target_pairs={{0,1},{1,0},{2,3},{3,2},{4,5},{5,4},{6,7},{7,6},{8,9},{9,8},{10,11... | collective-permute-start | bytes 884744 | tf_op jit(solution)/shard_map/ppermute | solution.py:401
  81.2 6.0 %collective-permute-start.5 = (bf16[8,208,128]{2,1,0:T(8,128)(2,1)S(1)}, bf16[8,208,128]{2,1,0:T(8,128)(2,1)S(1)}, u32[]{:S(2)}, u32[]{:S(2)}) collective-permute-start(bf16[8,208,128]{2,1,0:T(8,128)(2,1)S(1)} %all_to_all.23.mine_ref), channel_id=1, source_target_pairs={{0,1},{1,0},{2,3},{3,2},{4,5},{5,4},{6,7},{7,6},{8,9},{9,8},{10,11... | collective-permute-start | bytes 1277960 | tf_op jit(solution)/shard_map/ppermute | solution.py:401
  84.8 1.5 %collective-permute-start.4 = (bf16[8,48,128]{2,1,0:T(8,128)(2,1)S(1)}, bf16[8,48,128]{2,1,0:T(8,128)(2,1)S(1)}, u32[]{:S(2)}, u32[]{:S(2)}) collective-permute-start(bf16[8,48,128]{2,1,0:T(8,128)(2,1)S(1)} %get-tuple-element.45), channel_id=1, source_target_pairs={{0,1},{1,0},{2,3},{3,2},{4,5},{5,4},{6,7},{7,6},{8,9},{9,8},{10,11... | collective-permute-start | bytes 294920 | tf_op jit(solution)/shard_map/ppermute | solution.py:401
  86.4 0.9 %copy-start.2 = (bf16[512,128]{1,0:T(8,128)(2,1)S(1)}, bf16[512,128]{1,0:T(8,128)(2,1)}, u32[]{:S(2)}) copy-start(bf16[512,128]{1,0:T(8,128)(2,1)} %left_w_ref.1) | copy-start | bytes 393220

commit v7 on v6

--- a/solution.py
+++ b/solution.py
@@ -10,49 +10,10 @@
 BATCH = 2
 NEVER = -1e38
 VMEM = pl.BlockSpec(memory_space=pltpu.VMEM)
-HBM = pl.BlockSpec(memory_space=pl.ANY)
 
 
 def place():
     return lax.axis_index("tile")
-
-
-def project_kernel(
-    emb_hbm, left_hbm, right_hbm,
-    left_ref, right_ref,
-    emb_ref, left_w_ref, right_w_ref, full_ref, sems,
-):
-    copies = [
-        pltpu.make_async_copy(source, target, sems.at[k])
-        for k, (source, target) in enumerate(
-            ((left_hbm, left_w_ref), (right_hbm, right_w_ref), (emb_hbm, emb_ref))
-        )
-    ]
-    for copy in copies:
-        copy.start()
-    for copy in copies:
-        copy.wait()
-    tile = place()
-    width = left_w_ref.shape[1]
-    half = width // 2
-    blocks = emb_ref.shape[0] // width
-    step = right_ref.shape[0] // blocks
-    weights = jnp.concatenate([left_w_ref[...], right_w_ref[...]], axis=1)
-    for block in range(0, blocks, 2):
-        both = jnp.dot(
-            emb_ref[block * width : (block + 2) * width, :],
-            weights,
-            preferred_element_type=F32,
-        ).astype(BF16).astype(F32)
-        for k in range(2):
-            left = both[k * width : (k + 1) * width, :width]
-            at = (block + k) * half
-            left_ref[at : at + half, :width] = left[:half]
-            left_ref[at : at + half, width:] = left[half:]
-        full_ref[block * width : (block + 2) * width, :] = both[:, width:]
-    for block in range(blocks):
-        at = pl.multiple_of(block * width + tile * step, step)
-        right_ref[block * step : (block + 1) * step, :] = full_ref[pl.ds(at, step), :]
 
 
 def split_kernel(
@@ -102,20 +63,20 @@
 
 
 def pair_kernel(
-    left_ref, right_ref, emb_ref, cols_ref, next_ref, right_w_ref, bias_ref, target_ref,
-    w_ref, b_ref, out_ref,
+    emb_ref, cols_ref, next_ref, left_w_ref, right_w_ref, const_ref, target_ref, w_ref,
     keep_ref, send_ref, pred_ref, col_ref, edge_ref,
-    table, lists, list_sem, list_all, right_all, target_all, pred_all, row_all, col_all,
-    outer_all, bias_all, w_two, out_two, back_two, b_two, first_0, first_1, slope_0, slope_1,
+    table, lists, list_sem, list_all, left_ref, full_ref, right_all, target_all, pred_all, row_all, col_all,
+    outer_all, bias_all, w_two, out_two, back_two, b_two, scale_two, first_0, first_1, slope_0, slope_1,
 ):
+    tile = place()
     width = w_ref.shape[0]
     pairs = width // 2
-    blocks = left_ref.shape[0] // pairs
+    blocks = emb_ref.shape[0] // width
     chips = target_ref.shape[0]
     shares = 2 * chips
     step = width // shares
     slots = target_ref.shape[1] // (2 * step) - 1
-    core = place() & 1
+    core = tile & 1
     groups = target_all.shape[0] - 1
     spread_bits = (width // step).bit_length() - 1
 
@@ -129,17 +90,37 @@
     copy.start()
 
     w = w_ref[...].astype(F32)
-    w_out = out_ref[...]
+    w_out = const_ref[6:7, :]
+    b_pair = const_ref[5:6, :]
     back = (w * w_out).T.astype(BF16)
     spread = jnp.broadcast_to(w_out * (1.0 / width), (width, width)).T.astype(BF16)
     for ref, block in ((w_two, w_ref[...]), (out_two, spread), (back_two, back)):
         ref[...] = jnp.zeros_like(ref)
         ref[:width, :width] = block
         ref[width:, width:] = block
-    b_two[:, :width] = b_ref[...]
-    b_two[:, width:] = b_ref[...]
-    own = right_ref.shape[0]
-    right_all[:own, :] = right_ref[...]
+    w_low = (w_out * (1.0 / width)).astype(BF16).astype(F32)
+    scale = jnp.where(w_low == 0.0, 1.0, w_out * (1.0 / width) / jnp.where(w_low == 0.0, 1.0, w_low))
+    scale_two[:, :width] = scale
+    scale_two[:, width:] = scale
+    b_two[:, :width] = b_pair
+    b_two[:, width:] = b_pair
+    weights = jnp.concatenate([left_w_ref[...], right_w_ref[...]], axis=1)
+    for block in range(0, blocks, 2):
+        both = jnp.dot(
+            emb_ref[block * width : (block + 2) * width, :],
+            weights,
+            preferred_element_type=F32,
+        ).astype(BF16).astype(F32)
+        for k in range(2):
+            left = both[k * width : (k + 1) * width, :width]
+            at = (block + k) * pairs
+            left_ref[at : at + pairs, :width] = left[:pairs]
+            left_ref[at : at + pairs, width:] = left[pairs:]
+        full_ref[block * width : (block + 2) * width, :] = both[:, width:]
+    own = blocks * step
+    for block in range(blocks):
+        at = pl.multiple_of(block * width + tile * step, step)
+        right_all[block * step : (block + 1) * step, :] = full_ref[pl.ds(at, step), :]
     right_next = jnp.dot(next_ref[...], right_w_ref[...], preferred_element_type=F32)
     right_all[own:, :] = right_next.astype(BF16).astype(F32)
     rows = [target_ref[chip, : 2 * slots * step, :].astype(F32) for chip in range(chips)]
@@ -178,7 +159,7 @@
             shifts.append((slot >> spread_bits, shift))
             at = pl.multiple_of(block * pairs, pairs)
             col_at = pl.multiple_of((block + offset) * step, step)
-            right = right_all[pl.ds(col_at, step), :] + bias_ref[pl.ds(offset, 1), :]
+            right = right_all[pl.ds(col_at, step), :] + const_ref[pl.ds(offset, 1), :]
             right = jnp.concatenate([right, right], axis=1)
             left = left_ref[pl.ds(at, pairs), :]
             pre += [left + right[j : j + 1, :] for j in range(step)]
@@ -194,7 +175,7 @@
         first_ref[...] = first
         act = jnp.dot(first, w_two[...], preferred_element_type=F32)
         act = act + jnp.concatenate(floors, axis=0)
-        second = jnp.maximum(act, 0.0).astype(BF16)
+        second = (jnp.maximum(act, 0.0) * scale_two[...]).astype(BF16)
         contact = jnp.dot(second, out_two[...], preferred_element_type=F32)
         slope = (contact - jnp.concatenate(wanted, axis=0)).astype(BF16)
         slope_ref[...] = jnp.where(second > 0, slope, jnp.zeros_like(slope))
@@ -251,7 +232,7 @@
     sum_d = outer_all[2 * width : 2 * width + 1, :width] + outer_all[2 * width : 2 * width + 1, width:]
     bias = bias_all[...]
     line = lax.broadcasted_iota(jnp.int32, bias.shape, 0)
-    sum_out = jnp.sum(w * outer, axis=0, keepdims=True) + b_ref[...] * sum_d
+    sum_out = jnp.sum(w * outer, axis=0, keepdims=True) + b_pair * sum_d
     vectors = jnp.where(line == 5, sum_d * w_out, bias)
     vectors = jnp.where(line == 6, sum_out, vectors)
     outer = outer * w_out
@@ -380,21 +361,15 @@
     return jax.ShapeDtypeStruct(dims, dtype)
 
 
-def call(kernel, outs, scratch, *args, space=VMEM, limit=32):
+def call(kernel, outs, scratch, *args):
     return pl.pallas_call(
         kernel,
         out_shape=outs,
-        in_specs=[space] * len(args),
+        in_specs=[VMEM] * len(args),
         out_specs=(VMEM,) * len(outs),
         scratch_shapes=scratch,
-        compiler_params=pltpu.CompilerParams(vmem_limit_bytes=limit * 1024 * 1024),
+        compiler_params=pltpu.CompilerParams(vmem_limit_bytes=32 * 1024 * 1024),
     )(*args)
-
-
-def shifted(block, axis, distance):
-    devices = range(lax.axis_size(axis))
-    route = [(i - distance, i) for i in devices if i - distance in devices]
-    return lax.ppermute(block, axis, route)
 
 
 def swapped(block, axis, bits):
@@ -423,22 +398,13 @@
     emb_cols = lax.dynamic_slice_in_dim(
         embeddings.reshape(blocks, shares, step, features), tile, 1, 1
     ).reshape(part, features)
-    emb_next = shifted(emb_cols[:edge], "bin", -1)
     target_other = swapped(target, "tile", 1)
     lists_other = swapped(lists, "tile", 1)
-    left, right = call(
-        project_kernel,
-        (shape(rows // 2, 2 * width), shape(part, width)),
-        [
-            pltpu.VMEM((rows, features), BF16),
-            pltpu.VMEM((features, width), BF16),
-            pltpu.VMEM((features, width), BF16),
-            pltpu.VMEM((rows, width), F32),
-            pltpu.SemaphoreType.DMA((3,)),
-        ],
-        embeddings, w_left, w_right, space=HBM, limit=56,
-    )
-    target_other, emb_next, left = lax.optimization_barrier((target_other, emb_next, left))
+    bins = lax.axis_size("bin")
+    emb_next = lax.ppermute(emb_cols[:edge], "bin", [(k + 1, k) for k in range(bins - 1)])
+    consts = jnp.concatenate(
+        [pair_bias, b_pair[None], w_out[None], jnp.zeros((1, width), F32)], axis=0
+    )
     (target_send,) = call(
         split_kernel,
         (shape(chips, 2 * (slots + 1) * step, width, dtype=BF16),),
@@ -465,6 +431,8 @@
             pltpu.SMEM((3, shares, width), jnp.int32),
             pltpu.SemaphoreType.DMA,
             pltpu.VMEM((3, shares, width), jnp.int32),
+            pltpu.VMEM((rows // 2, 2 * width), F32),
+            pltpu.VMEM((rows, width), F32),
             pltpu.VMEM((part + edge, width), F32),
             pltpu.VMEM(grouped, F32),
             pltpu.VMEM(grouped, F32),
@@ -476,17 +444,16 @@
             pltpu.VMEM((2 * width, 2 * width), BF16),
             pltpu.VMEM((2 * width, 2 * width), BF16),
             pltpu.VMEM((1, 2 * width), F32),
+            pltpu.VMEM((1, 2 * width), F32),
             pltpu.VMEM(chunk, BF16),
             pltpu.VMEM(chunk, BF16),
             pltpu.VMEM(chunk, BF16),
             pltpu.VMEM(chunk, BF16),
         ],
-        left, right, embeddings, emb_cols, emb_next, w_right, pair_bias,
-        target_all, w_pair, b_pair[None], w_out[None],
+        embeddings, emb_cols, emb_next, w_left, w_right, consts, target_all, w_pair,
     )
     sums = (sums.astype(F32) + swapped(sums_send, "tile", 1).astype(F32)).astype(BF16)
     sums = across(jnp.concatenate([sums, pred], axis=1), "tile", groups)
-    bins = lax.axis_size("bin")
     row, weight, pred_mine, pred_send = call(
         share_kernel,
         (

time: 88.5 us -> 86.5 us (0.977)
  blocking collectives: 50.3 us -> 36.2 us
  starting transfers between devices: 8.87 us -> 14.5 us
  waiting for transfers between devices: 5.92 us -> 8.08 us
  Pallas kernels: 21.3 us -> 23.4 us
  local copies, waits for them, and re-layouts: 1.59 us -> 3.2 us
    all_to_all x4 -> x3, blocking collectives: 50.3 us -> 36.2 us  [across(): lax.all_to_all(block, axis, 0, 0, axis_index_groups=groups, tiled=True)]
    all_to_all x0 -> x1, starting transfers between devices: none -> 5.77 us  [across(): lax.all_to_all(block, axis, 0, 0, axis_index_groups=groups, tiled=True)]
    all_to_all x0 -> x1, waiting for transfers between devices: none -> 5.33 us  [across(): lax.all_to_all(block, axis, 0, 0, axis_index_groups=groups, tiled=True)]
    ppermute x1, waiting for transfers between devices: 3.17 us -> 0.01 us  [per_device(): lax.ppermute(emb_cols[:edge], 'bin', [(k + 1, k) for k in range(bins - 1)])]
    unnamed x22 -> x19, local copies, waits for them, and re-layouts: 0.74 us -> 3.13 us
    pallas_call x7 -> x6, Pallas kernels: 21.3 us -> 23.4 us  [call(): pl.pallas_call(kernel, out_shape=outs, in_specs=[VMEM] * len(args), out_s...]
  transfers between devices with their start and end apart: 6 -> 7, of which waited for: 3 -> 3; matrix products, arithmetic and copies ran while one was open for 1% -> 1% of each run, Pallas kernels for 4% -> 2%
where the time goes in v7:
time: 86.5 us; the launch traced here: 86.3 us
  blocking collectives  36.2 us (42%)
  Pallas kernels  23.4 us (27%)
  starting transfers between devices  14.5 us (17%)
  waiting for transfers between devices  8.08 us (9%)
  local copies, waits for them, and re-layouts  3.2 us (4%)
    all_to_all x3, blocking collectives, across(): lax.all_to_all(block, axis, 0, 0, axis_index_groups=groups, tiled=True)  36.2 us
    pallas_call x6, Pallas kernels, call(): pl.pallas_call(kernel, out_shape=outs, in_specs=[VMEM] * len(args), out_s...  23.4 us
    ppermute x5, starting transfers between devices, swapped(): lax.ppermute(block, axis, [(i, i ^ bits) for i in range(lax.axis_size(axi...  7.41 us
    all_to_all x1, starting transfers between devices, across(): lax.all_to_all(block, axis, 0, 0, axis_index_groups=groups, tiled=True)  5.77 us
    all_to_all x1, waiting for transfers between devices, across(): lax.all_to_all(block, axis, 0, 0, axis_index_groups=groups, tiled=True)  5.33 us
    unnamed x19, local copies, waits for them, and re-layouts  3.13 us
    ppermute x5, waiting for transfers between devices, swapped(): lax.ppermute(block, axis, [(i, i ^ bits) for i in range(lax.axis_size(axi...  2.75 us
  transfers between devices with their start and end apart: 7, of which 3 were waited for; matrix products, arithmetic and copies ran while one was open for 1% of the time, Pallas kernels for 2%

profile of v7, /device:TPU:1, one launch (start us, length us, event | category | flops | bytes accessed | tf_op | source)
XLA Modules:
  0.0 86.3 jit_solution(2438413821579821670)
XLA Ops:
  0.6 1.5 %collective-permute-start.1 = (s32[3,1,6]{2,1,0:T(1,128)}, s32[3,1,6]{2,1,0:T(1,128)S(1)}, u32[]{:S(2)}, u32[]{:S(2)}) collective-permute-start(s32[3,1,6]{2,1,0:T(1,128)} %bitcast.21), channel_id=1, source_target_pairs={{0,1},{1,0},{2,3},{3,2},{4,5},{5,4},{6,7},{7,6},{8,9},{9,8},{10,11... | collective-permute-start | bytes 224 | tf_op jit(solution)/shard_map/ppermute | solution.py:376
  2.1 0.1 collective-permute-start.2
  2.2 0.8 dynamic-slice_bitcast_fusion.1
  3.1 1.3 %collective-permute-start = (bf16[32,512]{1,0:T(8,128)(2,1)S(1)}, bf16[32,512]{1,0:T(8,128)(2,1)S(1)}, u32[]{:S(2)}, u32[]{:S(2)}) collective-permute-start(bf16[32,512]{1,0:T(8,128)(2,1)S(1)} %slice_bitcast_fusion), channel_id=1, source_target_pairs={{16,0},{32,16},{48,32},{64,48},{80,64},{96,80},{112,96},{17,1},{33... | collective-permute-start | bytes 98312 | tf_op jit(solution)/shard_map/ppermute | solution.py:404
  4.4 0.1 pad.5.clone
  4.5 0.0 collective-permute-done.1.list_other
  4.5 0.0 collective-permute-done.2.target_other
  4.5 0.9 %copy-done.3 = bf16[1,1,6,128,128]{4,3,2,1,0:T(8,128)(2,1)S(1)} copy-done((bf16[1,1,6,128,128]{4,3,2,1,0:T(8,128)(2,1)S(1)}, bf16[1,1,6,128,128]{4,3,2,1,0:T(8,128)(2,1)}, u32[]{:S(2)}) %copy-start.3) | copy-done | bytes 196632
  5.4 0.7 copy-done.5
  6.1 1.1 %shard_map.152 = bf16[8,112,128]{2,1,0:T(8,128)(2,1)} custom-call(s32[3,1,6]{2,1,0:T(1,128)S(1)} %bitcast.22, s32[3,1,6]{2,1,0:T(1,128)S(1)} %collective-permute-done.1.list_other, bf16[6,128,128]{2,1,0:T(8,128)(2,1)S(1)} %bitcast.20, bf16[6,128,128]{2,1,0:T(8,128)(2,1)S(1)} %collective-permute-done.2.target_other), custom_call_target="tpu_custom_call" | custom-call | tf_op jit(solution)/shard_map/pallas_call | solution.py:365
  7.2 5.8 %all-to-all-start = ((bf16[8,112,128]{2,1,0:T(8,128)(2,1)}), bf16[8,112,128]{2,1,0:T(8,128)(2,1)S(1)}, u32[]{:S(2)}, u32[]{:S(2)}) async-start(bf16[8,112,128]{2,1,0:T(8,128)(2,1)} %shard_map.152), calls=%async_computation | async-start | bytes 458752 | tf_op jit(solution)/shard_map/all_to_all | solution.py:380
  13.0 0.0 copy-start.8
  13.0 0.0 copy-done.6
  13.0 0.6 copy-done.7
  13.6 0.0 copy-done.8
  13.6 0.1 maximum_maximum_fusion.const_ref
  13.7 0.0 collective-permute-done.next_ref
  13.7 5.3 %all-to-all-done.target_ref = bf16[8,112,128]{2,1,0:T(8,128)(2,1)S(1)} async-done(((bf16[8,112,128]{2,1,0:T(8,128)(2,1)}), bf16[8,112,128]{2,1,0:T(8,128)(2,1)S(1)}, u32[]{:S(2)}, u32[]{:S(2)}) %all-to-all-start) | async-done | bytes 229408 | tf_op jit(solution)/shard_map/all_to_all | solution.py:380
  19.0 19.8 %shard_map.153 = (bf16[8,144,128]{2,1,0:T(8,128)(2,1)S(1)}, bf16[8,144,128]{2,1,0:T(8,128)(2,1)S(1)}, bf16[8,96,128]{2,1,0:T(8,128)(2,1)S(1)}, f32[64,128]{1,0:T(8,128)S(1)}, bf16[32,128]{1,0:T(8,128)(2,1)S(1)}) custom-call(bf16[1024,512]{1,0:T(8,128)(2,1)S(1)} %copy-done, bf16[64,512]{1,0:T(8,128)(2,1)S(1)} %get-tuple-element.45.cols_ref, ...), custom_call_target="tpu_custom_call" | custom-call | tf_op jit(solution)/shard_map/pallas_call | solution.py:365
  38.9 1.9 %collective-permute-start.3 = (bf16[8,144,128]{2,1,0:T(8,128)(2,1)S(1)}, bf16[8,144,128]{2,1,0:T(8,128)(2,1)S(1)}, u32[]{:S(2)}, u32[]{:S(2)}) collective-permute-start(bf16[8,144,128]{2,1,0:T(8,128)(2,1)S(1)} %get-tuple-element.27), channel_id=1, source_target_pairs={{0,1},{1,0},{2,3},{3,2},{4,5},{5,4},{6,7},{7,6},{8,9},{9,8},{10,11... | collective-permute-start | bytes 884744 | tf_op jit(solution)/shard_map/ppermute | solution.py:376
  40.8 1.2 %collective-permute-done.3 = bf16[8,144,128]{2,1,0:T(8,128)(2,1)S(1)} collective-permute-done((bf16[8,144,128]{2,1,0:T(8,128)(2,1)S(1)}, bf16[8,144,128]{2,1,0:T(8,128)(2,1)S(1)}, u32[]{:S(2)}, u32[]{:S(2)}) %collective-permute-start.3) | collective-permute-done | bytes 294944 | tf_op jit(solution)/shard_map/ppermute | solution.py:376
  42.0 0.1 add_convert_fusion
  42.1 11.9 %all_to_all.20.sum_ref = bf16[8,240,128]{2,1,0:T(8,128)(2,1)S(1)} all-to-all(bf16[8,240,128]{2,1,0:T(8,128)(2,1)S(1)} %pad_maximum_fusion), channel_id=1, replica_groups={{0,2,4,6,8,10,12,14},{1,3,5,7,9,11,13,15},{16,18,20,22,24,26,28,30},{17..., dimensions={0} | all-to-all | bytes 983040 | tf_op jit(solution)/shard_map/all_to_all | solution.py:380
  54.0 0.1 shard_map.154
  54.1 14.8 %all_to_all.21.met_ref = bf16[8,112,128]{2,1,0:T(8,128)(2,1)S(1)} all-to-all(bf16[8,112,128]{2,1,0:T(8,128)(2,1)S(1)} %get-tuple-element.31), channel_id=1, replica_groups=mesh['bin'=8,'tile'=16] {'bin'}, dimensions={0} | all-to-all | bytes 458752 | tf_op jit(solution)/shard_map/all_to_all | solution.py:380
  69.0 9.5 %all_to_all.22.mine_ref = bf16[8,208,128]{2,1,0:T(8,128)(2,1)S(1)} all-to-all(bf16[8,208,128]{2,1,0:T(8,128)(2,1)S(1)} %shard_map.155), channel_id=1, replica_groups={{0,2,4,6,8,10,12,14},{1,3,5,7,9,11,13,15},{16,18,20,22,24,26,28,30},{17..., dimensions={0} | all-to-all | bytes 851968 | tf_op jit(solution)/shard_map/all_to_all | solution.py:380
  78.4 3.9 %collective-permute-start.5 = (bf16[8,208,128]{2,1,0:T(8,128)(2,1)S(1)}, bf16[8,208,128]{2,1,0:T(8,128)(2,1)S(1)}, u32[]{:S(2)}, u32[]{:S(2)}) collective-permute-start(bf16[8,208,128]{2,1,0:T(8,128)(2,1)S(1)} %all_to_all.22.mine_ref), channel_id=1, source_target_pairs={{0,1},{1,0},{2,3},{3,2},{4,5},{5,4},{6,7},{7,6},{8,9},{9,8},{10,11... | collective-permute-start | bytes 1277960 | tf_op jit(solution)/shard_map/ppermute | solution.py:376
  82.3 0.0 collective-permute-start.4
  82.4 1.5 %collective-permute-done.4.other_ref = bf16[8,48,128]{2,1,0:T(8,128)(2,1)S(1)} collective-permute-done((bf16[8,48,128]{2,1,0:T(8,128)(2,1)S(1)}, bf16[8,48,128]{2,1,0:T(8,128)(2,1)S(1)}, u32[]{:S(2)}, u32[]{:S(2)}) %collective-permute-start.4) | collective-permute-done | bytes 98336 | tf_op jit(solution)/shard_map/ppermute | solution.py:376
  83.9 0.8 shard_map.156
  84.7 0.0 collective-permute-done.5.other_ref
  84.7 1.6 %shard_map.157 = (bf16[1024,512]{1,0:T(8,128)(2,1)}, f32[512,128]{1,0:T(8,128)}, f32[512,128]{1,0:T(8,128)}, f32[5,128]{1,0:T(8,128)}, f32[128,128]{1,0:T(8,128)}, /*index=5*/f32[1,128]{1,0:T(1,128)}, f32[1,128]{1,0:T(1,128)}) custom-call(bf16[8,208,128]{2,1,0:T(8,128)(2,1)S(1)} %all_to_all.22.mine_ref, ...), custom_call_target="tpu_custom_call" | custom-call | tf_op jit(solution)/shard_map/pallas_call | solution.py:365
  (15 shorter events, 0.1 us)
Async XLA Ops:
  0.6 18.4 %copy-start = (bf16[1024,512]{1,0:T(8,128)(2,1)S(1)}, bf16[1024,512]{1,0:T(8,128)(2,1)}, u32[]{:S(2)}) copy-start(bf16[1024,512]{1,0:T(8,128)(2,1)} %emb_ref.1) | copy-start | bytes 3145732
  0.6 3.8 %collective-permute-start.1 = (s32[3,1,6]{2,1,0:T(1,128)}, s32[3,1,6]{2,1,0:T(1,128)S(1)}, u32[]{:S(2)}, u32[]{:S(2)}) collective-permute-start(s32[3,1,6]{2,1,0:T(1,128)} %bitcast.21), channel_id=1, source_target_pairs={{0,1},{1,0},{2,3},{3,2},{4,5},{5,4},{6,7},{7,6},{8,9},{9,8},{10,11... | collective-permute-start | bytes 224 | tf_op jit(solution)/shard_map/ppermute | solution.py:376
  2.1 2.3 %collective-permute-start.2 = (bf16[6,128,128]{2,1,0:T(8,128)(2,1)}, bf16[6,128,128]{2,1,0:T(8,128)(2,1)S(1)}, u32[]{:S(2)}, u32[]{:S(2)}) collective-permute-start(bf16[6,128,128]{2,1,0:T(8,128)(2,1)} %bitcast.19), channel_id=1, source_target_pairs={{0,1},{1,0},{2,3},{3,2},{4,5},{5,4},{6,7},{7,6},{8,9},{9,8},{10,11... | collective-permute-start | bytes 589832 | tf_op jit(solution)/shard_map/ppermute | solution.py:376
  3.1 10.6 %collective-permute-start = (bf16[32,512]{1,0:T(8,128)(2,1)S(1)}, bf16[32,512]{1,0:T(8,128)(2,1)S(1)}, u32[]{:S(2)}, u32[]{:S(2)}) collective-permute-start(bf16[32,512]{1,0:T(8,128)(2,1)S(1)} %slice_bitcast_fusion), channel_id=1, source_target_pairs={{16,0},{32,16},{48,32},{64,48},{80,64},{96,80},{112,96},{17,1},{33... | collective-permute-start | bytes 98312 | tf_op jit(solution)/shard_map/ppermute | solution.py:404
  4.5 0.9 %copy-start.3 = (bf16[1,1,6,128,128]{4,3,2,1,0:T(8,128)(2,1)S(1)}, bf16[1,1,6,128,128]{4,3,2,1,0:T(8,128)(2,1)}, u32[]{:S(2)}) copy-start(bf16[1,1,6,128,128]{4,3,2,1,0:T(8,128)(2,1)} %param.17) | copy-start | bytes 589828
  5.4 0.7 copy-start.5
  7.2 5.8 %copy-start.6 = (f32[5,128]{1,0:T(8,128)S(1)}, f32[5,128]{1,0:T(8,128)}, u32[]{:S(2)}) copy-start(f32[5,128]{1,0:T(8,128)} %param.12) | copy-start | bytes 7684
  7.2 11.9 %copy-start.1 = (bf16[512,128]{1,0:T(8,128)(2,1)S(1)}, bf16[512,128]{1,0:T(8,128)(2,1)}, u32[]{:S(2)}) copy-start(bf16[512,128]{1,0:T(8,128)(2,1)} %left_w_ref.3) | copy-start | bytes 393220
  7.2 11.9 %copy-start.2 = (bf16[512,128]{1,0:T(8,128)(2,1)S(1)}, bf16[512,128]{1,0:T(8,128)(2,1)}, u32[]{:S(2)}) copy-start(bf16[512,128]{1,0:T(8,128)(2,1)} %right_w_ref.3) | copy-start | bytes 393220
  7.2 11.9 %copy-start.4 = (bf16[128,128]{1,0:T(8,128)(2,1)S(1)}, bf16[128,128]{1,0:T(8,128)(2,1)}, u32[]{:S(2)}) copy-start(bf16[128,128]{1,0:T(8,128)(2,1)} %w_ref.1) | copy-start | bytes 98308
  7.2 11.8 %all-to-all-start = ((bf16[8,112,128]{2,1,0:T(8,128)(2,1)}), bf16[8,112,128]{2,1,0:T(8,128)(2,1)S(1)}, u32[]{:S(2)}, u32[]{:S(2)}) async-start(bf16[8,112,128]{2,1,0:T(8,128)(2,1)} %shard_map.152), calls=%async_computation | async-start | bytes 458752 | tf_op jit(solution)/shard_map/all_to_all | solution.py:380
  13.0 0.7 copy-start.7
  13.0 0.7 copy-start.8
  38.9 3.1 %collective-permute-start.3 = (bf16[8,144,128]{2,1,0:T(8,128)(2,1)S(1)}, bf16[8,144,128]{2,1,0:T(8,128)(2,1)S(1)}, u32[]{:S(2)}, u32[]{:S(2)}) collective-permute-start(bf16[8,144,128]{2,1,0:T(8,128)(2,1)S(1)} %get-tuple-element.27), channel_id=1, source_target_pairs={{0,1},{1,0},{2,3},{3,2},{4,5},{5,4},{6,7},{7,6},{8,9},{9,8},{10,11... | collective-permute-start | bytes 884744 | tf_op jit(solution)/shard_map/ppermute | solution.py:376
  78.4 6.3 %collective-permute-start.5 = (bf16[8,208,128]{2,1,0:T(8,128)(2,1)S(1)}, bf16[8,208,128]{2,1,0:T(8,128)(2,1)S(1)}, u32[]{:S(2)}, u32[]{:S(2)}) collective-permute-start(bf16[8,208,128]{2,1,0:T(8,128)(2,1)S(1)} %all_to_all.22.mine_ref), channel_id=1, source_target_pairs={{0,1},{1,0},{2,3},{3,2},{4,5},{5,4},{6,7},{7,6},{8,9},{9,8},{10,11... | collective-permute-start | bytes 1277960 | tf_op jit(solution)/shard_map/ppermute | solution.py:376
  82.3 1.5 %collective-permute-start.4 = (bf16[8,48,128]{2,1,0:T(8,128)(2,1)S(1)}, bf16[8,48,128]{2,1,0:T(8,128)(2,1)S(1)}, u32[]{:S(2)}, u32[]{:S(2)}) collective-permute-start(bf16[8,48,128]{2,1,0:T(8,128)(2,1)S(1)} %get-tuple-element.35), channel_id=1, source_target_pairs={{0,1},{1,0},{2,3},{3,2},{4,5},{5,4},{6,7},{7,6},{8,9},{9,8},{10,11... | collective-permute-start | bytes 294920 | tf_op jit(solution)/shard_map/ppermute | solution.py:376

commit v8 on v7

--- a/solution.py
+++ b/solution.py
@@ -9,7 +9,9 @@
 BF16 = jnp.bfloat16
 BATCH = 2
 NEVER = -1e38
+TINY = 1e-30
 VMEM = pl.BlockSpec(memory_space=pltpu.VMEM)
+HBM = pl.BlockSpec(memory_space=pl.ANY)
 
 
 def place():
@@ -47,21 +49,6 @@
         send_ref[chip, 2 * slots * step :, :] = listed
 
 
-def join_kernel(mine_ref, other_ref, pred_ref, flip_ref):
-    core = place() & 1
-    slots, width, _ = pred_ref.shape
-    chips = mine_ref.shape[0]
-    step = width // (2 * chips)
-    for chip in range(chips):
-        for ref, side in ((mine_ref, core), (other_ref, 1 - core)):
-            block = ref[chip].astype(F32)
-            to = pl.multiple_of((2 * chip + side) * step, step)
-            for slot in range(slots):
-                flip_ref[slot, pl.ds(to, step), :] = block[slot * step : (slot + 1) * step]
-    for slot in range(slots):
-        pred_ref[slot] = flip_ref[slot].T.astype(BF16)
-
-
 def pair_kernel(
     emb_ref, cols_ref, next_ref, left_w_ref, right_w_ref, const_ref, target_ref, w_ref,
     keep_ref, send_ref, pred_ref, col_ref, edge_ref,
@@ -92,16 +79,19 @@
     w = w_ref[...].astype(F32)
     w_out = const_ref[6:7, :]
     b_pair = const_ref[5:6, :]
-    back = (w * w_out).T.astype(BF16)
-    spread = jnp.broadcast_to(w_out * (1.0 / width), (width, width)).T.astype(BF16)
+    size = jnp.abs(w_out)
+    power = jnp.exp2(jnp.floor(jnp.log2(jnp.maximum(size, TINY))))
+    power = jnp.where(size < TINY, 0.0, power).astype(BF16).astype(F32)
+    power = jnp.where(w_out < 0.0, -power, power)
+    ratio = jnp.where(size < TINY, 1.0, w_out / jnp.where(size < TINY, 1.0, power))
+    back = (w * power).T.astype(BF16)
+    spread = jnp.broadcast_to(power * (1.0 / width), (width, width)).T.astype(BF16)
     for ref, block in ((w_two, w_ref[...]), (out_two, spread), (back_two, back)):
         ref[...] = jnp.zeros_like(ref)
         ref[:width, :width] = block
         ref[width:, width:] = block
-    w_low = (w_out * (1.0 / width)).astype(BF16).astype(F32)
-    scale = jnp.where(w_low == 0.0, 1.0, w_out * (1.0 / width) / jnp.where(w_low == 0.0, 1.0, w_low))
-    scale_two[:, :width] = scale
-    scale_two[:, width:] = scale
+    scale_two[:, :width] = ratio
+    scale_two[:, width:] = ratio
     b_two[:, :width] = b_pair
     b_two[:, width:] = b_pair
     weights = jnp.concatenate([left_w_ref[...], right_w_ref[...]], axis=1)
@@ -177,7 +167,8 @@
         act = act + jnp.concatenate(floors, axis=0)
         second = (jnp.maximum(act, 0.0) * scale_two[...]).astype(BF16)
         contact = jnp.dot(second, out_two[...], preferred_element_type=F32)
-        slope = (contact - jnp.concatenate(wanted, axis=0)).astype(BF16)
+        slope = (contact - jnp.concatenate(wanted, axis=0)) * scale_two[...]
+        slope = slope.astype(BF16)
         slope_ref[...] = jnp.where(second > 0, slope, jnp.zeros_like(slope))
         for k, (group, shift) in enumerate(shifts):
             found = jnp.zeros((width, width), F32)
@@ -232,10 +223,10 @@
     sum_d = outer_all[2 * width : 2 * width + 1, :width] + outer_all[2 * width : 2 * width + 1, width:]
     bias = bias_all[...]
     line = lax.broadcasted_iota(jnp.int32, bias.shape, 0)
-    sum_out = jnp.sum(w * outer, axis=0, keepdims=True) + b_pair * sum_d
-    vectors = jnp.where(line == 5, sum_d * w_out, bias)
+    sum_out = (jnp.sum(w * outer, axis=0, keepdims=True) + b_pair * sum_d) / ratio
+    vectors = jnp.where(line == 5, sum_d * power, bias)
     vectors = jnp.where(line == 6, sum_out, vectors)
-    outer = outer * w_out
+    outer = outer * power
     high = vectors.astype(BF16).astype(F32)
     rest = (high, vectors - high)
     col = col_all[...].astype(BF16)
@@ -315,15 +306,23 @@
 
 
 def last_kernel(
-    mine_ref, other_ref, left_w_ref, right_w_ref,
-    emb_ref, left_ref, right_ref, bias_ref, w_ref, b_ref, out_ref,
-    both_ref, flat_ref, col_ref,
+    mine_ref, other_ref, pred_mine, pred_other, left_w_ref, right_w_ref,
+    pred_hbm, emb_hbm, left_hbm, right_hbm, bias_hbm, w_hbm, b_hbm, out_hbm,
+    pred_ref, emb_ref, left_ref, right_ref, bias_ref, w_ref, b_ref, out_ref,
+    both_ref, flat_ref, col_ref, flip_ref, sems,
 ):
-    core = lax.rem(place(), 2)
+    core = place() & 1
     width = left_w_ref.shape[1]
     pairs = width // 2
     chips = mine_ref.shape[0]
+    slots = pred_ref.shape[0]
     step = width // (2 * chips)
+    copies = []
+
+    def leave(source, target):
+        copies.append(pltpu.make_async_copy(source, target, sems.at[len(copies)]))
+        copies[-1].start()
+
     lows = []
     for share in range(2 * chips):
         block = jnp.where(core == share % 2, mine_ref[share // 2], other_ref[share // 2])
@@ -337,38 +336,51 @@
         small = block[width : width + 16]
         w_ref[8 * share : 8 * share + 8, :] = small[:8]
         lows.append(small[8:])
-    for side, grad_ref in enumerate((left_ref, right_ref)):
+    both_ref[:, width:] = col_ref[...].astype(BF16)
+    weights = jnp.concatenate([left_w_ref[...], right_w_ref[...]], axis=1)
+    part = 2 * width
+    for k in range(both_ref.shape[0] // part):
+        rows = pl.ds(k * part, part)
+        emb_ref[rows, :] = lax.dot_general(
+            both_ref[rows, :], weights, (((1,), (1,)), ((), ())), preferred_element_type=F32
+        ).astype(BF16)
+        leave(emb_ref.at[rows, :], emb_hbm.at[rows, :])
+    for side, (grad_ref, grad_hbm) in enumerate(((left_ref, left_hbm), (right_ref, right_hbm))):
         for k in range(chips // 2):
             at = (side * chips // 2 + k) * width
             grad_ref[k * width : (k + 1) * width, :] = flat_ref[at : at + width, :].T
-    both_ref[:, width:] = col_ref[...].astype(BF16)
+        leave(grad_ref, grad_hbm)
     vectors = lows[0] + lows[1]
     bias_ref[...] = vectors[:5]
     b_ref[...] = vectors[5:6]
     out_ref[...] = vectors[6:7]
-    weights = jnp.concatenate([left_w_ref[...], right_w_ref[...]], axis=1)
-    part = 2 * width
-    for k in range(both_ref.shape[0] // part):
-        emb_ref[k * part : (k + 1) * part, :] = lax.dot_general(
-            both_ref[k * part : (k + 1) * part, :],
-            weights,
-            (((1,), (1,)), ((), ())),
-            preferred_element_type=F32,
-        ).astype(BF16)
+    for source, target in ((w_ref, w_hbm), (bias_ref, bias_hbm), (b_ref, b_hbm), (out_ref, out_hbm)):
+        leave(source, target)
+    for chip in range(chips):
+        for ref, side in ((pred_mine, core), (pred_other, 1 - core)):
+            block = ref[chip].astype(F32)
+            to = pl.multiple_of((2 * chip + side) * step, step)
+            for slot in range(slots):
+                flip_ref[slot, pl.ds(to, step), :] = block[slot * step : (slot + 1) * step]
+    for slot in range(slots):
+        pred_ref[slot] = flip_ref[slot].T.astype(BF16)
+    leave(pred_ref, pred_hbm)
+    for copy in copies:
+        copy.wait()
 
 
 def shape(*dims, dtype=F32):
     return jax.ShapeDtypeStruct(dims, dtype)
 
 
-def call(kernel, outs, scratch, *args):
+def call(kernel, outs, scratch, *args, space=None, out_space=VMEM, limit=32):
     return pl.pallas_call(
         kernel,
         out_shape=outs,
-        in_specs=[VMEM] * len(args),
-        out_specs=(VMEM,) * len(outs),
+        in_specs=space or [VMEM] * len(args),
+        out_specs=(out_space,) * len(outs),
         scratch_shapes=scratch,
-        compiler_params=pltpu.CompilerParams(vmem_limit_bytes=32 * 1024 * 1024),
+        compiler_params=pltpu.CompilerParams(vmem_limit_bytes=limit * 1024 * 1024),
     )(*args)
 
 
@@ -474,30 +486,30 @@
     mine, pred_send = lax.optimization_barrier((mine, pred_send))
     pred_other = swapped(pred_send, "tile", 1)
     other = swapped(mine, "tile", 1)
-    (predicted,) = call(
-        join_kernel, (shape(slots, width, width, dtype=BF16),),
-        [pltpu.VMEM((slots, width, width), F32)],
-        pred_mine, pred_other,
-    )
-    grads = call(
+    outs = (
+        shape(slots, width, width, dtype=BF16),
+        shape(rows, features, dtype=BF16),
+        shape(features, width),
+        shape(features, width),
+        shape(5, width),
+        shape(width, width),
+        shape(1, width),
+        shape(1, width),
+    )
+    outs = call(
         last_kernel,
-        (
-            shape(rows, features, dtype=BF16),
-            shape(features, width),
-            shape(features, width),
-            shape(5, width),
-            shape(width, width),
-            shape(1, width),
-            shape(1, width),
-        ),
-        [
+        outs,
+        [pltpu.VMEM(out.shape, out.dtype) for out in outs]
+        + [
             pltpu.VMEM((rows, 2 * width), BF16),
             pltpu.VMEM((2 * features, width), F32),
             pltpu.VMEM((rows, width), F32),
+            pltpu.VMEM((slots, width, width), F32),
+            pltpu.SemaphoreType.DMA((rows // (2 * width) + 7,)),
         ],
-        mine, other, w_left, w_right,
-    )
-    return (predicted[None, None], *grads[:5], grads[5][0], grads[6][0])
+        mine, other, pred_mine, pred_other, w_left, w_right, out_space=HBM,
+    )
+    return (outs[0][None, None], *outs[1:6], outs[6][0], outs[7][0])
 
 
 def solution(mesh):

time: 86.5 us -> 86.6 us (level)
  blocking collectives: 36.2 us -> 39.7 us
  Pallas kernels: 23.4 us -> 20 us
    all_to_all x3, blocking collectives: 36.2 us -> 39.7 us  [across(): lax.all_to_all(block, axis, 0, 0, axis_index_groups=groups, tiled=True)]
    pallas_call x6 -> x5, Pallas kernels: 23.4 us -> 20 us  [call(): pl.pallas_call(kernel, out_shape=outs, in_specs=space or [VMEM] * len(arg...]
  transfers between devices with their start and end apart: 7 -> 7, of which waited for: 3 -> 3; matrix products, arithmetic and copies ran while one was open for 1% -> 1% of each run, Pallas kernels for 2% -> 1%
where the time goes in v8:
time: 86.6 us; the launch traced here: 86.4 us
  blocking collectives  39.7 us (46%)
  Pallas kernels  20 us (23%)
  starting transfers between devices  14.5 us (17%)
  waiting for transfers between devices  8.08 us (9%)
  local copies, waits for them, and re-layouts  3.2 us (4%)
    all_to_all x3, blocking collectives, across(): lax.all_to_all(block, axis, 0, 0, axis_index_groups=groups, tiled=True)  39.7 us
    pallas_call x5, Pallas kernels, call(): pl.pallas_call(kernel, out_shape=outs, in_specs=space or [VMEM] * len(arg...  20 us
    ppermute x5, starting transfers between devices, swapped(): lax.ppermute(block, axis, [(i, i ^ bits) for i in range(lax.axis_size(axi...  7.43 us
    all_to_all x1, starting transfers between devices, across(): lax.all_to_all(block, axis, 0, 0, axis_index_groups=groups, tiled=True)  5.77 us
    all_to_all x1, waiting for transfers between devices, across(): lax.all_to_all(block, axis, 0, 0, axis_index_groups=groups, tiled=True)  5.33 us
    unnamed x19, local copies, waits for them, and re-layouts  3.13 us
    ppermute x5, waiting for transfers between devices, swapped(): lax.ppermute(block, axis, [(i, i ^ bits) for i in range(lax.axis_size(axi...  2.75 us
  transfers between devices with their start and end apart: 7, of which 3 were waited for; matrix products, arithmetic and copies ran while one was open for 1% of the time, Pallas kernels for 1%

profile of v8, /device:TPU:1, one launch (start us, length us, event | category | flops | bytes accessed | tf_op | source)
XLA Modules:
  0.0 86.4 jit_solution(7987586304363845993)
XLA Ops:
  0.6 1.5 %collective-permute-start.1 = (s32[3,1,6]{2,1,0:T(1,128)}, s32[3,1,6]{2,1,0:T(1,128)S(1)}, u32[]{:S(2)}, u32[]{:S(2)}) collective-permute-start(s32[3,1,6]{2,1,0:T(1,128)} %bitcast.21), channel_id=1, source_target_pairs={{0,1},{1,0},{2,3},{3,2},{4,5},{5,4},{6,7},{7,6},{8,9},{9,8},{10,11... | collective-permute-start | bytes 224 | tf_op jit(solution)/shard_map/ppermute | solution.py:388
  2.1 0.1 collective-permute-start.2
  2.2 0.8 dynamic-slice_bitcast_fusion.1
  3.1 1.3 %collective-permute-start = (bf16[32,512]{1,0:T(8,128)(2,1)S(1)}, bf16[32,512]{1,0:T(8,128)(2,1)S(1)}, u32[]{:S(2)}, u32[]{:S(2)}) collective-permute-start(bf16[32,512]{1,0:T(8,128)(2,1)S(1)} %slice_bitcast_fusion), channel_id=1, source_target_pairs={{16,0},{32,16},{48,32},{64,48},{80,64},{96,80},{112,96},{17,1},{33... | collective-permute-start | bytes 98312 | tf_op jit(solution)/shard_map/ppermute | solution.py:416
  4.4 0.1 pad.5.clone
  4.5 0.0 collective-permute-done.1.list_other
  4.5 0.0 collective-permute-done.2.target_other
  4.5 0.9 %copy-done.3 = bf16[1,1,6,128,128]{4,3,2,1,0:T(8,128)(2,1)S(1)} copy-done((bf16[1,1,6,128,128]{4,3,2,1,0:T(8,128)(2,1)S(1)}, bf16[1,1,6,128,128]{4,3,2,1,0:T(8,128)(2,1)}, u32[]{:S(2)}) %copy-start.3) | copy-done | bytes 196632
  5.4 0.7 copy-done.5
  6.1 1.1 %shard_map.152 = bf16[8,112,128]{2,1,0:T(8,128)(2,1)} custom-call(s32[3,1,6]{2,1,0:T(1,128)S(1)} %bitcast.22, s32[3,1,6]{2,1,0:T(1,128)S(1)} %collective-permute-done.1.list_other, bf16[6,128,128]{2,1,0:T(8,128)(2,1)S(1)} %bitcast.20, bf16[6,128,128]{2,1,0:T(8,128)(2,1)S(1)} %collective-permute-done.2.target_other), custom_call_target="tpu_custom_call" | custom-call | tf_op jit(solution)/shard_map/pallas_call | solution.py:377
  7.2 5.8 %all-to-all-start = ((bf16[8,112,128]{2,1,0:T(8,128)(2,1)}), bf16[8,112,128]{2,1,0:T(8,128)(2,1)S(1)}, u32[]{:S(2)}, u32[]{:S(2)}) async-start(bf16[8,112,128]{2,1,0:T(8,128)(2,1)} %shard_map.152), calls=%async_computation | async-start | bytes 458752 | tf_op jit(solution)/shard_map/all_to_all | solution.py:392
  13.0 0.0 copy-start.8
  13.0 0.0 copy-done.6
  13.0 0.6 copy-done.7
  13.6 0.0 copy-done.8
  13.6 0.1 maximum_maximum_fusion.const_ref
  13.7 0.0 collective-permute-done.next_ref
  13.7 5.3 %all-to-all-done.target_ref = bf16[8,112,128]{2,1,0:T(8,128)(2,1)S(1)} async-done(((bf16[8,112,128]{2,1,0:T(8,128)(2,1)}), bf16[8,112,128]{2,1,0:T(8,128)(2,1)S(1)}, u32[]{:S(2)}, u32[]{:S(2)}) %all-to-all-start) | async-done | bytes 229408 | tf_op jit(solution)/shard_map/all_to_all | solution.py:392
  19.0 0.0 copy-done
  19.0 17.2 %shard_map.153 = (bf16[8,144,128]{2,1,0:T(8,128)(2,1)S(1)}, bf16[8,144,128]{2,1,0:T(8,128)(2,1)S(1)}, bf16[8,96,128]{2,1,0:T(8,128)(2,1)S(1)}, f32[64,128]{1,0:T(8,128)S(1)}, bf16[32,128]{1,0:T(8,128)(2,1)S(1)}) custom-call(bf16[1024,512]{1,0:T(8,128)(2,1)S(1)} %copy-done, bf16[64,512]{1,0:T(8,128)(2,1)S(1)} %get-tuple-element.47.cols_ref, ...), custom_call_target="tpu_custom_call" | custom-call | tf_op jit(solution)/shard_map/pallas_call | solution.py:377
  36.2 1.9 %collective-permute-start.3 = (bf16[8,144,128]{2,1,0:T(8,128)(2,1)S(1)}, bf16[8,144,128]{2,1,0:T(8,128)(2,1)S(1)}, u32[]{:S(2)}, u32[]{:S(2)}) collective-permute-start(bf16[8,144,128]{2,1,0:T(8,128)(2,1)S(1)} %get-tuple-element.28), channel_id=1, source_target_pairs={{0,1},{1,0},{2,3},{3,2},{4,5},{5,4},{6,7},{7,6},{8,9},{9,8},{10,11... | collective-permute-start | bytes 884744 | tf_op jit(solution)/shard_map/ppermute | solution.py:388
  38.1 1.2 %collective-permute-done.3 = bf16[8,144,128]{2,1,0:T(8,128)(2,1)S(1)} collective-permute-done((bf16[8,144,128]{2,1,0:T(8,128)(2,1)S(1)}, bf16[8,144,128]{2,1,0:T(8,128)(2,1)S(1)}, u32[]{:S(2)}, u32[]{:S(2)}) %collective-permute-start.3) | collective-permute-done | bytes 294944 | tf_op jit(solution)/shard_map/ppermute | solution.py:388
  39.3 0.1 add_convert_fusion
  39.5 11.9 %all_to_all.20.sum_ref = bf16[8,240,128]{2,1,0:T(8,128)(2,1)S(1)} all-to-all(bf16[8,240,128]{2,1,0:T(8,128)(2,1)S(1)} %pad_maximum_fusion), channel_id=1, replica_groups={{0,2,4,6,8,10,12,14},{1,3,5,7,9,11,13,15},{16,18,20,22,24,26,28,30},{17..., dimensions={0} | all-to-all | bytes 983040 | tf_op jit(solution)/shard_map/all_to_all | solution.py:392
  51.4 0.1 shard_map.154
  51.5 18.3 %all_to_all.21.met_ref = bf16[8,112,128]{2,1,0:T(8,128)(2,1)S(1)} all-to-all(bf16[8,112,128]{2,1,0:T(8,128)(2,1)S(1)} %get-tuple-element.31), channel_id=1, replica_groups=mesh['bin'=8,'tile'=16] {'bin'}, dimensions={0} | all-to-all | bytes 458752 | tf_op jit(solution)/shard_map/all_to_all | solution.py:392
  69.9 9.5 %all_to_all.22.mine_ref = bf16[8,208,128]{2,1,0:T(8,128)(2,1)S(1)} all-to-all(bf16[8,208,128]{2,1,0:T(8,128)(2,1)S(1)} %shard_map.155), channel_id=1, replica_groups={{0,2,4,6,8,10,12,14},{1,3,5,7,9,11,13,15},{16,18,20,22,24,26,28,30},{17..., dimensions={0} | all-to-all | bytes 851968 | tf_op jit(solution)/shard_map/all_to_all | solution.py:392
  79.3 3.9 %collective-permute-start.4 = (bf16[8,208,128]{2,1,0:T(8,128)(2,1)S(1)}, bf16[8,208,128]{2,1,0:T(8,128)(2,1)S(1)}, u32[]{:S(2)}, u32[]{:S(2)}) collective-permute-start(bf16[8,208,128]{2,1,0:T(8,128)(2,1)S(1)} %all_to_all.22.mine_ref), channel_id=1, source_target_pairs={{0,1},{1,0},{2,3},{3,2},{4,5},{5,4},{6,7},{7,6},{8,9},{9,8},{10,11... | collective-permute-start | bytes 1277960 | tf_op jit(solution)/shard_map/ppermute | solution.py:388
  83.3 0.0 collective-permute-start.5
  83.3 1.5 %collective-permute-done.5.pred_other = bf16[8,48,128]{2,1,0:T(8,128)(2,1)S(1)} collective-permute-done((bf16[8,48,128]{2,1,0:T(8,128)(2,1)S(1)}, bf16[8,48,128]{2,1,0:T(8,128)(2,1)S(1)}, u32[]{:S(2)}, u32[]{:S(2)}) %collective-permute-start.5) | collective-permute-done | bytes 98336 | tf_op jit(solution)/shard_map/ppermute | solution.py:388
  84.8 0.0 collective-permute-done.4.other_ref
  84.8 1.6 %shard_map.156 = (bf16[6,128,128]{2,1,0:T(8,128)(2,1)}, bf16[1024,512]{1,0:T(8,128)(2,1)}, f32[512,128]{1,0:T(8,128)}, f32[512,128]{1,0:T(8,128)}, f32[5,128]{1,...) custom-call(bf16[8,208,128]{2,1,0:T(8,128)(2,1)S(1)} %all_to_all.22.mine_ref, ...), custom_call_target="tpu_custom_call" | custom-call | tf_op jit(solution)/shard_map/pallas_call | solution.py:377
  (14 shorter events, 0.1 us)
Async XLA Ops:
  0.6 18.4 %copy-start = (bf16[1024,512]{1,0:T(8,128)(2,1)S(1)}, bf16[1024,512]{1,0:T(8,128)(2,1)}, u32[]{:S(2)}) copy-start(bf16[1024,512]{1,0:T(8,128)(2,1)} %emb_ref.1) | copy-start | bytes 3145732
  0.6 3.8 %collective-permute-start.1 = (s32[3,1,6]{2,1,0:T(1,128)}, s32[3,1,6]{2,1,0:T(1,128)S(1)}, u32[]{:S(2)}, u32[]{:S(2)}) collective-permute-start(s32[3,1,6]{2,1,0:T(1,128)} %bitcast.21), channel_id=1, source_target_pairs={{0,1},{1,0},{2,3},{3,2},{4,5},{5,4},{6,7},{7,6},{8,9},{9,8},{10,11... | collective-permute-start | bytes 224 | tf_op jit(solution)/shard_map/ppermute | solution.py:388
  2.1 2.3 %collective-permute-start.2 = (bf16[6,128,128]{2,1,0:T(8,128)(2,1)}, bf16[6,128,128]{2,1,0:T(8,128)(2,1)S(1)}, u32[]{:S(2)}, u32[]{:S(2)}) collective-permute-start(bf16[6,128,128]{2,1,0:T(8,128)(2,1)} %bitcast.19), channel_id=1, source_target_pairs={{0,1},{1,0},{2,3},{3,2},{4,5},{5,4},{6,7},{7,6},{8,9},{9,8},{10,11... | collective-permute-start | bytes 589832 | tf_op jit(solution)/shard_map/ppermute | solution.py:388
  3.1 10.6 %collective-permute-start = (bf16[32,512]{1,0:T(8,128)(2,1)S(1)}, bf16[32,512]{1,0:T(8,128)(2,1)S(1)}, u32[]{:S(2)}, u32[]{:S(2)}) collective-permute-start(bf16[32,512]{1,0:T(8,128)(2,1)S(1)} %slice_bitcast_fusion), channel_id=1, source_target_pairs={{16,0},{32,16},{48,32},{64,48},{80,64},{96,80},{112,96},{17,1},{33... | collective-permute-start | bytes 98312 | tf_op jit(solution)/shard_map/ppermute | solution.py:416
  4.5 0.9 %copy-start.3 = (bf16[1,1,6,128,128]{4,3,2,1,0:T(8,128)(2,1)S(1)}, bf16[1,1,6,128,128]{4,3,2,1,0:T(8,128)(2,1)}, u32[]{:S(2)}) copy-start(bf16[1,1,6,128,128]{4,3,2,1,0:T(8,128)(2,1)} %param.17) | copy-start | bytes 589828
  5.4 0.7 copy-start.5
  7.2 5.8 %copy-start.6 = (f32[5,128]{1,0:T(8,128)S(1)}, f32[5,128]{1,0:T(8,128)}, u32[]{:S(2)}) copy-start(f32[5,128]{1,0:T(8,128)} %param.12) | copy-start | bytes 7684
  7.2 11.9 %copy-start.1 = (bf16[512,128]{1,0:T(8,128)(2,1)S(1)}, bf16[512,128]{1,0:T(8,128)(2,1)}, u32[]{:S(2)}) copy-start(bf16[512,128]{1,0:T(8,128)(2,1)} %left_w_ref.3) | copy-start | bytes 393220
  7.2 11.9 %copy-start.2 = (bf16[512,128]{1,0:T(8,128)(2,1)S(1)}, bf16[512,128]{1,0:T(8,128)(2,1)}, u32[]{:S(2)}) copy-start(bf16[512,128]{1,0:T(8,128)(2,1)} %right_w_ref.3) | copy-start | bytes 393220
  7.2 11.9 %copy-start.4 = (bf16[128,128]{1,0:T(8,128)(2,1)S(1)}, bf16[128,128]{1,0:T(8,128)(2,1)}, u32[]{:S(2)}) copy-start(bf16[128,128]{1,0:T(8,128)(2,1)} %w_ref.1) | copy-start | bytes 98308
  7.2 11.8 %all-to-all-start = ((bf16[8,112,128]{2,1,0:T(8,128)(2,1)}), bf16[8,112,128]{2,1,0:T(8,128)(2,1)S(1)}, u32[]{:S(2)}, u32[]{:S(2)}) async-start(bf16[8,112,128]{2,1,0:T(8,128)(2,1)} %shard_map.152), calls=%async_computation | async-start | bytes 458752 | tf_op jit(solution)/shard_map/all_to_all | solution.py:392
  13.0 0.7 copy-start.7
  13.0 0.7 copy-start.8
  36.2 3.1 %collective-permute-start.3 = (bf16[8,144,128]{2,1,0:T(8,128)(2,1)S(1)}, bf16[8,144,128]{2,1,0:T(8,128)(2,1)S(1)}, u32[]{:S(2)}, u32[]{:S(2)}) collective-permute-start(bf16[8,144,128]{2,1,0:T(8,128)(2,1)S(1)} %get-tuple-element.28), channel_id=1, source_target_pairs={{0,1},{1,0},{2,3},{3,2},{4,5},{5,4},{6,7},{7,6},{8,9},{9,8},{10,11... | collective-permute-start | bytes 884744 | tf_op jit(solution)/shard_map/ppermute | solution.py:388
  79.3 5.5 %collective-permute-start.4 = (bf16[8,208,128]{2,1,0:T(8,128)(2,1)S(1)}, bf16[8,208,128]{2,1,0:T(8,128)(2,1)S(1)}, u32[]{:S(2)}, u32[]{:S(2)}) collective-permute-start(bf16[8,208,128]{2,1,0:T(8,128)(2,1)S(1)} %all_to_all.22.mine_ref), channel_id=1, source_target_pairs={{0,1},{1,0},{2,3},{3,2},{4,5},{5,4},{6,7},{7,6},{8,9},{9,8},{10,11... | collective-permute-start | bytes 1277960 | tf_op jit(solution)/shard_map/ppermute | solution.py:388
  83.3 1.5 %collective-permute-start.5 = (bf16[8,48,128]{2,1,0:T(8,128)(2,1)S(1)}, bf16[8,48,128]{2,1,0:T(8,128)(2,1)S(1)}, u32[]{:S(2)}, u32[]{:S(2)}) collective-permute-start(bf16[8,48,128]{2,1,0:T(8,128)(2,1)S(1)} %get-tuple-element.37), channel_id=1, source_target_pairs={{0,1},{1,0},{2,3},{3,2},{4,5},{5,4},{6,7},{7,6},{8,9},{9,8},{10,11... | collective-permute-start | bytes 294920 | tf_op jit(solution)/shard_map/ppermute | solution.py:388

commit v9 on v8

--- a/solution.py
+++ b/solution.py
@@ -84,7 +84,7 @@
     power = jnp.where(size < TINY, 0.0, power).astype(BF16).astype(F32)
     power = jnp.where(w_out < 0.0, -power, power)
     ratio = jnp.where(size < TINY, 1.0, w_out / jnp.where(size < TINY, 1.0, power))
-    back = (w * power).T.astype(BF16)
+    back = (w * w_out).T.astype(BF16)
     spread = jnp.broadcast_to(power * (1.0 / width), (width, width)).T.astype(BF16)
     for ref, block in ((w_two, w_ref[...]), (out_two, spread), (back_two, back)):
         ref[...] = jnp.zeros_like(ref)
@@ -155,20 +155,19 @@
             pre += [left + right[j : j + 1, :] for j in range(step)]
             target = pltpu.roll(
                 target_all[slot >> spread_bits], (width - shift) & (width - 1), 1
-            ).astype(BF16)
+            )
             for j in range(step):
-                want = jnp.broadcast_to(target[:, j : j + 1], (width, width)).astype(F32)
+                want = jnp.broadcast_to(target[:, j : j + 1], (width, width))
                 wanted.append(jnp.concatenate([want[:pairs], want[pairs:]], axis=1))
             floor = jnp.where(job < count, b_two[...], jnp.full((1, 2 * width), NEVER, F32))
             floors.append(jnp.broadcast_to(floor, (step * pairs, 2 * width)))
-        first = jnp.maximum(jnp.concatenate(pre, axis=0), 0.0).astype(BF16)
+        first = jnp.maximum(jnp.concatenate(pre, axis=0).astype(BF16), 0.0)
         first_ref[...] = first
         act = jnp.dot(first, w_two[...], preferred_element_type=F32)
         act = act + jnp.concatenate(floors, axis=0)
-        second = (jnp.maximum(act, 0.0) * scale_two[...]).astype(BF16)
+        second = jnp.maximum((act * scale_two[...]).astype(BF16), 0.0)
         contact = jnp.dot(second, out_two[...], preferred_element_type=F32)
-        slope = (contact - jnp.concatenate(wanted, axis=0)) * scale_two[...]
-        slope = slope.astype(BF16)
+        slope = (contact - jnp.concatenate(wanted, axis=0)).astype(BF16)
         slope_ref[...] = jnp.where(second > 0, slope, jnp.zeros_like(slope))
         for k, (group, shift) in enumerate(shifts):
             found = jnp.zeros((width, width), F32)
@@ -193,13 +192,11 @@
             for j in range(step):
                 here = back[(k * step + j) * pairs : (k * step + j + 1) * pairs]
                 rows = rows + here
-                col = jnp.sum(here, axis=0, keepdims=True)
-                cols.append(col[:, :width] + col[:, width:])
+                cols.append(sum(here[g : g + 8] for g in range(0, pairs, 8)))
             row_all[pl.ds(at, pairs), :] += rows
-            cols = jnp.concatenate(cols, axis=0)
-            col_at = pl.multiple_of((block + offset) * step, step)
-            col_all[pl.ds(col_at, step), :] += cols
-            bias_all[pl.ds(offset, 1), :] += jnp.sum(cols, axis=0, keepdims=True)
+            col_at = pl.multiple_of((block + offset) * (8 * step), 8 * step)
+            col_all[pl.ds(col_at, 8 * step), :] += jnp.concatenate(cols, axis=0)
+            bias_all[pl.ds(pl.multiple_of(offset * 8, 8), 8), :] += sum(cols)
         lhs = jnp.concatenate([first.T, ones], axis=0)
         outer_all[...] += jnp.dot(lhs, slope, preferred_element_type=F32)
 
@@ -219,17 +216,25 @@
     flat = jnp.concatenate(flat, axis=0).astype(BF16)
     for chip in range(chips):
         pred_ref[chip] = flat[chip * 2 * slots * step : (chip + 1) * 2 * slots * step]
+    def folded(ref, count):
+        sums = [
+            jnp.sum(ref[8 * k : 8 * k + 8, :], axis=0, keepdims=True) for k in range(count)
+        ]
+        sums = jnp.concatenate(sums, axis=0)
+        return sums[:, :width] + sums[:, width:]
+
+    col = folded(col_all, col_all.shape[0] // 8)
+    bias = folded(bias_all, 8)
     outer = outer_all[:width, :width] + outer_all[width : 2 * width, width:]
     sum_d = outer_all[2 * width : 2 * width + 1, :width] + outer_all[2 * width : 2 * width + 1, width:]
-    bias = bias_all[...]
     line = lax.broadcasted_iota(jnp.int32, bias.shape, 0)
-    sum_out = (jnp.sum(w * outer, axis=0, keepdims=True) + b_pair * sum_d) / ratio
-    vectors = jnp.where(line == 5, sum_d * power, bias)
+    sum_out = jnp.sum(w * outer, axis=0, keepdims=True) + b_pair * sum_d
+    vectors = jnp.where(line == 5, sum_d * w_out, bias)
     vectors = jnp.where(line == 6, sum_out, vectors)
-    outer = outer * power
+    outer = outer * w_out
     high = vectors.astype(BF16).astype(F32)
     rest = (high, vectors - high)
-    col = col_all[...].astype(BF16)
+    col_low = col.astype(BF16)
     rows = []
     for block in range(blocks):
         here = row_all[block * pairs : (block + 1) * pairs, :].astype(BF16)
@@ -241,7 +246,7 @@
             jnp.concatenate(rows, axis=0), emb_ref[...], contract, preferred_element_type=F32
         ).astype(BF16),
         lax.dot_general(
-            col, jnp.concatenate(embs, axis=0), contract, preferred_element_type=F32
+            col_low, jnp.concatenate(embs, axis=0), contract, preferred_element_type=F32
         ).astype(BF16),
     )
     def message(share):
@@ -257,8 +262,8 @@
         even, odd = message(2 * chip), message(2 * chip + 1)
         keep_ref[chip] = jnp.where(core == 0, even, odd)
         send_ref[chip] = jnp.where(core == 0, odd, even)
-    col_ref[...] = col_all[:own]
-    edge_ref[...] = col[own:]
+    col_ref[...] = col[:own]
+    edge_ref[...] = col_low[own:]
 
 
 def share_kernel(sum_ref, edge_ref, row_ref, message_ref, mine_ref, send_ref):
@@ -449,9 +454,9 @@
             pltpu.VMEM(grouped, F32),
             pltpu.VMEM(grouped, F32),
             pltpu.VMEM((rows // 2, 2 * width), F32),
-            pltpu.VMEM((part + edge, width), F32),
+            pltpu.VMEM((8 * (part + edge), 2 * width), F32),
             pltpu.VMEM((2 * width + 16, 2 * width), F32),
-            pltpu.VMEM((8, width), F32),
+            pltpu.VMEM((64, 2 * width), F32),
             pltpu.VMEM((2 * width, 2 * width), BF16),
             pltpu.VMEM((2 * width, 2 * width), BF16),
             pltpu.VMEM((2 * width, 2 * width), BF16),

time: 86.6 us -> 84.4 us (0.975); the launches traced: 86.4 us -> 83.1 us
  blocking collectives: 39.7 us -> 37.4 us
  Pallas kernels: 20 us -> 19.1 us
    all_to_all x3, blocking collectives: 39.7 us -> 37.4 us  [across(): lax.all_to_all(block, axis, 0, 0, axis_index_groups=groups, tiled=True)]
    pallas_call x5, Pallas kernels: 20 us -> 19.1 us  [call(): pl.pallas_call(kernel, out_shape=outs, in_specs=space or [VMEM] * len(arg...]
where the time goes in v9:
time: 84.4 us; the launch traced here: 83.1 us
  blocking collectives  37.4 us (44%)
  Pallas kernels  19.1 us (23%)
  starting transfers between devices  14.4 us (17%)
  waiting for transfers between devices  8.08 us (10%)
  local copies, waits for them, and re-layouts  3.2 us (4%)
    all_to_all x3, blocking collectives, across(): lax.all_to_all(block, axis, 0, 0, axis_index_groups=groups, tiled=True)  37.4 us
    pallas_call x5, Pallas kernels, call(): pl.pallas_call(kernel, out_shape=outs, in_specs=space or [VMEM] * len(arg...  19.1 us
    ppermute x5, starting transfers between devices, swapped(): lax.ppermute(block, axis, [(i, i ^ bits) for i in range(lax.axis_size(axi...  7.33 us
    all_to_all x1, starting transfers between devices, across(): lax.all_to_all(block, axis, 0, 0, axis_index_groups=groups, tiled=True)  5.77 us
    all_to_all x1, waiting for transfers between devices, across(): lax.all_to_all(block, axis, 0, 0, axis_index_groups=groups, tiled=True)  5.33 us
    unnamed x19, local copies, waits for them, and re-layouts  3.13 us
    ppermute x5, waiting for transfers between devices, swapped(): lax.ppermute(block, axis, [(i, i ^ bits) for i in range(lax.axis_size(axi...  2.75 us
  transfers between devices with their start and end apart: 7, of which 3 were waited for; matrix products, arithmetic and copies ran while one was open for 1% of the time, Pallas kernels for 1%

profile of v9, /device:TPU:1, one launch (start us, length us, event | category | flops | bytes accessed | tf_op | source)
XLA Modules:
  0.0 83.1 jit_solution(2666220867396717170)
XLA Ops:
  0.6 0.0 copy-start
  0.6 1.5 %collective-permute-start.1 = (s32[3,1,6]{2,1,0:T(1,128)}, s32[3,1,6]{2,1,0:T(1,128)S(1)}, u32[]{:S(2)}, u32[]{:S(2)}) collective-permute-start(s32[3,1,6]{2,1,0:T(1,128)} %bitcast.21), channel_id=1, source_target_pairs={{0,1},{1,0},{2,3},{3,2},{4,5},{5,4},{6,7},{7,6},{8,9},{9,8},{10,11... | collective-permute-start | bytes 224 | tf_op jit(solution)/shard_map/ppermute | solution.py:393
  2.1 0.1 collective-permute-start.2
  2.2 0.8 %dynamic-slice_bitcast_fusion.1 = (bf16[8,1,8,512]{3,2,0,1:T(8,128)(2,1)S(1)}, bf16[64,512]{1,0:T(8,128)(2,1)S(1)}) fusion(bf16[8,16,8,512]{3,2,1,0:T(8,128)(2,1)} %bitcast.18, s32[]{:T(128)S(6)} %select_n.3), kind=kLoop, calls=%fused_computation.3 | loop fusion | bytes 196612
  3.1 1.3 %collective-permute-start = (bf16[32,512]{1,0:T(8,128)(2,1)S(1)}, bf16[32,512]{1,0:T(8,128)(2,1)S(1)}, u32[]{:S(2)}, u32[]{:S(2)}) collective-permute-start(bf16[32,512]{1,0:T(8,128)(2,1)S(1)} %slice_bitcast_fusion), channel_id=1, source_target_pairs={{16,0},{32,16},{48,32},{64,48},{80,64},{96,80},{112,96},{17,1},{33... | collective-permute-start | bytes 98312 | tf_op jit(solution)/shard_map/ppermute | solution.py:421
  4.4 0.1 pad.5.clone
  4.5 0.0 collective-permute-done.1.list_other
  4.5 0.0 collective-permute-done.2.target_other
  4.5 0.9 %copy-done.3 = bf16[1,1,6,128,128]{4,3,2,1,0:T(8,128)(2,1)S(1)} copy-done((bf16[1,1,6,128,128]{4,3,2,1,0:T(8,128)(2,1)S(1)}, bf16[1,1,6,128,128]{4,3,2,1,0:T(8,128)(2,1)}, u32[]{:S(2)}) %copy-start.3) | copy-done | bytes 196632
  5.4 0.7 copy-done.5
  6.1 1.1 %shard_map.152 = bf16[8,112,128]{2,1,0:T(8,128)(2,1)} custom-call(s32[3,1,6]{2,1,0:T(1,128)S(1)} %bitcast.22, s32[3,1,6]{2,1,0:T(1,128)S(1)} %collective-permute-done.1.list_other, bf16[6,128,128]{2,1,0:T(8,128)(2,1)S(1)} %bitcast.20, bf16[6,128,128]{2,1,0:T(8,128)(2,1)S(1)} %collective-permute-done.2.target_other), custom_call_target="tpu_custom_call" | custom-call | tf_op jit(solution)/shard_map/pallas_call | solution.py:382
  7.2 5.8 %all-to-all-start = ((bf16[8,112,128]{2,1,0:T(8,128)(2,1)}), bf16[8,112,128]{2,1,0:T(8,128)(2,1)S(1)}, u32[]{:S(2)}, u32[]{:S(2)}) async-start(bf16[8,112,128]{2,1,0:T(8,128)(2,1)} %shard_map.152), calls=%async_computation | async-start | bytes 458752 | tf_op jit(solution)/shard_map/all_to_all | solution.py:397
  13.0 0.0 copy-start.8
  13.0 0.6 copy-done.7
  13.6 0.0 copy-done.8
  13.6 0.1 maximum_maximum_fusion.const_ref
  13.7 0.0 collective-permute-done.next_ref
  13.7 5.3 %all-to-all-done.target_ref = bf16[8,112,128]{2,1,0:T(8,128)(2,1)S(1)} async-done(((bf16[8,112,128]{2,1,0:T(8,128)(2,1)}), bf16[8,112,128]{2,1,0:T(8,128)(2,1)S(1)}, u32[]{:S(2)}, u32[]{:S(2)}) %all-to-all-start) | async-done | bytes 229408 | tf_op jit(solution)/shard_map/all_to_all | solution.py:397
  19.0 0.0 copy-done.4
  19.0 16.2 %shard_map.153 = (bf16[8,144,128]{2,1,0:T(8,128)(2,1)S(1)}, bf16[8,144,128]{2,1,0:T(8,128)(2,1)S(1)}, bf16[8,96,128]{2,1,0:T(8,128)(2,1)S(1)}, f32[64,128]{1,0:T(8,128)S(1)}, bf16[32,128]{1,0:T(8,128)(2,1)S(1)}) custom-call(bf16[1024,512]{1,0:T(8,128)(2,1)S(1)} %copy-done, bf16[64,512]{1,0:T(8,128)(2,1)S(1)} %get-tuple-element.47.cols_ref, ...), custom_call_target="tpu_custom_call" | custom-call | tf_op jit(solution)/shard_map/pallas_call | solution.py:382
  35.3 1.9 %collective-permute-start.3 = (bf16[8,144,128]{2,1,0:T(8,128)(2,1)S(1)}, bf16[8,144,128]{2,1,0:T(8,128)(2,1)S(1)}, u32[]{:S(2)}, u32[]{:S(2)}) collective-permute-start(bf16[8,144,128]{2,1,0:T(8,128)(2,1)S(1)} %get-tuple-element.28), channel_id=1, source_target_pairs={{0,1},{1,0},{2,3},{3,2},{4,5},{5,4},{6,7},{7,6},{8,9},{9,8},{10,11... | collective-permute-start | bytes 884744 | tf_op jit(solution)/shard_map/ppermute | solution.py:393
  37.2 1.2 %collective-permute-done.3 = bf16[8,144,128]{2,1,0:T(8,128)(2,1)S(1)} collective-permute-done((bf16[8,144,128]{2,1,0:T(8,128)(2,1)S(1)}, bf16[8,144,128]{2,1,0:T(8,128)(2,1)S(1)}, u32[]{:S(2)}, u32[]{:S(2)}) %collective-permute-start.3) | collective-permute-done | bytes 294944 | tf_op jit(solution)/shard_map/ppermute | solution.py:393
  38.4 0.1 add_convert_fusion
  38.5 11.9 %all_to_all.20.sum_ref = bf16[8,240,128]{2,1,0:T(8,128)(2,1)S(1)} all-to-all(bf16[8,240,128]{2,1,0:T(8,128)(2,1)S(1)} %pad_maximum_fusion), channel_id=1, replica_groups={{0,2,4,6,8,10,12,14},{1,3,5,7,9,11,13,15},{16,18,20,22,24,26,28,30},{17..., dimensions={0} | all-to-all | bytes 983040 | tf_op jit(solution)/shard_map/all_to_all | solution.py:397
  50.5 0.1 shard_map.154
  50.6 16.1 %all_to_all.21.met_ref = bf16[8,112,128]{2,1,0:T(8,128)(2,1)S(1)} all-to-all(bf16[8,112,128]{2,1,0:T(8,128)(2,1)S(1)} %get-tuple-element.31), channel_id=1, replica_groups=mesh['bin'=8,'tile'=16] {'bin'}, dimensions={0} | all-to-all | bytes 458752 | tf_op jit(solution)/shard_map/all_to_all | solution.py:397
  66.7 9.5 %all_to_all.22.mine_ref = bf16[8,208,128]{2,1,0:T(8,128)(2,1)S(1)} all-to-all(bf16[8,208,128]{2,1,0:T(8,128)(2,1)S(1)} %shard_map.155), channel_id=1, replica_groups={{0,2,4,6,8,10,12,14},{1,3,5,7,9,11,13,15},{16,18,20,22,24,26,28,30},{17..., dimensions={0} | all-to-all | bytes 851968 | tf_op jit(solution)/shard_map/all_to_all | solution.py:397
  76.1 3.9 %collective-permute-start.4 = (bf16[8,208,128]{2,1,0:T(8,128)(2,1)S(1)}, bf16[8,208,128]{2,1,0:T(8,128)(2,1)S(1)}, u32[]{:S(2)}, u32[]{:S(2)}) collective-permute-start(bf16[8,208,128]{2,1,0:T(8,128)(2,1)S(1)} %all_to_all.22.mine_ref), channel_id=1, source_target_pairs={{0,1},{1,0},{2,3},{3,2},{4,5},{5,4},{6,7},{7,6},{8,9},{9,8},{10,11... | collective-permute-start | bytes 1277960 | tf_op jit(solution)/shard_map/ppermute | solution.py:393
  80.0 0.0 collective-permute-start.5
  80.0 1.5 %collective-permute-done.5.pred_other = bf16[8,48,128]{2,1,0:T(8,128)(2,1)S(1)} collective-permute-done((bf16[8,48,128]{2,1,0:T(8,128)(2,1)S(1)}, bf16[8,48,128]{2,1,0:T(8,128)(2,1)S(1)}, u32[]{:S(2)}, u32[]{:S(2)}) %collective-permute-start.5) | collective-permute-done | bytes 98336 | tf_op jit(solution)/shard_map/ppermute | solution.py:393
  81.5 0.0 collective-permute-done.4.other_ref
  81.5 1.6 %shard_map.156 = (bf16[6,128,128]{2,1,0:T(8,128)(2,1)}, bf16[1024,512]{1,0:T(8,128)(2,1)}, f32[512,128]{1,0:T(8,128)}, f32[512,128]{1,0:T(8,128)}, f32[5,128]{1,...) custom-call(bf16[8,208,128]{2,1,0:T(8,128)(2,1)S(1)} %all_to_all.22.mine_ref, ...), custom_call_target="tpu_custom_call" | custom-call | tf_op jit(solution)/shard_map/pallas_call | solution.py:382
  (14 shorter events, 0.1 us)
Async XLA Ops:
  0.6 18.4 %copy-start = (bf16[1024,512]{1,0:T(8,128)(2,1)S(1)}, bf16[1024,512]{1,0:T(8,128)(2,1)}, u32[]{:S(2)}) copy-start(bf16[1024,512]{1,0:T(8,128)(2,1)} %emb_ref.1) | copy-start | bytes 3145732
  0.6 3.8 %collective-permute-start.1 = (s32[3,1,6]{2,1,0:T(1,128)}, s32[3,1,6]{2,1,0:T(1,128)S(1)}, u32[]{:S(2)}, u32[]{:S(2)}) collective-permute-start(s32[3,1,6]{2,1,0:T(1,128)} %bitcast.21), channel_id=1, source_target_pairs={{0,1},{1,0},{2,3},{3,2},{4,5},{5,4},{6,7},{7,6},{8,9},{9,8},{10,11... | collective-permute-start | bytes 224 | tf_op jit(solution)/shard_map/ppermute | solution.py:393
  2.1 2.3 %collective-permute-start.2 = (bf16[6,128,128]{2,1,0:T(8,128)(2,1)}, bf16[6,128,128]{2,1,0:T(8,128)(2,1)S(1)}, u32[]{:S(2)}, u32[]{:S(2)}) collective-permute-start(bf16[6,128,128]{2,1,0:T(8,128)(2,1)} %bitcast.19), channel_id=1, source_target_pairs={{0,1},{1,0},{2,3},{3,2},{4,5},{5,4},{6,7},{7,6},{8,9},{9,8},{10,11... | collective-permute-start | bytes 589832 | tf_op jit(solution)/shard_map/ppermute | solution.py:393
  3.1 10.6 %collective-permute-start = (bf16[32,512]{1,0:T(8,128)(2,1)S(1)}, bf16[32,512]{1,0:T(8,128)(2,1)S(1)}, u32[]{:S(2)}, u32[]{:S(2)}) collective-permute-start(bf16[32,512]{1,0:T(8,128)(2,1)S(1)} %slice_bitcast_fusion), channel_id=1, source_target_pairs={{16,0},{32,16},{48,32},{64,48},{80,64},{96,80},{112,96},{17,1},{33... | collective-permute-start | bytes 98312 | tf_op jit(solution)/shard_map/ppermute | solution.py:421
  4.5 0.9 %copy-start.3 = (bf16[1,1,6,128,128]{4,3,2,1,0:T(8,128)(2,1)S(1)}, bf16[1,1,6,128,128]{4,3,2,1,0:T(8,128)(2,1)}, u32[]{:S(2)}) copy-start(bf16[1,1,6,128,128]{4,3,2,1,0:T(8,128)(2,1)} %param.17) | copy-start | bytes 589828
  5.4 0.7 copy-start.5
  7.2 5.8 %copy-start.6 = (f32[5,128]{1,0:T(8,128)S(1)}, f32[5,128]{1,0:T(8,128)}, u32[]{:S(2)}) copy-start(f32[5,128]{1,0:T(8,128)} %param.12) | copy-start | bytes 7684
  7.2 11.9 %copy-start.1 = (bf16[512,128]{1,0:T(8,128)(2,1)S(1)}, bf16[512,128]{1,0:T(8,128)(2,1)}, u32[]{:S(2)}) copy-start(bf16[512,128]{1,0:T(8,128)(2,1)} %left_w_ref.3) | copy-start | bytes 393220
  7.2 11.9 %copy-start.2 = (bf16[512,128]{1,0:T(8,128)(2,1)S(1)}, bf16[512,128]{1,0:T(8,128)(2,1)}, u32[]{:S(2)}) copy-start(bf16[512,128]{1,0:T(8,128)(2,1)} %right_w_ref.3) | copy-start | bytes 393220
  7.2 11.9 %copy-start.4 = (bf16[128,128]{1,0:T(8,128)(2,1)S(1)}, bf16[128,128]{1,0:T(8,128)(2,1)}, u32[]{:S(2)}) copy-start(bf16[128,128]{1,0:T(8,128)(2,1)} %w_ref.1) | copy-start | bytes 98308
  7.2 11.8 %all-to-all-start = ((bf16[8,112,128]{2,1,0:T(8,128)(2,1)}), bf16[8,112,128]{2,1,0:T(8,128)(2,1)S(1)}, u32[]{:S(2)}, u32[]{:S(2)}) async-start(bf16[8,112,128]{2,1,0:T(8,128)(2,1)} %shard_map.152), calls=%async_computation | async-start | bytes 458752 | tf_op jit(solution)/shard_map/all_to_all | solution.py:397
  13.0 0.7 copy-start.7
  13.0 0.7 copy-start.8
  35.3 3.1 %collective-permute-start.3 = (bf16[8,144,128]{2,1,0:T(8,128)(2,1)S(1)}, bf16[8,144,128]{2,1,0:T(8,128)(2,1)S(1)}, u32[]{:S(2)}, u32[]{:S(2)}) collective-permute-start(bf16[8,144,128]{2,1,0:T(8,128)(2,1)S(1)} %get-tuple-element.28), channel_id=1, source_target_pairs={{0,1},{1,0},{2,3},{3,2},{4,5},{5,4},{6,7},{7,6},{8,9},{9,8},{10,11... | collective-permute-start | bytes 884744 | tf_op jit(solution)/shard_map/ppermute | solution.py:393
  76.1 5.4 %collective-permute-start.4 = (bf16[8,208,128]{2,1,0:T(8,128)(2,1)S(1)}, bf16[8,208,128]{2,1,0:T(8,128)(2,1)S(1)}, u32[]{:S(2)}, u32[]{:S(2)}) collective-permute-start(bf16[8,208,128]{2,1,0:T(8,128)(2,1)S(1)} %all_to_all.22.mine_ref), channel_id=1, source_target_pairs={{0,1},{1,0},{2,3},{3,2},{4,5},{5,4},{6,7},{7,6},{8,9},{9,8},{10,11... | collective-permute-start | bytes 1277960 | tf_op jit(solution)/shard_map/ppermute | solution.py:393
  80.0 1.5 %collective-permute-start.5 = (bf16[8,48,128]{2,1,0:T(8,128)(2,1)S(1)}, bf16[8,48,128]{2,1,0:T(8,128)(2,1)S(1)}, u32[]{:S(2)}, u32[]{:S(2)}) collective-permute-start(bf16[8,48,128]{2,1,0:T(8,128)(2,1)S(1)} %get-tuple-element.37), channel_id=1, source_target_pairs={{0,1},{1,0},{2,3},{3,2},{4,5},{5,4},{6,7},{7,6},{8,9},{9,8},{10,11... | collective-permute-start | bytes 294920 | tf_op jit(solution)/shard_map/ppermute | solution.py:393

commit v10 on v9

--- a/solution.py
+++ b/solution.py
@@ -49,33 +49,17 @@
         send_ref[chip, 2 * slots * step :, :] = listed
 
 
-def pair_kernel(
-    emb_ref, cols_ref, next_ref, left_w_ref, right_w_ref, const_ref, target_ref, w_ref,
-    keep_ref, send_ref, pred_ref, col_ref, edge_ref,
-    table, lists, list_sem, list_all, left_ref, full_ref, right_all, target_all, pred_all, row_all, col_all,
-    outer_all, bias_all, w_two, out_two, back_two, b_two, scale_two, first_0, first_1, slope_0, slope_1,
+def ready_kernel(
+    emb_ref, next_ref, left_w_ref, right_w_ref, const_ref, w_ref,
+    left_ref, right_ref, w_two, out_two, back_two, lines_ref, full_ref,
 ):
     tile = place()
     width = w_ref.shape[0]
     pairs = width // 2
     blocks = emb_ref.shape[0] // width
-    chips = target_ref.shape[0]
-    shares = 2 * chips
-    step = width // shares
-    slots = target_ref.shape[1] // (2 * step) - 1
-    core = tile & 1
-    groups = target_all.shape[0] - 1
-    spread_bits = (width // step).bit_length() - 1
-
-    for chip in range(chips):
-        rows = target_ref[chip, 2 * slots * step :, :].astype(F32).astype(jnp.int32)
-        for side in range(2):
-            for k in range(3):
-                at = 3 * side + k
-                list_all[k, 2 * chip + side : 2 * chip + side + 1] = rows[at : at + 1]
-    copy = pltpu.make_async_copy(list_all, lists, list_sem)
-    copy.start()
-
+    edge = next_ref.shape[0]
+    own = right_ref.shape[0] - edge
+    step = own // blocks
     w = w_ref[...].astype(F32)
     w_out = const_ref[6:7, :]
     b_pair = const_ref[5:6, :]
@@ -90,10 +74,9 @@
         ref[...] = jnp.zeros_like(ref)
         ref[:width, :width] = block
         ref[width:, width:] = block
-    scale_two[:, :width] = ratio
-    scale_two[:, width:] = ratio
-    b_two[:, :width] = b_pair
-    b_two[:, width:] = b_pair
+    lines = jnp.concatenate([ratio, b_pair, jnp.zeros((6, width), F32)], axis=0)
+    lines_ref[:, :width] = lines
+    lines_ref[:, width:] = lines
     weights = jnp.concatenate([left_w_ref[...], right_w_ref[...]], axis=1)
     for block in range(0, blocks, 2):
         both = jnp.dot(
@@ -107,12 +90,45 @@
             left_ref[at : at + pairs, :width] = left[:pairs]
             left_ref[at : at + pairs, width:] = left[pairs:]
         full_ref[block * width : (block + 2) * width, :] = both[:, width:]
-    own = blocks * step
     for block in range(blocks):
         at = pl.multiple_of(block * width + tile * step, step)
-        right_all[block * step : (block + 1) * step, :] = full_ref[pl.ds(at, step), :]
+        right_ref[block * step : (block + 1) * step, :] = full_ref[pl.ds(at, step), :]
     right_next = jnp.dot(next_ref[...], right_w_ref[...], preferred_element_type=F32)
-    right_all[own:, :] = right_next.astype(BF16).astype(F32)
+    right_ref[own:, :] = right_next.astype(BF16).astype(F32)
+
+
+def pair_kernel(
+    emb_ref, cols_ref, next_ref, const_ref, target_ref, w_ref,
+    left_ref, right_all, w_two, out_two, back_two, lines_ref,
+    keep_ref, send_ref, pred_ref, col_ref, edge_ref,
+    table, lists, list_sem, list_all, target_all, pred_all, row_all, col_all,
+    outer_all, bias_all, first_0, first_1, slope_0, slope_1,
+):
+    tile = place()
+    width = w_ref.shape[0]
+    pairs = width // 2
+    blocks = emb_ref.shape[0] // width
+    chips = target_ref.shape[0]
+    shares = 2 * chips
+    step = width // shares
+    slots = target_ref.shape[1] // (2 * step) - 1
+    core = tile & 1
+    groups = target_all.shape[0] - 1
+    spread_bits = (width // step).bit_length() - 1
+
+    for chip in range(chips):
+        rows = target_ref[chip, 2 * slots * step :, :].astype(F32).astype(jnp.int32)
+        for side in range(2):
+            for k in range(3):
+                at = 3 * side + k
+                list_all[k, 2 * chip + side : 2 * chip + side + 1] = rows[at : at + 1]
+    copy = pltpu.make_async_copy(list_all, lists, list_sem)
+    copy.start()
+
+    w = w_ref[...].astype(F32)
+    w_out = const_ref[6:7, :]
+    b_pair = const_ref[5:6, :]
+    own = blocks * step
     rows = [target_ref[chip, : 2 * slots * step, :].astype(F32) for chip in range(chips)]
     rows = jnp.concatenate(rows, axis=0)
     for group in range(groups):
@@ -159,13 +175,13 @@
             for j in range(step):
                 want = jnp.broadcast_to(target[:, j : j + 1], (width, width))
                 wanted.append(jnp.concatenate([want[:pairs], want[pairs:]], axis=1))
-            floor = jnp.where(job < count, b_two[...], jnp.full((1, 2 * width), NEVER, F32))
+            floor = jnp.where(job < count, lines_ref[1:2, :], jnp.full((1, 2 * width), NEVER, F32))
             floors.append(jnp.broadcast_to(floor, (step * pairs, 2 * width)))
         first = jnp.maximum(jnp.concatenate(pre, axis=0).astype(BF16), 0.0)
         first_ref[...] = first
         act = jnp.dot(first, w_two[...], preferred_element_type=F32)
         act = act + jnp.concatenate(floors, axis=0)
-        second = jnp.maximum((act * scale_two[...]).astype(BF16), 0.0)
+        second = jnp.maximum((act * lines_ref[0:1, :]).astype(BF16), 0.0)
         contact = jnp.dot(second, out_two[...], preferred_element_type=F32)
         slope = (contact - jnp.concatenate(wanted, axis=0)).astype(BF16)
         slope_ref[...] = jnp.where(second > 0, slope, jnp.zeros_like(slope))
@@ -429,10 +445,25 @@
         lists, lists_other, target, target_other,
     )
     groups = [list(range(k, shares, 2)) for k in range(2)]
+    target_send, consts = lax.optimization_barrier((target_send, consts))
     target_all = across(target_send, "tile", groups)
 
     chunk = (BATCH * step * pairs, 2 * width)
     grouped = (slots * shares * step // width + 1, width, width)
+    double = shape(2 * width, 2 * width, dtype=BF16)
+    ready = call(
+        ready_kernel,
+        (
+            shape(rows // 2, 2 * width),
+            shape(part + edge, width),
+            double,
+            double,
+            double,
+            shape(8, 2 * width),
+        ),
+        [pltpu.VMEM((rows, width), F32)],
+        embeddings, emb_next, w_left, w_right, consts, w_pair,
+    )
     half = shape(chips, width + 16, width, dtype=BF16)
     sums, sums_send, pred, col, col_edge = call(
         pair_kernel,
@@ -448,26 +479,18 @@
             pltpu.SMEM((3, shares, width), jnp.int32),
             pltpu.SemaphoreType.DMA,
             pltpu.VMEM((3, shares, width), jnp.int32),
-            pltpu.VMEM((rows // 2, 2 * width), F32),
-            pltpu.VMEM((rows, width), F32),
-            pltpu.VMEM((part + edge, width), F32),
             pltpu.VMEM(grouped, F32),
             pltpu.VMEM(grouped, F32),
             pltpu.VMEM((rows // 2, 2 * width), F32),
             pltpu.VMEM((8 * (part + edge), 2 * width), F32),
             pltpu.VMEM((2 * width + 16, 2 * width), F32),
             pltpu.VMEM((64, 2 * width), F32),
-            pltpu.VMEM((2 * width, 2 * width), BF16),
-            pltpu.VMEM((2 * width, 2 * width), BF16),
-            pltpu.VMEM((2 * width, 2 * width), BF16),
-            pltpu.VMEM((1, 2 * width), F32),
-            pltpu.VMEM((1, 2 * width), F32),
             pltpu.VMEM(chunk, BF16),
             pltpu.VMEM(chunk, BF16),
             pltpu.VMEM(chunk, BF16),
             pltpu.VMEM(chunk, BF16),
         ],
-        embeddings, emb_cols, emb_next, w_left, w_right, consts, target_all, w_pair,
+        embeddings, emb_cols, emb_next, consts, target_all, w_pair, *ready,
     )
     sums = (sums.astype(F32) + swapped(sums_send, "tile", 1).astype(F32)).astype(BF16)
     sums = across(jnp.concatenate([sums, pred], axis=1), "tile", groups)

time: 84.4 us -> 86.6 us (1.026); the launches traced: 83.1 us -> 86.9 us
  Pallas kernels: 19.1 us -> 21.7 us
    ppermute x1, waiting for transfers between devices: 0.01 us -> 5.58 us  [per_device(): lax.ppermute(emb_cols[:edge], 'bin', [(k + 1, k) for k in range(bins - 1)])]
    all_to_all x1, waiting for transfers between devices: 5.33 us -> 0.01 us  [across(): lax.all_to_all(block, axis, 0, 0, axis_index_groups=groups, tiled=True)]
    pallas_call x5 -> x6, Pallas kernels: 19.1 us -> 21.7 us  [call(): pl.pallas_call(kernel, out_shape=outs, in_specs=space or [VMEM] * len(arg...]
    unnamed x19 -> x13, local copies, waits for them, and re-layouts: 3.13 us -> 2.47 us
  transfers between devices with their start and end apart: 7 -> 7, of which waited for: 3 -> 3; matrix products, arithmetic and copies ran while one was open for 1% -> 2% of each run, Pallas kernels for 1% -> 1%
where the time goes in v10:
time: 86.6 us; the launch traced here: 86.9 us
  blocking collectives  37.6 us (43%)
  Pallas kernels  21.7 us (25%)
  starting transfers between devices  15 us (17%)
  waiting for transfers between devices  8.33 us (10%)
  local copies, waits for them, and re-layouts  2.55 us (3%)
  other arithmetic  0.91 us (1%)
    all_to_all x3, blocking collectives, across(): lax.all_to_all(block, axis, 0, 0, axis_index_groups=groups, tiled=True)  37.6 us
    pallas_call x6, Pallas kernels, call(): pl.pallas_call(kernel, out_shape=outs, in_specs=space or [VMEM] * len(arg...  21.7 us
    ppermute x5, starting transfers between devices, swapped(): lax.ppermute(block, axis, [(i, i ^ bits) for i in range(lax.axis_size(axi...  7.95 us
    all_to_all x1, starting transfers between devices, across(): lax.all_to_all(block, axis, 0, 0, axis_index_groups=groups, tiled=True)  5.76 us
    ppermute x1, waiting for transfers between devices, per_device(): lax.ppermute(emb_cols[:edge], 'bin', [(k + 1, k) for k in range(bins - 1)])  5.58 us
    ppermute x5, waiting for transfers between devices, swapped(): lax.ppermute(block, axis, [(i, i ^ bits) for i in range(lax.axis_size(axi...  2.75 us
    unnamed x13, local copies, waits for them, and re-layouts  2.47 us
  transfers between devices with their start and end apart: 7, of which 3 were waited for; matrix products, arithmetic and copies ran while one was open for 2% of the time, Pallas kernels for 1%

profile of v10, /device:TPU:1, one launch (start us, length us, event | category | flops | bytes accessed | tf_op | source)
XLA Modules:
  0.0 86.9 jit_solution(15652345305491922322)
XLA Ops:
  0.6 0.0 copy-start
  0.6 1.5 %collective-permute-start.1 = (s32[3,1,6]{2,1,0:T(1,128)}, s32[3,1,6]{2,1,0:T(1,128)S(1)}, u32[]{:S(2)}, u32[]{:S(2)}) collective-permute-start(s32[3,1,6]{2,1,0:T(1,128)} %bitcast.21), channel_id=1, source_target_pairs={{0,1},{1,0},{2,3},{3,2},{4,5},{5,4},{6,7},{7,6},{8,9},{9,8},{10,11... | collective-permute-start | bytes 224 | tf_op jit(solution)/shard_map/ppermute | solution.py:409
  2.1 0.1 collective-permute-start.2
  2.2 0.1 pad.5.clone
  2.3 0.8 maximum_maximum_fusion.const_ref
  3.1 0.8 dynamic-slice_bitcast_fusion.1
  4.0 0.0 collective-permute-done.1.list_other
  4.0 0.0 collective-permute-done.2.target_other
  4.0 0.0 copy-start.3
  4.0 0.9 %copy-done.3 = bf16[1,1,6,128,128]{4,3,2,1,0:T(8,128)(2,1)S(1)} copy-done((bf16[1,1,6,128,128]{4,3,2,1,0:T(8,128)(2,1)S(1)}, bf16[1,1,6,128,128]{4,3,2,1,0:T(8,128)(2,1)}, u32[]{:S(2)}) %copy-start.3) | copy-done | bytes 196632
  4.9 0.7 copy-done.5
  5.6 1.1 %shard_map.152 = bf16[8,112,128]{2,1,0:T(8,128)(2,1)} custom-call(s32[3,1,6]{2,1,0:T(1,128)S(1)} %bitcast.22, s32[3,1,6]{2,1,0:T(1,128)S(1)} %collective-permute-done.1.list_other, bf16[6,128,128]{2,1,0:T(8,128)(2,1)S(1)} %bitcast.20, bf16[6,128,128]{2,1,0:T(8,128)(2,1)S(1)} %collective-permute-done.2.target_other), custom_call_target="tpu_custom_call" | custom-call | tf_op jit(solution)/shard_map/pallas_call | solution.py:398
  6.7 5.8 %all-to-all-start = ((bf16[8,112,128]{2,1,0:T(8,128)(2,1)}), bf16[8,112,128]{2,1,0:T(8,128)(2,1)S(1)}, u32[]{:S(2)}, u32[]{:S(2)}) async-start(bf16[8,112,128]{2,1,0:T(8,128)(2,1)} %shard_map.152), calls=%async_computation | async-start | bytes 458752 | tf_op jit(solution)/shard_map/all_to_all | solution.py:413
  12.4 1.3 %collective-permute-start = (bf16[32,512]{1,0:T(8,128)(2,1)S(1)}, bf16[32,512]{1,0:T(8,128)(2,1)S(1)}, u32[]{:S(2)}, u32[]{:S(2)}) collective-permute-start(bf16[32,512]{1,0:T(8,128)(2,1)S(1)} %slice_bitcast_fusion), channel_id=1, source_target_pairs={{16,0},{32,16},{48,32},{64,48},{80,64},{96,80},{112,96},{17,1},{33... | collective-permute-start | bytes 98312 | tf_op jit(solution)/shard_map/ppermute | solution.py:437
  13.7 5.6 %collective-permute-done.next_ref = bf16[32,512]{1,0:T(8,128)(2,1)S(1)} collective-permute-done((bf16[32,512]{1,0:T(8,128)(2,1)S(1)}, bf16[32,512]{1,0:T(8,128)(2,1)S(1)}, u32[]{:S(2)}, u32[]{:S(2)}) %collective-permute-start) | collective-permute-done | bytes 32800 | tf_op jit(solution)/shard_map/ppermute | solution.py:437
  19.3 0.0 copy-done
  19.3 0.0 copy-done.1
  19.3 0.5 shard_map.153
  19.8 0.0 all-to-all-done.target_ref
  19.8 18.4 %shard_map.154 = (bf16[8,144,128]{2,1,0:T(8,128)(2,1)S(1)}, bf16[8,144,128]{2,1,0:T(8,128)(2,1)S(1)}, bf16[8,96,128]{2,1,0:T(8,128)(2,1)S(1)}, f32[64,128]{1,0:T(8,128)S(1)}, bf16[32,128]{1,0:T(8,128)(2,1)S(1)}) custom-call(bf16[1024,512]{1,0:T(8,128)(2,1)S(1)} %copy-done, bf16[64,512]{1,0:T(8,128)(2,1)S(1)} %get-tuple-element.63.cols_ref, ...), custom_call_target="tpu_custom_call" | custom-call | tf_op jit(solution)/shard_map/pallas_call | solution.py:398
  38.3 2.1 %collective-permute-start.3 = (bf16[8,144,128]{2,1,0:T(8,128)(2,1)S(1)}, bf16[8,144,128]{2,1,0:T(8,128)(2,1)S(1)}, u32[]{:S(2)}, u32[]{:S(2)}) collective-permute-start(bf16[8,144,128]{2,1,0:T(8,128)(2,1)S(1)} %get-tuple-element.44), channel_id=1, source_target_pairs={{0,1},{1,0},{2,3},{3,2},{4,5},{5,4},{6,7},{7,6},{8,9},{9,8},{10,11... | collective-permute-start | bytes 884744 | tf_op jit(solution)/shard_map/ppermute | solution.py:409
  40.4 1.2 %collective-permute-done.3 = bf16[8,144,128]{2,1,0:T(8,128)(2,1)S(1)} collective-permute-done((bf16[8,144,128]{2,1,0:T(8,128)(2,1)S(1)}, bf16[8,144,128]{2,1,0:T(8,128)(2,1)S(1)}, u32[]{:S(2)}, u32[]{:S(2)}) %collective-permute-start.3) | collective-permute-done | bytes 294944 | tf_op jit(solution)/shard_map/ppermute | solution.py:409
  41.6 0.1 add_convert_fusion
  41.7 13.2 %all_to_all.20.sum_ref = bf16[8,240,128]{2,1,0:T(8,128)(2,1)S(1)} all-to-all(bf16[8,240,128]{2,1,0:T(8,128)(2,1)S(1)} %pad_maximum_fusion), channel_id=1, replica_groups={{0,2,4,6,8,10,12,14},{1,3,5,7,9,11,13,15},{16,18,20,22,24,26,28,30},{17..., dimensions={0} | all-to-all | bytes 983040 | tf_op jit(solution)/shard_map/all_to_all | solution.py:413
  54.9 0.1 shard_map.155
  55.0 15.0 %all_to_all.21.met_ref = bf16[8,112,128]{2,1,0:T(8,128)(2,1)S(1)} all-to-all(bf16[8,112,128]{2,1,0:T(8,128)(2,1)S(1)} %get-tuple-element.47), channel_id=1, replica_groups=mesh['bin'=8,'tile'=16] {'bin'}, dimensions={0} | all-to-all | bytes 458752 | tf_op jit(solution)/shard_map/all_to_all | solution.py:413
  70.0 9.5 %all_to_all.22.mine_ref = bf16[8,208,128]{2,1,0:T(8,128)(2,1)S(1)} all-to-all(bf16[8,208,128]{2,1,0:T(8,128)(2,1)S(1)} %shard_map.156), channel_id=1, replica_groups={{0,2,4,6,8,10,12,14},{1,3,5,7,9,11,13,15},{16,18,20,22,24,26,28,30},{17..., dimensions={0} | all-to-all | bytes 851968 | tf_op jit(solution)/shard_map/all_to_all | solution.py:413
  79.5 4.2 %collective-permute-start.4 = (bf16[8,208,128]{2,1,0:T(8,128)(2,1)S(1)}, bf16[8,208,128]{2,1,0:T(8,128)(2,1)S(1)}, u32[]{:S(2)}, u32[]{:S(2)}) collective-permute-start(bf16[8,208,128]{2,1,0:T(8,128)(2,1)S(1)} %all_to_all.22.mine_ref), channel_id=1, source_target_pairs={{0,1},{1,0},{2,3},{3,2},{4,5},{5,4},{6,7},{7,6},{8,9},{9,8},{10,11... | collective-permute-start | bytes 1277960 | tf_op jit(solution)/shard_map/ppermute | solution.py:409
  83.7 0.0 collective-permute-start.5
  83.7 1.5 %collective-permute-done.5.pred_other = bf16[8,48,128]{2,1,0:T(8,128)(2,1)S(1)} collective-permute-done((bf16[8,48,128]{2,1,0:T(8,128)(2,1)S(1)}, bf16[8,48,128]{2,1,0:T(8,128)(2,1)S(1)}, u32[]{:S(2)}, u32[]{:S(2)}) %collective-permute-start.5) | collective-permute-done | bytes 98336 | tf_op jit(solution)/shard_map/ppermute | solution.py:409
  85.2 0.0 collective-permute-done.4.other_ref
  85.2 1.6 %shard_map.157 = (bf16[6,128,128]{2,1,0:T(8,128)(2,1)}, bf16[1024,512]{1,0:T(8,128)(2,1)}, f32[512,128]{1,0:T(8,128)}, f32[512,128]{1,0:T(8,128)}, f32[5,128]{1,...) custom-call(bf16[8,208,128]{2,1,0:T(8,128)(2,1)S(1)} %all_to_all.22.mine_ref, ...), custom_call_target="tpu_custom_call" | custom-call | tf_op jit(solution)/shard_map/pallas_call | solution.py:398
  (9 shorter events, 0.1 us)
Async XLA Ops:
  0.6 18.7 %copy-start = (bf16[1024,512]{1,0:T(8,128)(2,1)S(1)}, bf16[1024,512]{1,0:T(8,128)(2,1)}, u32[]{:S(2)}) copy-start(bf16[1024,512]{1,0:T(8,128)(2,1)} %emb_ref.3) | copy-start | bytes 3145732
  0.6 3.3 %collective-permute-start.1 = (s32[3,1,6]{2,1,0:T(1,128)}, s32[3,1,6]{2,1,0:T(1,128)S(1)}, u32[]{:S(2)}, u32[]{:S(2)}) collective-permute-start(s32[3,1,6]{2,1,0:T(1,128)} %bitcast.21), channel_id=1, source_target_pairs={{0,1},{1,0},{2,3},{3,2},{4,5},{5,4},{6,7},{7,6},{8,9},{9,8},{10,11... | collective-permute-start | bytes 224 | tf_op jit(solution)/shard_map/ppermute | solution.py:409
  2.1 1.8 %collective-permute-start.2 = (bf16[6,128,128]{2,1,0:T(8,128)(2,1)}, bf16[6,128,128]{2,1,0:T(8,128)(2,1)S(1)}, u32[]{:S(2)}, u32[]{:S(2)}) collective-permute-start(bf16[6,128,128]{2,1,0:T(8,128)(2,1)} %bitcast.19), channel_id=1, source_target_pairs={{0,1},{1,0},{2,3},{3,2},{4,5},{5,4},{6,7},{7,6},{8,9},{9,8},{10,11... | collective-permute-start | bytes 589832 | tf_op jit(solution)/shard_map/ppermute | solution.py:409
  4.0 0.9 %copy-start.3 = (bf16[1,1,6,128,128]{4,3,2,1,0:T(8,128)(2,1)S(1)}, bf16[1,1,6,128,128]{4,3,2,1,0:T(8,128)(2,1)}, u32[]{:S(2)}) copy-start(bf16[1,1,6,128,128]{4,3,2,1,0:T(8,128)(2,1)} %param.17) | copy-start | bytes 589828
  4.9 0.7 copy-start.5
  6.7 12.7 %copy-start.1 = (bf16[512,128]{1,0:T(8,128)(2,1)S(1)}, bf16[512,128]{1,0:T(8,128)(2,1)}, u32[]{:S(2)}) copy-start(bf16[512,128]{1,0:T(8,128)(2,1)} %left_w_ref.3) | copy-start | bytes 393220
  6.7 12.7 %copy-start.2 = (bf16[512,128]{1,0:T(8,128)(2,1)S(1)}, bf16[512,128]{1,0:T(8,128)(2,1)}, u32[]{:S(2)}) copy-start(bf16[512,128]{1,0:T(8,128)(2,1)} %right_w_ref.3) | copy-start | bytes 393220
  6.7 13.1 %all-to-all-start = ((bf16[8,112,128]{2,1,0:T(8,128)(2,1)}), bf16[8,112,128]{2,1,0:T(8,128)(2,1)S(1)}, u32[]{:S(2)}, u32[]{:S(2)}) async-start(bf16[8,112,128]{2,1,0:T(8,128)(2,1)} %shard_map.152), calls=%async_computation | async-start | bytes 458752 | tf_op jit(solution)/shard_map/all_to_all | solution.py:413
  12.4 6.9 %copy-start.4 = (bf16[128,128]{1,0:T(8,128)(2,1)S(1)}, bf16[128,128]{1,0:T(8,128)(2,1)}, u32[]{:S(2)}) copy-start(bf16[128,128]{1,0:T(8,128)(2,1)} %w_ref.3) | copy-start | bytes 98308
  12.4 6.9 %collective-permute-start = (bf16[32,512]{1,0:T(8,128)(2,1)S(1)}, bf16[32,512]{1,0:T(8,128)(2,1)S(1)}, u32[]{:S(2)}, u32[]{:S(2)}) collective-permute-start(bf16[32,512]{1,0:T(8,128)(2,1)S(1)} %slice_bitcast_fusion), channel_id=1, source_target_pairs={{16,0},{32,16},{48,32},{64,48},{80,64},{96,80},{112,96},{17,1},{33... | collective-permute-start | bytes 98312 | tf_op jit(solution)/shard_map/ppermute | solution.py:437
  38.3 3.3 %collective-permute-start.3 = (bf16[8,144,128]{2,1,0:T(8,128)(2,1)S(1)}, bf16[8,144,128]{2,1,0:T(8,128)(2,1)S(1)}, u32[]{:S(2)}, u32[]{:S(2)}) collective-permute-start(bf16[8,144,128]{2,1,0:T(8,128)(2,1)S(1)} %get-tuple-element.44), channel_id=1, source_target_pairs={{0,1},{1,0},{2,3},{3,2},{4,5},{5,4},{6,7},{7,6},{8,9},{9,8},{10,11... | collective-permute-start | bytes 884744 | tf_op jit(solution)/shard_map/ppermute | solution.py:409
  79.5 5.8 %collective-permute-start.4 = (bf16[8,208,128]{2,1,0:T(8,128)(2,1)S(1)}, bf16[8,208,128]{2,1,0:T(8,128)(2,1)S(1)}, u32[]{:S(2)}, u32[]{:S(2)}) collective-permute-start(bf16[8,208,128]{2,1,0:T(8,128)(2,1)S(1)} %all_to_all.22.mine_ref), channel_id=1, source_target_pairs={{0,1},{1,0},{2,3},{3,2},{4,5},{5,4},{6,7},{7,6},{8,9},{9,8},{10,11... | collective-permute-start | bytes 1277960 | tf_op jit(solution)/shard_map/ppermute | solution.py:409
  83.7 1.5 %collective-permute-start.5 = (bf16[8,48,128]{2,1,0:T(8,128)(2,1)S(1)}, bf16[8,48,128]{2,1,0:T(8,128)(2,1)S(1)}, u32[]{:S(2)}, u32[]{:S(2)}) collective-permute-start(bf16[8,48,128]{2,1,0:T(8,128)(2,1)S(1)} %get-tuple-element.53), channel_id=1, source_target_pairs={{0,1},{1,0},{2,3},{3,2},{4,5},{5,4},{6,7},{7,6},{8,9},{9,8},{10,11... | collective-permute-start | bytes 294920 | tf_op jit(solution)/shard_map/ppermute | solution.py:409

commit v11 on v10

--- a/solution.py
+++ b/solution.py
@@ -50,16 +50,14 @@
 
 
 def ready_kernel(
-    emb_ref, next_ref, left_w_ref, right_w_ref, const_ref, w_ref,
+    emb_ref, left_w_ref, right_w_ref, const_ref, w_ref,
     left_ref, right_ref, w_two, out_two, back_two, lines_ref, full_ref,
 ):
     tile = place()
     width = w_ref.shape[0]
     pairs = width // 2
     blocks = emb_ref.shape[0] // width
-    edge = next_ref.shape[0]
-    own = right_ref.shape[0] - edge
-    step = own // blocks
+    step = right_ref.shape[0] // blocks
     w = w_ref[...].astype(F32)
     w_out = const_ref[6:7, :]
     b_pair = const_ref[5:6, :]
@@ -93,16 +91,14 @@
     for block in range(blocks):
         at = pl.multiple_of(block * width + tile * step, step)
         right_ref[block * step : (block + 1) * step, :] = full_ref[pl.ds(at, step), :]
-    right_next = jnp.dot(next_ref[...], right_w_ref[...], preferred_element_type=F32)
-    right_ref[own:, :] = right_next.astype(BF16).astype(F32)
 
 
 def pair_kernel(
-    emb_ref, cols_ref, next_ref, const_ref, target_ref, w_ref,
-    left_ref, right_all, w_two, out_two, back_two, lines_ref,
+    emb_ref, cols_ref, next_ref, right_w_ref, const_ref, target_ref, w_ref,
+    left_ref, right_ref, w_two, out_two, back_two, lines_ref,
     keep_ref, send_ref, pred_ref, col_ref, edge_ref,
     table, lists, list_sem, list_all, target_all, pred_all, row_all, col_all,
-    outer_all, bias_all, first_0, first_1, slope_0, slope_1,
+    outer_all, bias_all, right_all, first_0, first_1, slope_0, slope_1,
 ):
     tile = place()
     width = w_ref.shape[0]
@@ -129,6 +125,9 @@
     w_out = const_ref[6:7, :]
     b_pair = const_ref[5:6, :]
     own = blocks * step
+    right_all[:own, :] = right_ref[...]
+    right_next = jnp.dot(next_ref[...], right_w_ref[...], preferred_element_type=F32)
+    right_all[own:, :] = right_next.astype(BF16).astype(F32)
     rows = [target_ref[chip, : 2 * slots * step, :].astype(F32) for chip in range(chips)]
     rows = jnp.concatenate(rows, axis=0)
     for group in range(groups):
@@ -455,14 +454,14 @@
         ready_kernel,
         (
             shape(rows // 2, 2 * width),
-            shape(part + edge, width),
+            shape(part, width),
             double,
             double,
             double,
             shape(8, 2 * width),
         ),
         [pltpu.VMEM((rows, width), F32)],
-        embeddings, emb_next, w_left, w_right, consts, w_pair,
+        embeddings, w_left, w_right, consts, w_pair,
     )
     half = shape(chips, width + 16, width, dtype=BF16)
     sums, sums_send, pred, col, col_edge = call(
@@ -485,12 +484,13 @@
             pltpu.VMEM((8 * (part + edge), 2 * width), F32),
             pltpu.VMEM((2 * width + 16, 2 * width), F32),
             pltpu.VMEM((64, 2 * width), F32),
+            pltpu.VMEM((part + edge, width), F32),
             pltpu.VMEM(chunk, BF16),
             pltpu.VMEM(chunk, BF16),
             pltpu.VMEM(chunk, BF16),
             pltpu.VMEM(chunk, BF16),
         ],
-        embeddings, emb_cols, emb_next, consts, target_all, w_pair, *ready,
+        embeddings, emb_cols, emb_next, w_right, consts, target_all, w_pair, *ready,
     )
     sums = (sums.astype(F32) + swapped(sums_send, "tile", 1).astype(F32)).astype(BF16)
     sums = across(jnp.concatenate([sums, pred], axis=1), "tile", groups)

time: 86.6 us -> 86.1 us (level)
  no operation moved by 1% of the time
where the time goes in v11:
time: 86.1 us; the launch traced here: 86.4 us
  blocking collectives  37.6 us (44%)
  Pallas kernels  21.7 us (25%)
  starting transfers between devices  15 us (17%)
  waiting for transfers between devices  7.84 us (9%)
  local copies, waits for them, and re-layouts  2.55 us (3%)
  other arithmetic  0.9 us (1%)
    all_to_all x3, blocking collectives, across(): lax.all_to_all(block, axis, 0, 0, axis_index_groups=groups, tiled=True)  37.6 us
    pallas_call x6, Pallas kernels, call(): pl.pallas_call(kernel, out_shape=outs, in_specs=space or [VMEM] * len(arg...  21.7 us
    ppermute x5, starting transfers between devices, swapped(): lax.ppermute(block, axis, [(i, i ^ bits) for i in range(lax.axis_size(axi...  7.95 us
    all_to_all x1, starting transfers between devices, across(): lax.all_to_all(block, axis, 0, 0, axis_index_groups=groups, tiled=True)  5.76 us
    ppermute x1, waiting for transfers between devices, per_device(): lax.ppermute(emb_cols[:edge], 'bin', [(k + 1, k) for k in range(bins - 1)])  5.08 us
    ppermute x5, waiting for transfers between devices, swapped(): lax.ppermute(block, axis, [(i, i ^ bits) for i in range(lax.axis_size(axi...  2.75 us
    unnamed x13, local copies, waits for them, and re-layouts  2.47 us
  transfers between devices with their start and end apart: 7, of which 3 were waited for; matrix products, arithmetic and copies ran while one was open for 2% of the time, Pallas kernels for 1%

profile of v11, /device:TPU:1, one launch (start us, length us, event | category | flops | bytes accessed | tf_op | source)
XLA Modules:
  0.0 86.4 jit_solution(13424072677781904216)
XLA Ops:
  0.6 0.0 copy-start
  0.6 1.5 %collective-permute-start.1 = (s32[3,1,6]{2,1,0:T(1,128)}, s32[3,1,6]{2,1,0:T(1,128)S(1)}, u32[]{:S(2)}, u32[]{:S(2)}) collective-permute-start(s32[3,1,6]{2,1,0:T(1,128)} %bitcast.21), channel_id=1, source_target_pairs={{0,1},{1,0},{2,3},{3,2},{4,5},{5,4},{6,7},{7,6},{8,9},{9,8},{10,11... | collective-permute-start | bytes 224 | tf_op jit(solution)/shard_map/ppermute | solution.py:408
  2.1 0.1 collective-permute-start.2
  2.2 0.1 pad.5.clone
  2.3 0.8 maximum_maximum_fusion.const_ref
  3.1 0.8 dynamic-slice_bitcast_fusion.1
  4.0 0.0 collective-permute-done.1.list_other
  4.0 0.0 collective-permute-done.2.target_other
  4.0 0.0 copy-start.3
  4.0 0.9 %copy-done.3 = bf16[1,1,6,128,128]{4,3,2,1,0:T(8,128)(2,1)S(1)} copy-done((bf16[1,1,6,128,128]{4,3,2,1,0:T(8,128)(2,1)S(1)}, bf16[1,1,6,128,128]{4,3,2,1,0:T(8,128)(2,1)}, u32[]{:S(2)}) %copy-start.3) | copy-done | bytes 196632
  4.9 0.7 copy-done.5
  5.6 1.1 %shard_map.152 = bf16[8,112,128]{2,1,0:T(8,128)(2,1)} custom-call(s32[3,1,6]{2,1,0:T(1,128)S(1)} %bitcast.22, s32[3,1,6]{2,1,0:T(1,128)S(1)} %collective-permute-done.1.list_other, bf16[6,128,128]{2,1,0:T(8,128)(2,1)S(1)} %bitcast.20, bf16[6,128,128]{2,1,0:T(8,128)(2,1)S(1)} %collective-permute-done.2.target_other), custom_call_target="tpu_custom_call" | custom-call | tf_op jit(solution)/shard_map/pallas_call | solution.py:397
  6.7 5.8 %all-to-all-start = ((bf16[8,112,128]{2,1,0:T(8,128)(2,1)}), bf16[8,112,128]{2,1,0:T(8,128)(2,1)S(1)}, u32[]{:S(2)}, u32[]{:S(2)}) async-start(bf16[8,112,128]{2,1,0:T(8,128)(2,1)} %shard_map.152), calls=%async_computation | async-start | bytes 458752 | tf_op jit(solution)/shard_map/all_to_all | solution.py:412
  12.4 1.3 %collective-permute-start = (bf16[32,512]{1,0:T(8,128)(2,1)S(1)}, bf16[32,512]{1,0:T(8,128)(2,1)S(1)}, u32[]{:S(2)}, u32[]{:S(2)}) collective-permute-start(bf16[32,512]{1,0:T(8,128)(2,1)S(1)} %slice_bitcast_fusion), channel_id=1, source_target_pairs={{16,0},{32,16},{48,32},{64,48},{80,64},{96,80},{112,96},{17,1},{33... | collective-permute-start | bytes 98312 | tf_op jit(solution)/shard_map/ppermute | solution.py:436
  13.7 0.0 copy-done
  13.8 0.0 copy-done.1
  13.8 0.4 shard_map.153
  14.2 5.1 %collective-permute-done.next_ref = bf16[32,512]{1,0:T(8,128)(2,1)S(1)} collective-permute-done((bf16[32,512]{1,0:T(8,128)(2,1)S(1)}, bf16[32,512]{1,0:T(8,128)(2,1)S(1)}, u32[]{:S(2)}, u32[]{:S(2)}) %collective-permute-start) | collective-permute-done | bytes 32800 | tf_op jit(solution)/shard_map/ppermute | solution.py:436
  19.3 0.0 all-to-all-done.target_ref
  19.3 18.4 %shard_map.154 = (bf16[8,144,128]{2,1,0:T(8,128)(2,1)S(1)}, bf16[8,144,128]{2,1,0:T(8,128)(2,1)S(1)}, bf16[8,96,128]{2,1,0:T(8,128)(2,1)S(1)}, f32[64,128]{1,0:T(8,128)S(1)}, bf16[32,128]{1,0:T(8,128)(2,1)S(1)}) custom-call(bf16[1024,512]{1,0:T(8,128)(2,1)S(1)} %copy-done, bf16[64,512]{1,0:T(8,128)(2,1)S(1)} %get-tuple-element.63.cols_ref, ...), custom_call_target="tpu_custom_call" | custom-call | tf_op jit(solution)/shard_map/pallas_call | solution.py:397
  37.8 2.1 %collective-permute-start.3 = (bf16[8,144,128]{2,1,0:T(8,128)(2,1)S(1)}, bf16[8,144,128]{2,1,0:T(8,128)(2,1)S(1)}, u32[]{:S(2)}, u32[]{:S(2)}) collective-permute-start(bf16[8,144,128]{2,1,0:T(8,128)(2,1)S(1)} %get-tuple-element.44), channel_id=1, source_target_pairs={{0,1},{1,0},{2,3},{3,2},{4,5},{5,4},{6,7},{7,6},{8,9},{9,8},{10,11... | collective-permute-start | bytes 884744 | tf_op jit(solution)/shard_map/ppermute | solution.py:408
  39.9 1.2 %collective-permute-done.3 = bf16[8,144,128]{2,1,0:T(8,128)(2,1)S(1)} collective-permute-done((bf16[8,144,128]{2,1,0:T(8,128)(2,1)S(1)}, bf16[8,144,128]{2,1,0:T(8,128)(2,1)S(1)}, u32[]{:S(2)}, u32[]{:S(2)}) %collective-permute-start.3) | collective-permute-done | bytes 294944 | tf_op jit(solution)/shard_map/ppermute | solution.py:408
  41.1 0.1 add_convert_fusion
  41.3 13.2 %all_to_all.20.sum_ref = bf16[8,240,128]{2,1,0:T(8,128)(2,1)S(1)} all-to-all(bf16[8,240,128]{2,1,0:T(8,128)(2,1)S(1)} %pad_maximum_fusion), channel_id=1, replica_groups={{0,2,4,6,8,10,12,14},{1,3,5,7,9,11,13,15},{16,18,20,22,24,26,28,30},{17..., dimensions={0} | all-to-all | bytes 983040 | tf_op jit(solution)/shard_map/all_to_all | solution.py:412
  54.4 0.1 shard_map.155
  54.5 15.0 %all_to_all.21.met_ref = bf16[8,112,128]{2,1,0:T(8,128)(2,1)S(1)} all-to-all(bf16[8,112,128]{2,1,0:T(8,128)(2,1)S(1)} %get-tuple-element.47), channel_id=1, replica_groups=mesh['bin'=8,'tile'=16] {'bin'}, dimensions={0} | all-to-all | bytes 458752 | tf_op jit(solution)/shard_map/all_to_all | solution.py:412
  69.5 9.5 %all_to_all.22.mine_ref = bf16[8,208,128]{2,1,0:T(8,128)(2,1)S(1)} all-to-all(bf16[8,208,128]{2,1,0:T(8,128)(2,1)S(1)} %shard_map.156), channel_id=1, replica_groups={{0,2,4,6,8,10,12,14},{1,3,5,7,9,11,13,15},{16,18,20,22,24,26,28,30},{17..., dimensions={0} | all-to-all | bytes 851968 | tf_op jit(solution)/shard_map/all_to_all | solution.py:412
  79.0 4.2 %collective-permute-start.4 = (bf16[8,208,128]{2,1,0:T(8,128)(2,1)S(1)}, bf16[8,208,128]{2,1,0:T(8,128)(2,1)S(1)}, u32[]{:S(2)}, u32[]{:S(2)}) collective-permute-start(bf16[8,208,128]{2,1,0:T(8,128)(2,1)S(1)} %all_to_all.22.mine_ref), channel_id=1, source_target_pairs={{0,1},{1,0},{2,3},{3,2},{4,5},{5,4},{6,7},{7,6},{8,9},{9,8},{10,11... | collective-permute-start | bytes 1277960 | tf_op jit(solution)/shard_map/ppermute | solution.py:408
  83.2 0.0 collective-permute-start.5
  83.2 1.5 %collective-permute-done.5.pred_other = bf16[8,48,128]{2,1,0:T(8,128)(2,1)S(1)} collective-permute-done((bf16[8,48,128]{2,1,0:T(8,128)(2,1)S(1)}, bf16[8,48,128]{2,1,0:T(8,128)(2,1)S(1)}, u32[]{:S(2)}, u32[]{:S(2)}) %collective-permute-start.5) | collective-permute-done | bytes 98336 | tf_op jit(solution)/shard_map/ppermute | solution.py:408
  84.7 0.0 collective-permute-done.4.other_ref
  84.7 1.6 %shard_map.157 = (bf16[6,128,128]{2,1,0:T(8,128)(2,1)}, bf16[1024,512]{1,0:T(8,128)(2,1)}, f32[512,128]{1,0:T(8,128)}, f32[512,128]{1,0:T(8,128)}, f32[5,128]{1,...) custom-call(bf16[8,208,128]{2,1,0:T(8,128)(2,1)S(1)} %all_to_all.22.mine_ref, ...), custom_call_target="tpu_custom_call" | custom-call | tf_op jit(solution)/shard_map/pallas_call | solution.py:397
  (9 shorter events, 0.1 us)
Async XLA Ops:
  0.6 13.1 %copy-start = (bf16[1024,512]{1,0:T(8,128)(2,1)S(1)}, bf16[1024,512]{1,0:T(8,128)(2,1)}, u32[]{:S(2)}) copy-start(bf16[1024,512]{1,0:T(8,128)(2,1)} %emb_ref.3) | copy-start | bytes 3145732
  0.6 3.3 %collective-permute-start.1 = (s32[3,1,6]{2,1,0:T(1,128)}, s32[3,1,6]{2,1,0:T(1,128)S(1)}, u32[]{:S(2)}, u32[]{:S(2)}) collective-permute-start(s32[3,1,6]{2,1,0:T(1,128)} %bitcast.21), channel_id=1, source_target_pairs={{0,1},{1,0},{2,3},{3,2},{4,5},{5,4},{6,7},{7,6},{8,9},{9,8},{10,11... | collective-permute-start | bytes 224 | tf_op jit(solution)/shard_map/ppermute | solution.py:408
  2.1 1.8 %collective-permute-start.2 = (bf16[6,128,128]{2,1,0:T(8,128)(2,1)}, bf16[6,128,128]{2,1,0:T(8,128)(2,1)S(1)}, u32[]{:S(2)}, u32[]{:S(2)}) collective-permute-start(bf16[6,128,128]{2,1,0:T(8,128)(2,1)} %bitcast.19), channel_id=1, source_target_pairs={{0,1},{1,0},{2,3},{3,2},{4,5},{5,4},{6,7},{7,6},{8,9},{9,8},{10,11... | collective-permute-start | bytes 589832 | tf_op jit(solution)/shard_map/ppermute | solution.py:408
  4.0 0.9 %copy-start.3 = (bf16[1,1,6,128,128]{4,3,2,1,0:T(8,128)(2,1)S(1)}, bf16[1,1,6,128,128]{4,3,2,1,0:T(8,128)(2,1)}, u32[]{:S(2)}) copy-start(bf16[1,1,6,128,128]{4,3,2,1,0:T(8,128)(2,1)} %param.17) | copy-start | bytes 589828
  4.9 0.7 copy-start.5
  6.7 7.1 %copy-start.1 = (bf16[512,128]{1,0:T(8,128)(2,1)S(1)}, bf16[512,128]{1,0:T(8,128)(2,1)}, u32[]{:S(2)}) copy-start(bf16[512,128]{1,0:T(8,128)(2,1)} %right_w_ref.5) | copy-start | bytes 393220
  6.7 7.1 %copy-start.2 = (bf16[512,128]{1,0:T(8,128)(2,1)S(1)}, bf16[512,128]{1,0:T(8,128)(2,1)}, u32[]{:S(2)}) copy-start(bf16[512,128]{1,0:T(8,128)(2,1)} %left_w_ref.3) | copy-start | bytes 393220
  6.7 12.7 %all-to-all-start = ((bf16[8,112,128]{2,1,0:T(8,128)(2,1)}), bf16[8,112,128]{2,1,0:T(8,128)(2,1)S(1)}, u32[]{:S(2)}, u32[]{:S(2)}) async-start(bf16[8,112,128]{2,1,0:T(8,128)(2,1)} %shard_map.152), calls=%async_computation | async-start | bytes 458752 | tf_op jit(solution)/shard_map/all_to_all | solution.py:412
  12.4 1.3 %copy-start.4 = (bf16[128,128]{1,0:T(8,128)(2,1)S(1)}, bf16[128,128]{1,0:T(8,128)(2,1)}, u32[]{:S(2)}) copy-start(bf16[128,128]{1,0:T(8,128)(2,1)} %w_ref.3) | copy-start | bytes 98308
  12.4 6.9 %collective-permute-start = (bf16[32,512]{1,0:T(8,128)(2,1)S(1)}, bf16[32,512]{1,0:T(8,128)(2,1)S(1)}, u32[]{:S(2)}, u32[]{:S(2)}) collective-permute-start(bf16[32,512]{1,0:T(8,128)(2,1)S(1)} %slice_bitcast_fusion), channel_id=1, source_target_pairs={{16,0},{32,16},{48,32},{64,48},{80,64},{96,80},{112,96},{17,1},{33... | collective-permute-start | bytes 98312 | tf_op jit(solution)/shard_map/ppermute | solution.py:436
  37.8 3.4 %collective-permute-start.3 = (bf16[8,144,128]{2,1,0:T(8,128)(2,1)S(1)}, bf16[8,144,128]{2,1,0:T(8,128)(2,1)S(1)}, u32[]{:S(2)}, u32[]{:S(2)}) collective-permute-start(bf16[8,144,128]{2,1,0:T(8,128)(2,1)S(1)} %get-tuple-element.44), channel_id=1, source_target_pairs={{0,1},{1,0},{2,3},{3,2},{4,5},{5,4},{6,7},{7,6},{8,9},{9,8},{10,11... | collective-permute-start | bytes 884744 | tf_op jit(solution)/shard_map/ppermute | solution.py:408
  79.0 5.8 %collective-permute-start.4 = (bf16[8,208,128]{2,1,0:T(8,128)(2,1)S(1)}, bf16[8,208,128]{2,1,0:T(8,128)(2,1)S(1)}, u32[]{:S(2)}, u32[]{:S(2)}) collective-permute-start(bf16[8,208,128]{2,1,0:T(8,128)(2,1)S(1)} %all_to_all.22.mine_ref), channel_id=1, source_target_pairs={{0,1},{1,0},{2,3},{3,2},{4,5},{5,4},{6,7},{7,6},{8,9},{9,8},{10,11... | collective-permute-start | bytes 1277960 | tf_op jit(solution)/shard_map/ppermute | solution.py:408
  83.2 1.5 %collective-permute-start.5 = (bf16[8,48,128]{2,1,0:T(8,128)(2,1)S(1)}, bf16[8,48,128]{2,1,0:T(8,128)(2,1)S(1)}, u32[]{:S(2)}, u32[]{:S(2)}) collective-permute-start(bf16[8,48,128]{2,1,0:T(8,128)(2,1)S(1)} %get-tuple-element.53), channel_id=1, source_target_pairs={{0,1},{1,0},{2,3},{3,2},{4,5},{5,4},{6,7},{7,6},{8,9},{9,8},{10,11... | collective-permute-start | bytes 294920 | tf_op jit(solution)/shard_map/ppermute | solution.py:408

commit v12 on v11

--- a/solution.py
+++ b/solution.py
@@ -393,14 +393,15 @@
     return jax.ShapeDtypeStruct(dims, dtype)
 
 
-def call(kernel, outs, scratch, *args, space=None, out_space=VMEM, limit=32):
+def call(kernel, outs, scratch, *args, out_space=VMEM, cost=None):
     return pl.pallas_call(
         kernel,
         out_shape=outs,
-        in_specs=space or [VMEM] * len(args),
+        in_specs=[VMEM] * len(args),
         out_specs=(out_space,) * len(outs),
         scratch_shapes=scratch,
-        compiler_params=pltpu.CompilerParams(vmem_limit_bytes=limit * 1024 * 1024),
+        cost_estimate=cost,
+        compiler_params=pltpu.CompilerParams(vmem_limit_bytes=32 * 1024 * 1024),
     )(*args)
 
 
@@ -462,6 +463,7 @@
         ),
         [pltpu.VMEM((rows, width), F32)],
         embeddings, w_left, w_right, consts, w_pair,
+        cost=pl.CostEstimate(flops=1, bytes_accessed=1, transcendentals=0),
     )
     half = shape(chips, width + 16, width, dtype=BF16)
     sums, sums_send, pred, col, col_edge = call(

time: 86.1 us -> 86.1 us (level); the launches traced: 86.4 us -> 84.8 us
  Pallas kernels: 21.7 us -> 20.1 us
    pallas_call x6, Pallas kernels: 21.7 us -> 20.1 us  [call(): pl.pallas_call(kernel, out_shape=outs, in_specs=[VMEM] * len(args), out_s...]
where the time goes in v12:
time: 86.1 us; the launch traced here: 84.8 us
  blocking collectives  37.6 us (44%)
  Pallas kernels  20.1 us (23%)
  starting transfers between devices  15 us (17%)
  waiting for transfers between devices  7.84 us (9%)
  local copies, waits for them, and re-layouts  2.55 us (3%)
  other arithmetic  0.9 us (1%)
    all_to_all x3, blocking collectives, across(): lax.all_to_all(block, axis, 0, 0, axis_index_groups=groups, tiled=True)  37.6 us
    pallas_call x6, Pallas kernels, call(): pl.pallas_call(kernel, out_shape=outs, in_specs=[VMEM] * len(args), out_s...  20.1 us
    ppermute x5, starting transfers between devices, swapped(): lax.ppermute(block, axis, [(i, i ^ bits) for i in range(lax.axis_size(axi...  7.95 us
    all_to_all x1, starting transfers between devices, across(): lax.all_to_all(block, axis, 0, 0, axis_index_groups=groups, tiled=True)  5.76 us
    ppermute x1, waiting for transfers between devices, per_device(): lax.ppermute(emb_cols[:edge], 'bin', [(k + 1, k) for k in range(bins - 1)])  5.08 us
    ppermute x5, waiting for transfers between devices, swapped(): lax.ppermute(block, axis, [(i, i ^ bits) for i in range(lax.axis_size(axi...  2.75 us
    unnamed x13, local copies, waits for them, and re-layouts  2.47 us
  transfers between devices with their start and end apart: 7, of which 3 were waited for; matrix products, arithmetic and copies ran while one was open for 2% of the time, Pallas kernels for 1%

profile of v12, /device:TPU:1, one launch (start us, length us, event | category | flops | bytes accessed | tf_op | source)
XLA Modules:
  0.0 84.8 jit_solution(13424072677781904216)
XLA Ops:
  0.6 0.0 copy-start
  0.6 1.5 %collective-permute-start.1 = (s32[3,1,6]{2,1,0:T(1,128)}, s32[3,1,6]{2,1,0:T(1,128)S(1)}, u32[]{:S(2)}, u32[]{:S(2)}) collective-permute-start(s32[3,1,6]{2,1,0:T(1,128)} %bitcast.21), channel_id=1, source_target_pairs={{0,1},{1,0},{2,3},{3,2},{4,5},{5,4},{6,7},{7,6},{8,9},{9,8},{10,11... | collective-permute-start | bytes 224 | tf_op jit(solution)/shard_map/ppermute | solution.py:409
  2.1 0.1 collective-permute-start.2
  2.2 0.1 pad.5.clone
  2.3 0.8 maximum_maximum_fusion.const_ref
  3.1 0.8 dynamic-slice_bitcast_fusion.1
  4.0 0.0 collective-permute-done.1.list_other
  4.0 0.0 collective-permute-done.2.target_other
  4.0 0.0 copy-start.3
  4.0 0.9 %copy-done.3 = bf16[1,1,6,128,128]{4,3,2,1,0:T(8,128)(2,1)S(1)} copy-done((bf16[1,1,6,128,128]{4,3,2,1,0:T(8,128)(2,1)S(1)}, bf16[1,1,6,128,128]{4,3,2,1,0:T(8,128)(2,1)}, u32[]{:S(2)}) %copy-start.3) | copy-done | bytes 196632
  4.9 0.7 copy-done.5
  5.6 1.1 %shard_map.152 = bf16[8,112,128]{2,1,0:T(8,128)(2,1)} custom-call(s32[3,1,6]{2,1,0:T(1,128)S(1)} %bitcast.22, s32[3,1,6]{2,1,0:T(1,128)S(1)} %collective-permute-done.1.list_other, bf16[6,128,128]{2,1,0:T(8,128)(2,1)S(1)} %bitcast.20, bf16[6,128,128]{2,1,0:T(8,128)(2,1)S(1)} %collective-permute-done.2.target_other), custom_call_target="tpu_custom_call" | custom-call | tf_op jit(solution)/shard_map/pallas_call | solution.py:397
  6.7 5.8 %all-to-all-start = ((bf16[8,112,128]{2,1,0:T(8,128)(2,1)}), bf16[8,112,128]{2,1,0:T(8,128)(2,1)S(1)}, u32[]{:S(2)}, u32[]{:S(2)}) async-start(bf16[8,112,128]{2,1,0:T(8,128)(2,1)} %shard_map.152), calls=%async_computation | async-start | bytes 458752 | tf_op jit(solution)/shard_map/all_to_all | solution.py:413
  12.4 1.3 %collective-permute-start = (bf16[32,512]{1,0:T(8,128)(2,1)S(1)}, bf16[32,512]{1,0:T(8,128)(2,1)S(1)}, u32[]{:S(2)}, u32[]{:S(2)}) collective-permute-start(bf16[32,512]{1,0:T(8,128)(2,1)S(1)} %slice_bitcast_fusion), channel_id=1, source_target_pairs={{16,0},{32,16},{48,32},{64,48},{80,64},{96,80},{112,96},{17,1},{33... | collective-permute-start | bytes 98312 | tf_op jit(solution)/shard_map/ppermute | solution.py:437
  13.7 0.0 copy-done
  13.8 0.0 copy-done.1
  13.8 0.4 shard_map.153
  14.2 5.1 %collective-permute-done.next_ref = bf16[32,512]{1,0:T(8,128)(2,1)S(1)} collective-permute-done((bf16[32,512]{1,0:T(8,128)(2,1)S(1)}, bf16[32,512]{1,0:T(8,128)(2,1)S(1)}, u32[]{:S(2)}, u32[]{:S(2)}) %collective-permute-start) | collective-permute-done | bytes 32800 | tf_op jit(solution)/shard_map/ppermute | solution.py:437
  19.3 0.0 all-to-all-done.target_ref
  19.3 16.9 %shard_map.154 = (bf16[8,144,128]{2,1,0:T(8,128)(2,1)S(1)}, bf16[8,144,128]{2,1,0:T(8,128)(2,1)S(1)}, bf16[8,96,128]{2,1,0:T(8,128)(2,1)S(1)}, f32[64,128]{1,0:T(8,128)S(1)}, bf16[32,128]{1,0:T(8,128)(2,1)S(1)}) custom-call(bf16[1024,512]{1,0:T(8,128)(2,1)S(1)} %copy-done, bf16[64,512]{1,0:T(8,128)(2,1)S(1)} %get-tuple-element.63.cols_ref, ...), custom_call_target="tpu_custom_call" | custom-call | tf_op jit(solution)/shard_map/pallas_call | solution.py:397
  36.2 2.1 %collective-permute-start.3 = (bf16[8,144,128]{2,1,0:T(8,128)(2,1)S(1)}, bf16[8,144,128]{2,1,0:T(8,128)(2,1)S(1)}, u32[]{:S(2)}, u32[]{:S(2)}) collective-permute-start(bf16[8,144,128]{2,1,0:T(8,128)(2,1)S(1)} %get-tuple-element.44), channel_id=1, source_target_pairs={{0,1},{1,0},{2,3},{3,2},{4,5},{5,4},{6,7},{7,6},{8,9},{9,8},{10,11... | collective-permute-start | bytes 884744 | tf_op jit(solution)/shard_map/ppermute | solution.py:409
  38.3 1.2 %collective-permute-done.3 = bf16[8,144,128]{2,1,0:T(8,128)(2,1)S(1)} collective-permute-done((bf16[8,144,128]{2,1,0:T(8,128)(2,1)S(1)}, bf16[8,144,128]{2,1,0:T(8,128)(2,1)S(1)}, u32[]{:S(2)}, u32[]{:S(2)}) %collective-permute-start.3) | collective-permute-done | bytes 294944 | tf_op jit(solution)/shard_map/ppermute | solution.py:409
  39.5 0.1 add_convert_fusion
  39.7 13.2 %all_to_all.20.sum_ref = bf16[8,240,128]{2,1,0:T(8,128)(2,1)S(1)} all-to-all(bf16[8,240,128]{2,1,0:T(8,128)(2,1)S(1)} %pad_maximum_fusion), channel_id=1, replica_groups={{0,2,4,6,8,10,12,14},{1,3,5,7,9,11,13,15},{16,18,20,22,24,26,28,30},{17..., dimensions={0} | all-to-all | bytes 983040 | tf_op jit(solution)/shard_map/all_to_all | solution.py:413
  52.8 0.1 shard_map.155
  52.9 15.0 %all_to_all.21.met_ref = bf16[8,112,128]{2,1,0:T(8,128)(2,1)S(1)} all-to-all(bf16[8,112,128]{2,1,0:T(8,128)(2,1)S(1)} %get-tuple-element.47), channel_id=1, replica_groups=mesh['bin'=8,'tile'=16] {'bin'}, dimensions={0} | all-to-all | bytes 458752 | tf_op jit(solution)/shard_map/all_to_all | solution.py:413
  68.0 9.5 %all_to_all.22.mine_ref = bf16[8,208,128]{2,1,0:T(8,128)(2,1)S(1)} all-to-all(bf16[8,208,128]{2,1,0:T(8,128)(2,1)S(1)} %shard_map.156), channel_id=1, replica_groups={{0,2,4,6,8,10,12,14},{1,3,5,7,9,11,13,15},{16,18,20,22,24,26,28,30},{17..., dimensions={0} | all-to-all | bytes 851968 | tf_op jit(solution)/shard_map/all_to_all | solution.py:413
  77.4 4.2 %collective-permute-start.4 = (bf16[8,208,128]{2,1,0:T(8,128)(2,1)S(1)}, bf16[8,208,128]{2,1,0:T(8,128)(2,1)S(1)}, u32[]{:S(2)}, u32[]{:S(2)}) collective-permute-start(bf16[8,208,128]{2,1,0:T(8,128)(2,1)S(1)} %all_to_all.22.mine_ref), channel_id=1, source_target_pairs={{0,1},{1,0},{2,3},{3,2},{4,5},{5,4},{6,7},{7,6},{8,9},{9,8},{10,11... | collective-permute-start | bytes 1277960 | tf_op jit(solution)/shard_map/ppermute | solution.py:409
  81.6 0.0 collective-permute-start.5
  81.6 1.5 %collective-permute-done.5.pred_other = bf16[8,48,128]{2,1,0:T(8,128)(2,1)S(1)} collective-permute-done((bf16[8,48,128]{2,1,0:T(8,128)(2,1)S(1)}, bf16[8,48,128]{2,1,0:T(8,128)(2,1)S(1)}, u32[]{:S(2)}, u32[]{:S(2)}) %collective-permute-start.5) | collective-permute-done | bytes 98336 | tf_op jit(solution)/shard_map/ppermute | solution.py:409
  83.2 0.0 collective-permute-done.4.other_ref
  83.2 1.6 %shard_map.157 = (bf16[6,128,128]{2,1,0:T(8,128)(2,1)}, bf16[1024,512]{1,0:T(8,128)(2,1)}, f32[512,128]{1,0:T(8,128)}, f32[512,128]{1,0:T(8,128)}, f32[5,128]{1,...) custom-call(bf16[8,208,128]{2,1,0:T(8,128)(2,1)S(1)} %all_to_all.22.mine_ref, ...), custom_call_target="tpu_custom_call" | custom-call | tf_op jit(solution)/shard_map/pallas_call | solution.py:397
  (9 shorter events, 0.1 us)
Async XLA Ops:
  0.6 13.1 %copy-start = (bf16[1024,512]{1,0:T(8,128)(2,1)S(1)}, bf16[1024,512]{1,0:T(8,128)(2,1)}, u32[]{:S(2)}) copy-start(bf16[1024,512]{1,0:T(8,128)(2,1)} %emb_ref.3) | copy-start | bytes 3145732
  0.6 3.3 %collective-permute-start.1 = (s32[3,1,6]{2,1,0:T(1,128)}, s32[3,1,6]{2,1,0:T(1,128)S(1)}, u32[]{:S(2)}, u32[]{:S(2)}) collective-permute-start(s32[3,1,6]{2,1,0:T(1,128)} %bitcast.21), channel_id=1, source_target_pairs={{0,1},{1,0},{2,3},{3,2},{4,5},{5,4},{6,7},{7,6},{8,9},{9,8},{10,11... | collective-permute-start | bytes 224 | tf_op jit(solution)/shard_map/ppermute | solution.py:409
  2.1 1.8 %collective-permute-start.2 = (bf16[6,128,128]{2,1,0:T(8,128)(2,1)}, bf16[6,128,128]{2,1,0:T(8,128)(2,1)S(1)}, u32[]{:S(2)}, u32[]{:S(2)}) collective-permute-start(bf16[6,128,128]{2,1,0:T(8,128)(2,1)} %bitcast.19), channel_id=1, source_target_pairs={{0,1},{1,0},{2,3},{3,2},{4,5},{5,4},{6,7},{7,6},{8,9},{9,8},{10,11... | collective-permute-start | bytes 589832 | tf_op jit(solution)/shard_map/ppermute | solution.py:409
  4.0 0.9 %copy-start.3 = (bf16[1,1,6,128,128]{4,3,2,1,0:T(8,128)(2,1)S(1)}, bf16[1,1,6,128,128]{4,3,2,1,0:T(8,128)(2,1)}, u32[]{:S(2)}) copy-start(bf16[1,1,6,128,128]{4,3,2,1,0:T(8,128)(2,1)} %param.17) | copy-start | bytes 589828
  4.9 0.7 copy-start.5
  6.7 7.1 %copy-start.1 = (bf16[512,128]{1,0:T(8,128)(2,1)S(1)}, bf16[512,128]{1,0:T(8,128)(2,1)}, u32[]{:S(2)}) copy-start(bf16[512,128]{1,0:T(8,128)(2,1)} %right_w_ref.5) | copy-start | bytes 393220
  6.7 7.1 %copy-start.2 = (bf16[512,128]{1,0:T(8,128)(2,1)S(1)}, bf16[512,128]{1,0:T(8,128)(2,1)}, u32[]{:S(2)}) copy-start(bf16[512,128]{1,0:T(8,128)(2,1)} %left_w_ref.3) | copy-start | bytes 393220
  6.7 12.7 %all-to-all-start = ((bf16[8,112,128]{2,1,0:T(8,128)(2,1)}), bf16[8,112,128]{2,1,0:T(8,128)(2,1)S(1)}, u32[]{:S(2)}, u32[]{:S(2)}) async-start(bf16[8,112,128]{2,1,0:T(8,128)(2,1)} %shard_map.152), calls=%async_computation | async-start | bytes 458752 | tf_op jit(solution)/shard_map/all_to_all | solution.py:413
  12.4 1.3 %copy-start.4 = (bf16[128,128]{1,0:T(8,128)(2,1)S(1)}, bf16[128,128]{1,0:T(8,128)(2,1)}, u32[]{:S(2)}) copy-start(bf16[128,128]{1,0:T(8,128)(2,1)} %w_ref.3) | copy-start | bytes 98308
  12.4 6.9 %collective-permute-start = (bf16[32,512]{1,0:T(8,128)(2,1)S(1)}, bf16[32,512]{1,0:T(8,128)(2,1)S(1)}, u32[]{:S(2)}, u32[]{:S(2)}) collective-permute-start(bf16[32,512]{1,0:T(8,128)(2,1)S(1)} %slice_bitcast_fusion), channel_id=1, source_target_pairs={{16,0},{32,16},{48,32},{64,48},{80,64},{96,80},{112,96},{17,1},{33... | collective-permute-start | bytes 98312 | tf_op jit(solution)/shard_map/ppermute | solution.py:437
  36.2 3.4 %collective-permute-start.3 = (bf16[8,144,128]{2,1,0:T(8,128)(2,1)S(1)}, bf16[8,144,128]{2,1,0:T(8,128)(2,1)S(1)}, u32[]{:S(2)}, u32[]{:S(2)}) collective-permute-start(bf16[8,144,128]{2,1,0:T(8,128)(2,1)S(1)} %get-tuple-element.44), channel_id=1, source_target_pairs={{0,1},{1,0},{2,3},{3,2},{4,5},{5,4},{6,7},{7,6},{8,9},{9,8},{10,11... | collective-permute-start | bytes 884744 | tf_op jit(solution)/shard_map/ppermute | solution.py:409
  77.4 5.8 %collective-permute-start.4 = (bf16[8,208,128]{2,1,0:T(8,128)(2,1)S(1)}, bf16[8,208,128]{2,1,0:T(8,128)(2,1)S(1)}, u32[]{:S(2)}, u32[]{:S(2)}) collective-permute-start(bf16[8,208,128]{2,1,0:T(8,128)(2,1)S(1)} %all_to_all.22.mine_ref), channel_id=1, source_target_pairs={{0,1},{1,0},{2,3},{3,2},{4,5},{5,4},{6,7},{7,6},{8,9},{9,8},{10,11... | collective-permute-start | bytes 1277960 | tf_op jit(solution)/shard_map/ppermute | solution.py:409
  81.6 1.5 %collective-permute-start.5 = (bf16[8,48,128]{2,1,0:T(8,128)(2,1)S(1)}, bf16[8,48,128]{2,1,0:T(8,128)(2,1)S(1)}, u32[]{:S(2)}, u32[]{:S(2)}) collective-permute-start(bf16[8,48,128]{2,1,0:T(8,128)(2,1)S(1)} %get-tuple-element.53), channel_id=1, source_target_pairs={{0,1},{1,0},{2,3},{3,2},{4,5},{5,4},{6,7},{7,6},{8,9},{9,8},{10,11... | collective-permute-start | bytes 294920 | tf_op jit(solution)/shard_map/ppermute | solution.py:409

commit v13 on v9

--- a/solution.py
+++ b/solution.py
@@ -51,7 +51,7 @@
 
 def pair_kernel(
     emb_ref, cols_ref, next_ref, left_w_ref, right_w_ref, const_ref, target_ref, w_ref,
-    keep_ref, send_ref, pred_ref, col_ref, edge_ref,
+    keep_ref, send_ref, col_ref, edge_ref,
     table, lists, list_sem, list_all, left_ref, full_ref, right_all, target_all, pred_all, row_all, col_all,
     outer_all, bias_all, w_two, out_two, back_two, b_two, scale_two, first_0, first_1, slope_0, slope_1,
 ):
@@ -215,7 +215,11 @@
     flat = [(pred_all[group] * float(width)).T for group in range(groups)]
     flat = jnp.concatenate(flat, axis=0).astype(BF16)
     for chip in range(chips):
-        pred_ref[chip] = flat[chip * 2 * slots * step : (chip + 1) * 2 * slots * step]
+        at = chip * 2 * slots * step
+        even = flat[at : at + slots * step]
+        odd = flat[at + slots * step : at + 2 * slots * step]
+        keep_ref[chip, width + 16 :, :] = jnp.where(core == 0, even, odd)
+        send_ref[chip, width + 16 :, :] = jnp.where(core == 0, odd, even)
     def folded(ref, count):
         sums = [
             jnp.sum(ref[8 * k : 8 * k + 8, :], axis=0, keepdims=True) for k in range(count)
@@ -260,25 +264,19 @@
 
     for chip in range(chips):
         even, odd = message(2 * chip), message(2 * chip + 1)
-        keep_ref[chip] = jnp.where(core == 0, even, odd)
-        send_ref[chip] = jnp.where(core == 0, odd, even)
+        keep_ref[chip, : width + 16, :] = jnp.where(core == 0, even, odd)
+        send_ref[chip, : width + 16, :] = jnp.where(core == 0, odd, even)
     col_ref[...] = col[:own]
     edge_ref[...] = col_low[own:]
 
 
-def share_kernel(sum_ref, edge_ref, row_ref, message_ref, mine_ref, send_ref):
-    core = place() & 1
+def share_kernel(sum_ref, edge_ref, row_ref, message_ref):
     chips, _, width = sum_ref.shape
     pairs = width // 2
     head = width + 16
-    slot_rows = mine_ref.shape[1]
     total = jnp.zeros((head, width), F32)
     for chip in range(chips):
         total = total + sum_ref[chip, :head, :].astype(F32)
-        first = sum_ref[chip, head : head + slot_rows, :]
-        second = sum_ref[chip, head + slot_rows :, :]
-        mine_ref[chip] = jnp.where(core == 0, first, second)
-        send_ref[chip] = jnp.where(core == 0, second, first)
     total = total.astype(BF16)
     row_ref[...] = total[:pairs]
     for bin_at in range(message_ref.shape[0]):
@@ -311,7 +309,7 @@
 
 
 def last_kernel(
-    mine_ref, other_ref, pred_mine, pred_other, left_w_ref, right_w_ref,
+    mine_ref, other_ref, sum_ref, left_w_ref, right_w_ref,
     pred_hbm, emb_hbm, left_hbm, right_hbm, bias_hbm, w_hbm, b_hbm, out_hbm,
     pred_ref, emb_ref, left_ref, right_ref, bias_ref, w_ref, b_ref, out_ref,
     both_ref, flat_ref, col_ref, flip_ref, sems,
@@ -362,8 +360,9 @@
     for source, target in ((w_ref, w_hbm), (bias_ref, bias_hbm), (b_ref, b_hbm), (out_ref, out_hbm)):
         leave(source, target)
     for chip in range(chips):
-        for ref, side in ((pred_mine, core), (pred_other, 1 - core)):
-            block = ref[chip].astype(F32)
+        for part_at, side in enumerate((core, 1 - core)):
+            at = width + 16 + part_at * slots * step
+            block = sum_ref[chip, at : at + slots * step, :].astype(F32)
             to = pl.multiple_of((2 * chip + side) * step, step)
             for slot in range(slots):
                 flip_ref[slot, pl.ds(to, step), :] = block[slot * step : (slot + 1) * step]
@@ -433,13 +432,13 @@
 
     chunk = (BATCH * step * pairs, 2 * width)
     grouped = (slots * shares * step // width + 1, width, width)
-    half = shape(chips, width + 16, width, dtype=BF16)
-    sums, sums_send, pred, col, col_edge = call(
+    head = width + 16
+    half = shape(chips, head + slots * step, width, dtype=BF16)
+    sums, sums_send, col, col_edge = call(
         pair_kernel,
         (
             half,
             half,
-            shape(chips, 2 * slots * step, width, dtype=BF16),
             shape(part, width),
             shape(edge, width, dtype=BF16),
         ),
@@ -469,15 +468,16 @@
         ],
         embeddings, emb_cols, emb_next, w_left, w_right, consts, target_all, w_pair,
     )
-    sums = (sums.astype(F32) + swapped(sums_send, "tile", 1).astype(F32)).astype(BF16)
-    sums = across(jnp.concatenate([sums, pred], axis=1), "tile", groups)
-    row, weight, pred_mine, pred_send = call(
+    met = swapped(sums_send, "tile", 1)
+    both = (sums[:, :head].astype(F32) + met[:, :head].astype(F32)).astype(BF16)
+    sums = across(
+        jnp.concatenate([both, sums[:, head:], met[:, head:]], axis=1), "tile", groups
+    )
+    row, weight = call(
         share_kernel,
         (
             shape(pairs, width, dtype=BF16),
             shape(bins, pairs + 16 + edge, width, dtype=BF16),
-            shape(chips, slots * step, width, dtype=BF16),
-            shape(chips, slots * step, width, dtype=BF16),
         ),
         [], sums, col_edge,
     )
@@ -488,8 +488,6 @@
         [], weight, row, col,
     )
     mine = across(mine, "tile", groups)
-    mine, pred_send = lax.optimization_barrier((mine, pred_send))
-    pred_other = swapped(pred_send, "tile", 1)
     other = swapped(mine, "tile", 1)
     outs = (
         shape(slots, width, width, dtype=BF16),
@@ -512,7 +510,7 @@
             pltpu.VMEM((slots, width, width), F32),
             pltpu.SemaphoreType.DMA((rows // (2 * width) + 7,)),
         ],
-        mine, other, pred_mine, pred_other, w_left, w_right, out_space=HBM,
+        mine, other, sums, w_left, w_right, out_space=HBM,
     )
     return (outs[0][None, None], *outs[1:6], outs[6][0], outs[7][0])
 

time: 84.4 us -> 85.2 us (level)
  Pallas kernels: 19.1 us -> 22.4 us
  blocking collectives: 37.4 us -> 35.8 us
    pallas_call x5, Pallas kernels: 19.1 us -> 22.4 us  [call(): pl.pallas_call(kernel, out_shape=outs, in_specs=space or [VMEM] * len(arg...]
    all_to_all x3, blocking collectives: 37.4 us -> 35.8 us  [across(): lax.all_to_all(block, axis, 0, 0, axis_index_groups=groups, tiled=True)]
    ppermute x5 -> x4, starting transfers between devices: 7.33 us -> 7.31 us  [swapped(): lax.ppermute(block, axis, [(i, i ^ bits) for i in range(lax.axis_size(axi...]
    ppermute x5 -> x4, waiting for transfers between devices: 2.75 us -> 2.74 us  [swapped(): lax.ppermute(block, axis, [(i, i ^ bits) for i in range(lax.axis_size(axi...]
  transfers between devices with their start and end apart: 7 -> 6, of which waited for: 3 -> 3; matrix products, arithmetic and copies ran while one was open for 1% -> 1% of each run, Pallas kernels for 1% -> 1%
where the time goes in v13:
time: 85.2 us; the launch traced here: 84.7 us
  blocking collectives  35.8 us (42%)
  Pallas kernels  22.4 us (26%)
  starting transfers between devices  14.4 us (17%)
  waiting for transfers between devices  8.07 us (9%)
  local copies, waits for them, and re-layouts  3.22 us (4%)
    all_to_all x3, blocking collectives, across(): lax.all_to_all(block, axis, 0, 0, axis_index_groups=groups, tiled=True)  35.8 us
    pallas_call x5, Pallas kernels, call(): pl.pallas_call(kernel, out_shape=outs, in_specs=space or [VMEM] * len(arg...  22.4 us
    ppermute x4, starting transfers between devices, swapped(): lax.ppermute(block, axis, [(i, i ^ bits) for i in range(lax.axis_size(axi...  7.31 us
    all_to_all x1, starting transfers between devices, across(): lax.all_to_all(block, axis, 0, 0, axis_index_groups=groups, tiled=True)  5.77 us
    all_to_all x1, waiting for transfers between devices, across(): lax.all_to_all(block, axis, 0, 0, axis_index_groups=groups, tiled=True)  5.33 us
    unnamed x19, local copies, waits for them, and re-layouts  3.13 us
    ppermute x4, waiting for transfers between devices, swapped(): lax.ppermute(block, axis, [(i, i ^ bits) for i in range(lax.axis_size(axi...  2.74 us
  transfers between devices with their start and end apart: 6, of which 3 were waited for; matrix products, arithmetic and copies ran while one was open for 1% of the time, Pallas kernels for 1%

profile of v13, /device:TPU:1, one launch (start us, length us, event | category | flops | bytes accessed | tf_op | source)
XLA Modules:
  0.0 84.7 jit_solution(16865812356273346051)
XLA Ops:
  0.6 0.0 copy-start
  0.6 1.5 %collective-permute-start.1 = (s32[3,1,6]{2,1,0:T(1,128)}, s32[3,1,6]{2,1,0:T(1,128)S(1)}, u32[]{:S(2)}, u32[]{:S(2)}) collective-permute-start(s32[3,1,6]{2,1,0:T(1,128)} %bitcast.21), channel_id=1, source_target_pairs={{0,1},{1,0},{2,3},{3,2},{4,5},{5,4},{6,7},{7,6},{8,9},{9,8},{10,11... | collective-permute-start | bytes 224 | tf_op jit(solution)/shard_map/ppermute | solution.py:392
  2.1 0.1 collective-permute-start.2
  2.2 0.8 %dynamic-slice_bitcast_fusion.1 = (bf16[8,1,8,512]{3,2,0,1:T(8,128)(2,1)S(1)}, bf16[64,512]{1,0:T(8,128)(2,1)S(1)}) fusion(bf16[8,16,8,512]{3,2,1,0:T(8,128)(2,1)} %bitcast.18, s32[]{:T(128)S(6)} %select_n.3), kind=kLoop, calls=%fused_computation.3 | loop fusion | bytes 196612
  3.1 1.3 %collective-permute-start = (bf16[32,512]{1,0:T(8,128)(2,1)S(1)}, bf16[32,512]{1,0:T(8,128)(2,1)S(1)}, u32[]{:S(2)}, u32[]{:S(2)}) collective-permute-start(bf16[32,512]{1,0:T(8,128)(2,1)S(1)} %slice_bitcast_fusion), channel_id=1, source_target_pairs={{16,0},{32,16},{48,32},{64,48},{80,64},{96,80},{112,96},{17,1},{33... | collective-permute-start | bytes 98312 | tf_op jit(solution)/shard_map/ppermute | solution.py:420
  4.4 0.1 pad.6.clone
  4.5 0.0 collective-permute-done.1.list_other
  4.5 0.0 collective-permute-done.2.target_other
  4.5 0.9 %copy-done.3 = bf16[1,1,6,128,128]{4,3,2,1,0:T(8,128)(2,1)S(1)} copy-done((bf16[1,1,6,128,128]{4,3,2,1,0:T(8,128)(2,1)S(1)}, bf16[1,1,6,128,128]{4,3,2,1,0:T(8,128)(2,1)}, u32[]{:S(2)}) %copy-start.3) | copy-done | bytes 196632
  5.4 0.7 copy-done.5
  6.1 1.1 %shard_map.152 = bf16[8,112,128]{2,1,0:T(8,128)(2,1)} custom-call(s32[3,1,6]{2,1,0:T(1,128)S(1)} %bitcast.22, s32[3,1,6]{2,1,0:T(1,128)S(1)} %collective-permute-done.1.list_other, bf16[6,128,128]{2,1,0:T(8,128)(2,1)S(1)} %bitcast.20, bf16[6,128,128]{2,1,0:T(8,128)(2,1)S(1)} %collective-permute-done.2.target_other), custom_call_target="tpu_custom_call" | custom-call | tf_op jit(solution)/shard_map/pallas_call | solution.py:381
  7.2 5.8 %all-to-all-start = ((bf16[8,112,128]{2,1,0:T(8,128)(2,1)}), bf16[8,112,128]{2,1,0:T(8,128)(2,1)S(1)}, u32[]{:S(2)}, u32[]{:S(2)}) async-start(bf16[8,112,128]{2,1,0:T(8,128)(2,1)} %shard_map.152), calls=%async_computation | async-start | bytes 458752 | tf_op jit(solution)/shard_map/all_to_all | solution.py:396
  13.0 0.0 copy-start.8
  13.0 0.0 copy-done.6
  13.0 0.6 copy-done.7
  13.6 0.0 copy-done.8
  13.6 0.1 maximum_maximum_fusion.const_ref
  13.7 0.0 collective-permute-done.next_ref
  13.7 5.3 %all-to-all-done.target_ref = bf16[8,112,128]{2,1,0:T(8,128)(2,1)S(1)} async-done(((bf16[8,112,128]{2,1,0:T(8,128)(2,1)}), bf16[8,112,128]{2,1,0:T(8,128)(2,1)S(1)}, u32[]{:S(2)}, u32[]{:S(2)}) %all-to-all-start) | async-done | bytes 229408 | tf_op jit(solution)/shard_map/all_to_all | solution.py:396
  19.0 0.0 copy-done
  19.0 0.0 copy-done.1
  19.0 0.0 copy-done.2
  19.0 19.6 %shard_map.153 = (bf16[8,192,128]{2,1,0:T(8,128)(2,1)S(1)}, bf16[8,192,128]{2,1,0:T(8,128)(2,1)S(1)}, f32[64,128]{1,0:T(8,128)S(1)}, bf16[32,128]{1,0:T(8,128)(2,1)S(1)}) custom-call(bf16[1024,512]{1,0:T(8,128)(2,1)S(1)} %copy-done, bf16[64,512]{1,0:T(8,128)(2,1)S(1)} %get-tuple-element.37.cols_ref, bf16[32,512]{1,0:T(8,128)(2,1)S(1)} %collective-permute-done.next_ref, ...), custom_call_target="tpu_custom_call" | custom-call | tf_op jit(solution)/shard_map/pallas_call | solution.py:381
  38.6 1.9 %collective-permute-start.3 = (bf16[8,192,128]{2,1,0:T(8,128)(2,1)S(1)}, bf16[8,192,128]{2,1,0:T(8,128)(2,1)S(1)}, u32[]{:S(2)}, u32[]{:S(2)}) collective-permute-start(bf16[8,192,128]{2,1,0:T(8,128)(2,1)S(1)} %get-tuple-element.23), channel_id=1, source_target_pairs={{0,1},{1,0},{2,3},{3,2},{4,5},{5,4},{6,7},{7,6},{8,9},{9,8},{10,11... | collective-permute-start | bytes 1179656 | tf_op jit(solution)/shard_map/ppermute | solution.py:392
  40.5 1.3 %collective-permute-done.3 = bf16[8,192,128]{2,1,0:T(8,128)(2,1)S(1)} collective-permute-done((bf16[8,192,128]{2,1,0:T(8,128)(2,1)S(1)}, bf16[8,192,128]{2,1,0:T(8,128)(2,1)S(1)}, u32[]{:S(2)}, u32[]{:S(2)}) %collective-permute-start.3) | collective-permute-done | bytes 393248 | tf_op jit(solution)/shard_map/ppermute | solution.py:392
  41.8 0.1 add_convert_fusion
  42.0 11.6 %all_to_all.20.sum_ref = bf16[8,240,128]{2,1,0:T(8,128)(2,1)S(1)} all-to-all(bf16[8,240,128]{2,1,0:T(8,128)(2,1)S(1)} %pad_maximum_fusion), channel_id=1, replica_groups={{0,2,4,6,8,10,12,14},{1,3,5,7,9,11,13,15},{16,18,20,22,24,26,28,30},{17..., dimensions={0} | all-to-all | bytes 983040 | tf_op jit(solution)/shard_map/all_to_all | solution.py:396
  53.6 14.7 %all_to_all.21.met_ref = bf16[8,112,128]{2,1,0:T(8,128)(2,1)S(1)} all-to-all(bf16[8,112,128]{2,1,0:T(8,128)(2,1)S(1)} %get-tuple-element.25), channel_id=1, replica_groups=mesh['bin'=8,'tile'=16] {'bin'}, dimensions={0} | all-to-all | bytes 458752 | tf_op jit(solution)/shard_map/all_to_all | solution.py:396
  68.4 9.5 %all_to_all.22.mine_ref = bf16[8,208,128]{2,1,0:T(8,128)(2,1)S(1)} all-to-all(bf16[8,208,128]{2,1,0:T(8,128)(2,1)S(1)} %shard_map.155), channel_id=1, replica_groups={{0,2,4,6,8,10,12,14},{1,3,5,7,9,11,13,15},{16,18,20,22,24,26,28,30},{17..., dimensions={0} | all-to-all | bytes 851968 | tf_op jit(solution)/shard_map/all_to_all | solution.py:396
  77.9 3.8 %collective-permute-start.4 = (bf16[8,208,128]{2,1,0:T(8,128)(2,1)S(1)}, bf16[8,208,128]{2,1,0:T(8,128)(2,1)S(1)}, u32[]{:S(2)}, u32[]{:S(2)}) collective-permute-start(bf16[8,208,128]{2,1,0:T(8,128)(2,1)S(1)} %all_to_all.22.mine_ref), channel_id=1, source_target_pairs={{0,1},{1,0},{2,3},{3,2},{4,5},{5,4},{6,7},{7,6},{8,9},{9,8},{10,11... | collective-permute-start | bytes 1277960 | tf_op jit(solution)/shard_map/ppermute | solution.py:392
  81.7 1.4 %collective-permute-done.4.other_ref = bf16[8,208,128]{2,1,0:T(8,128)(2,1)S(1)} collective-permute-done((bf16[8,208,128]{2,1,0:T(8,128)(2,1)S(1)}, bf16[8,208,128]{2,1,0:T(8,128)(2,1)S(1)}, u32[]{:S(2)}, u32[]{:S(2)}) %collective-permute-start.4) | collective-permute-done | bytes 426016 | tf_op jit(solution)/shard_map/ppermute | solution.py:392
  83.1 1.6 %shard_map.156 = (bf16[6,128,128]{2,1,0:T(8,128)(2,1)}, bf16[1024,512]{1,0:T(8,128)(2,1)}, f32[512,128]{1,0:T(8,128)}, f32[512,128]{1,0:T(8,128)}, f32[5,128]{1,...) custom-call(bf16[8,208,128]{2,1,0:T(8,128)(2,1)S(1)} %all_to_all.22.mine_ref, ...), custom_call_target="tpu_custom_call" | custom-call | tf_op jit(solution)/shard_map/pallas_call | solution.py:381
  (14 shorter events, 0.2 us)
Async XLA Ops:
  0.6 18.4 %copy-start = (bf16[1024,512]{1,0:T(8,128)(2,1)S(1)}, bf16[1024,512]{1,0:T(8,128)(2,1)}, u32[]{:S(2)}) copy-start(bf16[1024,512]{1,0:T(8,128)(2,1)} %emb_ref.1) | copy-start | bytes 3145732
  0.6 3.8 %collective-permute-start.1 = (s32[3,1,6]{2,1,0:T(1,128)}, s32[3,1,6]{2,1,0:T(1,128)S(1)}, u32[]{:S(2)}, u32[]{:S(2)}) collective-permute-start(s32[3,1,6]{2,1,0:T(1,128)} %bitcast.21), channel_id=1, source_target_pairs={{0,1},{1,0},{2,3},{3,2},{4,5},{5,4},{6,7},{7,6},{8,9},{9,8},{10,11... | collective-permute-start | bytes 224 | tf_op jit(solution)/shard_map/ppermute | solution.py:392
  2.1 2.3 %collective-permute-start.2 = (bf16[6,128,128]{2,1,0:T(8,128)(2,1)}, bf16[6,128,128]{2,1,0:T(8,128)(2,1)S(1)}, u32[]{:S(2)}, u32[]{:S(2)}) collective-permute-start(bf16[6,128,128]{2,1,0:T(8,128)(2,1)} %bitcast.19), channel_id=1, source_target_pairs={{0,1},{1,0},{2,3},{3,2},{4,5},{5,4},{6,7},{7,6},{8,9},{9,8},{10,11... | collective-permute-start | bytes 589832 | tf_op jit(solution)/shard_map/ppermute | solution.py:392
  3.1 10.6 %collective-permute-start = (bf16[32,512]{1,0:T(8,128)(2,1)S(1)}, bf16[32,512]{1,0:T(8,128)(2,1)S(1)}, u32[]{:S(2)}, u32[]{:S(2)}) collective-permute-start(bf16[32,512]{1,0:T(8,128)(2,1)S(1)} %slice_bitcast_fusion), channel_id=1, source_target_pairs={{16,0},{32,16},{48,32},{64,48},{80,64},{96,80},{112,96},{17,1},{33... | collective-permute-start | bytes 98312 | tf_op jit(solution)/shard_map/ppermute | solution.py:420
  4.5 0.9 %copy-start.3 = (bf16[1,1,6,128,128]{4,3,2,1,0:T(8,128)(2,1)S(1)}, bf16[1,1,6,128,128]{4,3,2,1,0:T(8,128)(2,1)}, u32[]{:S(2)}) copy-start(bf16[1,1,6,128,128]{4,3,2,1,0:T(8,128)(2,1)} %param.17) | copy-start | bytes 589828
  5.4 0.7 copy-start.5
  7.2 5.8 %copy-start.6 = (f32[5,128]{1,0:T(8,128)S(1)}, f32[5,128]{1,0:T(8,128)}, u32[]{:S(2)}) copy-start(f32[5,128]{1,0:T(8,128)} %param.12) | copy-start | bytes 7684
  7.2 11.9 %copy-start.1 = (bf16[512,128]{1,0:T(8,128)(2,1)S(1)}, bf16[512,128]{1,0:T(8,128)(2,1)}, u32[]{:S(2)}) copy-start(bf16[512,128]{1,0:T(8,128)(2,1)} %left_w_ref.3) | copy-start | bytes 393220
  7.2 11.9 %copy-start.2 = (bf16[512,128]{1,0:T(8,128)(2,1)S(1)}, bf16[512,128]{1,0:T(8,128)(2,1)}, u32[]{:S(2)}) copy-start(bf16[512,128]{1,0:T(8,128)(2,1)} %right_w_ref.3) | copy-start | bytes 393220
  7.2 11.9 %copy-start.4 = (bf16[128,128]{1,0:T(8,128)(2,1)S(1)}, bf16[128,128]{1,0:T(8,128)(2,1)}, u32[]{:S(2)}) copy-start(bf16[128,128]{1,0:T(8,128)(2,1)} %w_ref.1) | copy-start | bytes 98308
  7.2 11.8 %all-to-all-start = ((bf16[8,112,128]{2,1,0:T(8,128)(2,1)}), bf16[8,112,128]{2,1,0:T(8,128)(2,1)S(1)}, u32[]{:S(2)}, u32[]{:S(2)}) async-start(bf16[8,112,128]{2,1,0:T(8,128)(2,1)} %shard_map.152), calls=%async_computation | async-start | bytes 458752 | tf_op jit(solution)/shard_map/all_to_all | solution.py:396
  13.0 0.7 copy-start.7
  13.0 0.7 copy-start.8
  38.6 3.2 %collective-permute-start.3 = (bf16[8,192,128]{2,1,0:T(8,128)(2,1)S(1)}, bf16[8,192,128]{2,1,0:T(8,128)(2,1)S(1)}, u32[]{:S(2)}, u32[]{:S(2)}) collective-permute-start(bf16[8,192,128]{2,1,0:T(8,128)(2,1)S(1)} %get-tuple-element.23), channel_id=1, source_target_pairs={{0,1},{1,0},{2,3},{3,2},{4,5},{5,4},{6,7},{7,6},{8,9},{9,8},{10,11... | collective-permute-start | bytes 1179656 | tf_op jit(solution)/shard_map/ppermute | solution.py:392
  77.9 5.2 %collective-permute-start.4 = (bf16[8,208,128]{2,1,0:T(8,128)(2,1)S(1)}, bf16[8,208,128]{2,1,0:T(8,128)(2,1)S(1)}, u32[]{:S(2)}, u32[]{:S(2)}) collective-permute-start(bf16[8,208,128]{2,1,0:T(8,128)(2,1)S(1)} %all_to_all.22.mine_ref), channel_id=1, source_target_pairs={{0,1},{1,0},{2,3},{3,2},{4,5},{5,4},{6,7},{7,6},{8,9},{9,8},{10,11... | collective-permute-start | bytes 1277960 | tf_op jit(solution)/shard_map/ppermute | solution.py:392

commit v14 on v9

--- a/solution.py
+++ b/solution.py
@@ -7,7 +7,7 @@
 
 F32 = jnp.float32
 BF16 = jnp.bfloat16
-BATCH = 2
+BATCH = 3
 NEVER = -1e38
 TINY = 1e-30
 VMEM = pl.BlockSpec(memory_space=pltpu.VMEM)

time: 84.4 us -> 86.9 us (1.030); the launches traced: 83.1 us -> 86.7 us
  Pallas kernels: 19.1 us -> 21.3 us
  blocking collectives: 37.4 us -> 38.7 us
    pallas_call x5, Pallas kernels: 19.1 us -> 21.3 us  [call(): pl.pallas_call(kernel, out_shape=outs, in_specs=space or [VMEM] * len(arg...]
    all_to_all x3, blocking collectives: 37.4 us -> 38.7 us  [across(): lax.all_to_all(block, axis, 0, 0, axis_index_groups=groups, tiled=True)]
where the time goes in v14:
time: 86.9 us; the launch traced here: 86.7 us
  blocking collectives  38.7 us (45%)
  Pallas kernels  21.3 us (25%)
  starting transfers between devices  14.5 us (17%)
  waiting for transfers between devices  8.08 us (9%)
  local copies, waits for them, and re-layouts  3.2 us (4%)
    all_to_all x3, blocking collectives, across(): lax.all_to_all(block, axis, 0, 0, axis_index_groups=groups, tiled=True)  38.7 us
    pallas_call x5, Pallas kernels, call(): pl.pallas_call(kernel, out_shape=outs, in_specs=space or [VMEM] * len(arg...  21.3 us
    ppermute x5, starting transfers between devices, swapped(): lax.ppermute(block, axis, [(i, i ^ bits) for i in range(lax.axis_size(axi...  7.41 us
    all_to_all x1, starting transfers between devices, across(): lax.all_to_all(block, axis, 0, 0, axis_index_groups=groups, tiled=True)  5.77 us
    all_to_all x1, waiting for transfers between devices, across(): lax.all_to_all(block, axis, 0, 0, axis_index_groups=groups, tiled=True)  5.33 us
    unnamed x19, local copies, waits for them, and re-layouts  3.13 us
    ppermute x5, waiting for transfers between devices, swapped(): lax.ppermute(block, axis, [(i, i ^ bits) for i in range(lax.axis_size(axi...  2.75 us
  transfers between devices with their start and end apart: 7, of which 3 were waited for; matrix products, arithmetic and copies ran while one was open for 1% of the time, Pallas kernels for 1%

profile of v14, /device:TPU:1, one launch (start us, length us, event | category | flops | bytes accessed | tf_op | source)
XLA Modules:
  0.0 86.7 jit_solution(7346942744044818130)
XLA Ops:
  0.6 0.0 copy-start
  0.6 1.5 %collective-permute-start.1 = (s32[3,1,6]{2,1,0:T(1,128)}, s32[3,1,6]{2,1,0:T(1,128)S(1)}, u32[]{:S(2)}, u32[]{:S(2)}) collective-permute-start(s32[3,1,6]{2,1,0:T(1,128)} %bitcast.21), channel_id=1, source_target_pairs={{0,1},{1,0},{2,3},{3,2},{4,5},{5,4},{6,7},{7,6},{8,9},{9,8},{10,11... | collective-permute-start | bytes 224 | tf_op jit(solution)/shard_map/ppermute | solution.py:393
  2.1 0.1 collective-permute-start.2
  2.2 0.8 dynamic-slice_bitcast_fusion.1
  3.1 1.3 %collective-permute-start = (bf16[32,512]{1,0:T(8,128)(2,1)S(1)}, bf16[32,512]{1,0:T(8,128)(2,1)S(1)}, u32[]{:S(2)}, u32[]{:S(2)}) collective-permute-start(bf16[32,512]{1,0:T(8,128)(2,1)S(1)} %slice_bitcast_fusion), channel_id=1, source_target_pairs={{16,0},{32,16},{48,32},{64,48},{80,64},{96,80},{112,96},{17,1},{33... | collective-permute-start | bytes 98312 | tf_op jit(solution)/shard_map/ppermute | solution.py:421
  4.4 0.1 pad.5.clone
  4.5 0.0 collective-permute-done.1.list_other
  4.5 0.0 collective-permute-done.2.target_other
  4.5 0.9 %copy-done.3 = bf16[1,1,6,128,128]{4,3,2,1,0:T(8,128)(2,1)S(1)} copy-done((bf16[1,1,6,128,128]{4,3,2,1,0:T(8,128)(2,1)S(1)}, bf16[1,1,6,128,128]{4,3,2,1,0:T(8,128)(2,1)}, u32[]{:S(2)}) %copy-start.3) | copy-done | bytes 196632
  5.4 0.7 copy-done.5
  6.1 1.1 %shard_map.152 = bf16[8,112,128]{2,1,0:T(8,128)(2,1)} custom-call(s32[3,1,6]{2,1,0:T(1,128)S(1)} %bitcast.22, s32[3,1,6]{2,1,0:T(1,128)S(1)} %collective-permute-done.1.list_other, bf16[6,128,128]{2,1,0:T(8,128)(2,1)S(1)} %bitcast.20, bf16[6,128,128]{2,1,0:T(8,128)(2,1)S(1)} %collective-permute-done.2.target_other), custom_call_target="tpu_custom_call" | custom-call | tf_op jit(solution)/shard_map/pallas_call | solution.py:382
  7.2 5.8 %all-to-all-start = ((bf16[8,112,128]{2,1,0:T(8,128)(2,1)}), bf16[8,112,128]{2,1,0:T(8,128)(2,1)S(1)}, u32[]{:S(2)}, u32[]{:S(2)}) async-start(bf16[8,112,128]{2,1,0:T(8,128)(2,1)} %shard_map.152), calls=%async_computation | async-start | bytes 458752 | tf_op jit(solution)/shard_map/all_to_all | solution.py:397
  13.0 0.0 copy-start.8
  13.0 0.0 copy-done.6
  13.0 0.6 copy-done.7
  13.6 0.0 copy-done.8
  13.6 0.1 maximum_maximum_fusion.const_ref
  13.7 0.0 collective-permute-done.next_ref
  13.7 5.3 %all-to-all-done.target_ref = bf16[8,112,128]{2,1,0:T(8,128)(2,1)S(1)} async-done(((bf16[8,112,128]{2,1,0:T(8,128)(2,1)}), bf16[8,112,128]{2,1,0:T(8,128)(2,1)S(1)}, u32[]{:S(2)}, u32[]{:S(2)}) %all-to-all-start) | async-done | bytes 229408 | tf_op jit(solution)/shard_map/all_to_all | solution.py:397
  19.0 18.4 %shard_map.153 = (bf16[8,144,128]{2,1,0:T(8,128)(2,1)S(1)}, bf16[8,144,128]{2,1,0:T(8,128)(2,1)S(1)}, bf16[8,96,128]{2,1,0:T(8,128)(2,1)S(1)}, f32[64,128]{1,0:T(8,128)S(1)}, bf16[32,128]{1,0:T(8,128)(2,1)S(1)}) custom-call(bf16[1024,512]{1,0:T(8,128)(2,1)S(1)} %copy-done, bf16[64,512]{1,0:T(8,128)(2,1)S(1)} %get-tuple-element.47.cols_ref, ...), custom_call_target="tpu_custom_call" | custom-call | tf_op jit(solution)/shard_map/pallas_call | solution.py:382
  37.5 1.9 %collective-permute-start.3 = (bf16[8,144,128]{2,1,0:T(8,128)(2,1)S(1)}, bf16[8,144,128]{2,1,0:T(8,128)(2,1)S(1)}, u32[]{:S(2)}, u32[]{:S(2)}) collective-permute-start(bf16[8,144,128]{2,1,0:T(8,128)(2,1)S(1)} %get-tuple-element.28), channel_id=1, source_target_pairs={{0,1},{1,0},{2,3},{3,2},{4,5},{5,4},{6,7},{7,6},{8,9},{9,8},{10,11... | collective-permute-start | bytes 884744 | tf_op jit(solution)/shard_map/ppermute | solution.py:393
  39.4 1.2 %collective-permute-done.3 = bf16[8,144,128]{2,1,0:T(8,128)(2,1)S(1)} collective-permute-done((bf16[8,144,128]{2,1,0:T(8,128)(2,1)S(1)}, bf16[8,144,128]{2,1,0:T(8,128)(2,1)S(1)}, u32[]{:S(2)}, u32[]{:S(2)}) %collective-permute-start.3) | collective-permute-done | bytes 294944 | tf_op jit(solution)/shard_map/ppermute | solution.py:393
  40.6 0.1 add_convert_fusion
  40.7 11.9 %all_to_all.20.sum_ref = bf16[8,240,128]{2,1,0:T(8,128)(2,1)S(1)} all-to-all(bf16[8,240,128]{2,1,0:T(8,128)(2,1)S(1)} %pad_maximum_fusion), channel_id=1, replica_groups={{0,2,4,6,8,10,12,14},{1,3,5,7,9,11,13,15},{16,18,20,22,24,26,28,30},{17..., dimensions={0} | all-to-all | bytes 983040 | tf_op jit(solution)/shard_map/all_to_all | solution.py:397
  52.6 0.1 shard_map.154
  52.7 17.3 %all_to_all.21.met_ref = bf16[8,112,128]{2,1,0:T(8,128)(2,1)S(1)} all-to-all(bf16[8,112,128]{2,1,0:T(8,128)(2,1)S(1)} %get-tuple-element.31), channel_id=1, replica_groups=mesh['bin'=8,'tile'=16] {'bin'}, dimensions={0} | all-to-all | bytes 458752 | tf_op jit(solution)/shard_map/all_to_all | solution.py:397
  70.1 9.5 %all_to_all.22.mine_ref = bf16[8,208,128]{2,1,0:T(8,128)(2,1)S(1)} all-to-all(bf16[8,208,128]{2,1,0:T(8,128)(2,1)S(1)} %shard_map.155), channel_id=1, replica_groups={{0,2,4,6,8,10,12,14},{1,3,5,7,9,11,13,15},{16,18,20,22,24,26,28,30},{17..., dimensions={0} | all-to-all | bytes 851968 | tf_op jit(solution)/shard_map/all_to_all | solution.py:397
  79.5 3.9 %collective-permute-start.4 = (bf16[8,208,128]{2,1,0:T(8,128)(2,1)S(1)}, bf16[8,208,128]{2,1,0:T(8,128)(2,1)S(1)}, u32[]{:S(2)}, u32[]{:S(2)}) collective-permute-start(bf16[8,208,128]{2,1,0:T(8,128)(2,1)S(1)} %all_to_all.22.mine_ref), channel_id=1, source_target_pairs={{0,1},{1,0},{2,3},{3,2},{4,5},{5,4},{6,7},{7,6},{8,9},{9,8},{10,11... | collective-permute-start | bytes 1277960 | tf_op jit(solution)/shard_map/ppermute | solution.py:393
  83.5 0.0 collective-permute-start.5
  83.5 1.5 %collective-permute-done.5.pred_other = bf16[8,48,128]{2,1,0:T(8,128)(2,1)S(1)} collective-permute-done((bf16[8,48,128]{2,1,0:T(8,128)(2,1)S(1)}, bf16[8,48,128]{2,1,0:T(8,128)(2,1)S(1)}, u32[]{:S(2)}, u32[]{:S(2)}) %collective-permute-start.5) | collective-permute-done | bytes 98336 | tf_op jit(solution)/shard_map/ppermute | solution.py:393
  85.0 0.0 collective-permute-done.4.other_ref
  85.0 1.6 %shard_map.156 = (bf16[6,128,128]{2,1,0:T(8,128)(2,1)}, bf16[1024,512]{1,0:T(8,128)(2,1)}, f32[512,128]{1,0:T(8,128)}, f32[512,128]{1,0:T(8,128)}, f32[5,128]{1,...) custom-call(bf16[8,208,128]{2,1,0:T(8,128)(2,1)S(1)} %all_to_all.22.mine_ref, ...), custom_call_target="tpu_custom_call" | custom-call | tf_op jit(solution)/shard_map/pallas_call | solution.py:382
  (14 shorter events, 0.1 us)
Async XLA Ops:
  0.6 18.4 %copy-start = (bf16[1024,512]{1,0:T(8,128)(2,1)S(1)}, bf16[1024,512]{1,0:T(8,128)(2,1)}, u32[]{:S(2)}) copy-start(bf16[1024,512]{1,0:T(8,128)(2,1)} %emb_ref.1) | copy-start | bytes 3145732
  0.6 3.8 %collective-permute-start.1 = (s32[3,1,6]{2,1,0:T(1,128)}, s32[3,1,6]{2,1,0:T(1,128)S(1)}, u32[]{:S(2)}, u32[]{:S(2)}) collective-permute-start(s32[3,1,6]{2,1,0:T(1,128)} %bitcast.21), channel_id=1, source_target_pairs={{0,1},{1,0},{2,3},{3,2},{4,5},{5,4},{6,7},{7,6},{8,9},{9,8},{10,11... | collective-permute-start | bytes 224 | tf_op jit(solution)/shard_map/ppermute | solution.py:393
  2.1 2.3 %collective-permute-start.2 = (bf16[6,128,128]{2,1,0:T(8,128)(2,1)}, bf16[6,128,128]{2,1,0:T(8,128)(2,1)S(1)}, u32[]{:S(2)}, u32[]{:S(2)}) collective-permute-start(bf16[6,128,128]{2,1,0:T(8,128)(2,1)} %bitcast.19), channel_id=1, source_target_pairs={{0,1},{1,0},{2,3},{3,2},{4,5},{5,4},{6,7},{7,6},{8,9},{9,8},{10,11... | collective-permute-start | bytes 589832 | tf_op jit(solution)/shard_map/ppermute | solution.py:393
  3.1 10.6 %collective-permute-start = (bf16[32,512]{1,0:T(8,128)(2,1)S(1)}, bf16[32,512]{1,0:T(8,128)(2,1)S(1)}, u32[]{:S(2)}, u32[]{:S(2)}) collective-permute-start(bf16[32,512]{1,0:T(8,128)(2,1)S(1)} %slice_bitcast_fusion), channel_id=1, source_target_pairs={{16,0},{32,16},{48,32},{64,48},{80,64},{96,80},{112,96},{17,1},{33... | collective-permute-start | bytes 98312 | tf_op jit(solution)/shard_map/ppermute | solution.py:421
  4.5 0.9 %copy-start.3 = (bf16[1,1,6,128,128]{4,3,2,1,0:T(8,128)(2,1)S(1)}, bf16[1,1,6,128,128]{4,3,2,1,0:T(8,128)(2,1)}, u32[]{:S(2)}) copy-start(bf16[1,1,6,128,128]{4,3,2,1,0:T(8,128)(2,1)} %param.17) | copy-start | bytes 589828
  5.4 0.7 copy-start.5
  7.2 5.8 %copy-start.6 = (f32[5,128]{1,0:T(8,128)S(1)}, f32[5,128]{1,0:T(8,128)}, u32[]{:S(2)}) copy-start(f32[5,128]{1,0:T(8,128)} %param.12) | copy-start | bytes 7684
  7.2 11.9 %copy-start.1 = (bf16[512,128]{1,0:T(8,128)(2,1)S(1)}, bf16[512,128]{1,0:T(8,128)(2,1)}, u32[]{:S(2)}) copy-start(bf16[512,128]{1,0:T(8,128)(2,1)} %left_w_ref.3) | copy-start | bytes 393220
  7.2 11.9 %copy-start.2 = (bf16[512,128]{1,0:T(8,128)(2,1)S(1)}, bf16[512,128]{1,0:T(8,128)(2,1)}, u32[]{:S(2)}) copy-start(bf16[512,128]{1,0:T(8,128)(2,1)} %right_w_ref.3) | copy-start | bytes 393220
  7.2 11.9 %copy-start.4 = (bf16[128,128]{1,0:T(8,128)(2,1)S(1)}, bf16[128,128]{1,0:T(8,128)(2,1)}, u32[]{:S(2)}) copy-start(bf16[128,128]{1,0:T(8,128)(2,1)} %w_ref.1) | copy-start | bytes 98308
  7.2 11.8 %all-to-all-start = ((bf16[8,112,128]{2,1,0:T(8,128)(2,1)}), bf16[8,112,128]{2,1,0:T(8,128)(2,1)S(1)}, u32[]{:S(2)}, u32[]{:S(2)}) async-start(bf16[8,112,128]{2,1,0:T(8,128)(2,1)} %shard_map.152), calls=%async_computation | async-start | bytes 458752 | tf_op jit(solution)/shard_map/all_to_all | solution.py:397
  13.0 0.7 copy-start.7
  13.0 0.7 copy-start.8
  37.5 3.1 %collective-permute-start.3 = (bf16[8,144,128]{2,1,0:T(8,128)(2,1)S(1)}, bf16[8,144,128]{2,1,0:T(8,128)(2,1)S(1)}, u32[]{:S(2)}, u32[]{:S(2)}) collective-permute-start(bf16[8,144,128]{2,1,0:T(8,128)(2,1)S(1)} %get-tuple-element.28), channel_id=1, source_target_pairs={{0,1},{1,0},{2,3},{3,2},{4,5},{5,4},{6,7},{7,6},{8,9},{9,8},{10,11... | collective-permute-start | bytes 884744 | tf_op jit(solution)/shard_map/ppermute | solution.py:393
  79.5 5.5 %collective-permute-start.4 = (bf16[8,208,128]{2,1,0:T(8,128)(2,1)S(1)}, bf16[8,208,128]{2,1,0:T(8,128)(2,1)S(1)}, u32[]{:S(2)}, u32[]{:S(2)}) collective-permute-start(bf16[8,208,128]{2,1,0:T(8,128)(2,1)S(1)} %all_to_all.22.mine_ref), channel_id=1, source_target_pairs={{0,1},{1,0},{2,3},{3,2},{4,5},{5,4},{6,7},{7,6},{8,9},{9,8},{10,11... | collective-permute-start | bytes 1277960 | tf_op jit(solution)/shard_map/ppermute | solution.py:393
  83.5 1.5 %collective-permute-start.5 = (bf16[8,48,128]{2,1,0:T(8,128)(2,1)S(1)}, bf16[8,48,128]{2,1,0:T(8,128)(2,1)S(1)}, u32[]{:S(2)}, u32[]{:S(2)}) collective-permute-start(bf16[8,48,128]{2,1,0:T(8,128)(2,1)S(1)} %get-tuple-element.37), channel_id=1, source_target_pairs={{0,1},{1,0},{2,3},{3,2},{4,5},{5,4},{6,7},{7,6},{8,9},{9,8},{10,11... | collective-permute-start | bytes 294920 | tf_op jit(solution)/shard_map/ppermute | solution.py:393
